TPU v7x, 32 devices: a whole 2x2x4 slice. The times are simulated.
32 devices in a mesh: req: 16 (over z, y, x), tp: 2 (over core).
Axes of the slice: x: 2, y: 2, z: 4, core: 2. Of those that a mesh axis runs over, the one named last changes fastest.
Arguments:
- tokens: bfloat16 [3072, 1536], P('req', 'tp'), may hold values from -6 to 6
- video_lengths: int32 [5], replicated, may hold values from 1 to 1920, 3072 in all
- timestep: int32 [1], replicated, may hold values from 1 to 1000
- time_weight: float32 [256, 4608], replicated, may hold values from -0.375 to 0.375
- block_mod: float32 [3, 1536], replicated, may hold values from -3 to 3
- w_query: bfloat16 [1536, 1536], P(None, 'tp')
- w_key: bfloat16 [1536, 1536], P(None, 'tp')
- w_value: bfloat16 [1536, 1536], P(None, 'tp'), may hold values from -0.15625 to 0.15625
- w_out: bfloat16 [1536, 1536], P('tp'), may hold values from -0.15625 to 0.15625
Outputs:
- velocity: bfloat16 [3072, 1536], P('req', 'tp')
- stepped: bfloat16 [3072, 1536], P('req', 'tp')
Inputs may be any that keep to these rules, and one draw needn't show every extreme that they name: `video_lengths`: the videos' lengths in packing order; they sum to 3072 and the longest has exactly 1920 tokens.
All inputs are finite; a program needn't handle non-finite values.
Results may differ from a plain program's by a relative error of at most 0.017.
Values may be sent and summed in bfloat16 or wider, within the bound.
No kernel may reach another device: no remote copies, remote signals or barrier semaphores. Data moves between devices by JAX's collectives and lax.ppermute only.
A program may use at most 256 MiB of HBM per device.

v0:
```python
import math

import jax
import jax.numpy as jnp
from jax import lax
from jax.sharding import PartitionSpec as P

HEAD_DIM = 128
STEPS = 1000


def noise_level(step_value):
    frac = step_value / STEPS
    return 5.0 * frac / (1.0 + 4.0 * frac)


def on_device(
    tokens, video_lengths, timestep, time_weight, block_mod, w_query, w_key, w_value, w_out
):
    tok_rows = tokens.shape[0]
    width = time_weight.shape[1] // 3
    full_rows = lax.all_gather(tokens, "tp", axis=1, tiled=True)
    time_value = timestep[0].astype(jnp.float32)
    sigma = noise_level(time_value)
    delta_sigma = noise_level(time_value - 1.0) - sigma
    half_freq = time_weight.shape[0] // 2
    frequency = jnp.exp(-math.log(10000.0) * jnp.arange(half_freq, dtype=jnp.float32) / half_freq)
    angle = 1000.0 * sigma * frequency
    embedding = jnp.concatenate([jnp.cos(angle), jnp.sin(angle)])
    modulation = jnp.dot(
        jax.nn.silu(embedding)[None, :],
        time_weight,
        precision=lax.Precision.HIGHEST,
        preferred_element_type=jnp.float32,
    )[0]
    modulation = modulation.reshape(3, width) + block_mod
    shift, scale, gate = (modulation[0], modulation[1], modulation[2])
    as_float = full_rows.astype(jnp.float32)
    mean = jnp.mean(as_float, axis=1, keepdims=True)
    centred = as_float - mean
    variance = jnp.mean(centred * centred, axis=1, keepdims=True)
    normed = (centred * lax.rsqrt(variance + 1e-06) * (1.0 + scale) + shift).astype(jnp.bfloat16)
    query = jnp.dot(normed, w_query, preferred_element_type=jnp.float32).astype(jnp.bfloat16)
    keys = jnp.dot(normed, w_key, preferred_element_type=jnp.float32).astype(jnp.bfloat16)
    values = jnp.dot(normed, w_value, preferred_element_type=jnp.float32).astype(jnp.bfloat16)
    heads_here = query.shape[1] // HEAD_DIM
    query_heads = query.reshape(tok_rows, heads_here, HEAD_DIM)
    start_row = lax.axis_index("req") * tok_rows
    query_index = start_row + jnp.arange(tok_rows, dtype=jnp.int32)
    video_ends = jnp.cumsum(video_lengths)
    video_starts = video_ends - video_lengths
    inside = jnp.logical_and(
        query_index[:, None] >= video_starts[None, :], query_index[:, None] < video_ends[None, :]
    )
    query_low = jnp.sum(jnp.where(inside, video_starts[None, :], 0), axis=1)
    query_high = jnp.sum(jnp.where(inside, video_ends[None, :], 0), axis=1)
    span_low = jnp.min(query_low)
    span_high = jnp.max(query_high)

    def score_block(carry, pieces):
        row_max, row_sum, weighted = carry
        key_piece, value_piece = pieces
        count = key_piece.shape[0]
        key_heads = key_piece.reshape(count, heads_here, HEAD_DIM)
        value_heads = value_piece.reshape(count, heads_here, HEAD_DIM)
        scores = jnp.einsum(
            "qhd,khd->hqk", query_heads, key_heads, preferred_element_type=jnp.float32
        ) / math.sqrt(HEAD_DIM)
        key_index = jnp.arange(count, dtype=jnp.int32)
        valid = jnp.logical_and(
            key_index[None, :] >= query_low[:, None], key_index[None, :] < query_high[:, None]
        )[None, :, :]
        block_max = jnp.max(jnp.where(valid, scores, -1e30), axis=2)
        new_max = jnp.maximum(row_max, block_max)
        probs = jnp.where(valid, jnp.exp(scores - new_max[:, :, None]), 0.0)
        new_sum = jnp.sum(probs, axis=2)
        update = jnp.einsum(
            "hqk,khd->hqd",
            probs.astype(jnp.bfloat16),
            value_heads,
            preferred_element_type=jnp.float32,
        )
        return (new_max, new_sum, update)

    initial = (
        jnp.full((heads_here, tok_rows), -1e30, jnp.float32),
        jnp.zeros((heads_here, tok_rows), jnp.float32),
        jnp.zeros((heads_here, tok_rows, HEAD_DIM), jnp.float32),
    )
    pieces = (
        lax.all_gather(keys, "req", axis=0, tiled=True),
        lax.all_gather(values, "req", axis=0, tiled=True),
    )
    start = jnp.int32(0)
    count = pieces[0].shape[0]
    touches = jnp.logical_and(start < span_high, start + count > span_low)
    carry = lax.cond(
        touches, lambda state: score_block(state, pieces), lambda state: state, initial
    )
    row_max, row_sum, weighted = carry
    attended = (weighted / row_sum[:, :, None]).astype(jnp.bfloat16)
    attended = jnp.transpose(attended, (1, 0, 2)).reshape(tok_rows, heads_here * HEAD_DIM)
    partial_value = jnp.dot(attended, w_out, preferred_element_type=jnp.float32)
    own_sum = lax.psum_scatter(
        partial_value.astype(jnp.bfloat16), "tp", scatter_dimension=1, tiled=True
    ).astype(jnp.float32)
    share = own_sum.shape[1]
    gate_share = lax.dynamic_slice_in_dim(gate, lax.axis_index("tp") * share, share)
    branch = gate_share[None, :] * own_sum
    velocity = branch.astype(jnp.bfloat16)
    stepped = (tokens.astype(jnp.float32) + delta_sigma * branch).astype(jnp.bfloat16)
    return (velocity, stepped)


def solution(mesh):
    return jax.shard_map(
        on_device,
        mesh=mesh,
        in_specs=(
            P("req", "tp"),
            P(),
            P(),
            P(),
            P(),
            P(None, "tp"),
            P(None, "tp"),
            P(None, "tp"),
            P("tp", None),
        ),
        out_specs=(P("req", "tp"), P("req", "tp")),
        check_vma=False,
    )
```

profile of v0, /device:TPU:0, one launch (start us, length us, event | category | flops | bytes accessed | tf_op | source)
XLA Modules:
  0.0 251.7 jit_solution(5012958011825898485)
XLA Ops:
  7.2 0.0 copy-start
  7.2 0.0 all-gather.5.cloned.1.call-start
  8.1 6.0 %copy.24 = f32[256,4608]{0,1:T(8,128)} copy(f32[256,4608]{1,0:T(8,128)} %param.14) | data formatting | bytes 9437184 | tf_op args[3]
  14.2 0.0 copy-start.2
  14.2 6.4 %fusion.27 = f32[1,3,1536]{2,0,1:T(1,128)S(1)} fusion(f32[256,1,1]{0,1,2:T(1,128)S(1)} %bitcast.41, f32[3,1536,256]{2,1,0:T(8,128)} %bitcast.39), kind=kOutput, calls=%fused_computation.51 | convolution fusion | flops 14155776 | bytes 4738048 | tf_op jit(solution)/shard_map/dot_general | solution.py:30
  20.7 2.3 all_gather.9
  23.0 0.2 convert_reduce_fusion
  23.2 0.3 fusion.13
  23.5 1.5 convolution_convert_fusion.1
  24.9 0.0 all-gather.5.cloned.1.call-update
  25.0 0.0 all-gather.3.cloned.1.call-start
  25.1 3.1 %convolution_convert_fusion.2 = bf16[192,768]{1,0:T(8,128)(2,1)} fusion(bf16[1536,768]{1,0:T(8,128)(2,1)} %param.17, bf16[192,1536]{1,0:T(8,128)(2,1)S(1)} %all_gather.9, f32[1536]{0:T(1024)S(1)} %get-tuple-element.33, f32[1536]{0:T(1024)S(1)} %get-tuple-element.32, f32[192]{0:T(256)S(1)} %add_rsqrt_fusion, f32[192]{0:T(256)S(1)} %broadcast_multiply_fusion), kind=kOutput, calls=%fused_computation.21 | convolution fusion | flops 454901760 | bytes 3257856 | tf_op jit(solution)/shard_map/dot_general | solution.py:44
  28.2 0.0 all-gather.3.cloned.1.call-update
  28.2 0.0 reduce-scatter.2.cloned.1.call-start
  28.3 0.2 reduce-window.8
  28.4 0.1 select_reduce_fusion.1
  28.5 0.7 reduce_max.18
  29.8 0.7 reduce_min.9
  31.1 2.4 convolution_convert_fusion.3
  33.5 74.7 %all-gather.5.cloned.1.call-done = bf16[3072,768]{1,0:T(8,128)(2,1)} async-done(((bf16[192,768]{1,0:T(8,128)(2,1)}), bf16[3072,768]{1,0:T(8,128)(2,1)}) %all-gather.5.cloned.1.call-update) | async-done | bytes 4718608 | tf_op jit(solution)/shard_map/all_gather | solution.py:92
  108.2 82.5 %all-gather.3.cloned.1.call-done = bf16[3072,768]{1,0:T(8,128)(2,1)} async-done(((bf16[192,768]{1,0:T(8,128)(2,1)}), bf16[3072,768]{1,0:T(8,128)(2,1)}) %all-gather.3.cloned.1.call-update) | async-done | bytes 4718608 | tf_op jit(solution)/shard_map/all_gather | solution.py:91
  190.7 43.2 %conditional.1 = (f32[6,192]{1,0:T(8,128)}, f32[6,192,128]{2,1,0:T(8,128)}) conditional(s32[]{:T(128)} %convert_element_type.44, () %tuple.16, (s32[192]{0:T(256)S(1)}, s32[192]{0:T(256)S(1)}, bf16[192,768]{1,0:T(8,128)(2,1)S(1)}, bf16[3072,768]{1,0:T(8,128)(2,1)}, bf16[3072,768]{1,0:T(8,128)(2,1)}) %tuple.17), branch_computations={%region_7.8_spmd, %region_8.11_spmd} | conditional | flops 1852636032 | bytes 74052112 | solution.py:97
  190.7 0.5 fusion.5
  191.3 6.7 %copy.25 = bf16[3072,768]{0,1:T(8,128)(2,1)} copy(bf16[3072,768]{1,0:T(8,128)(2,1)} %get-tuple-element.30) | data formatting | bytes 9437184 | tf_op jit(solution)/shard_map
  197.9 10.3 %select_reduce_fusion = (f32[6,192]{1,0:T(8,128)S(1)}, f32[6,192,3072]{2,1,0:T(8,128)}) fusion(pred[192,3072]{1,0:T(8,128)(4,1)S(1)} %fusion.5, bf16[3072,6,128]{0,2,1:T(8,128)(2,1)} %bitcast.38, bf16[192,768]{1,0:T(8,128)(2,1)S(1)} %get-tuple-element.13), kind=kOutput, calls=%fused_computation.1 | convolution fusion | flops 916585344 | bytes 19763712 | tf_op jit(solution)/shard_map/cond/branch_1_fun/qhd,khd->hqk/dot_general | solution.py:66
  208.3 6.7 %copy.26 = bf16[3072,768]{0,1:T(8,128)(2,1)} copy(bf16[3072,768]{1,0:T(8,128)(2,1)} %get-tuple-element.31) | data formatting | bytes 9437184 | tf_op jit(solution)/shard_map
  214.9 9.9 %fusion.2 = f32[6,192,128]{2,1,0:T(8,128)} fusion(bf16[3072,6,128]{0,2,1:T(8,128)(2,1)} %bitcast.40, f32[6,192,3072]{2,1,0:T(8,128)} %get-tuple-element.37, f32[6,192]{1,0:T(8,128)S(1)} %broadcast_maximum_fusion, pred[192,3072]{1,0:T(8,128)(4,1)S(1)} %fusion.5), kind=kOutput, calls=%fused_computation.4 | convolution fusion | flops 920125440 | bytes 20058624 | tf_op jit(solution)/shard_map/cond/branch_1_fun/hqk,khd->hqd/dot_general | solution.py:77
  224.8 9.1 %fusion.1 = f32[6,192]{1,0:T(8,128)} fusion(f32[6,192,3072]{2,1,0:T(8,128)} %get-tuple-element.37, f32[6,192]{1,0:T(8,128)S(1)} %broadcast_maximum_fusion, pred[192,3072]{1,0:T(8,128)(4,1)S(1)} %fusion.5), kind=kLoop, calls=%fused_computation.3 | loop fusion | flops 14154624 | bytes 14754816 | tf_op jit(solution)/shard_map/cond/branch_1_fun/reduce_sum | solution.py:76
  233.9 2.6 %convolution_convert_fusion = bf16[192,1536]{1,0:T(8,128)(2,1)} fusion(bf16[768,1536]{1,0:T(8,128)(2,1)S(1)} %copy-done, f32[6,192,128]{2,1,0:T(8,128)} %get-tuple-element.20, f32[6,192]{1,0:T(8,128)} %get-tuple-element.21), kind=kOutput, calls=%fused_computation.15 | convolution fusion | flops 453574656 | bytes 3543552 | tf_op jit(solution)/shard_map/dot_general | solution.py:103
  236.5 0.0 reduce-scatter.2.cloned.1.call-update
  236.6 6.7 %reduce-scatter.2.cloned.1.call-done = bf16[192,768]{1,0:T(8,128)(2,1)} async-done(((bf16[192,1536]{1,0:T(8,128)(2,1)}), bf16[192,768]{1,0:T(8,128)(2,1)}) %reduce-scatter.2.cloned.1.call-update) | async-done | bytes 294928 | tf_op jit(solution)/shard_map/reduce_scatter | solution.py:104
  243.3 1.9 add_convert_fusion
  (26 shorter events, 0.2 us)
Async XLA Ops:
  7.2 226.8 %copy-start = (bf16[768,1536]{1,0:T(8,128)(2,1)S(1)}, bf16[768,1536]{1,0:T(8,128)(2,1)}, u32[]{:S(2)}) copy-start(bf16[768,1536]{1,0:T(8,128)(2,1)} %param.19) | copy-start | bytes 7077892
  7.2 101.0 %all-gather.5.cloned.1.call-start = ((), (), s32[]{:S(2)}) async-start(), calls=%async_computation.2 | async-start | bytes 5013504 | tf_op jit(solution)/shard_map/all_gather | solution.py:92
  14.2 6.4 %copy-start.2 = (f32[3,1536]{1,0:T(4,128)S(1)}, f32[3,1536]{1,0:T(4,128)}, u32[]{:S(2)}) copy-start(f32[3,1536]{1,0:T(4,128)} %param.15) | copy-start | bytes 55300
  14.2 6.5 %copy-start.1 = (bf16[192,768]{1,0:T(8,128)(2,1)S(1)}, bf16[192,768]{1,0:T(8,128)(2,1)}, u32[]{:S(2)}) copy-start(bf16[192,768]{1,0:T(8,128)(2,1)} %param.11) | copy-start | bytes 884740
  14.2 9.3 %copy-start.7 = (bf16[1536,768]{1,0:T(8,128)(2,1)S(1)}, bf16[1536,768]{1,0:T(8,128)(2,1)}, u32[]{:S(2)}) copy-start(bf16[1536,768]{1,0:T(8,128)(2,1)} %param.18) | copy-start | bytes 7077892
  20.6 4.4 %copy-start.3 = (f32[1536]{0:T(1024)}, f32[1536]{0:T(1024)S(1)}, u32[]{:S(2)}) copy-start(f32[1536]{0:T(1024)S(1)} %get-tuple-element.32) | copy-start | bytes 18436
  20.7 4.4 %copy-start.4 = (f32[1536]{0:T(1024)}, f32[1536]{0:T(1024)S(1)}, u32[]{:S(2)}) copy-start(f32[1536]{0:T(1024)S(1)} %get-tuple-element.33) | copy-start | bytes 18436
  23.1 1.9 copy-start.5
  23.5 4.7 %copy-start.6 = (f32[192]{0:T(256)}, f32[192]{0:T(256)S(1)}, u32[]{:S(2)}) copy-start(f32[192]{0:T(256)S(1)} %add_rsqrt_fusion) | copy-start | bytes 2308
  25.0 3.3 %copy-start.8 = (s32[5]{0:T(128)S(1)}, s32[5]{0:T(128)}, u32[]{:S(2)}) copy-start(s32[5]{0:T(128)} %param.12) | copy-start | bytes 64
  25.0 165.7 %all-gather.3.cloned.1.call-start = ((), (), s32[]{:S(2)}) async-start(), calls=%async_computation.1 | async-start | bytes 5013504 | tf_op jit(solution)/shard_map/all_gather | solution.py:91
  28.2 215.1 %reduce-scatter.2.cloned.1.call-start = ((), (), s32[]{:S(2)}) async-start(), calls=%async_computation.3 | async-start | bytes 884736 | tf_op jit(solution)/shard_map/reduce_scatter | solution.py:104
Sparse Core Ops, SparseCore 0:
  25.1 83.0 all-gather.4
  111.6 79.0 all-gather.2
  236.6 6.6 reduce-scatter.1
where the time goes:
time: 252 us
  waiting for transfers between devices  164 us (65%)
  matrix products  36.1 us (14%)
  local copies, waits for them, and re-layouts  19.5 us (8%)
  between operations  16 us (6%)
  other arithmetic  13.7 us (5%)
    all_gather x1, waiting for transfers between devices, on_device(): lax.all_gather(keys, 'req', axis=0, tiled=True)  82.5 us
    all_gather x1, waiting for transfers between devices, on_device(): lax.all_gather(values, 'req', axis=0, tiled=True)  74.7 us
    another operation x2, local copies, waits for them, and re-layouts  13.4 us
    dot_general x1, matrix products, score_block(): jnp.einsum('qhd,khd->hqk', query_heads, key_heads, preferred_element_type...  10.3 us
    dot_general x1, matrix products, score_block(): jnp.einsum('hqk,khd->hqd', probs.astype(jnp.bfloat16), value_heads, prefe...  9.9 us
    reduce_sum x1, other arithmetic, score_block(): new_sum = jnp.sum(probs, axis=2)  9.07 us
    reduce_scatter x1, waiting for transfers between devices, on_device(): lax.psum_scatter(partial_value.astype(jnp.bfloat16), 'tp', scatter_dimens...  6.72 us
    dot_general x1, matrix products, on_device(): jnp.dot(jax.nn.silu(embedding)[None, :], time_weight, precision=lax.Preci...  6.35 us
  transfers between devices with their start and end apart: 3, of which 3 were waited for; matrix products, arithmetic and copies ran while one was open for 3% of the time, Pallas kernels for 0%

commit v1 on v0

v1 whole, which is shorter than its diff:
```python
import math

import jax
import jax.numpy as jnp
import numpy as np
from jax import lax
from jax.sharding import PartitionSpec as P

HEAD_DIM = 128
STEPS = 1000


def noise_level(step_value):
    frac = step_value / STEPS
    return 5.0 * frac / (1.0 + 4.0 * frac)


def head_tables(chips, tp, heads_here):
    order = [chip for chip in range(chips) if chip % 4 != 3]
    owner = np.zeros((tp, heads_here), np.int32)
    slot = np.full((tp, chips), -1, np.int32)
    for place in range(tp * heads_here):
        core, head = place % tp, place // tp
        chip = order[(place * len(order)) // (tp * heads_here)]
        owner[core, head] = chip
        slot[core, chip] = head
    return owner, slot


def make(mesh):
    chips, tp = mesh.shape["req"], mesh.shape["tp"]

    def on_device(tokens, video_lengths, timestep, time_weight, block_mod, w_query, w_key, w_value, w_out):
        rows = tokens.shape[0]
        width = time_weight.shape[1] // 3
        heads_here = w_query.shape[1] // HEAD_DIM
        owner, slot = head_tables(chips, tp, heads_here)
        me, core = lax.axis_index("req"), lax.axis_index("tp")
        full_rows = lax.all_gather(tokens, "tp", axis=1, tiled=True)
        time_value = timestep[0].astype(jnp.float32)
        sigma = noise_level(time_value)
        delta_sigma = noise_level(time_value - 1.0) - sigma
        half_freq = time_weight.shape[0] // 2
        frequency = jnp.exp(-math.log(10000.0) * jnp.arange(half_freq, dtype=jnp.float32) / half_freq)
        angle = 1000.0 * sigma * frequency
        embedding = jnp.concatenate([jnp.cos(angle), jnp.sin(angle)])
        modulation = jnp.sum(jax.nn.silu(embedding)[:, None] * time_weight, axis=0)
        modulation = modulation.reshape(3, width) + block_mod
        shift, scale, gate = (modulation[0], modulation[1], modulation[2])
        as_float = full_rows.astype(jnp.float32)
        mean = jnp.mean(as_float, axis=1, keepdims=True)
        centred = as_float - mean
        variance = jnp.mean(centred * centred, axis=1, keepdims=True)
        normed = (centred * lax.rsqrt(variance + 1e-06) * (1.0 + scale) + shift).astype(jnp.bfloat16)

        def project(weight):
            out = jnp.dot(normed, weight, preferred_element_type=jnp.float32).astype(jnp.bfloat16)
            return jnp.transpose(out.reshape(rows, heads_here, HEAD_DIM), (1, 0, 2))

        packed = jnp.stack([project(w) for w in (w_query, w_key, w_value)], axis=1)
        slots = jnp.asarray(slot)[core]
        pieces = []
        for hop in range(chips):
            head = jnp.maximum(slots[me ^ hop], 0)
            piece = lax.dynamic_index_in_dim(packed, head, 0, keepdims=False)
            if hop:
                pairs = [
                    ((chip ^ hop) * tp + c, chip * tp + c)
                    for c in range(tp) for chip in range(chips) if slot[c, chip] >= 0
                ]
                piece = lax.ppermute(piece, ("req", "tp"), pairs)
            pieces.append(piece)
        stacked = jnp.stack(pieces)
        stacked = stacked[jnp.arange(chips) ^ me]
        query, keys, values = (stacked[:, k].reshape(chips * rows, HEAD_DIM) for k in range(3))
        ends = jnp.cumsum(video_lengths)
        index = jnp.arange(chips * rows, dtype=jnp.int32)
        video = jnp.sum((index[:, None] >= ends[None, :]).astype(jnp.int32), axis=1)
        step = chips * rows // 4

        def block(args):
            q, v = args
            scores = jnp.dot(q, keys.T, preferred_element_type=jnp.float32) / math.sqrt(HEAD_DIM)
            same = v[:, None] == video[None, :]
            scores = jnp.where(same, scores, -1e30)
            top = jnp.max(scores, axis=1, keepdims=True)
            probs = jnp.where(same, jnp.exp(scores - top), 0.0)
            total = jnp.sum(probs, axis=1, keepdims=True)
            out = jnp.dot(probs.astype(jnp.bfloat16), values, preferred_element_type=jnp.float32)
            return (out / total).astype(jnp.bfloat16)

        done = lax.map(block, (query.reshape(-1, step, HEAD_DIM), video.reshape(-1, step)))
        done = done.reshape(chips, rows, HEAD_DIM)
        back = []
        for hop in range(chips):
            piece = lax.dynamic_index_in_dim(done, me ^ hop, 0, keepdims=False)
            if hop:
                pairs = [
                    (chip * tp + c, (chip ^ hop) * tp + c)
                    for c in range(tp) for chip in range(chips) if slot[c, chip] >= 0
                ]
                piece = lax.ppermute(piece, ("req", "tp"), pairs)
            back.append(piece)
        back = jnp.stack(back)
        attended = back[jnp.asarray(owner)[core] ^ me]
        attended = jnp.transpose(attended, (1, 0, 2)).reshape(rows, heads_here * HEAD_DIM)
        partial_value = jnp.dot(attended, w_out, preferred_element_type=jnp.float32).astype(jnp.bfloat16)
        share = width // tp
        mine = lax.dynamic_slice_in_dim(partial_value, core * share, share, axis=1)
        other = lax.dynamic_slice_in_dim(partial_value, (1 - core) * share, share, axis=1)
        other = lax.ppermute(other, "tp", [(0, 1), (1, 0)])
        own_sum = mine.astype(jnp.float32) + other.astype(jnp.float32)
        gate_share = lax.dynamic_slice_in_dim(gate, core * share, share)
        branch = gate_share[None, :] * own_sum
        velocity = branch.astype(jnp.bfloat16)
        stepped = (tokens.astype(jnp.float32) + delta_sigma * branch).astype(jnp.bfloat16)
        return (velocity, stepped)

    return on_device


def solution(mesh):
    return jax.shard_map(
        make(mesh),
        mesh=mesh,
        in_specs=(
            P("req", "tp"), P(), P(), P(), P(), P(None, "tp"), P(None, "tp"), P(None, "tp"), P("tp", None),
        ),
        out_specs=(P("req", "tp"), P("req", "tp")),
        check_vma=False,
    )
```

time: 252 us -> 180 us (0.71)
  the two profiles are of different devices: /device:TPU:0 before, /device:TPU:27 now
where the time goes in v1:
time: 180 us; the launch traced here: 179 us
  starting transfers between devices  58.4 us (32%)
  local copies, waits for them, and re-layouts  39.7 us (22%)
  matrix products  32.1 us (18%)
  waiting for transfers between devices  17.1 us (10%)
  other arithmetic  16.7 us (9%)
  between operations  12.1 us (7%)
  blocking collectives  2.53 us (1%)
    ppermute x30, starting transfers between devices, on_device(): piece = lax.ppermute(piece, ('req', 'tp'), pairs)  41.6 us
    unnamed x42, local copies, waits for them, and re-layouts  23.5 us
    ppermute x1, starting transfers between devices, on_device(): other = lax.ppermute(other, 'tp', [(0, 1), (1, 0)])  16.8 us
    ppermute x30, waiting for transfers between devices, on_device(): piece = lax.ppermute(piece, ('req', 'tp'), pairs)  15.8 us
    dot_general x4, matrix products, block(): jnp.dot(probs.astype(jnp.bfloat16), values, preferred_element_type=jnp.fl...  15.1 us
    dot_general x4, matrix products, block(): jnp.dot(q, keys.T, preferred_element_type=jnp.float32) / math.sqrt(HEAD_DIM)  12.4 us
    reduce_sum x4, other arithmetic, block(): total = jnp.sum(probs, axis=1, keepdims=True)  11.8 us
    dot_general x3, matrix products, project(): jnp.dot(normed, weight, preferred_element_type=jnp.float32)  3.98 us
  transfers between devices with their start and end apart: 31, of which 5 were waited for; matrix products, arithmetic and copies ran while one was open for 13% of the time, Pallas kernels for 0%

profile of v1, /device:TPU:27, one launch (start us, length us, event | category | flops | bytes accessed | tf_op | source)
XLA Modules:
  0.0 178.8 jit_solution(7439613627855321623)
XLA Ops:
  0.8 2.0 %fusion.48 = (s32[1,1]{1,0:T(1,128)}, s32[1,1]{1,0:T(1,128)}, s32[1,1]{1,0:T(1,128)}, s32[1,1]{1,0:T(1,128)}, s32[1,1]{1,0:T(1,128)}, /*index=5*/s32[1,1]{1,0:T(...) fusion(s32[2,16]{1,0:T(2,128)} %constant.397.clone, ...), kind=kLoop, calls=%fused_computation.132 | loop fusion | bytes 196 | tf_op jit(solution)/shard_map/dynamic_slice | solution.py:64
  13.7 2.9 %multiply_reduce_fusion = f32[4608]{0:T(1024)S(1)} fusion(f32[256,4608]{1,0:T(8,128)} %param.16, f32[256]{0:T(256)S(1)} %divide_multiply_fusion), kind=kLoop, calls=%fused_computation.20 | loop fusion | flops 2354688 | bytes 4738048 | tf_op jit(solution)/shard_map/reduce_sum | solution.py:47
  16.8 2.5 %all_gather.3 = bf16[192,1536]{1,0:T(8,128)(2,1)S(1)} all-gather(bf16[192,768]{1,0:T(8,128)(2,1)S(1)} %copy-done.1), channel_id=1, replica_groups=mesh['req'=16,'tp'=2] {'tp'}, dimensions={1}, use_global_device_ids=true | all-gather | bytes 884736 | tf_op jit(solution)/shard_map/all_gather | solution.py:39
  19.8 2.5 %fusion.30 = bf16[24,6,8,128]{3,2,1,0:T(8,128)(2,1)S(1)} fusion(bf16[1536,768]{1,0:T(8,128)(2,1)} %param.18, bf16[192,1536]{1,0:T(8,128)(2,1)S(1)} %all_gather.3, f32[1536]{0:T(1024)S(1)} %get-tuple-element.41, f32[1536]{0:T(1024)S(1)} %get-tuple-element.40, f32[192]{0:T(256)S(1)} %add_rsqrt_fusion, f32[192]{0:T(256)S(1)} %broadcast_multiply_fusion), kind=kOutput, calls=%fused_computation.33 | convolution fusion | flops 454901760 | bytes 3257856 | tf_op jit(solution)/shard_map/dot_general | solution.py:57
  26.4 2.8 %collective-permute-start = (bf16[3,192,128]{2,1,0:T(8,128)(2,1)}, bf16[3,192,128]{2,1,0:T(8,128)(2,1)}, u32[]{:S(2)}, u32[]{:S(2)}) collective-permute-start(bf16[3,192,128]{2,1,0:T(8,128)(2,1)} %get-tuple-element.77), channel_id=1, source_target_pairs={{2,0},{6,4},{8,10},{18,16},{22,20},{24,26},{1,3},{11,9},{15,13},{1... | collective-permute-start | bytes 442376 | tf_op jit(solution)/shard_map/ppermute | solution.py:71
  30.5 3.1 %collective-permute-start.2 = (bf16[3,192,128]{2,1,0:T(8,128)(2,1)}, bf16[3,192,128]{2,1,0:T(8,128)(2,1)}, u32[]{:S(2)}, u32[]{:S(2)}) collective-permute-start(bf16[3,192,128]{2,1,0:T(8,128)(2,1)} %get-tuple-element.75), channel_id=1, source_target_pairs={{6,0},{2,4},{12,10},{22,16},{18,20},{28,26},{5,3},{15,9},{11,13},{... | collective-permute-start | bytes 442376 | tf_op jit(solution)/shard_map/ppermute | solution.py:71
  33.6 1.9 %collective-permute-start.3 = (bf16[3,192,128]{2,1,0:T(8,128)(2,1)}, bf16[3,192,128]{2,1,0:T(8,128)(2,1)}, u32[]{:S(2)}, u32[]{:S(2)}) collective-permute-start(bf16[3,192,128]{2,1,0:T(8,128)(2,1)} %get-tuple-element.74), channel_id=1, source_target_pairs={{8,0},{12,4},{2,10},{24,16},{28,20},{18,26},{11,3},{1,9},{5,13},{2... | collective-permute-start | bytes 442376 | tf_op jit(solution)/shard_map/ppermute | solution.py:71
  44.0 5.2 %collective-permute-start.8 = (bf16[3,192,128]{2,1,0:T(8,128)(2,1)}, bf16[3,192,128]{2,1,0:T(8,128)(2,1)S(1)}, u32[]{:S(2)}, u32[]{:S(2)}) collective-permute-start(bf16[3,192,128]{2,1,0:T(8,128)(2,1)} %get-tuple-element.69), channel_id=1, source_target_pairs={{18,0},{22,4},{24,10},{2,16},{6,20},{8,26},{17,3},{27,9},{31,13},{... | collective-permute-start | bytes 442376 | tf_op jit(solution)/shard_map/ppermute | solution.py:71
  49.2 1.6 bitcast_dynamic-update-slice_fusion.11
  53.1 6.4 %collective-permute-start.10 = (bf16[3,192,128]{2,1,0:T(8,128)(2,1)S(1)}, bf16[3,192,128]{2,1,0:T(8,128)(2,1)S(1)}, u32[]{:S(2)}, u32[]{:S(2)}) collective-permute-start(bf16[3,192,128]{2,1,0:T(8,128)(2,1)S(1)} %get-tuple-element.67), channel_id=1, source_target_pairs={{22,0},{18,4},{28,10},{6,16},{2,20},{12,26},{21,3},{31,9},{27,13},... | collective-permute-start | bytes 442376 | tf_op jit(solution)/shard_map/ppermute | solution.py:71
  69.5 3.9 %gather_fusion = bf16[16,3,192,128]{3,2,1,0:T(8,128)(2,1)} fusion(bf16[16,3,192,128]{3,2,1,0:T(8,128)(2,1)} %bitcast_dynamic-update-slice_fusion, s32[1024]{0:T(1024)S(1)} %pad_clamp_fusion.1), kind=kCustom, calls=%fused_computation | custom fusion | bytes 4718656 | tf_op jit(solution)/shard_map/gather | solution.py:74
  73.4 2.9 %fusion.47 = (bf16[16,1,192,128]{3,2,1,0:T(8,128)(2,1)S(1)}, bf16[16,1,192,128]{3,2,1,0:T(8,128)(2,1)}, bf16[16,1,192,128]{3,2,1,0:T(8,128)(2,1)}) fusion(bf16[16,3,192,128]{3,2,1,0:T(8,128)(2,1)} %gather_fusion), kind=kLoop, calls=%fused_computation.131 | loop fusion | bytes 4718592 | tf_op jit(solution)/shard_map/slice | solution.py:75
  76.4 39.4 %while.10 = (s32[]{:T(128)}, bf16[4,768,128]{2,1,0:T(8,128)(2,1)}, s32[4,768]{1,0:T(4,128)S(1)}, s32[3072]{0:T(1024)S(1)}, bf16[4,768,128]{2,1,0:T(8,128)(2,1)},...) while((s32[]{:T(128)}, bf16[4,768,128]{2,1,0:T(8,128)(2,1)}, ...), condition=%wide.region_8.9_spmd, body=%wide.region_5.8_spmd.sunk | while | flops 1245903360 | bytes 30346328 | solution.py:92
  76.4 3.1 %fusion.65 = (f32[768]{0:T(1024)S(1)}, f32[768,3072]{1,0:T(8,128)S(1)}) fusion(s32[3072]{0:T(1024)S(1)} %get-tuple-element.180, s32[768]{0:T(1024)S(1)} %dynamic-slice_reduce_fusion.2, bf16[3072,128]{1,0:T(8,128)(2,1)} %get-tuple-element.182, bf16[4,768,128]{2,1,0:T(8,128)(2,1)} %get-tuple-element.181, s32[]{:T(128)} %get-tuple-element.169), kind=kOutput, calls=%fused_computation.4.clone.1 | convolution fusion | flops 613416192 | bytes 10439168 | tf_op jit(solution)/shard_map/while/body/eval_jaxpr/dot_general | solution.py:83
  79.5 3.0 %fusion.66 = f32[768]{0:T(1024)S(1)} fusion(f32[768,3072]{1,0:T(8,128)S(1)} %get-tuple-element.159, f32[768]{0:T(1024)S(1)} %get-tuple-element.160, s32[3072]{0:T(1024)S(1)} %get-tuple-element.180, s32[768]{0:T(1024)S(1)} %dynamic-slice_reduce_fusion.2), kind=kLoop, calls=%fused_computation.5.clone.1 | loop fusion | flops 14155008 | bytes 9458688 | tf_op jit(solution)/shard_map/while/body/eval_jaxpr/reduce_sum | solution.py:88
  82.4 3.8 %fusion.67 = bf16[4,768,128]{2,1,0:T(8,128)(2,1)} fusion(bf16[4,768,128]{2,1,0:T(8,128)(2,1)} %get-tuple-element.170, s32[]{:T(128)} %get-tuple-element.169, bf16[3072,128]{1,0:T(8,128)(2,1)S(1)} %get-tuple-element.183, f32[768,3072]{1,0:T(8,128)S(1)} %get-tuple-element.159, f32[768]{0:T(1024)S(1)} %get-tuple-element.160, ...), kind=kOutput, calls=%fused_computation.11.clone.1 | convolution fusion | flops 618332160 | bytes 10442240 | tf_op jit(solution)/shard_map/while/body/eval_jaxpr/dot_general | solution.py:89
  86.2 3.1 %fusion.65 = (f32[768]{0:T(1024)S(1)}, f32[768,3072]{1,0:T(8,128)S(1)}) fusion(s32[3072]{0:T(1024)S(1)} %get-tuple-element.180, s32[768]{0:T(1024)S(1)} %dynamic-slice_reduce_fusion.2, bf16[3072,128]{1,0:T(8,128)(2,1)} %get-tuple-element.182, bf16[4,768,128]{2,1,0:T(8,128)(2,1)} %get-tuple-element.181, s32[]{:T(128)} %get-tuple-element.169), kind=kOutput, calls=%fused_computation.4.clone.1 | convolution fusion | flops 613416192 | bytes 10439168 | tf_op jit(solution)/shard_map/while/body/eval_jaxpr/dot_general | solution.py:83
  89.3 3.0 %fusion.66 = f32[768]{0:T(1024)S(1)} fusion(f32[768,3072]{1,0:T(8,128)S(1)} %get-tuple-element.159, f32[768]{0:T(1024)S(1)} %get-tuple-element.160, s32[3072]{0:T(1024)S(1)} %get-tuple-element.180, s32[768]{0:T(1024)S(1)} %dynamic-slice_reduce_fusion.2), kind=kLoop, calls=%fused_computation.5.clone.1 | loop fusion | flops 14155008 | bytes 9458688 | tf_op jit(solution)/shard_map/while/body/eval_jaxpr/reduce_sum | solution.py:88
  92.3 3.8 %fusion.67 = bf16[4,768,128]{2,1,0:T(8,128)(2,1)} fusion(bf16[4,768,128]{2,1,0:T(8,128)(2,1)} %get-tuple-element.170, s32[]{:T(128)} %get-tuple-element.169, bf16[3072,128]{1,0:T(8,128)(2,1)S(1)} %get-tuple-element.183, f32[768,3072]{1,0:T(8,128)S(1)} %get-tuple-element.159, f32[768]{0:T(1024)S(1)} %get-tuple-element.160, ...), kind=kOutput, calls=%fused_computation.11.clone.1 | convolution fusion | flops 618332160 | bytes 10442240 | tf_op jit(solution)/shard_map/while/body/eval_jaxpr/dot_general | solution.py:89
  96.1 3.1 %fusion.65 = (f32[768]{0:T(1024)S(1)}, f32[768,3072]{1,0:T(8,128)S(1)}) fusion(s32[3072]{0:T(1024)S(1)} %get-tuple-element.180, s32[768]{0:T(1024)S(1)} %dynamic-slice_reduce_fusion.2, bf16[3072,128]{1,0:T(8,128)(2,1)} %get-tuple-element.182, bf16[4,768,128]{2,1,0:T(8,128)(2,1)} %get-tuple-element.181, s32[]{:T(128)} %get-tuple-element.169), kind=kOutput, calls=%fused_computation.4.clone.1 | convolution fusion | flops 613416192 | bytes 10439168 | tf_op jit(solution)/shard_map/while/body/eval_jaxpr/dot_general | solution.py:83
  99.2 3.0 %fusion.66 = f32[768]{0:T(1024)S(1)} fusion(f32[768,3072]{1,0:T(8,128)S(1)} %get-tuple-element.159, f32[768]{0:T(1024)S(1)} %get-tuple-element.160, s32[3072]{0:T(1024)S(1)} %get-tuple-element.180, s32[768]{0:T(1024)S(1)} %dynamic-slice_reduce_fusion.2), kind=kLoop, calls=%fused_computation.5.clone.1 | loop fusion | flops 14155008 | bytes 9458688 | tf_op jit(solution)/shard_map/while/body/eval_jaxpr/reduce_sum | solution.py:88
  102.1 3.8 %fusion.67 = bf16[4,768,128]{2,1,0:T(8,128)(2,1)} fusion(bf16[4,768,128]{2,1,0:T(8,128)(2,1)} %get-tuple-element.170, s32[]{:T(128)} %get-tuple-element.169, bf16[3072,128]{1,0:T(8,128)(2,1)S(1)} %get-tuple-element.183, f32[768,3072]{1,0:T(8,128)S(1)} %get-tuple-element.159, f32[768]{0:T(1024)S(1)} %get-tuple-element.160, ...), kind=kOutput, calls=%fused_computation.11.clone.1 | convolution fusion | flops 618332160 | bytes 10442240 | tf_op jit(solution)/shard_map/while/body/eval_jaxpr/dot_general | solution.py:89
  105.9 3.1 %fusion.65 = (f32[768]{0:T(1024)S(1)}, f32[768,3072]{1,0:T(8,128)S(1)}) fusion(s32[3072]{0:T(1024)S(1)} %get-tuple-element.180, s32[768]{0:T(1024)S(1)} %dynamic-slice_reduce_fusion.2, bf16[3072,128]{1,0:T(8,128)(2,1)} %get-tuple-element.182, bf16[4,768,128]{2,1,0:T(8,128)(2,1)} %get-tuple-element.181, s32[]{:T(128)} %get-tuple-element.169), kind=kOutput, calls=%fused_computation.4.clone.1 | convolution fusion | flops 613416192 | bytes 10439168 | tf_op jit(solution)/shard_map/while/body/eval_jaxpr/dot_general | solution.py:83
  109.0 3.0 %fusion.66 = f32[768]{0:T(1024)S(1)} fusion(f32[768,3072]{1,0:T(8,128)S(1)} %get-tuple-element.159, f32[768]{0:T(1024)S(1)} %get-tuple-element.160, s32[3072]{0:T(1024)S(1)} %get-tuple-element.180, s32[768]{0:T(1024)S(1)} %dynamic-slice_reduce_fusion.2), kind=kLoop, calls=%fused_computation.5.clone.1 | loop fusion | flops 14155008 | bytes 9458688 | tf_op jit(solution)/shard_map/while/body/eval_jaxpr/reduce_sum | solution.py:88
  112.0 3.8 %fusion.67 = bf16[4,768,128]{2,1,0:T(8,128)(2,1)} fusion(bf16[4,768,128]{2,1,0:T(8,128)(2,1)} %get-tuple-element.170, s32[]{:T(128)} %get-tuple-element.169, bf16[3072,128]{1,0:T(8,128)(2,1)S(1)} %get-tuple-element.183, f32[768,3072]{1,0:T(8,128)S(1)} %get-tuple-element.159, f32[768]{0:T(1024)S(1)} %get-tuple-element.160, ...), kind=kOutput, calls=%fused_computation.11.clone.1 | convolution fusion | flops 618332160 | bytes 10442240 | tf_op jit(solution)/shard_map/while/body/eval_jaxpr/dot_general | solution.py:89
  115.8 1.9 %dynamic-slice_bitcast_fusion.15 = (bf16[192,128]{1,0:T(8,128)(2,1)S(1)}, bf16[192,128]{1,0:T(8,128)(2,1)S(1)}, bf16[192,128]{1,0:T(8,128)(2,1)S(1)}, bf16[192,1...) fusion(bf16[16,192,128]{2,1,0:T(8,128)(2,1)} %bitcast.61, ...), kind=kLoop, calls=%fused_computation.94 | loop fusion | bytes 1572928 | tf_op jit(solution)/shard_map/jit(dynamic_index_in_dim)/squeeze | solution.py:96
  122.9 5.7 %collective-permute-done.15 = bf16[192,128]{1,0:T(8,128)(2,1)S(1)} collective-permute-done((bf16[192,128]{1,0:T(8,128)(2,1)S(1)}, bf16[192,128]{1,0:T(8,128)(2,1)S(1)}, u32[]{:S(2)}, u32[]{:S(2)}) %collective-permute-start.15) | collective-permute-done | bytes 49184 | tf_op jit(solution)/shard_map/ppermute | solution.py:102
  131.2 1.9 %collective-permute-done.17 = bf16[192,128]{1,0:T(8,128)(2,1)S(1)} collective-permute-done((bf16[192,128]{1,0:T(8,128)(2,1)S(1)}, bf16[192,128]{1,0:T(8,128)(2,1)S(1)}, u32[]{:S(2)}, u32[]{:S(2)}) %collective-permute-start.17) | collective-permute-done | bytes 49184 | tf_op jit(solution)/shard_map/ppermute | solution.py:102
  142.6 2.5 %collective-permute-done.23 = bf16[192,128]{1,0:T(8,128)(2,1)S(1)} collective-permute-done((bf16[192,128]{1,0:T(8,128)(2,1)S(1)}, bf16[192,128]{1,0:T(8,128)(2,1)S(1)}, u32[]{:S(2)}, u32[]{:S(2)}) %collective-permute-start.23) | collective-permute-done | bytes 49184 | tf_op jit(solution)/shard_map/ppermute | solution.py:102
  147.7 5.6 %collective-permute-done.25 = bf16[192,128]{1,0:T(8,128)(2,1)S(1)} collective-permute-done((bf16[192,128]{1,0:T(8,128)(2,1)S(1)}, bf16[192,128]{1,0:T(8,128)(2,1)S(1)}, u32[]{:S(2)}, u32[]{:S(2)}) %collective-permute-start.25) | collective-permute-done | bytes 49184 | tf_op jit(solution)/shard_map/ppermute | solution.py:102
  156.4 1.7 gather_fusion.1
  159.6 16.8 %collective-permute-start.30 = (bf16[192,768]{1,0:T(8,128)(2,1)}, bf16[192,768]{1,0:T(8,128)(2,1)S(1)}, u32[]{:S(2)}, u32[]{:S(2)}) collective-permute-start(bf16[192,768]{1,0:T(8,128)(2,1)} %constant_dynamic-slice_fusion), channel_id=1, source_target_pairs={{0,1},{1,0},{2,3},{3,2},{4,5},{5,4},{6,7},{7,6},{8,9},{9,8},{10,11... | collective-permute-start | bytes 884744 | tf_op jit(solution)/shard_map/ppermute | solution.py:111
  (127 shorter events, 53.2 us)
Async XLA Ops:
  0.6 157.6 %copy-start = (bf16[768,1536]{1,0:T(8,128)(2,1)S(1)}, bf16[768,1536]{1,0:T(8,128)(2,1)}, u32[]{:S(2)}) copy-start(bf16[768,1536]{1,0:T(8,128)(2,1)} %param.21) | copy-start | bytes 7077892
  26.4 10.8 %collective-permute-start = (bf16[3,192,128]{2,1,0:T(8,128)(2,1)}, bf16[3,192,128]{2,1,0:T(8,128)(2,1)}, u32[]{:S(2)}, u32[]{:S(2)}) collective-permute-start(bf16[3,192,128]{2,1,0:T(8,128)(2,1)} %get-tuple-element.77), channel_id=1, source_target_pairs={{2,0},{6,4},{8,10},{18,16},{22,20},{24,26},{1,3},{11,9},{15,13},{1... | collective-permute-start | bytes 442376 | tf_op jit(solution)/shard_map/ppermute | solution.py:71
  29.2 10.3 %collective-permute-start.1 = (bf16[3,192,128]{2,1,0:T(8,128)(2,1)}, bf16[3,192,128]{2,1,0:T(8,128)(2,1)}, u32[]{:S(2)}, u32[]{:S(2)}) collective-permute-start(bf16[3,192,128]{2,1,0:T(8,128)(2,1)} %get-tuple-element.76), channel_id=1, source_target_pairs={{4,0},{0,4},{14,10},{20,16},{16,20},{30,26},{7,3},{13,9},{9,13},{2... | collective-permute-start | bytes 442376 | tf_op jit(solution)/shard_map/ppermute | solution.py:71
  30.5 11.2 %collective-permute-start.2 = (bf16[3,192,128]{2,1,0:T(8,128)(2,1)}, bf16[3,192,128]{2,1,0:T(8,128)(2,1)}, u32[]{:S(2)}, u32[]{:S(2)}) collective-permute-start(bf16[3,192,128]{2,1,0:T(8,128)(2,1)} %get-tuple-element.75), channel_id=1, source_target_pairs={{6,0},{2,4},{12,10},{22,16},{18,20},{28,26},{5,3},{15,9},{11,13},{... | collective-permute-start | bytes 442376 | tf_op jit(solution)/shard_map/ppermute | solution.py:71
  33.6 10.4 %collective-permute-start.3 = (bf16[3,192,128]{2,1,0:T(8,128)(2,1)}, bf16[3,192,128]{2,1,0:T(8,128)(2,1)}, u32[]{:S(2)}, u32[]{:S(2)}) collective-permute-start(bf16[3,192,128]{2,1,0:T(8,128)(2,1)} %get-tuple-element.74), channel_id=1, source_target_pairs={{8,0},{12,4},{2,10},{24,16},{28,20},{18,26},{11,3},{1,9},{5,13},{2... | collective-permute-start | bytes 442376 | tf_op jit(solution)/shard_map/ppermute | solution.py:71
  35.6 15.3 %collective-permute-start.4 = (bf16[3,192,128]{2,1,0:T(8,128)(2,1)}, bf16[3,192,128]{2,1,0:T(8,128)(2,1)}, u32[]{:S(2)}, u32[]{:S(2)}) collective-permute-start(bf16[3,192,128]{2,1,0:T(8,128)(2,1)} %get-tuple-element.73), channel_id=1, source_target_pairs={{10,0},{14,4},{0,10},{26,16},{30,20},{16,26},{9,3},{3,9},{7,13},{2... | collective-permute-start | bytes 442376 | tf_op jit(solution)/shard_map/ppermute | solution.py:71
  37.2 15.8 %collective-permute-start.5 = (bf16[3,192,128]{2,1,0:T(8,128)(2,1)}, bf16[3,192,128]{2,1,0:T(8,128)(2,1)S(1)}, u32[]{:S(2)}, u32[]{:S(2)}) collective-permute-start(bf16[3,192,128]{2,1,0:T(8,128)(2,1)} %get-tuple-element.72), channel_id=1, source_target_pairs={{12,0},{8,4},{6,10},{28,16},{24,20},{22,26},{15,3},{5,9},{1,13},{3... | collective-permute-start | bytes 442376 | tf_op jit(solution)/shard_map/ppermute | solution.py:71
  39.5 20.7 %collective-permute-start.6 = (bf16[3,192,128]{2,1,0:T(8,128)(2,1)}, bf16[3,192,128]{2,1,0:T(8,128)(2,1)S(1)}, u32[]{:S(2)}, u32[]{:S(2)}) collective-permute-start(bf16[3,192,128]{2,1,0:T(8,128)(2,1)} %get-tuple-element.71), channel_id=1, source_target_pairs={{14,0},{10,4},{4,10},{30,16},{26,20},{20,26},{13,3},{7,9},{3,13},{... | collective-permute-start | bytes 442376 | tf_op jit(solution)/shard_map/ppermute | solution.py:71
  41.8 20.4 %collective-permute-start.7 = (bf16[3,192,128]{2,1,0:T(8,128)(2,1)}, bf16[3,192,128]{2,1,0:T(8,128)(2,1)S(1)}, u32[]{:S(2)}, u32[]{:S(2)}) collective-permute-start(bf16[3,192,128]{2,1,0:T(8,128)(2,1)} %get-tuple-element.70), channel_id=1, source_target_pairs={{16,0},{20,4},{26,10},{0,16},{4,20},{10,26},{19,3},{25,9},{29,13},... | collective-permute-start | bytes 442376 | tf_op jit(solution)/shard_map/ppermute | solution.py:71
  44.0 19.5 %collective-permute-start.8 = (bf16[3,192,128]{2,1,0:T(8,128)(2,1)}, bf16[3,192,128]{2,1,0:T(8,128)(2,1)S(1)}, u32[]{:S(2)}, u32[]{:S(2)}) collective-permute-start(bf16[3,192,128]{2,1,0:T(8,128)(2,1)} %get-tuple-element.69), channel_id=1, source_target_pairs={{18,0},{22,4},{24,10},{2,16},{6,20},{8,26},{17,3},{27,9},{31,13},{... | collective-permute-start | bytes 442376 | tf_op jit(solution)/shard_map/ppermute | solution.py:71
  50.8 14.0 %collective-permute-start.9 = (bf16[3,192,128]{2,1,0:T(8,128)(2,1)}, bf16[3,192,128]{2,1,0:T(8,128)(2,1)S(1)}, u32[]{:S(2)}, u32[]{:S(2)}) collective-permute-start(bf16[3,192,128]{2,1,0:T(8,128)(2,1)} %get-tuple-element.68), channel_id=1, source_target_pairs={{20,0},{16,4},{30,10},{4,16},{0,20},{14,26},{23,3},{29,9},{25,13},... | collective-permute-start | bytes 442376 | tf_op jit(solution)/shard_map/ppermute | solution.py:71
  53.1 13.1 %collective-permute-start.10 = (bf16[3,192,128]{2,1,0:T(8,128)(2,1)S(1)}, bf16[3,192,128]{2,1,0:T(8,128)(2,1)S(1)}, u32[]{:S(2)}, u32[]{:S(2)}) collective-permute-start(bf16[3,192,128]{2,1,0:T(8,128)(2,1)S(1)} %get-tuple-element.67), channel_id=1, source_target_pairs={{22,0},{18,4},{28,10},{6,16},{2,20},{12,26},{21,3},{31,9},{27,13},... | collective-permute-start | bytes 442376 | tf_op jit(solution)/shard_map/ppermute | solution.py:71
  60.2 6.7 %collective-permute-start.11 = (bf16[3,192,128]{2,1,0:T(8,128)(2,1)S(1)}, bf16[3,192,128]{2,1,0:T(8,128)(2,1)S(1)}, u32[]{:S(2)}, u32[]{:S(2)}) collective-permute-start(bf16[3,192,128]{2,1,0:T(8,128)(2,1)S(1)} %get-tuple-element.66), channel_id=1, source_target_pairs={{24,0},{28,4},{18,10},{8,16},{12,20},{2,26},{27,3},{17,9},{21,13},... | collective-permute-start | bytes 442376 | tf_op jit(solution)/shard_map/ppermute | solution.py:71
  62.1 5.4 %collective-permute-start.12 = (bf16[3,192,128]{2,1,0:T(8,128)(2,1)S(1)}, bf16[3,192,128]{2,1,0:T(8,128)(2,1)S(1)}, u32[]{:S(2)}, u32[]{:S(2)}) collective-permute-start(bf16[3,192,128]{2,1,0:T(8,128)(2,1)S(1)} %get-tuple-element.65), channel_id=1, source_target_pairs={{26,0},{30,4},{16,10},{10,16},{14,20},{0,26},{25,3},{19,9},{23,13}... | collective-permute-start | bytes 442376 | tf_op jit(solution)/shard_map/ppermute | solution.py:71
  63.5 4.7 %collective-permute-start.13 = (bf16[3,192,128]{2,1,0:T(8,128)(2,1)S(1)}, bf16[3,192,128]{2,1,0:T(8,128)(2,1)S(1)}, u32[]{:S(2)}, u32[]{:S(2)}) collective-permute-start(bf16[3,192,128]{2,1,0:T(8,128)(2,1)S(1)} %get-tuple-element.64), channel_id=1, source_target_pairs={{28,0},{24,4},{22,10},{12,16},{8,20},{6,26},{31,3},{21,9},{17,13},... | collective-permute-start | bytes 442376 | tf_op jit(solution)/shard_map/ppermute | solution.py:71
  64.8 4.0 %collective-permute-start.14 = (bf16[3,192,128]{2,1,0:T(8,128)(2,1)S(1)}, bf16[3,192,128]{2,1,0:T(8,128)(2,1)S(1)}, u32[]{:S(2)}, u32[]{:S(2)}) collective-permute-start(bf16[3,192,128]{2,1,0:T(8,128)(2,1)S(1)} %get-tuple-element.63), channel_id=1, source_target_pairs={{30,0},{26,4},{20,10},{14,16},{10,20},{4,26},{29,3},{23,9},{19,13}... | collective-permute-start | bytes 442376 | tf_op jit(solution)/shard_map/ppermute | solution.py:71
  117.7 11.0 %collective-permute-start.15 = (bf16[192,128]{1,0:T(8,128)(2,1)S(1)}, bf16[192,128]{1,0:T(8,128)(2,1)S(1)}, u32[]{:S(2)}, u32[]{:S(2)}) collective-permute-start(bf16[192,128]{1,0:T(8,128)(2,1)S(1)} %get-tuple-element.93), channel_id=1, source_target_pairs={{0,2},{4,6},{10,8},{16,18},{20,22},{26,24},{3,1},{9,11},{13,15},{1... | collective-permute-start | bytes 147464 | tf_op jit(solution)/shard_map/ppermute | solution.py:102
  119.0 11.0 %collective-permute-start.16 = (bf16[192,128]{1,0:T(8,128)(2,1)S(1)}, bf16[192,128]{1,0:T(8,128)(2,1)S(1)}, u32[]{:S(2)}, u32[]{:S(2)}) collective-permute-start(bf16[192,128]{1,0:T(8,128)(2,1)S(1)} %get-tuple-element.92), channel_id=1, source_target_pairs={{0,4},{4,0},{10,14},{16,20},{20,16},{26,30},{3,7},{9,13},{13,9},{1... | collective-permute-start | bytes 147464 | tf_op jit(solution)/shard_map/ppermute | solution.py:102
  119.6 13.4 %collective-permute-start.17 = (bf16[192,128]{1,0:T(8,128)(2,1)S(1)}, bf16[192,128]{1,0:T(8,128)(2,1)S(1)}, u32[]{:S(2)}, u32[]{:S(2)}) collective-permute-start(bf16[192,128]{1,0:T(8,128)(2,1)S(1)} %get-tuple-element.91), channel_id=1, source_target_pairs={{0,6},{4,2},{10,12},{16,22},{20,18},{26,28},{3,5},{9,15},{13,11},{... | collective-permute-start | bytes 147464 | tf_op jit(solution)/shard_map/ppermute | solution.py:102
  120.9 13.4 %collective-permute-start.18 = (bf16[192,128]{1,0:T(8,128)(2,1)S(1)}, bf16[192,128]{1,0:T(8,128)(2,1)S(1)}, u32[]{:S(2)}, u32[]{:S(2)}) collective-permute-start(bf16[192,128]{1,0:T(8,128)(2,1)S(1)} %get-tuple-element.90), channel_id=1, source_target_pairs={{0,8},{4,12},{10,2},{16,24},{20,28},{26,18},{3,11},{9,1},{13,5},{1... | collective-permute-start | bytes 147464 | tf_op jit(solution)/shard_map/ppermute | solution.py:102
  122.2 14.0 %collective-permute-start.19 = (bf16[192,128]{1,0:T(8,128)(2,1)S(1)}, bf16[192,128]{1,0:T(8,128)(2,1)S(1)}, u32[]{:S(2)}, u32[]{:S(2)}) collective-permute-start(bf16[192,128]{1,0:T(8,128)(2,1)S(1)} %get-tuple-element.89), channel_id=1, source_target_pairs={{0,10},{4,14},{10,0},{16,26},{20,30},{26,16},{3,9},{9,3},{13,7},{1... | collective-permute-start | bytes 147464 | tf_op jit(solution)/shard_map/ppermute | solution.py:102
  128.6 8.9 %collective-permute-start.20 = (bf16[192,128]{1,0:T(8,128)(2,1)S(1)}, bf16[192,128]{1,0:T(8,128)(2,1)S(1)}, u32[]{:S(2)}, u32[]{:S(2)}) collective-permute-start(bf16[192,128]{1,0:T(8,128)(2,1)S(1)} %get-tuple-element.88), channel_id=1, source_target_pairs={{0,12},{4,8},{10,6},{16,28},{20,24},{26,22},{3,15},{9,5},{13,1},{1... | collective-permute-start | bytes 147464 | tf_op jit(solution)/shard_map/ppermute | solution.py:102
  129.9 9.5 %collective-permute-start.21 = (bf16[192,128]{1,0:T(8,128)(2,1)S(1)}, bf16[192,128]{1,0:T(8,128)(2,1)S(1)}, u32[]{:S(2)}, u32[]{:S(2)}) collective-permute-start(bf16[192,128]{1,0:T(8,128)(2,1)S(1)} %get-tuple-element.87), channel_id=1, source_target_pairs={{0,14},{4,10},{10,4},{16,30},{20,26},{26,20},{3,13},{9,7},{13,3},{... | collective-permute-start | bytes 147464 | tf_op jit(solution)/shard_map/ppermute | solution.py:102
  133.1 8.3 %collective-permute-start.22 = (bf16[192,128]{1,0:T(8,128)(2,1)S(1)}, bf16[192,128]{1,0:T(8,128)(2,1)S(1)}, u32[]{:S(2)}, u32[]{:S(2)}) collective-permute-start(bf16[192,128]{1,0:T(8,128)(2,1)S(1)} %get-tuple-element.86), channel_id=1, source_target_pairs={{0,16},{4,20},{10,26},{16,0},{20,4},{26,10},{3,19},{9,25},{13,29},... | collective-permute-start | bytes 147464 | tf_op jit(solution)/shard_map/ppermute | solution.py:102
  134.3 10.8 %collective-permute-start.23 = (bf16[192,128]{1,0:T(8,128)(2,1)S(1)}, bf16[192,128]{1,0:T(8,128)(2,1)S(1)}, u32[]{:S(2)}, u32[]{:S(2)}) collective-permute-start(bf16[192,128]{1,0:T(8,128)(2,1)S(1)} %get-tuple-element.85), channel_id=1, source_target_pairs={{0,18},{4,22},{10,24},{16,2},{20,6},{26,8},{3,17},{9,27},{13,31},{... | collective-permute-start | bytes 147464 | tf_op jit(solution)/shard_map/ppermute | solution.py:102
  136.3 10.2 %collective-permute-start.24 = (bf16[192,128]{1,0:T(8,128)(2,1)S(1)}, bf16[192,128]{1,0:T(8,128)(2,1)S(1)}, u32[]{:S(2)}, u32[]{:S(2)}) collective-permute-start(bf16[192,128]{1,0:T(8,128)(2,1)S(1)} %get-tuple-element.84), channel_id=1, source_target_pairs={{0,20},{4,16},{10,30},{16,4},{20,0},{26,14},{3,23},{9,29},{13,25},... | collective-permute-start | bytes 147464 | tf_op jit(solution)/shard_map/ppermute | solution.py:102
  137.5 15.8 %collective-permute-start.25 = (bf16[192,128]{1,0:T(8,128)(2,1)S(1)}, bf16[192,128]{1,0:T(8,128)(2,1)S(1)}, u32[]{:S(2)}, u32[]{:S(2)}) collective-permute-start(bf16[192,128]{1,0:T(8,128)(2,1)S(1)} %get-tuple-element.83), channel_id=1, source_target_pairs={{0,22},{4,18},{10,28},{16,6},{20,2},{26,12},{3,21},{9,31},{13,27},... | collective-permute-start | bytes 147464 | tf_op jit(solution)/shard_map/ppermute | solution.py:102
  139.4 14.5 %collective-permute-start.26 = (bf16[192,128]{1,0:T(8,128)(2,1)S(1)}, bf16[192,128]{1,0:T(8,128)(2,1)S(1)}, u32[]{:S(2)}, u32[]{:S(2)}) collective-permute-start(bf16[192,128]{1,0:T(8,128)(2,1)S(1)} %get-tuple-element.82), channel_id=1, source_target_pairs={{0,24},{4,28},{10,18},{16,8},{20,12},{26,2},{3,27},{9,17},{13,21},... | collective-permute-start | bytes 147464 | tf_op jit(solution)/shard_map/ppermute | solution.py:102
  141.4 13.2 %collective-permute-start.27 = (bf16[192,128]{1,0:T(8,128)(2,1)S(1)}, bf16[192,128]{1,0:T(8,128)(2,1)S(1)}, u32[]{:S(2)}, u32[]{:S(2)}) collective-permute-start(bf16[192,128]{1,0:T(8,128)(2,1)S(1)} %get-tuple-element.81), channel_id=1, source_target_pairs={{0,26},{4,30},{10,16},{16,10},{20,14},{26,0},{3,25},{9,19},{13,23}... | collective-permute-start | bytes 147464 | tf_op jit(solution)/shard_map/ppermute | solution.py:102
  145.1 10.1 %collective-permute-start.28 = (bf16[192,128]{1,0:T(8,128)(2,1)S(1)}, bf16[192,128]{1,0:T(8,128)(2,1)S(1)}, u32[]{:S(2)}, u32[]{:S(2)}) collective-permute-start(bf16[192,128]{1,0:T(8,128)(2,1)S(1)} %get-tuple-element.80), channel_id=1, source_target_pairs={{0,28},{4,24},{10,22},{16,12},{20,8},{26,6},{3,31},{9,21},{13,17},... | collective-permute-start | bytes 147464 | tf_op jit(solution)/shard_map/ppermute | solution.py:102
  146.4 9.4 %collective-permute-start.29 = (bf16[192,128]{1,0:T(8,128)(2,1)S(1)}, bf16[192,128]{1,0:T(8,128)(2,1)S(1)}, u32[]{:S(2)}, u32[]{:S(2)}) collective-permute-start(bf16[192,128]{1,0:T(8,128)(2,1)S(1)} %get-tuple-element.79), channel_id=1, source_target_pairs={{0,30},{4,26},{10,20},{16,14},{20,10},{26,4},{3,29},{9,23},{13,19}... | collective-permute-start | bytes 147464 | tf_op jit(solution)/shard_map/ppermute | solution.py:102
  159.6 18.2 %collective-permute-start.30 = (bf16[192,768]{1,0:T(8,128)(2,1)}, bf16[192,768]{1,0:T(8,128)(2,1)S(1)}, u32[]{:S(2)}, u32[]{:S(2)}) collective-permute-start(bf16[192,768]{1,0:T(8,128)(2,1)} %constant_dynamic-slice_fusion), channel_id=1, source_target_pairs={{0,1},{1,0},{2,3},{3,2},{4,5},{5,4},{6,7},{7,6},{8,9},{9,8},{10,11... | collective-permute-start | bytes 884744 | tf_op jit(solution)/shard_map/ppermute | solution.py:111
  (6 other events, 34.4 us)

commit v2 on v1

v2 whole, which is shorter than its diff:
```python
import functools
import math

import jax
import jax.numpy as jnp
from jax import lax
from jax.experimental import pallas as pl
from jax.experimental.pallas import tpu as pltpu
from jax.sharding import PartitionSpec as P

HEAD_DIM = 128
STEPS = 1000
KEY_BLOCK = 512
QUERY_BLOCK = 256
NEG = -1e30
VMEM_LIMIT = 40 * 1024 * 1024


def noise_level(step_value):
    frac = step_value / STEPS
    return 5.0 * frac / (1.0 + 4.0 * frac)


def head_slots(half, heads_here):
    return [slot for slot in range(half) if slot % 4 != 3][:heads_here]


def pairs_out(chips, tp, heads_here, colour):
    half = chips // 2
    slots = head_slots(half, heads_here)
    pairs = []
    for chip in range(chips):
        for core in range(tp):
            slot = (chip % half) ^ colour
            if slot in slots:
                owner = slot + half * (1 - core)
                pairs.append((chip * tp + core, owner * tp + chip // half))
    return pairs


def any_spec():
    return pl.BlockSpec(memory_space=pl.ANY)


def vmem_spec():
    return pl.BlockSpec(memory_space=pltpu.VMEM)


def smem_spec():
    return pl.BlockSpec(memory_space=pltpu.SMEM)


def modulation_kernel(act_ref, weight_ref, block_ref, out_ref):
    row = pl.program_id(0)
    act = jnp.transpose(jnp.broadcast_to(act_ref[...], (8, act_ref.shape[1])))[:, :1]
    total = jnp.sum(act * weight_ref[...], axis=0, keepdims=True)
    out_ref[0] = total + block_ref[pl.ds(row, 1), :]


def modulate(act, time_weight, block_mod):
    freq, wide = time_weight.shape
    width = wide // 3
    return pl.pallas_call(
        modulation_kernel,
        grid=(3,),
        in_specs=[
            pl.BlockSpec((1, freq), lambda i: (0, 0)),
            pl.BlockSpec((freq, width), lambda i: (0, i)),
            pl.BlockSpec((3, width), lambda i: (0, 0)),
        ],
        out_specs=pl.BlockSpec((1, 1, width), lambda i: (i, 0, 0)),
        out_shape=jax.ShapeDtypeStruct((3, 1, width), jnp.float32),
        compiler_params=pltpu.CompilerParams(vmem_limit_bytes=VMEM_LIMIT),
        cost_estimate=pl.CostEstimate(flops=2 * freq * wide, bytes_accessed=4 * freq * wide, transcendentals=0),
    )(act, time_weight, block_mod)


def project_kernel(half, slots, own_ref, other_ref, mod_ref, wq_ref, wk_ref, wv_ref, *rest):
    outs, (full, normed, packed, sems) = rest[:half], rest[half:]
    step = pl.program_id(0)
    share = own_ref.shape[1]
    core = lax.axis_index("tp")
    place = lax.rem(lax.axis_index("req"), half)

    @pl.when(step == 0)
    def _():
        full[:, pl.ds(pl.multiple_of(core * share, 128), share)] = own_ref[...].astype(jnp.float32)
        full[:, pl.ds(pl.multiple_of((1 - core) * share, 128), share)] = other_ref[...].astype(jnp.float32)
        rows = full[...]
        centred = rows - jnp.mean(rows, axis=1, keepdims=True)
        variance = jnp.mean(centred * centred, axis=1, keepdims=True)
        normed[...] = (centred * lax.rsqrt(variance + 1e-06) * (1.0 + mod_ref[1]) + mod_ref[0]).astype(jnp.bfloat16)

    factor = math.log2(math.e) / math.sqrt(HEAD_DIM)
    heads_step = wq_ref.shape[1] // HEAD_DIM
    for part, weight in enumerate((wq_ref, wk_ref, wv_ref)):
        out = jnp.dot(normed[...], weight[...], preferred_element_type=jnp.float32)
        if part == 0:
            out = out * factor
        out = out.astype(jnp.bfloat16)
        for e in range(heads_step):
            packed[step * heads_step + e, part] = out[:, e * HEAD_DIM:(e + 1) * HEAD_DIM]

    def each_copy(head, act):
        for colour in range(half):
            @pl.when((place ^ colour) == slots[head])
            def _():
                act(pltpu.make_async_copy(packed.at[head], outs[colour], sems.at[head]))

    for group in range(len(slots) // heads_step):
        @pl.when(step == group)
        def _():
            for e in range(heads_step):
                each_copy(group * heads_step + e, lambda copy: copy.start())

    @pl.when(step == len(slots) // heads_step - 1)
    def _():
        for head in range(len(slots)):
            each_copy(head, lambda copy: copy.wait())


def project(own, other, mod, w_query, w_key, w_value, half, slots):
    rows, share = own.shape
    depth, columns = w_query.shape
    heads_step = 2 if len(slots) % 2 == 0 else 1
    wide = heads_step * HEAD_DIM
    weight = pl.BlockSpec((depth, wide), lambda i: (0, i))
    piece = jax.ShapeDtypeStruct((3, rows, HEAD_DIM), jnp.bfloat16)
    return pl.pallas_call(
        functools.partial(project_kernel, half, slots),
        grid=(columns // wide,),
        in_specs=[
            pl.BlockSpec((rows, share), lambda i: (0, 0)),
            pl.BlockSpec((rows, share), lambda i: (0, 0)),
            pl.BlockSpec(mod.shape, lambda i: (0, 0, 0)),
            weight, weight, weight,
        ],
        out_specs=[any_spec()] * half,
        out_shape=[piece] * half,
        scratch_shapes=[
            pltpu.VMEM((rows, depth), jnp.float32),
            pltpu.VMEM((rows, depth), jnp.bfloat16),
            pltpu.VMEM((len(slots), 3, rows, HEAD_DIM), jnp.bfloat16),
            pltpu.SemaphoreType.DMA((len(slots),)),
        ],
        compiler_params=pltpu.CompilerParams(vmem_limit_bytes=VMEM_LIMIT),
    )(own, other, mod, w_query, w_key, w_value)


def collect_kernel(*refs):
    pieces, out, sems = refs[:-2], refs[-2], refs[-1]
    copies = [pltpu.make_async_copy(p.at[pl.ds(1, 2)], out.at[k], sems.at[k]) for k, p in enumerate(pieces)]
    for copy in copies:
        copy.start()
    for copy in copies:
        copy.wait()


def collect(pieces):
    _, rows, wide = pieces[0].shape
    return pl.pallas_call(
        collect_kernel,
        in_specs=[any_spec()] * len(pieces),
        out_specs=any_spec(),
        out_shape=jax.ShapeDtypeStruct((len(pieces), 2, rows, wide), jnp.bfloat16),
        scratch_shapes=[pltpu.SemaphoreType.DMA((len(pieces),))],
    )(*pieces)


def attend_kernel(half, slots, lengths_ref, *refs):
    pieces, swapped = refs[:half], refs[half]
    outs = refs[half + 1:2 * half + 1]
    query, keys, values, result, top, total, sems, out_sems = refs[2 * half + 1:]
    rows = pieces[0].shape[1]
    side = lax.axis_index("tp")
    place = lax.rem(lax.axis_index("req"), half)
    active = functools.reduce(jnp.logical_or, [place == slot for slot in slots])

    def at(colour, whole):
        here = (place ^ colour) * rows
        return pl.ds(pl.multiple_of(here if whole is None else here + whole * (half * rows), 64), rows)

    @pl.when(active)
    def _():
        copies = []
        for colour in range(half):
            mine, theirs = at(colour, side), at(colour, 1 - side)
            for source, target in (
                (pieces[colour].at[0], query.at[at(colour, None)]),
                (pieces[colour].at[1], keys.at[mine]),
                (pieces[colour].at[2], values.at[mine, pl.ds(0, HEAD_DIM)]),
                (swapped.at[colour, 0], keys.at[theirs]),
                (swapped.at[colour, 1], values.at[theirs, pl.ds(0, HEAD_DIM)]),
            ):
                copies.append(pltpu.make_async_copy(source, target, sems.at[len(copies)]))
        for copy in copies:
            copy.start()
        values[:, HEAD_DIM:] = jnp.ones((values.shape[0], HEAD_DIM), jnp.bfloat16)
        for copy in copies:
            copy.wait()
        ends, end = [], jnp.int32(0)
        for video in range(lengths_ref.shape[0]):
            end = end + lengths_ref[video]
            ends.append(end)
        starts = [jnp.int32(0)] + ends[:-1]

        def query_block(block, carry):
            local = pl.multiple_of(block * QUERY_BLOCK, QUERY_BLOCK)
            first = side * (half * rows) + local
            last = first + QUERY_BLOCK - 1
            low, high = jnp.int32(0), jnp.int32(0)
            index = first + lax.broadcasted_iota(jnp.int32, (QUERY_BLOCK, 1), 0)
            row_low = jnp.zeros((QUERY_BLOCK, 1), jnp.int32)
            row_high = jnp.zeros((QUERY_BLOCK, 1), jnp.int32)
            for start, stop in zip(starts, ends):
                low = jnp.where(first >= start, start, low)
                high = jnp.where(last >= start, stop, high)
                row_low = jnp.where(index >= start, start, row_low)
                row_high = jnp.where(index >= start, stop, row_high)
            q = query[pl.ds(local, QUERY_BLOCK), :]
            top[...] = jnp.full(top.shape, NEG, jnp.float32)
            total[...] = jnp.zeros(total.shape, jnp.float32)

            def key_block(number, carry):
                begin = pl.multiple_of(number * KEY_BLOCK, KEY_BLOCK)
                score = lax.dot_general(
                    q, keys[pl.ds(begin, KEY_BLOCK), :], (((1,), (1,)), ((), ())), preferred_element_type=jnp.float32
                )
                column = begin + lax.broadcasted_iota(jnp.int32, score.shape, 1)
                score = jnp.where((column >= row_low) & (column < row_high), score, NEG)
                before = top[...]
                now = jnp.maximum(before, jnp.max(score, axis=1, keepdims=True))
                probs = jnp.exp2(score - now).astype(jnp.bfloat16)
                update = jnp.dot(probs, values[pl.ds(begin, KEY_BLOCK), :], preferred_element_type=jnp.float32)
                total[...] = total[...] * jnp.exp2(before - now) + update
                top[...] = now
                return carry

            lax.fori_loop(low // KEY_BLOCK, (high + KEY_BLOCK - 1) // KEY_BLOCK, key_block, 0)
            out = total[:, :HEAD_DIM] / total[:, HEAD_DIM:]
            result[pl.ds(local, QUERY_BLOCK), :] = out.astype(jnp.bfloat16)
            return carry

        lax.fori_loop(0, half * rows // QUERY_BLOCK, query_block, 0)
        copies = [
            pltpu.make_async_copy(result.at[at(colour, None)], outs[colour], out_sems.at[colour])
            for colour in range(half)
        ]
        for copy in copies:
            copy.start()
        for copy in copies:
            copy.wait()


def attend(lengths, pieces, swapped, half, slots):
    rows = pieces[0].shape[1]
    own = half * rows
    piece = jax.ShapeDtypeStruct((rows, HEAD_DIM), jnp.bfloat16)
    return pl.pallas_call(
        functools.partial(attend_kernel, half, slots),
        in_specs=[smem_spec()] + [any_spec()] * (half + 1),
        out_specs=[any_spec()] * half,
        out_shape=[piece] * half,
        scratch_shapes=[
            pltpu.VMEM((own, HEAD_DIM), jnp.bfloat16),
            pltpu.VMEM((2 * own, HEAD_DIM), jnp.bfloat16),
            pltpu.VMEM((2 * own, 2 * HEAD_DIM), jnp.bfloat16),
            pltpu.VMEM((own, HEAD_DIM), jnp.bfloat16),
            pltpu.VMEM((QUERY_BLOCK, 1), jnp.float32),
            pltpu.VMEM((QUERY_BLOCK, 2 * HEAD_DIM), jnp.float32),
            pltpu.SemaphoreType.DMA((5 * half,)),
            pltpu.SemaphoreType.DMA((half,)),
        ],
        compiler_params=pltpu.CompilerParams(vmem_limit_bytes=VMEM_LIMIT),
    )(lengths, *pieces, swapped)


def combine_kernel(half, slots, *refs):
    pieces, weight = refs[:half], refs[half]
    mine, theirs, attended, sems = refs[half + 1:]
    share = mine.shape[1]
    core = lax.axis_index("tp")
    place = lax.rem(lax.axis_index("req"), half)

    def each_copy(act):
        for head, slot in enumerate(slots):
            for colour in range(half):
                @pl.when((place ^ colour) == slot)
                def _():
                    target = attended.at[:, pl.ds(head * HEAD_DIM, HEAD_DIM)]
                    act(pltpu.make_async_copy(pieces[colour], target, sems.at[head]))

    each_copy(lambda copy: copy.start())
    each_copy(lambda copy: copy.wait())
    left = attended[...]
    for out, where in ((theirs, 1 - core), (mine, core)):
        columns = pl.ds(pl.multiple_of(where * share, 128), share)
        out[...] = jnp.dot(left, weight[:, columns], preferred_element_type=jnp.float32).astype(out.dtype)


def combine(pieces, w_out, half, slots):
    rows = pieces[0].shape[0]
    depth, width = w_out.shape
    return pl.pallas_call(
        functools.partial(combine_kernel, half, slots),
        in_specs=[any_spec()] * half + [vmem_spec()],
        out_specs=[vmem_spec(), vmem_spec()],
        out_shape=[
            jax.ShapeDtypeStruct((rows, width // 2), jnp.float32),
            jax.ShapeDtypeStruct((rows, width // 2), jnp.bfloat16),
        ],
        scratch_shapes=[
            pltpu.VMEM((rows, depth), jnp.bfloat16),
            pltpu.SemaphoreType.DMA((len(slots),)),
        ],
        compiler_params=pltpu.CompilerParams(vmem_limit_bytes=VMEM_LIMIT),
    )(*pieces, w_out)


def finish_kernel(timestep_ref, mine, theirs, tokens, mod_ref, velocity, stepped):
    share = tokens.shape[1]
    core = lax.axis_index("tp")
    step_value = jnp.full((1, 128), timestep_ref[0], jnp.int32).astype(jnp.float32)
    delta = (noise_level(step_value - 1.0) - noise_level(step_value))[:, :1]
    gate = mod_ref[2, :, pl.ds(pl.multiple_of(core * share, 128), share)]
    branch = gate * (mine[...] + theirs[...].astype(jnp.float32))
    velocity[...] = branch.astype(jnp.bfloat16)
    stepped[...] = (tokens[...].astype(jnp.float32) + delta * branch).astype(jnp.bfloat16)


def finish(timestep, mine, theirs, tokens, mod):
    shape = jax.ShapeDtypeStruct(tokens.shape, jnp.bfloat16)
    return pl.pallas_call(
        finish_kernel,
        in_specs=[smem_spec()] + [vmem_spec()] * 4,
        out_specs=[vmem_spec(), vmem_spec()],
        out_shape=[shape, shape],
    )(timestep, mine, theirs, tokens, mod)


def make(mesh):
    chips, tp = mesh.shape["req"], mesh.shape["tp"]
    half = chips // 2
    swap = [(0, 1), (1, 0)]

    def on_device(tokens, video_lengths, timestep, time_weight, block_mod, w_query, w_key, w_value, w_out):
        heads_here = w_query.shape[1] // HEAD_DIM
        slots = head_slots(half, heads_here)
        routes = [pairs_out(chips, tp, heads_here, colour) for colour in range(half)]
        other = lax.ppermute(tokens, "tp", swap)
        half_freq = time_weight.shape[0] // 2
        time_value = jnp.broadcast_to(timestep, (half_freq,)).astype(jnp.float32)
        sigma = noise_level(time_value)
        frequency = jnp.exp(-math.log(10000.0) * jnp.arange(half_freq, dtype=jnp.float32) / half_freq)
        angle = 1000.0 * sigma * frequency
        act = jax.nn.silu(jnp.concatenate([jnp.cos(angle), jnp.sin(angle)]))[None, :]
        mod = modulate(act, time_weight, block_mod)
        sent = project(tokens, other, mod, w_query, w_key, w_value, half, slots)
        got = [lax.ppermute(piece, ("req", "tp"), route) for piece, route in zip(sent, routes)]
        swapped = lax.ppermute(collect(got), "tp", swap)
        done = attend(video_lengths, got, swapped, half, slots)
        back = [
            lax.ppermute(piece, ("req", "tp"), [(b, a) for a, b in route]) for piece, route in zip(done, routes)
        ]
        mine, theirs = combine(back, w_out, half, slots)
        theirs = lax.ppermute(theirs, "tp", swap)
        velocity, stepped = finish(timestep, mine, theirs, tokens, mod)
        return (velocity, stepped)

    return on_device


def solution(mesh):
    return jax.shard_map(
        make(mesh),
        mesh=mesh,
        in_specs=(
            P("req", "tp"), P(), P(), P(), P(), P(None, "tp"), P(None, "tp"), P(None, "tp"), P("tp", None),
        ),
        out_specs=(P("req", "tp"), P("req", "tp")),
        check_vma=False,
    )
```

time: 180 us -> 145 us (0.81)
  the two profiles are of different devices: /device:TPU:27 before, /device:TPU:5 now
where the time goes in v2:
time: 145 us; the launch traced here: 144 us
  Pallas kernels  55.4 us (38%)
  starting transfers between devices  53.2 us (37%)
  waiting for transfers between devices  17.2 us (12%)
  local copies, waits for them, and re-layouts  16.2 us (11%)
  between operations  1.77 us (1%)
    ppermute x8, starting transfers between devices, on_device(): lax.ppermute(piece, ('req', 'tp'), route)  25.9 us
    pallas_call x1, Pallas kernels, collect(): pl.pallas_call(collect_kernel, in_specs=[any_spec()] * len(pieces), out_s...  25 us
    ppermute x8, starting transfers between devices, on_device(): lax.ppermute(piece, ('req', 'tp'), [(b, a) for a, b in route])  21.8 us
    pallas_call x1, Pallas kernels, attend(): pl.pallas_call(functools.partial(attend_kernel, half, slots), in_specs=[s...  21.5 us
    unnamed x54, local copies, waits for them, and re-layouts  16.2 us
    ppermute x8, waiting for transfers between devices, on_device(): lax.ppermute(piece, ('req', 'tp'), route)  8.82 us
    ppermute x1, starting transfers between devices, on_device(): theirs = lax.ppermute(theirs, 'tp', swap)  4.75 us
    ppermute x8, waiting for transfers between devices, on_device(): lax.ppermute(piece, ('req', 'tp'), [(b, a) for a, b in route])  4.68 us
  transfers between devices with their start and end apart: 19, of which 6 were waited for; matrix products, arithmetic and copies ran while one was open for 0% of the time, Pallas kernels for 1%

profile of v2, /device:TPU:5, one launch (start us, length us, event | category | flops | bytes accessed | tf_op | source)
XLA Modules:
  0.0 143.9 jit_solution(13443066603471727809)
XLA Ops:
  2.2 2.3 %copy-done = f32[256,4608]{1,0:T(8,128)S(1)} copy-done((f32[256,4608]{1,0:T(8,128)S(1)}, f32[256,4608]{1,0:T(8,128)}, u32[]{:S(2)}) %copy-start) | copy-done | bytes 4718616
  5.2 1.3 shard_map.104.mod_ref
  7.6 1.7 %copy-done.4 = bf16[1536,768]{1,0:T(8,128)(2,1)S(1)} copy-done((bf16[1536,768]{1,0:T(8,128)(2,1)S(1)}, bf16[1536,768]{1,0:T(8,128)(2,1)}, u32[]{:S(2)}) %copy-start.4) | copy-done | bytes 2359320
  9.3 1.0 copy-done.5
  10.2 4.5 %shard_map.105 = (bf16[3,192,128]{2,1,0:T(8,128)(2,1)S(1)}, bf16[3,192,128]{2,1,0:T(8,128)(2,1)S(1)}, bf16[3,192,128]{2,1,0:T(8,128)(2,1)S(1)}, bf16[3,192,128]{...) custom-call(bf16[192,768]{1,0:T(8,128)(2,1)S(1)} %copy-done.5, ...), custom_call_target="tpu_custom_call" | custom-call | tf_op jit(solution)/shard_map/pallas_call | solution.py:129
  14.8 2.1 %collective-permute-start.1 = (bf16[3,192,128]{2,1,0:T(8,128)(2,1)S(1)}, bf16[3,192,128]{2,1,0:T(8,128)(2,1)S(1)}, u32[]{:S(2)}, u32[]{:S(2)}) collective-permute-start(bf16[3,192,128]{2,1,0:T(8,128)(2,1)S(1)} %get-tuple-element.20), channel_id=1, source_target_pairs={{0,16},{1,0},{2,18},{3,2},{4,20},{5,4},{8,24},{9,8},{10,26},{11,10... | collective-permute-start | bytes 442376 | tf_op jit(solution)/shard_map/ppermute | solution.py:359
  16.8 1.3 collective-permute-start.2
  18.1 6.7 %collective-permute-start.3 = (bf16[3,192,128]{2,1,0:T(8,128)(2,1)S(1)}, bf16[3,192,128]{2,1,0:T(8,128)(2,1)S(1)}, u32[]{:S(2)}, u32[]{:S(2)}) collective-permute-start(bf16[3,192,128]{2,1,0:T(8,128)(2,1)S(1)} %get-tuple-element.22), channel_id=1, source_target_pairs={{0,20},{1,4},{4,16},{5,0},{6,18},{7,2},{8,28},{9,12},{12,24},{13,8... | collective-permute-start | bytes 442376 | tf_op jit(solution)/shard_map/ppermute | solution.py:359
  24.8 1.9 %collective-permute-start.4 = (bf16[3,192,128]{2,1,0:T(8,128)(2,1)S(1)}, bf16[3,192,128]{2,1,0:T(8,128)(2,1)S(1)}, u32[]{:S(2)}, u32[]{:S(2)}) collective-permute-start(bf16[3,192,128]{2,1,0:T(8,128)(2,1)S(1)} %get-tuple-element.23), channel_id=1, source_target_pairs={{2,20},{3,4},{4,18},{5,2},{6,16},{7,0},{10,28},{11,12},{12,26},{13... | collective-permute-start | bytes 442376 | tf_op jit(solution)/shard_map/ppermute | solution.py:359
  26.7 3.1 %collective-permute-start.5 = (bf16[3,192,128]{2,1,0:T(8,128)(2,1)S(1)}, bf16[3,192,128]{2,1,0:T(8,128)(2,1)S(1)}, u32[]{:S(2)}, u32[]{:S(2)}) collective-permute-start(bf16[3,192,128]{2,1,0:T(8,128)(2,1)S(1)} %get-tuple-element.24), channel_id=1, source_target_pairs={{0,24},{1,8},{2,26},{3,10},{4,28},{5,12},{8,16},{9,0},{10,18},{11,... | collective-permute-start | bytes 442376 | tf_op jit(solution)/shard_map/ppermute | solution.py:359
  29.9 1.3 collective-permute-start.6
  31.2 7.6 %collective-permute-start.7 = (bf16[3,192,128]{2,1,0:T(8,128)(2,1)S(1)}, bf16[3,192,128]{2,1,0:T(8,128)(2,1)S(1)}, u32[]{:S(2)}, u32[]{:S(2)}) collective-permute-start(bf16[3,192,128]{2,1,0:T(8,128)(2,1)S(1)} %get-tuple-element.26), channel_id=1, source_target_pairs={{0,28},{1,12},{4,24},{5,8},{6,26},{7,10},{8,20},{9,4},{12,16},{13,... | collective-permute-start | bytes 442376 | tf_op jit(solution)/shard_map/ppermute | solution.py:359
  38.8 1.9 %collective-permute-start.8 = (bf16[3,192,128]{2,1,0:T(8,128)(2,1)S(1)}, bf16[3,192,128]{2,1,0:T(8,128)(2,1)S(1)}, u32[]{:S(2)}, u32[]{:S(2)}) collective-permute-start(bf16[3,192,128]{2,1,0:T(8,128)(2,1)S(1)} %get-tuple-element.27), channel_id=1, source_target_pairs={{2,28},{3,12},{4,26},{5,10},{6,24},{7,8},{10,20},{11,4},{12,18},{1... | collective-permute-start | bytes 442376 | tf_op jit(solution)/shard_map/ppermute | solution.py:359
  40.8 3.4 %collective-permute-done.7.refs_6_ = bf16[3,192,128]{2,1,0:T(8,128)(2,1)S(1)} collective-permute-done((bf16[3,192,128]{2,1,0:T(8,128)(2,1)S(1)}, bf16[3,192,128]{2,1,0:T(8,128)(2,1)S(1)}, u32[]{:S(2)}, u32[]{:S(2)}) %collective-permute-start.7) | collective-permute-done | bytes 147488 | tf_op jit(solution)/shard_map/ppermute | solution.py:359
  44.2 5.5 %collective-permute-done.8.refs_7_ = bf16[3,192,128]{2,1,0:T(8,128)(2,1)S(1)} collective-permute-done((bf16[3,192,128]{2,1,0:T(8,128)(2,1)S(1)}, bf16[3,192,128]{2,1,0:T(8,128)(2,1)S(1)}, u32[]{:S(2)}, u32[]{:S(2)}) %collective-permute-start.8) | collective-permute-done | bytes 147488 | tf_op jit(solution)/shard_map/ppermute | solution.py:359
  50.3 25.0 %shard_map.106 = bf16[8,2,192,128]{3,2,1,0:T(8,128)(2,1)} custom-call(bf16[3,192,128]{2,1,0:T(8,128)(2,1)} %copy-done.7, bf16[3,192,128]{2,1,0:T(8,128)(2,1)} %copy-done.9, bf16[3,192,128]{2,1,0:T(8,128)(2,1)} %copy-done.11, bf16[3,192,128]{2,1,0:T(8,128)(2,1)} %copy-done.13, bf16[3,192,128]{2,1,0:T(8,128)(2,1)} %copy-done.15, ...), custom_call_target="tpu_custom_call" | custom-call | tf_op jit(solution)/shard_map/pallas_call | solution.py:161
  75.4 2.5 %collective-permute-done.9.refs_8_ = bf16[8,2,192,128]{3,2,1,0:T(8,128)(2,1)S(1)} collective-permute-done((bf16[8,2,192,128]{3,2,1,0:T(8,128)(2,1)}, bf16[8,2,192,128]{3,2,1,0:T(8,128)(2,1)S(1)}, u32[]{:S(2)}, u32[]{:S(2)}) %collective-permute-start.9) | collective-permute-done | bytes 786464 | tf_op jit(solution)/shard_map/ppermute | solution.py:360
  85.2 21.5 %shard_map.107 = (bf16[192,128]{1,0:T(8,128)(2,1)S(1)}, bf16[192,128]{1,0:T(8,128)(2,1)S(1)}, bf16[192,128]{1,0:T(8,128)(2,1)S(1)}, bf16[192,128]{1,0:T(8,128)(2...) custom-call(s32[5]{0:T(128)S(1)} %copy-done.25, ...), custom_call_target="tpu_custom_call" | custom-call | tf_op jit(solution)/shard_map/pallas_call | solution.py:259
  106.7 2.5 %collective-permute-start.10 = (bf16[192,128]{1,0:T(8,128)(2,1)S(1)}, bf16[192,128]{1,0:T(8,128)(2,1)S(1)}, u32[]{:S(2)}, u32[]{:S(2)}) collective-permute-start(bf16[192,128]{1,0:T(8,128)(2,1)S(1)} %get-tuple-element.28), channel_id=1, source_target_pairs={{16,0},{0,1},{18,2},{2,3},{20,4},{4,5},{24,8},{8,9},{26,10},{10,11... | collective-permute-start | bytes 147464 | tf_op jit(solution)/shard_map/ppermute | solution.py:363
  109.2 1.3 collective-permute-start.11
  110.5 1.9 %collective-permute-start.12 = (bf16[192,128]{1,0:T(8,128)(2,1)S(1)}, bf16[192,128]{1,0:T(8,128)(2,1)S(1)}, u32[]{:S(2)}, u32[]{:S(2)}) collective-permute-start(bf16[192,128]{1,0:T(8,128)(2,1)S(1)} %get-tuple-element.30), channel_id=1, source_target_pairs={{20,0},{4,1},{16,4},{0,5},{18,6},{2,7},{28,8},{12,9},{24,12},{8,13... | collective-permute-start | bytes 147464 | tf_op jit(solution)/shard_map/ppermute | solution.py:363
  112.4 1.9 %collective-permute-start.13 = (bf16[192,128]{1,0:T(8,128)(2,1)S(1)}, bf16[192,128]{1,0:T(8,128)(2,1)S(1)}, u32[]{:S(2)}, u32[]{:S(2)}) collective-permute-start(bf16[192,128]{1,0:T(8,128)(2,1)S(1)} %get-tuple-element.31), channel_id=1, source_target_pairs={{20,2},{4,3},{18,4},{2,5},{16,6},{0,7},{28,10},{12,11},{26,12},{10... | collective-permute-start | bytes 147464 | tf_op jit(solution)/shard_map/ppermute | solution.py:363
  114.3 5.6 %collective-permute-start.14 = (bf16[192,128]{1,0:T(8,128)(2,1)S(1)}, bf16[192,128]{1,0:T(8,128)(2,1)S(1)}, u32[]{:S(2)}, u32[]{:S(2)}) collective-permute-start(bf16[192,128]{1,0:T(8,128)(2,1)S(1)} %get-tuple-element.32), channel_id=1, source_target_pairs={{24,0},{8,1},{26,2},{10,3},{28,4},{12,5},{16,8},{0,9},{18,10},{2,1... | collective-permute-start | bytes 147464 | tf_op jit(solution)/shard_map/ppermute | solution.py:363
  120.0 1.3 collective-permute-start.15
  121.3 4.7 %collective-permute-start.16 = (bf16[192,128]{1,0:T(8,128)(2,1)S(1)}, bf16[192,128]{1,0:T(8,128)(2,1)S(1)}, u32[]{:S(2)}, u32[]{:S(2)}) collective-permute-start(bf16[192,128]{1,0:T(8,128)(2,1)S(1)} %get-tuple-element.34), channel_id=1, source_target_pairs={{28,0},{12,1},{24,4},{8,5},{26,6},{10,7},{20,8},{4,9},{16,12},{0,1... | collective-permute-start | bytes 147464 | tf_op jit(solution)/shard_map/ppermute | solution.py:363
  126.1 2.5 %collective-permute-start.17 = (bf16[192,128]{1,0:T(8,128)(2,1)S(1)}, bf16[192,128]{1,0:T(8,128)(2,1)S(1)}, u32[]{:S(2)}, u32[]{:S(2)}) collective-permute-start(bf16[192,128]{1,0:T(8,128)(2,1)S(1)} %get-tuple-element.35), channel_id=1, source_target_pairs={{28,2},{12,3},{26,4},{10,5},{24,6},{8,7},{20,10},{4,11},{18,12},{2... | collective-permute-start | bytes 147464 | tf_op jit(solution)/shard_map/ppermute | solution.py:363
  128.6 2.4 %collective-permute-done.16.refs_6_ = bf16[192,128]{1,0:T(8,128)(2,1)S(1)} collective-permute-done((bf16[192,128]{1,0:T(8,128)(2,1)S(1)}, bf16[192,128]{1,0:T(8,128)(2,1)S(1)}, u32[]{:S(2)}, u32[]{:S(2)}) %collective-permute-start.16) | collective-permute-done | bytes 49184 | tf_op jit(solution)/shard_map/ppermute | solution.py:363
  131.0 2.2 %collective-permute-done.17.refs_7_ = bf16[192,128]{1,0:T(8,128)(2,1)S(1)} collective-permute-done((bf16[192,128]{1,0:T(8,128)(2,1)S(1)}, bf16[192,128]{1,0:T(8,128)(2,1)S(1)}, u32[]{:S(2)}, u32[]{:S(2)}) %collective-permute-start.17) | collective-permute-done | bytes 49184 | tf_op jit(solution)/shard_map/ppermute | solution.py:363
  133.3 1.0 shard_map.108
  135.1 4.7 %collective-permute-start.18 = (bf16[192,768]{1,0:T(8,128)(2,1)S(1)}, bf16[192,768]{1,0:T(8,128)(2,1)S(1)}, u32[]{:S(2)}, u32[]{:S(2)}) collective-permute-start(bf16[192,768]{1,0:T(8,128)(2,1)S(1)} %get-tuple-element.37), channel_id=1, source_target_pairs={{0,1},{1,0},{2,3},{3,2},{4,5},{5,4},{6,7},{7,6},{8,9},{9,8},{10,11... | collective-permute-start | bytes 884744 | tf_op jit(solution)/shard_map/ppermute | solution.py:366
  139.8 1.2 collective-permute-done.18.theirs
  141.7 2.1 %shard_map.109 = (bf16[192,768]{1,0:T(8,128)(2,1)}, bf16[192,768]{1,0:T(8,128)(2,1)}) custom-call(s32[1]{0:T(128)S(6)} %copy.11.timestep_ref, f32[192,768]{1,0:T(8,128)} %copy-done.6, bf16[192,768]{1,0:T(8,128)(2,1)} %copy-done.26, bf16[192,768]{1,0:T(8,128)(2,1)} %tokens.1, f32[3,1,1536]{2,1,0:T(1,128)} %copy-done.23), custom_call_target="tpu_custom_call" | custom-call | tf_op jit(solution)/shard_map/pallas_call | solution.py:333
  (68 shorter events, 12.2 us)
Async XLA Ops:
  0.6 5.9 %collective-permute-start = (bf16[192,768]{1,0:T(8,128)(2,1)}, bf16[192,768]{1,0:T(8,128)(2,1)S(1)}, u32[]{:S(2)}, u32[]{:S(2)}) collective-permute-start(bf16[192,768]{1,0:T(8,128)(2,1)} %tokens.1), channel_id=1, source_target_pairs={{0,1},{1,0},{2,3},{3,2},{4,5},{5,4},{6,7},{7,6},{8,9},{9,8},{10,11... | collective-permute-start | bytes 884744 | tf_op jit(solution)/shard_map/ppermute | solution.py:350
  2.1 2.3 %copy-start = (f32[256,4608]{1,0:T(8,128)S(1)}, f32[256,4608]{1,0:T(8,128)}, u32[]{:S(2)}) copy-start(f32[256,4608]{1,0:T(8,128)} %weight_ref.1) | copy-start | bytes 14155780
  5.2 1.7 %copy-start.2 = (bf16[1536,768]{1,0:T(8,128)(2,1)S(1)}, bf16[1536,768]{1,0:T(8,128)(2,1)}, u32[]{:S(2)}) copy-start(bf16[1536,768]{1,0:T(8,128)(2,1)} %wq_ref.1) | copy-start | bytes 7077892
  5.2 2.4 %copy-start.3 = (bf16[1536,768]{1,0:T(8,128)(2,1)S(1)}, bf16[1536,768]{1,0:T(8,128)(2,1)}, u32[]{:S(2)}) copy-start(bf16[1536,768]{1,0:T(8,128)(2,1)} %wk_ref.1) | copy-start | bytes 7077892
  6.5 8.2 %copy-start.23 = (f32[3,1,1536]{2,1,0:T(1,128)}, f32[3,1,1536]{2,1,0:T(1,128)S(1)}, u32[]{:S(2)}) copy-start(f32[3,1,1536]{2,1,0:T(1,128)S(1)} %shard_map.104.mod_ref) | copy-start | bytes 55300
  10.2 67.6 %copy-start.25 = (s32[5]{0:T(128)S(1)}, s32[5]{0:T(128)}, u32[]{:S(2)}) copy-start(s32[5]{0:T(128)} %lengths_ref.1) | copy-start | bytes 64
  14.7 118.5 %copy-start.1 = (bf16[768,1536]{1,0:T(8,128)(2,1)S(1)}, bf16[768,1536]{1,0:T(8,128)(2,1)}, u32[]{:S(2)}) copy-start(bf16[768,1536]{1,0:T(8,128)(2,1)} %refs_8_.1) | copy-start | bytes 7077892
  14.8 15.1 %collective-permute-start.1 = (bf16[3,192,128]{2,1,0:T(8,128)(2,1)S(1)}, bf16[3,192,128]{2,1,0:T(8,128)(2,1)S(1)}, u32[]{:S(2)}, u32[]{:S(2)}) collective-permute-start(bf16[3,192,128]{2,1,0:T(8,128)(2,1)S(1)} %get-tuple-element.20), channel_id=1, source_target_pairs={{0,16},{1,0},{2,18},{3,2},{4,20},{5,4},{8,24},{9,8},{10,26},{11,10... | collective-permute-start | bytes 442376 | tf_op jit(solution)/shard_map/ppermute | solution.py:359
  16.8 14.4 %collective-permute-start.2 = (bf16[3,192,128]{2,1,0:T(8,128)(2,1)S(1)}, bf16[3,192,128]{2,1,0:T(8,128)(2,1)S(1)}, u32[]{:S(2)}, u32[]{:S(2)}) collective-permute-start(bf16[3,192,128]{2,1,0:T(8,128)(2,1)S(1)} %get-tuple-element.21), channel_id=1, source_target_pairs={{0,18},{1,2},{2,16},{3,0},{6,20},{7,4},{8,26},{9,10},{10,24},{11,8... | collective-permute-start | bytes 442376 | tf_op jit(solution)/shard_map/ppermute | solution.py:359
  18.1 20.7 %collective-permute-start.3 = (bf16[3,192,128]{2,1,0:T(8,128)(2,1)S(1)}, bf16[3,192,128]{2,1,0:T(8,128)(2,1)S(1)}, u32[]{:S(2)}, u32[]{:S(2)}) collective-permute-start(bf16[3,192,128]{2,1,0:T(8,128)(2,1)S(1)} %get-tuple-element.22), channel_id=1, source_target_pairs={{0,20},{1,4},{4,16},{5,0},{6,18},{7,2},{8,28},{9,12},{12,24},{13,8... | collective-permute-start | bytes 442376 | tf_op jit(solution)/shard_map/ppermute | solution.py:359
  24.8 16.0 %collective-permute-start.4 = (bf16[3,192,128]{2,1,0:T(8,128)(2,1)S(1)}, bf16[3,192,128]{2,1,0:T(8,128)(2,1)S(1)}, u32[]{:S(2)}, u32[]{:S(2)}) collective-permute-start(bf16[3,192,128]{2,1,0:T(8,128)(2,1)S(1)} %get-tuple-element.23), channel_id=1, source_target_pairs={{2,20},{3,4},{4,18},{5,2},{6,16},{7,0},{10,28},{11,12},{12,26},{13... | collective-permute-start | bytes 442376 | tf_op jit(solution)/shard_map/ppermute | solution.py:359
  26.7 14.1 %collective-permute-start.5 = (bf16[3,192,128]{2,1,0:T(8,128)(2,1)S(1)}, bf16[3,192,128]{2,1,0:T(8,128)(2,1)S(1)}, u32[]{:S(2)}, u32[]{:S(2)}) collective-permute-start(bf16[3,192,128]{2,1,0:T(8,128)(2,1)S(1)} %get-tuple-element.24), channel_id=1, source_target_pairs={{0,24},{1,8},{2,26},{3,10},{4,28},{5,12},{8,16},{9,0},{10,18},{11,... | collective-permute-start | bytes 442376 | tf_op jit(solution)/shard_map/ppermute | solution.py:359
  29.9 19.7 %copy-start.7 = (bf16[3,192,128]{2,1,0:T(8,128)(2,1)}, bf16[3,192,128]{2,1,0:T(8,128)(2,1)S(1)}, u32[]{:S(2)}) copy-start(bf16[3,192,128]{2,1,0:T(8,128)(2,1)S(1)} %collective-permute-done.1.refs_0_) | copy-start | bytes 442372
  29.9 10.9 %collective-permute-start.6 = (bf16[3,192,128]{2,1,0:T(8,128)(2,1)S(1)}, bf16[3,192,128]{2,1,0:T(8,128)(2,1)S(1)}, u32[]{:S(2)}, u32[]{:S(2)}) collective-permute-start(bf16[3,192,128]{2,1,0:T(8,128)(2,1)S(1)} %get-tuple-element.25), channel_id=1, source_target_pairs={{0,26},{1,10},{2,24},{3,8},{6,28},{7,12},{8,18},{9,2},{10,16},{11,... | collective-permute-start | bytes 442376 | tf_op jit(solution)/shard_map/ppermute | solution.py:359
  31.2 18.4 %copy-start.9 = (bf16[3,192,128]{2,1,0:T(8,128)(2,1)}, bf16[3,192,128]{2,1,0:T(8,128)(2,1)S(1)}, u32[]{:S(2)}) copy-start(bf16[3,192,128]{2,1,0:T(8,128)(2,1)S(1)} %collective-permute-done.2.refs_1_) | copy-start | bytes 442372
  31.2 12.9 %collective-permute-start.7 = (bf16[3,192,128]{2,1,0:T(8,128)(2,1)S(1)}, bf16[3,192,128]{2,1,0:T(8,128)(2,1)S(1)}, u32[]{:S(2)}, u32[]{:S(2)}) collective-permute-start(bf16[3,192,128]{2,1,0:T(8,128)(2,1)S(1)} %get-tuple-element.26), channel_id=1, source_target_pairs={{0,28},{1,12},{4,24},{5,8},{6,26},{7,10},{8,20},{9,4},{12,16},{13,... | collective-permute-start | bytes 442376 | tf_op jit(solution)/shard_map/ppermute | solution.py:359
  38.8 10.8 %copy-start.11 = (bf16[3,192,128]{2,1,0:T(8,128)(2,1)}, bf16[3,192,128]{2,1,0:T(8,128)(2,1)S(1)}, u32[]{:S(2)}) copy-start(bf16[3,192,128]{2,1,0:T(8,128)(2,1)S(1)} %collective-permute-done.3.refs_2_) | copy-start | bytes 442372
  38.8 10.8 %collective-permute-start.8 = (bf16[3,192,128]{2,1,0:T(8,128)(2,1)S(1)}, bf16[3,192,128]{2,1,0:T(8,128)(2,1)S(1)}, u32[]{:S(2)}, u32[]{:S(2)}) collective-permute-start(bf16[3,192,128]{2,1,0:T(8,128)(2,1)S(1)} %get-tuple-element.27), channel_id=1, source_target_pairs={{2,28},{3,12},{4,26},{5,10},{6,24},{7,8},{10,20},{11,4},{12,18},{1... | collective-permute-start | bytes 442376 | tf_op jit(solution)/shard_map/ppermute | solution.py:359
  40.8 8.9 %copy-start.13 = (bf16[3,192,128]{2,1,0:T(8,128)(2,1)}, bf16[3,192,128]{2,1,0:T(8,128)(2,1)S(1)}, u32[]{:S(2)}) copy-start(bf16[3,192,128]{2,1,0:T(8,128)(2,1)S(1)} %collective-permute-done.4.refs_3_) | copy-start | bytes 442372
  40.8 8.9 %copy-start.15 = (bf16[3,192,128]{2,1,0:T(8,128)(2,1)}, bf16[3,192,128]{2,1,0:T(8,128)(2,1)S(1)}, u32[]{:S(2)}) copy-start(bf16[3,192,128]{2,1,0:T(8,128)(2,1)S(1)} %collective-permute-done.5.refs_4_) | copy-start | bytes 442372
  40.8 8.9 %copy-start.17 = (bf16[3,192,128]{2,1,0:T(8,128)(2,1)}, bf16[3,192,128]{2,1,0:T(8,128)(2,1)S(1)}, u32[]{:S(2)}) copy-start(bf16[3,192,128]{2,1,0:T(8,128)(2,1)S(1)} %collective-permute-done.6.refs_5_) | copy-start | bytes 442372
  44.2 5.5 %copy-start.19 = (bf16[3,192,128]{2,1,0:T(8,128)(2,1)}, bf16[3,192,128]{2,1,0:T(8,128)(2,1)S(1)}, u32[]{:S(2)}) copy-start(bf16[3,192,128]{2,1,0:T(8,128)(2,1)S(1)} %collective-permute-done.7.refs_6_) | copy-start | bytes 442372
  75.3 2.6 %collective-permute-start.9 = (bf16[8,2,192,128]{3,2,1,0:T(8,128)(2,1)}, bf16[8,2,192,128]{3,2,1,0:T(8,128)(2,1)S(1)}, u32[]{:S(2)}, u32[]{:S(2)}) collective-permute-start(bf16[8,2,192,128]{3,2,1,0:T(8,128)(2,1)} %shard_map.106), channel_id=1, source_target_pairs={{0,1},{1,0},{2,3},{3,2},{4,5},{5,4},{6,7},{7,6},{8,9},{9,8},{10,11... | collective-permute-start | bytes 2359304 | tf_op jit(solution)/shard_map/ppermute | solution.py:360
  106.7 13.3 %collective-permute-start.10 = (bf16[192,128]{1,0:T(8,128)(2,1)S(1)}, bf16[192,128]{1,0:T(8,128)(2,1)S(1)}, u32[]{:S(2)}, u32[]{:S(2)}) collective-permute-start(bf16[192,128]{1,0:T(8,128)(2,1)S(1)} %get-tuple-element.28), channel_id=1, source_target_pairs={{16,0},{0,1},{18,2},{2,3},{20,4},{4,5},{24,8},{8,9},{26,10},{10,11... | collective-permute-start | bytes 147464 | tf_op jit(solution)/shard_map/ppermute | solution.py:363
  109.2 12.1 %collective-permute-start.11 = (bf16[192,128]{1,0:T(8,128)(2,1)S(1)}, bf16[192,128]{1,0:T(8,128)(2,1)S(1)}, u32[]{:S(2)}, u32[]{:S(2)}) collective-permute-start(bf16[192,128]{1,0:T(8,128)(2,1)S(1)} %get-tuple-element.29), channel_id=1, source_target_pairs={{18,0},{2,1},{16,2},{0,3},{20,6},{4,7},{26,8},{10,9},{24,10},{8,11... | collective-permute-start | bytes 147464 | tf_op jit(solution)/shard_map/ppermute | solution.py:363
  110.5 15.6 %collective-permute-start.12 = (bf16[192,128]{1,0:T(8,128)(2,1)S(1)}, bf16[192,128]{1,0:T(8,128)(2,1)S(1)}, u32[]{:S(2)}, u32[]{:S(2)}) collective-permute-start(bf16[192,128]{1,0:T(8,128)(2,1)S(1)} %get-tuple-element.30), channel_id=1, source_target_pairs={{20,0},{4,1},{16,4},{0,5},{18,6},{2,7},{28,8},{12,9},{24,12},{8,13... | collective-permute-start | bytes 147464 | tf_op jit(solution)/shard_map/ppermute | solution.py:363
  112.4 16.2 %collective-permute-start.13 = (bf16[192,128]{1,0:T(8,128)(2,1)S(1)}, bf16[192,128]{1,0:T(8,128)(2,1)S(1)}, u32[]{:S(2)}, u32[]{:S(2)}) collective-permute-start(bf16[192,128]{1,0:T(8,128)(2,1)S(1)} %get-tuple-element.31), channel_id=1, source_target_pairs={{20,2},{4,3},{18,4},{2,5},{16,6},{0,7},{28,10},{12,11},{26,12},{10... | collective-permute-start | bytes 147464 | tf_op jit(solution)/shard_map/ppermute | solution.py:363
  114.3 14.3 %collective-permute-start.14 = (bf16[192,128]{1,0:T(8,128)(2,1)S(1)}, bf16[192,128]{1,0:T(8,128)(2,1)S(1)}, u32[]{:S(2)}, u32[]{:S(2)}) collective-permute-start(bf16[192,128]{1,0:T(8,128)(2,1)S(1)} %get-tuple-element.32), channel_id=1, source_target_pairs={{24,0},{8,1},{26,2},{10,3},{28,4},{12,5},{16,8},{0,9},{18,10},{2,1... | collective-permute-start | bytes 147464 | tf_op jit(solution)/shard_map/ppermute | solution.py:363
  120.0 8.6 %collective-permute-start.15 = (bf16[192,128]{1,0:T(8,128)(2,1)S(1)}, bf16[192,128]{1,0:T(8,128)(2,1)S(1)}, u32[]{:S(2)}, u32[]{:S(2)}) collective-permute-start(bf16[192,128]{1,0:T(8,128)(2,1)S(1)} %get-tuple-element.33), channel_id=1, source_target_pairs={{26,0},{10,1},{24,2},{8,3},{28,6},{12,7},{18,8},{2,9},{16,10},{0,1... | collective-permute-start | bytes 147464 | tf_op jit(solution)/shard_map/ppermute | solution.py:363
  121.3 9.7 %collective-permute-start.16 = (bf16[192,128]{1,0:T(8,128)(2,1)S(1)}, bf16[192,128]{1,0:T(8,128)(2,1)S(1)}, u32[]{:S(2)}, u32[]{:S(2)}) collective-permute-start(bf16[192,128]{1,0:T(8,128)(2,1)S(1)} %get-tuple-element.34), channel_id=1, source_target_pairs={{28,0},{12,1},{24,4},{8,5},{26,6},{10,7},{20,8},{4,9},{16,12},{0,1... | collective-permute-start | bytes 147464 | tf_op jit(solution)/shard_map/ppermute | solution.py:363
  126.1 7.2 %collective-permute-start.17 = (bf16[192,128]{1,0:T(8,128)(2,1)S(1)}, bf16[192,128]{1,0:T(8,128)(2,1)S(1)}, u32[]{:S(2)}, u32[]{:S(2)}) collective-permute-start(bf16[192,128]{1,0:T(8,128)(2,1)S(1)} %get-tuple-element.35), channel_id=1, source_target_pairs={{28,2},{12,3},{26,4},{10,5},{24,6},{8,7},{20,10},{4,11},{18,12},{2... | collective-permute-start | bytes 147464 | tf_op jit(solution)/shard_map/ppermute | solution.py:363
  135.1 6.0 %collective-permute-start.18 = (bf16[192,768]{1,0:T(8,128)(2,1)S(1)}, bf16[192,768]{1,0:T(8,128)(2,1)S(1)}, u32[]{:S(2)}, u32[]{:S(2)}) collective-permute-start(bf16[192,768]{1,0:T(8,128)(2,1)S(1)} %get-tuple-element.37), channel_id=1, source_target_pairs={{0,1},{1,0},{2,3},{3,2},{4,5},{5,4},{6,7},{7,6},{8,9},{9,8},{10,11... | collective-permute-start | bytes 884744 | tf_op jit(solution)/shard_map/ppermute | solution.py:366
  (14 other events, 12.8 us)

commit v3 on v2

--- a/solution.py
+++ b/solution.py
@@ -11,9 +11,10 @@
 HEAD_DIM = 128
 STEPS = 1000
 KEY_BLOCK = 512
-QUERY_BLOCK = 256
+QUERY_BLOCK = 512
 NEG = -1e30
-VMEM_LIMIT = 40 * 1024 * 1024
+STREAM_LIMIT = 60 * 1024 * 1024
+VMEM_LIMIT = 32 * 1024 * 1024
 
 
 def noise_level(step_value):
@@ -32,10 +33,14 @@
     for chip in range(chips):
         for core in range(tp):
             slot = (chip % half) ^ colour
-            if slot in slots:
-                owner = slot + half * (1 - core)
-                pairs.append((chip * tp + core, owner * tp + chip // half))
+            source, target = chip * tp + core, (slot + half * core) * tp + chip // half
+            if slot in slots and source != target:
+                pairs.append((source, target))
     return pairs
+
+
+def is_own(half):
+    return lax.axis_index("req") // half == lax.axis_index("tp")
 
 
 def any_spec():
@@ -70,7 +75,7 @@
         ],
         out_specs=pl.BlockSpec((1, 1, width), lambda i: (i, 0, 0)),
         out_shape=jax.ShapeDtypeStruct((3, 1, width), jnp.float32),
-        compiler_params=pltpu.CompilerParams(vmem_limit_bytes=VMEM_LIMIT),
+        compiler_params=pltpu.CompilerParams(vmem_limit_bytes=STREAM_LIMIT),
         cost_estimate=pl.CostEstimate(flops=2 * freq * wide, bytes_accessed=4 * freq * wide, transcendentals=0),
     )(act, time_weight, block_mod)
 
@@ -143,82 +148,120 @@
             pltpu.VMEM((len(slots), 3, rows, HEAD_DIM), jnp.bfloat16),
             pltpu.SemaphoreType.DMA((len(slots),)),
         ],
+        compiler_params=pltpu.CompilerParams(vmem_limit_bytes=STREAM_LIMIT),
+    )(own, other, mod, w_query, w_key, w_value)
+
+
+def collect_kernel(half, sent_ref, *refs):
+    pieces, out, sems = refs[:half], refs[half], refs[half + 1]
+    own = is_own(half)
+
+    def each_copy(act):
+        for colour, piece in enumerate(pieces):
+            copy = pltpu.make_async_copy(piece.at[pl.ds(1, 2)], out.at[colour], sems.at[colour])
+            if colour:
+                act(copy)
+            else:
+                pl.when(jnp.logical_not(own))(functools.partial(act, copy))
+                local = pltpu.make_async_copy(sent_ref.at[pl.ds(1, 2)], out.at[colour], sems.at[colour])
+                pl.when(own)(functools.partial(act, local))
+
+    each_copy(lambda copy: copy.start())
+    each_copy(lambda copy: copy.wait())
+
+
+def collect(sent, pieces, half):
+    _, rows, wide = sent.shape
+    return pl.pallas_call(
+        functools.partial(collect_kernel, half),
+        in_specs=[any_spec()] * (half + 1),
+        out_specs=any_spec(),
+        out_shape=jax.ShapeDtypeStruct((half, 2, rows, wide), jnp.bfloat16),
+        scratch_shapes=[pltpu.SemaphoreType.DMA((half,))],
         compiler_params=pltpu.CompilerParams(vmem_limit_bytes=VMEM_LIMIT),
-    )(own, other, mod, w_query, w_key, w_value)
-
-
-def collect_kernel(*refs):
-    pieces, out, sems = refs[:-2], refs[-2], refs[-1]
-    copies = [pltpu.make_async_copy(p.at[pl.ds(1, 2)], out.at[k], sems.at[k]) for k, p in enumerate(pieces)]
-    for copy in copies:
-        copy.start()
-    for copy in copies:
-        copy.wait()
-
-
-def collect(pieces):
-    _, rows, wide = pieces[0].shape
-    return pl.pallas_call(
-        collect_kernel,
-        in_specs=[any_spec()] * len(pieces),
-        out_specs=any_spec(),
-        out_shape=jax.ShapeDtypeStruct((len(pieces), 2, rows, wide), jnp.bfloat16),
-        scratch_shapes=[pltpu.SemaphoreType.DMA((len(pieces),))],
-    )(*pieces)
-
-
-def attend_kernel(half, slots, lengths_ref, *refs):
+    )(sent, *pieces)
+
+
+def attend_kernel(half, slots, lengths_ref, sent_ref, *refs):
     pieces, swapped = refs[:half], refs[half]
     outs = refs[half + 1:2 * half + 1]
     query, keys, values, result, top, total, sems, out_sems = refs[2 * half + 1:]
     rows = pieces[0].shape[1]
     side = lax.axis_index("tp")
     place = lax.rem(lax.axis_index("req"), half)
+    own = is_own(half)
     active = functools.reduce(jnp.logical_or, [place == slot for slot in slots])
-
-    def at(colour, whole):
-        here = (place ^ colour) * rows
-        return pl.ds(pl.multiple_of(here if whole is None else here + whole * (half * rows), 64), rows)
+    front = pl.ds(0, HEAD_DIM)
+
+    def at(colour, which):
+        return pl.ds(pl.multiple_of((place ^ colour) * rows + which * (half * rows), 64), rows)
+
+    def each_copy(act):
+        for colour in range(half):
+            def load(piece, colour=colour):
+                for part, target in enumerate((
+                    query.at[at(colour, 0), front],
+                    keys.at[at(colour, side), front],
+                    values.at[at(colour, side), front],
+                )):
+                    act(pltpu.make_async_copy(piece.at[part], target, sems.at[5 * colour + part]))
+
+            if colour:
+                load(pieces[colour])
+            else:
+                pl.when(jnp.logical_not(own))(functools.partial(load, pieces[0]))
+                pl.when(own)(functools.partial(load, sent_ref))
+            for part, target in enumerate((keys, values)):
+                target = target.at[at(colour, 1 - side), front]
+                act(pltpu.make_async_copy(swapped.at[colour, part], target, sems.at[5 * colour + 3 + part]))
 
     @pl.when(active)
     def _():
-        copies = []
-        for colour in range(half):
-            mine, theirs = at(colour, side), at(colour, 1 - side)
-            for source, target in (
-                (pieces[colour].at[0], query.at[at(colour, None)]),
-                (pieces[colour].at[1], keys.at[mine]),
-                (pieces[colour].at[2], values.at[mine, pl.ds(0, HEAD_DIM)]),
-                (swapped.at[colour, 0], keys.at[theirs]),
-                (swapped.at[colour, 1], values.at[theirs, pl.ds(0, HEAD_DIM)]),
-            ):
-                copies.append(pltpu.make_async_copy(source, target, sems.at[len(copies)]))
-        for copy in copies:
-            copy.start()
-        values[:, HEAD_DIM:] = jnp.ones((values.shape[0], HEAD_DIM), jnp.bfloat16)
-        for copy in copies:
-            copy.wait()
+        each_copy(lambda copy: copy.start())
         ends, end = [], jnp.int32(0)
         for video in range(lengths_ref.shape[0]):
             end = end + lengths_ref[video]
             ends.append(end)
         starts = [jnp.int32(0)] + ends[:-1]
+        lane = lax.broadcasted_iota(jnp.int32, (1, HEAD_DIM), 1)
+        lane_start = jnp.zeros((1, HEAD_DIM), jnp.int32)
+        lane_stop = jnp.zeros((1, HEAD_DIM), jnp.int32)
+        for video, (start, stop) in enumerate(zip(starts, ends)):
+            lane_start = jnp.where(lane == video, start, lane_start)
+            lane_stop = jnp.where(lane == video, stop, lane_stop)
+
+        def inside(first, count):
+            index = first + lax.broadcasted_iota(jnp.int32, (count, HEAD_DIM), 0)
+            return (index >= lane_start) & (index < lane_stop)
+
+        def fill_query(block, carry):
+            local = pl.multiple_of(block * QUERY_BLOCK, QUERY_BLOCK)
+            member = inside(side * (half * rows) + local, QUERY_BLOCK)
+            query[pl.ds(local, QUERY_BLOCK), HEAD_DIM:] = jnp.where(member, 1.0, 0.0).astype(jnp.bfloat16)
+            return carry
+
+        def fill_keys(block, carry):
+            begin = pl.multiple_of(block * KEY_BLOCK, KEY_BLOCK)
+            keys[pl.ds(begin, KEY_BLOCK), HEAD_DIM:] = jnp.where(
+                inside(begin, KEY_BLOCK) | (lane >= lengths_ref.shape[0]), 0.0, NEG
+            ).astype(jnp.bfloat16)
+            values[pl.ds(begin, KEY_BLOCK), HEAD_DIM:] = jnp.ones((KEY_BLOCK, HEAD_DIM), jnp.bfloat16)
+            return carry
+
+        lax.fori_loop(0, half * rows // QUERY_BLOCK, fill_query, 0)
+        lax.fori_loop(0, 2 * half * rows // KEY_BLOCK, fill_keys, 0)
+        each_copy(lambda copy: copy.wait())
 
         def query_block(block, carry):
             local = pl.multiple_of(block * QUERY_BLOCK, QUERY_BLOCK)
             first = side * (half * rows) + local
             last = first + QUERY_BLOCK - 1
             low, high = jnp.int32(0), jnp.int32(0)
-            index = first + lax.broadcasted_iota(jnp.int32, (QUERY_BLOCK, 1), 0)
-            row_low = jnp.zeros((QUERY_BLOCK, 1), jnp.int32)
-            row_high = jnp.zeros((QUERY_BLOCK, 1), jnp.int32)
             for start, stop in zip(starts, ends):
                 low = jnp.where(first >= start, start, low)
                 high = jnp.where(last >= start, stop, high)
-                row_low = jnp.where(index >= start, start, row_low)
-                row_high = jnp.where(index >= start, stop, row_high)
             q = query[pl.ds(local, QUERY_BLOCK), :]
-            top[...] = jnp.full(top.shape, NEG, jnp.float32)
+            top[...] = jnp.full(top.shape, 2 * NEG, jnp.float32)
             total[...] = jnp.zeros(total.shape, jnp.float32)
 
             def key_block(number, carry):
@@ -226,13 +269,15 @@
                 score = lax.dot_general(
                     q, keys[pl.ds(begin, KEY_BLOCK), :], (((1,), (1,)), ((), ())), preferred_element_type=jnp.float32
                 )
-                column = begin + lax.broadcasted_iota(jnp.int32, score.shape, 1)
-                score = jnp.where((column >= row_low) & (column < row_high), score, NEG)
+                tiles = [score[:, k:k + HEAD_DIM] for k in range(0, KEY_BLOCK, HEAD_DIM)]
+                most = jnp.max(functools.reduce(jnp.maximum, tiles), axis=1, keepdims=True)
                 before = top[...]
-                now = jnp.maximum(before, jnp.max(score, axis=1, keepdims=True))
-                probs = jnp.exp2(score - now).astype(jnp.bfloat16)
+                now = jnp.maximum(before, most)
+                probs = jnp.concatenate([jnp.exp2(tile - now).astype(jnp.bfloat16) for tile in tiles], axis=1)
                 update = jnp.dot(probs, values[pl.ds(begin, KEY_BLOCK), :], preferred_element_type=jnp.float32)
-                total[...] = total[...] * jnp.exp2(before - now) + update
+                shrink = jnp.exp2(before - now)
+                total[:, :HEAD_DIM] = total[:, :HEAD_DIM] * shrink + update[:, :HEAD_DIM]
+                total[:, HEAD_DIM:] = total[:, HEAD_DIM:] * shrink + update[:, HEAD_DIM:]
                 top[...] = now
                 return carry
 
@@ -243,7 +288,7 @@
 
         lax.fori_loop(0, half * rows // QUERY_BLOCK, query_block, 0)
         copies = [
-            pltpu.make_async_copy(result.at[at(colour, None)], outs[colour], out_sems.at[colour])
+            pltpu.make_async_copy(result.at[at(colour, 0)], outs[colour], out_sems.at[colour])
             for colour in range(half)
         ]
         for copy in copies:
@@ -252,31 +297,32 @@
             copy.wait()
 
 
-def attend(lengths, pieces, swapped, half, slots):
-    rows = pieces[0].shape[1]
+def attend(lengths, sent, pieces, swapped, half, slots):
+    rows = sent.shape[1]
     own = half * rows
     piece = jax.ShapeDtypeStruct((rows, HEAD_DIM), jnp.bfloat16)
     return pl.pallas_call(
         functools.partial(attend_kernel, half, slots),
-        in_specs=[smem_spec()] + [any_spec()] * (half + 1),
+        in_specs=[smem_spec()] + [any_spec()] * (half + 2),
         out_specs=[any_spec()] * half,
         out_shape=[piece] * half,
         scratch_shapes=[
-            pltpu.VMEM((own, HEAD_DIM), jnp.bfloat16),
-            pltpu.VMEM((2 * own, HEAD_DIM), jnp.bfloat16),
+            pltpu.VMEM((own, 2 * HEAD_DIM), jnp.bfloat16),
+            pltpu.VMEM((2 * own, 2 * HEAD_DIM), jnp.bfloat16),
             pltpu.VMEM((2 * own, 2 * HEAD_DIM), jnp.bfloat16),
             pltpu.VMEM((own, HEAD_DIM), jnp.bfloat16),
-            pltpu.VMEM((QUERY_BLOCK, 1), jnp.float32),
+            pltpu.VMEM((QUERY_BLOCK, HEAD_DIM), jnp.float32),
             pltpu.VMEM((QUERY_BLOCK, 2 * HEAD_DIM), jnp.float32),
             pltpu.SemaphoreType.DMA((5 * half,)),
             pltpu.SemaphoreType.DMA((half,)),
         ],
         compiler_params=pltpu.CompilerParams(vmem_limit_bytes=VMEM_LIMIT),
-    )(lengths, *pieces, swapped)
-
-
-def combine_kernel(half, slots, *refs):
+    )(lengths, sent, *pieces, swapped)
+
+
+def combine_kernel(half, slots, done_ref, *refs):
     pieces, weight = refs[:half], refs[half]
+    own = is_own(half)
     mine, theirs, attended, sems = refs[half + 1:]
     share = mine.shape[1]
     core = lax.axis_index("tp")
@@ -288,7 +334,13 @@
                 @pl.when((place ^ colour) == slot)
                 def _():
                     target = attended.at[:, pl.ds(head * HEAD_DIM, HEAD_DIM)]
-                    act(pltpu.make_async_copy(pieces[colour], target, sems.at[head]))
+                    copy = pltpu.make_async_copy(pieces[colour], target, sems.at[head])
+                    if colour:
+                        act(copy)
+                    else:
+                        pl.when(jnp.logical_not(own))(functools.partial(act, copy))
+                        local = pltpu.make_async_copy(done_ref, target, sems.at[head])
+                        pl.when(own)(functools.partial(act, local))
 
     each_copy(lambda copy: copy.start())
     each_copy(lambda copy: copy.wait())
@@ -298,12 +350,12 @@
         out[...] = jnp.dot(left, weight[:, columns], preferred_element_type=jnp.float32).astype(out.dtype)
 
 
-def combine(pieces, w_out, half, slots):
-    rows = pieces[0].shape[0]
+def combine(done, pieces, w_out, half, slots):
+    rows = done.shape[0]
     depth, width = w_out.shape
     return pl.pallas_call(
         functools.partial(combine_kernel, half, slots),
-        in_specs=[any_spec()] * half + [vmem_spec()],
+        in_specs=[any_spec()] * (half + 1) + [vmem_spec()],
         out_specs=[vmem_spec(), vmem_spec()],
         out_shape=[
             jax.ShapeDtypeStruct((rows, width // 2), jnp.float32),
@@ -314,7 +366,7 @@
             pltpu.SemaphoreType.DMA((len(slots),)),
         ],
         compiler_params=pltpu.CompilerParams(vmem_limit_bytes=VMEM_LIMIT),
-    )(*pieces, w_out)
+    )(done, *pieces, w_out)
 
 
 def finish_kernel(timestep_ref, mine, theirs, tokens, mod_ref, velocity, stepped):
@@ -335,6 +387,7 @@
         in_specs=[smem_spec()] + [vmem_spec()] * 4,
         out_specs=[vmem_spec(), vmem_spec()],
         out_shape=[shape, shape],
+        compiler_params=pltpu.CompilerParams(vmem_limit_bytes=VMEM_LIMIT),
     )(timestep, mine, theirs, tokens, mod)
 
 
@@ -357,12 +410,12 @@
         mod = modulate(act, time_weight, block_mod)
         sent = project(tokens, other, mod, w_query, w_key, w_value, half, slots)
         got = [lax.ppermute(piece, ("req", "tp"), route) for piece, route in zip(sent, routes)]
-        swapped = lax.ppermute(collect(got), "tp", swap)
-        done = attend(video_lengths, got, swapped, half, slots)
+        swapped = lax.ppermute(collect(sent[0], got, half), "tp", swap)
+        done = attend(video_lengths, sent[0], got, swapped, half, slots)
         back = [
             lax.ppermute(piece, ("req", "tp"), [(b, a) for a, b in route]) for piece, route in zip(done, routes)
         ]
-        mine, theirs = combine(back, w_out, half, slots)
+        mine, theirs = combine(done[0], back, w_out, half, slots)
         theirs = lax.ppermute(theirs, "tp", swap)
         velocity, stepped = finish(timestep, mine, theirs, tokens, mod)
         return (velocity, stepped)

time: 145 us -> 106 us (0.73)
  the two profiles are of different devices: /device:TPU:5 before, /device:TPU:3 now
where the time goes in v3:
time: 106 us; the launch traced here: 107 us
  starting transfers between devices  62 us (58%)
  Pallas kernels  27.1 us (26%)
  waiting for transfers between devices  14.2 us (13%)
  local copies, waits for them, and re-layouts  1.64 us (2%)
  between operations  1.64 us (2%)
    ppermute x8, starting transfers between devices, on_device(): lax.ppermute(piece, ('req', 'tp'), route)  30.9 us
    ppermute x8, starting transfers between devices, on_device(): lax.ppermute(piece, ('req', 'tp'), [(b, a) for a, b in route])  30.2 us
    pallas_call x1, Pallas kernels, attend(): pl.pallas_call(functools.partial(attend_kernel, half, slots), in_specs=[s...  13.5 us
    pallas_call x1, Pallas kernels, project(): pl.pallas_call(functools.partial(project_kernel, half, slots), grid=(colu...  6.54 us
    ppermute x8, waiting for transfers between devices, on_device(): lax.ppermute(piece, ('req', 'tp'), route)  5.97 us
    ppermute x8, waiting for transfers between devices, on_device(): lax.ppermute(piece, ('req', 'tp'), [(b, a) for a, b in route])  4.36 us
    pallas_call x1, Pallas kernels, modulate(): pl.pallas_call(modulation_kernel, grid=(3,), in_specs=[pl.BlockSpec((1, f...  4.11 us
    ppermute x1, waiting for transfers between devices, on_device(): swapped = lax.ppermute(collect(sent[0], got, half), 'tp', swap)  2.27 us
  transfers between devices with their start and end apart: 19, of which 5 were waited for; matrix products, arithmetic and copies ran while one was open for 1% of the time, Pallas kernels for 4%

profile of v3, /device:TPU:3, one launch (start us, length us, event | category | flops | bytes accessed | tf_op | source)
XLA Modules:
  0.0 107.2 jit_solution(7802518696681945850)
XLA Ops:
  0.6 0.7 collective-permute-start
  2.1 0.6 divide_multiply_fusion.act_ref
  2.7 4.1 %shard_map.104.mod_ref = f32[3,1,1536]{2,1,0:T(1,128)} custom-call(f32[1,256]{1,0:T(1,128)} %divide_multiply_fusion.act_ref, f32[256,4608]{1,0:T(8,128)} %weight_ref.1, f32[3,1536]{1,0:T(4,128)} %block_ref.1), custom_call_target="tpu_custom_call" | custom-call | flops 2359296 | bytes 4718592 | tf_op jit(solution)/shard_map/pallas_call | solution.py:68
  6.8 0.7 copy-done.5
  7.5 6.5 %shard_map.105 = (bf16[3,192,128]{2,1,0:T(8,128)(2,1)}, bf16[3,192,128]{2,1,0:T(8,128)(2,1)}, bf16[3,192,128]{2,1,0:T(8,128)(2,1)}, bf16[3,192,128]{2,1,0:T(8,12...) custom-call(bf16[192,768]{1,0:T(8,128)(2,1)} %tokens.1, ...), custom_call_target="tpu_custom_call" | custom-call | tf_op jit(solution)/shard_map/pallas_call | solution.py:134
  14.1 4.2 %collective-permute-start.2 = (bf16[3,192,128]{2,1,0:T(8,128)(2,1)}, bf16[3,192,128]{2,1,0:T(8,128)(2,1)S(1)}, u32[]{:S(2)}, u32[]{:S(2)}) collective-permute-start(bf16[3,192,128]{2,1,0:T(8,128)(2,1)} %get-tuple-element.21), channel_id=1, source_target_pairs={{0,2},{1,18},{2,0},{3,16},{6,4},{7,20},{8,10},{9,26},{10,8},{11,24... | collective-permute-start | bytes 442376 | tf_op jit(solution)/shard_map/ppermute | solution.py:412
  18.3 1.3 %collective-permute-start.3 = (bf16[3,192,128]{2,1,0:T(8,128)(2,1)}, bf16[3,192,128]{2,1,0:T(8,128)(2,1)S(1)}, u32[]{:S(2)}, u32[]{:S(2)}) collective-permute-start(bf16[3,192,128]{2,1,0:T(8,128)(2,1)} %get-tuple-element.22), channel_id=1, source_target_pairs={{0,4},{1,20},{4,0},{5,16},{6,2},{7,18},{8,12},{9,28},{12,8},{13,24... | collective-permute-start | bytes 442376 | tf_op jit(solution)/shard_map/ppermute | solution.py:412
  19.6 7.0 %collective-permute-start.4 = (bf16[3,192,128]{2,1,0:T(8,128)(2,1)}, bf16[3,192,128]{2,1,0:T(8,128)(2,1)S(1)}, u32[]{:S(2)}, u32[]{:S(2)}) collective-permute-start(bf16[3,192,128]{2,1,0:T(8,128)(2,1)} %get-tuple-element.23), channel_id=1, source_target_pairs={{2,4},{3,20},{4,2},{5,18},{6,0},{7,16},{10,12},{11,28},{12,10},{13... | collective-permute-start | bytes 442376 | tf_op jit(solution)/shard_map/ppermute | solution.py:412
  26.6 3.3 %collective-permute-start.5 = (bf16[3,192,128]{2,1,0:T(8,128)(2,1)}, bf16[3,192,128]{2,1,0:T(8,128)(2,1)S(1)}, u32[]{:S(2)}, u32[]{:S(2)}) collective-permute-start(bf16[3,192,128]{2,1,0:T(8,128)(2,1)} %get-tuple-element.24), channel_id=1, source_target_pairs={{0,8},{1,24},{2,10},{3,26},{4,12},{5,28},{8,0},{9,16},{10,2},{11,1... | collective-permute-start | bytes 442376 | tf_op jit(solution)/shard_map/ppermute | solution.py:412
  29.9 1.9 %collective-permute-start.6 = (bf16[3,192,128]{2,1,0:T(8,128)(2,1)}, bf16[3,192,128]{2,1,0:T(8,128)(2,1)S(1)}, u32[]{:S(2)}, u32[]{:S(2)}) collective-permute-start(bf16[3,192,128]{2,1,0:T(8,128)(2,1)} %get-tuple-element.25), channel_id=1, source_target_pairs={{0,10},{1,26},{2,8},{3,24},{6,12},{7,28},{8,2},{9,18},{10,0},{11,1... | collective-permute-start | bytes 442376 | tf_op jit(solution)/shard_map/ppermute | solution.py:412
  31.9 1.3 %collective-permute-start.7 = (bf16[3,192,128]{2,1,0:T(8,128)(2,1)}, bf16[3,192,128]{2,1,0:T(8,128)(2,1)S(1)}, u32[]{:S(2)}, u32[]{:S(2)}) collective-permute-start(bf16[3,192,128]{2,1,0:T(8,128)(2,1)} %get-tuple-element.26), channel_id=1, source_target_pairs={{0,12},{1,28},{4,8},{5,24},{6,10},{7,26},{8,4},{9,20},{12,0},{13,1... | collective-permute-start | bytes 442376 | tf_op jit(solution)/shard_map/ppermute | solution.py:412
  33.2 10.0 %collective-permute-start.8 = (bf16[3,192,128]{2,1,0:T(8,128)(2,1)}, bf16[3,192,128]{2,1,0:T(8,128)(2,1)S(1)}, u32[]{:S(2)}, u32[]{:S(2)}) collective-permute-start(bf16[3,192,128]{2,1,0:T(8,128)(2,1)} %get-tuple-element.27), channel_id=1, source_target_pairs={{2,12},{3,28},{4,10},{5,26},{6,8},{7,24},{10,4},{11,20},{12,2},{13... | collective-permute-start | bytes 442376 | tf_op jit(solution)/shard_map/ppermute | solution.py:412
  43.2 1.9 %collective-permute-start.1 = (bf16[3,192,128]{2,1,0:T(8,128)(2,1)}, bf16[3,192,128]{2,1,0:T(8,128)(2,1)S(1)}, u32[]{:S(2)}, u32[]{:S(2)}) collective-permute-start(bf16[3,192,128]{2,1,0:T(8,128)(2,1)} %get-tuple-element.20.sent_ref), channel_id=1, source_target_pairs={{1,16},{3,18},{5,20},{9,24},{11,26},{13,28},{16,1},{18,3},{20,5},{... | collective-permute-start | bytes 442376 | tf_op jit(solution)/shard_map/ppermute | solution.py:412
  45.2 1.1 collective-permute-done.8.refs_7_
  46.2 4.9 %collective-permute-done.1.refs_0_ = bf16[3,192,128]{2,1,0:T(8,128)(2,1)S(1)} collective-permute-done((bf16[3,192,128]{2,1,0:T(8,128)(2,1)}, bf16[3,192,128]{2,1,0:T(8,128)(2,1)S(1)}, u32[]{:S(2)}, u32[]{:S(2)}) %collective-permute-start.1) | collective-permute-done | bytes 147488 | tf_op jit(solution)/shard_map/ppermute | solution.py:412
  51.1 0.9 copy-done.2
  52.0 1.1 shard_map.106
  53.2 2.3 %collective-permute-done.9.refs_8_ = bf16[8,2,192,128]{3,2,1,0:T(8,128)(2,1)S(1)} collective-permute-done((bf16[8,2,192,128]{3,2,1,0:T(8,128)(2,1)S(1)}, bf16[8,2,192,128]{3,2,1,0:T(8,128)(2,1)S(1)}, u32[]{:S(2)}, u32[]{:S(2)}) %collective-permute-start.9) | collective-permute-done | bytes 786464 | tf_op jit(solution)/shard_map/ppermute | solution.py:413
  55.5 13.5 %shard_map.107 = (bf16[192,128]{1,0:T(8,128)(2,1)S(1)}, bf16[192,128]{1,0:T(8,128)(2,1)S(1)}, bf16[192,128]{1,0:T(8,128)(2,1)S(1)}, bf16[192,128]{1,0:T(8,128)(2...) custom-call(s32[5]{0:T(128)S(1)} %copy-done.4, ...), custom_call_target="tpu_custom_call" | custom-call | tf_op jit(solution)/shard_map/pallas_call | solution.py:304
  69.0 1.9 %collective-permute-start.11 = (bf16[192,128]{1,0:T(8,128)(2,1)S(1)}, bf16[192,128]{1,0:T(8,128)(2,1)S(1)}, u32[]{:S(2)}, u32[]{:S(2)}) collective-permute-start(bf16[192,128]{1,0:T(8,128)(2,1)S(1)} %get-tuple-element.29), channel_id=1, source_target_pairs={{2,0},{18,1},{0,2},{16,3},{4,6},{20,7},{10,8},{26,9},{8,10},{24,11... | collective-permute-start | bytes 147464 | tf_op jit(solution)/shard_map/ppermute | solution.py:416
  70.9 1.3 %collective-permute-start.12 = (bf16[192,128]{1,0:T(8,128)(2,1)S(1)}, bf16[192,128]{1,0:T(8,128)(2,1)S(1)}, u32[]{:S(2)}, u32[]{:S(2)}) collective-permute-start(bf16[192,128]{1,0:T(8,128)(2,1)S(1)} %get-tuple-element.30), channel_id=1, source_target_pairs={{4,0},{20,1},{0,4},{16,5},{2,6},{18,7},{12,8},{28,9},{8,12},{24,13... | collective-permute-start | bytes 147464 | tf_op jit(solution)/shard_map/ppermute | solution.py:416
  72.2 8.5 %collective-permute-start.13 = (bf16[192,128]{1,0:T(8,128)(2,1)S(1)}, bf16[192,128]{1,0:T(8,128)(2,1)S(1)}, u32[]{:S(2)}, u32[]{:S(2)}) collective-permute-start(bf16[192,128]{1,0:T(8,128)(2,1)S(1)} %get-tuple-element.31), channel_id=1, source_target_pairs={{4,2},{20,3},{2,4},{18,5},{0,6},{16,7},{12,10},{28,11},{10,12},{26... | collective-permute-start | bytes 147464 | tf_op jit(solution)/shard_map/ppermute | solution.py:416
  80.7 1.9 %collective-permute-start.14 = (bf16[192,128]{1,0:T(8,128)(2,1)S(1)}, bf16[192,128]{1,0:T(8,128)(2,1)S(1)}, u32[]{:S(2)}, u32[]{:S(2)}) collective-permute-start(bf16[192,128]{1,0:T(8,128)(2,1)S(1)} %get-tuple-element.32), channel_id=1, source_target_pairs={{8,0},{24,1},{10,2},{26,3},{12,4},{28,5},{0,8},{16,9},{2,10},{18,1... | collective-permute-start | bytes 147464 | tf_op jit(solution)/shard_map/ppermute | solution.py:416
  82.6 1.9 %collective-permute-start.15 = (bf16[192,128]{1,0:T(8,128)(2,1)S(1)}, bf16[192,128]{1,0:T(8,128)(2,1)S(1)}, u32[]{:S(2)}, u32[]{:S(2)}) collective-permute-start(bf16[192,128]{1,0:T(8,128)(2,1)S(1)} %get-tuple-element.33), channel_id=1, source_target_pairs={{10,0},{26,1},{8,2},{24,3},{12,6},{28,7},{2,8},{18,9},{0,10},{16,1... | collective-permute-start | bytes 147464 | tf_op jit(solution)/shard_map/ppermute | solution.py:416
  84.6 1.3 %collective-permute-start.16 = (bf16[192,128]{1,0:T(8,128)(2,1)S(1)}, bf16[192,128]{1,0:T(8,128)(2,1)S(1)}, u32[]{:S(2)}, u32[]{:S(2)}) collective-permute-start(bf16[192,128]{1,0:T(8,128)(2,1)S(1)} %get-tuple-element.34), channel_id=1, source_target_pairs={{12,0},{28,1},{8,4},{24,5},{10,6},{26,7},{4,8},{20,9},{0,12},{16,1... | collective-permute-start | bytes 147464 | tf_op jit(solution)/shard_map/ppermute | solution.py:416
  85.9 11.4 %collective-permute-start.17 = (bf16[192,128]{1,0:T(8,128)(2,1)S(1)}, bf16[192,128]{1,0:T(8,128)(2,1)S(1)}, u32[]{:S(2)}, u32[]{:S(2)}) collective-permute-start(bf16[192,128]{1,0:T(8,128)(2,1)S(1)} %get-tuple-element.35), channel_id=1, source_target_pairs={{12,2},{28,3},{10,4},{26,5},{8,6},{24,7},{4,10},{20,11},{2,12},{18... | collective-permute-start | bytes 147464 | tf_op jit(solution)/shard_map/ppermute | solution.py:416
  97.3 1.9 %collective-permute-start.10 = (bf16[192,128]{1,0:T(8,128)(2,1)S(1)}, bf16[192,128]{1,0:T(8,128)(2,1)S(1)}, u32[]{:S(2)}, u32[]{:S(2)}) collective-permute-start(bf16[192,128]{1,0:T(8,128)(2,1)S(1)} %get-tuple-element.28.done_ref), channel_id=1, source_target_pairs={{16,1},{18,3},{20,5},{24,9},{26,11},{28,13},{1,16},{3,18},{5,20},{... | collective-permute-start | bytes 147464 | tf_op jit(solution)/shard_map/ppermute | solution.py:416
  99.3 4.3 %collective-permute-done.10.refs_0_ = bf16[192,128]{1,0:T(8,128)(2,1)S(1)} collective-permute-done((bf16[192,128]{1,0:T(8,128)(2,1)S(1)}, bf16[192,128]{1,0:T(8,128)(2,1)S(1)}, u32[]{:S(2)}, u32[]{:S(2)}) %collective-permute-start.10) | collective-permute-done | bytes 49184 | tf_op jit(solution)/shard_map/ppermute | solution.py:416
  103.6 1.0 shard_map.108
  104.6 0.1 collective-permute-start.18
  104.7 1.6 %collective-permute-done.18.theirs = bf16[192,768]{1,0:T(8,128)(2,1)S(1)} collective-permute-done((bf16[192,768]{1,0:T(8,128)(2,1)S(1)}, bf16[192,768]{1,0:T(8,128)(2,1)S(1)}, u32[]{:S(2)}, u32[]{:S(2)}) %collective-permute-start.18) | collective-permute-done | bytes 294944 | tf_op jit(solution)/shard_map/ppermute | solution.py:419
  106.3 0.9 shard_map.109
  (26 shorter events, 0.2 us)
Async XLA Ops:
  0.6 6.2 %collective-permute-start = (bf16[192,768]{1,0:T(8,128)(2,1)}, bf16[192,768]{1,0:T(8,128)(2,1)S(1)}, u32[]{:S(2)}, u32[]{:S(2)}) collective-permute-start(bf16[192,768]{1,0:T(8,128)(2,1)} %tokens.1), channel_id=1, source_target_pairs={{0,1},{1,0},{2,3},{3,2},{4,5},{5,4},{6,7},{7,6},{8,9},{9,8},{10,11... | collective-permute-start | bytes 884744 | tf_op jit(solution)/shard_map/ppermute | solution.py:403
  6.8 48.7 %copy-start.4 = (s32[5]{0:T(128)S(1)}, s32[5]{0:T(128)}, u32[]{:S(2)}) copy-start(s32[5]{0:T(128)} %lengths_ref.1) | copy-start | bytes 64
  6.8 0.7 copy-start.5
  14.1 89.5 %copy-start = (bf16[768,1536]{1,0:T(8,128)(2,1)S(1)}, bf16[768,1536]{1,0:T(8,128)(2,1)}, u32[]{:S(2)}) copy-start(bf16[768,1536]{1,0:T(8,128)(2,1)} %refs_8_.1) | copy-start | bytes 7077892
  14.1 17.8 %collective-permute-start.2 = (bf16[3,192,128]{2,1,0:T(8,128)(2,1)}, bf16[3,192,128]{2,1,0:T(8,128)(2,1)S(1)}, u32[]{:S(2)}, u32[]{:S(2)}) collective-permute-start(bf16[3,192,128]{2,1,0:T(8,128)(2,1)} %get-tuple-element.21), channel_id=1, source_target_pairs={{0,2},{1,18},{2,0},{3,16},{6,4},{7,20},{8,10},{9,26},{10,8},{11,24... | collective-permute-start | bytes 442376 | tf_op jit(solution)/shard_map/ppermute | solution.py:412
  18.3 14.9 %collective-permute-start.3 = (bf16[3,192,128]{2,1,0:T(8,128)(2,1)}, bf16[3,192,128]{2,1,0:T(8,128)(2,1)S(1)}, u32[]{:S(2)}, u32[]{:S(2)}) collective-permute-start(bf16[3,192,128]{2,1,0:T(8,128)(2,1)} %get-tuple-element.22), channel_id=1, source_target_pairs={{0,4},{1,20},{4,0},{5,16},{6,2},{7,18},{8,12},{9,28},{12,8},{13,24... | collective-permute-start | bytes 442376 | tf_op jit(solution)/shard_map/ppermute | solution.py:412
  19.6 23.6 %collective-permute-start.4 = (bf16[3,192,128]{2,1,0:T(8,128)(2,1)}, bf16[3,192,128]{2,1,0:T(8,128)(2,1)S(1)}, u32[]{:S(2)}, u32[]{:S(2)}) collective-permute-start(bf16[3,192,128]{2,1,0:T(8,128)(2,1)} %get-tuple-element.23), channel_id=1, source_target_pairs={{2,4},{3,20},{4,2},{5,18},{6,0},{7,16},{10,12},{11,28},{12,10},{13... | collective-permute-start | bytes 442376 | tf_op jit(solution)/shard_map/ppermute | solution.py:412
  26.6 18.5 %collective-permute-start.5 = (bf16[3,192,128]{2,1,0:T(8,128)(2,1)}, bf16[3,192,128]{2,1,0:T(8,128)(2,1)S(1)}, u32[]{:S(2)}, u32[]{:S(2)}) collective-permute-start(bf16[3,192,128]{2,1,0:T(8,128)(2,1)} %get-tuple-element.24), channel_id=1, source_target_pairs={{0,8},{1,24},{2,10},{3,26},{4,12},{5,28},{8,0},{9,16},{10,2},{11,1... | collective-permute-start | bytes 442376 | tf_op jit(solution)/shard_map/ppermute | solution.py:412
  29.9 15.2 %collective-permute-start.6 = (bf16[3,192,128]{2,1,0:T(8,128)(2,1)}, bf16[3,192,128]{2,1,0:T(8,128)(2,1)S(1)}, u32[]{:S(2)}, u32[]{:S(2)}) collective-permute-start(bf16[3,192,128]{2,1,0:T(8,128)(2,1)} %get-tuple-element.25), channel_id=1, source_target_pairs={{0,10},{1,26},{2,8},{3,24},{6,12},{7,28},{8,2},{9,18},{10,0},{11,1... | collective-permute-start | bytes 442376 | tf_op jit(solution)/shard_map/ppermute | solution.py:412
  31.9 13.3 %collective-permute-start.7 = (bf16[3,192,128]{2,1,0:T(8,128)(2,1)}, bf16[3,192,128]{2,1,0:T(8,128)(2,1)S(1)}, u32[]{:S(2)}, u32[]{:S(2)}) collective-permute-start(bf16[3,192,128]{2,1,0:T(8,128)(2,1)} %get-tuple-element.26), channel_id=1, source_target_pairs={{0,12},{1,28},{4,8},{5,24},{6,10},{7,26},{8,4},{9,20},{12,0},{13,1... | collective-permute-start | bytes 442376 | tf_op jit(solution)/shard_map/ppermute | solution.py:412
  33.2 13.0 %collective-permute-start.8 = (bf16[3,192,128]{2,1,0:T(8,128)(2,1)}, bf16[3,192,128]{2,1,0:T(8,128)(2,1)S(1)}, u32[]{:S(2)}, u32[]{:S(2)}) collective-permute-start(bf16[3,192,128]{2,1,0:T(8,128)(2,1)} %get-tuple-element.27), channel_id=1, source_target_pairs={{2,12},{3,28},{4,10},{5,26},{6,8},{7,24},{10,4},{11,20},{12,2},{13... | collective-permute-start | bytes 442376 | tf_op jit(solution)/shard_map/ppermute | solution.py:412
  43.2 7.9 %collective-permute-start.1 = (bf16[3,192,128]{2,1,0:T(8,128)(2,1)}, bf16[3,192,128]{2,1,0:T(8,128)(2,1)S(1)}, u32[]{:S(2)}, u32[]{:S(2)}) collective-permute-start(bf16[3,192,128]{2,1,0:T(8,128)(2,1)} %get-tuple-element.20.sent_ref), channel_id=1, source_target_pairs={{1,16},{3,18},{5,20},{9,24},{11,26},{13,28},{16,1},{18,3},{20,5},{... | collective-permute-start | bytes 442376 | tf_op jit(solution)/shard_map/ppermute | solution.py:412
  51.1 0.9 copy-start.2
  53.1 53.2 %copy-start.1 = (bf16[192,768]{1,0:T(8,128)(2,1)S(1)}, bf16[192,768]{1,0:T(8,128)(2,1)}, u32[]{:S(2)}) copy-start(bf16[192,768]{1,0:T(8,128)(2,1)} %tokens.1) | copy-start | bytes 884740
  53.1 53.2 %copy-start.3 = (f32[3,1,1536]{2,1,0:T(1,128)S(1)}, f32[3,1,1536]{2,1,0:T(1,128)}, u32[]{:S(2)}) copy-start(f32[3,1,1536]{2,1,0:T(1,128)} %shard_map.104.mod_ref) | copy-start | bytes 55300
  53.1 2.4 %collective-permute-start.9 = (bf16[8,2,192,128]{3,2,1,0:T(8,128)(2,1)S(1)}, bf16[8,2,192,128]{3,2,1,0:T(8,128)(2,1)S(1)}, u32[]{:S(2)}, u32[]{:S(2)}) collective-permute-start(bf16[8,2,192,128]{3,2,1,0:T(8,128)(2,1)S(1)} %shard_map.106), channel_id=1, source_target_pairs={{0,1},{1,0},{2,3},{3,2},{4,5},{5,4},{6,7},{7,6},{8,9},{9,8},{10,11... | collective-permute-start | bytes 2359304 | tf_op jit(solution)/shard_map/ppermute | solution.py:413
  69.0 15.6 %collective-permute-start.11 = (bf16[192,128]{1,0:T(8,128)(2,1)S(1)}, bf16[192,128]{1,0:T(8,128)(2,1)S(1)}, u32[]{:S(2)}, u32[]{:S(2)}) collective-permute-start(bf16[192,128]{1,0:T(8,128)(2,1)S(1)} %get-tuple-element.29), channel_id=1, source_target_pairs={{2,0},{18,1},{0,2},{16,3},{4,6},{20,7},{10,8},{26,9},{8,10},{24,11... | collective-permute-start | bytes 147464 | tf_op jit(solution)/shard_map/ppermute | solution.py:416
  70.9 15.0 %collective-permute-start.12 = (bf16[192,128]{1,0:T(8,128)(2,1)S(1)}, bf16[192,128]{1,0:T(8,128)(2,1)S(1)}, u32[]{:S(2)}, u32[]{:S(2)}) collective-permute-start(bf16[192,128]{1,0:T(8,128)(2,1)S(1)} %get-tuple-element.30), channel_id=1, source_target_pairs={{4,0},{20,1},{0,4},{16,5},{2,6},{18,7},{12,8},{28,9},{8,12},{24,13... | collective-permute-start | bytes 147464 | tf_op jit(solution)/shard_map/ppermute | solution.py:416
  72.2 25.1 %collective-permute-start.13 = (bf16[192,128]{1,0:T(8,128)(2,1)S(1)}, bf16[192,128]{1,0:T(8,128)(2,1)S(1)}, u32[]{:S(2)}, u32[]{:S(2)}) collective-permute-start(bf16[192,128]{1,0:T(8,128)(2,1)S(1)} %get-tuple-element.31), channel_id=1, source_target_pairs={{4,2},{20,3},{2,4},{18,5},{0,6},{16,7},{12,10},{28,11},{10,12},{26... | collective-permute-start | bytes 147464 | tf_op jit(solution)/shard_map/ppermute | solution.py:416
  80.7 18.5 %collective-permute-start.14 = (bf16[192,128]{1,0:T(8,128)(2,1)S(1)}, bf16[192,128]{1,0:T(8,128)(2,1)S(1)}, u32[]{:S(2)}, u32[]{:S(2)}) collective-permute-start(bf16[192,128]{1,0:T(8,128)(2,1)S(1)} %get-tuple-element.32), channel_id=1, source_target_pairs={{8,0},{24,1},{10,2},{26,3},{12,4},{28,5},{0,8},{16,9},{2,10},{18,1... | collective-permute-start | bytes 147464 | tf_op jit(solution)/shard_map/ppermute | solution.py:416
  82.6 16.6 %collective-permute-start.15 = (bf16[192,128]{1,0:T(8,128)(2,1)S(1)}, bf16[192,128]{1,0:T(8,128)(2,1)S(1)}, u32[]{:S(2)}, u32[]{:S(2)}) collective-permute-start(bf16[192,128]{1,0:T(8,128)(2,1)S(1)} %get-tuple-element.33), channel_id=1, source_target_pairs={{10,0},{26,1},{8,2},{24,3},{12,6},{28,7},{2,8},{18,9},{0,10},{16,1... | collective-permute-start | bytes 147464 | tf_op jit(solution)/shard_map/ppermute | solution.py:416
  84.6 14.7 %collective-permute-start.16 = (bf16[192,128]{1,0:T(8,128)(2,1)S(1)}, bf16[192,128]{1,0:T(8,128)(2,1)S(1)}, u32[]{:S(2)}, u32[]{:S(2)}) collective-permute-start(bf16[192,128]{1,0:T(8,128)(2,1)S(1)} %get-tuple-element.34), channel_id=1, source_target_pairs={{12,0},{28,1},{8,4},{24,5},{10,6},{26,7},{4,8},{20,9},{0,12},{16,1... | collective-permute-start | bytes 147464 | tf_op jit(solution)/shard_map/ppermute | solution.py:416
  85.9 13.4 %collective-permute-start.17 = (bf16[192,128]{1,0:T(8,128)(2,1)S(1)}, bf16[192,128]{1,0:T(8,128)(2,1)S(1)}, u32[]{:S(2)}, u32[]{:S(2)}) collective-permute-start(bf16[192,128]{1,0:T(8,128)(2,1)S(1)} %get-tuple-element.35), channel_id=1, source_target_pairs={{12,2},{28,3},{10,4},{26,5},{8,6},{24,7},{4,10},{20,11},{2,12},{18... | collective-permute-start | bytes 147464 | tf_op jit(solution)/shard_map/ppermute | solution.py:416
  97.3 6.3 %collective-permute-start.10 = (bf16[192,128]{1,0:T(8,128)(2,1)S(1)}, bf16[192,128]{1,0:T(8,128)(2,1)S(1)}, u32[]{:S(2)}, u32[]{:S(2)}) collective-permute-start(bf16[192,128]{1,0:T(8,128)(2,1)S(1)} %get-tuple-element.28.done_ref), channel_id=1, source_target_pairs={{16,1},{18,3},{20,5},{24,9},{26,11},{28,13},{1,16},{3,18},{5,20},{... | collective-permute-start | bytes 147464 | tf_op jit(solution)/shard_map/ppermute | solution.py:416
  104.6 1.6 %collective-permute-start.18 = (bf16[192,768]{1,0:T(8,128)(2,1)S(1)}, bf16[192,768]{1,0:T(8,128)(2,1)S(1)}, u32[]{:S(2)}, u32[]{:S(2)}) collective-permute-start(bf16[192,768]{1,0:T(8,128)(2,1)S(1)} %get-tuple-element.37), channel_id=1, source_target_pairs={{0,1},{1,0},{2,3},{3,2},{4,5},{5,4},{6,7},{7,6},{8,9},{9,8},{10,11... | collective-permute-start | bytes 884744 | tf_op jit(solution)/shard_map/ppermute | solution.py:419

commit v4 on v1

v4 whole, which is shorter than its diff:
```python
import functools
import math

import jax
import jax.numpy as jnp
from jax import lax
from jax.experimental import pallas as pl
from jax.experimental.pallas import tpu as pltpu
from jax.sharding import PartitionSpec as P

HEAD_DIM = 128
STEPS = 1000
KEY_CHIPS = 4
QUERY_CHIPS = 4
NEG = -1e30
STREAM_LIMIT = 56 * 1024 * 1024
VMEM_LIMIT = 32 * 1024 * 1024


def noise_level(step_value):
    frac = step_value / STEPS
    return 5.0 * frac / (1.0 + 4.0 * frac)


def owners(chips, tp, heads_here):
    order = [chip for chip in range(chips) if chip % 4 != 3]
    return [[order[head * tp + core] for head in range(heads_here)] for core in range(tp)]


def owner_of(table, core, head):
    return jnp.where(core == 0, table[0][head], table[1][head])


def any_spec():
    return pl.BlockSpec(memory_space=pl.ANY)


def vmem_spec():
    return pl.BlockSpec(memory_space=pltpu.VMEM)


def smem_spec():
    return pl.BlockSpec(memory_space=pltpu.SMEM)


def modulation_kernel(act_ref, weight_ref, block_ref, out_ref, weight, sems):
    freq, width = weight.shape[0], block_ref.shape[1]
    parts = sems.shape[0]
    rows = freq // parts
    copies = []
    for part in range(parts):
        here = pl.ds(part * rows, rows)
        copies.append(pltpu.make_async_copy(weight_ref.at[here], weight.at[here], sems.at[part]))
        copies[-1].start()
    act = jnp.transpose(jnp.broadcast_to(act_ref[...], (8, freq)))[:, :1]
    for part in range(parts):
        copies[part].wait()
        here = slice(part * rows, (part + 1) * rows)
        for k in range(3):
            columns = slice(k * width, (k + 1) * width)
            term = jnp.sum(act[here] * weight[here, columns], axis=0, keepdims=True)
            out_ref[k] = term + (out_ref[k] if part else block_ref[k:k + 1, :])


def modulate(act, time_weight, block_mod):
    freq, wide = time_weight.shape
    width = wide // 3
    return pl.pallas_call(
        modulation_kernel,
        in_specs=[vmem_spec(), any_spec(), vmem_spec()],
        out_specs=vmem_spec(),
        out_shape=jax.ShapeDtypeStruct((3, 1, width), jnp.float32),
        scratch_shapes=[pltpu.VMEM((freq, wide), jnp.float32), pltpu.SemaphoreType.DMA((8,))],
        compiler_params=pltpu.CompilerParams(vmem_limit_bytes=STREAM_LIMIT),
        cost_estimate=pl.CostEstimate(flops=2 * freq * wide, bytes_accessed=4 * freq * wide, transcendentals=0),
    )(act, time_weight, block_mod)


def project_kernel(table, own_ref, other_ref, mod_ref, wq_ref, wk_ref, wv_ref, *rest):
    near_ref, far_ref, weights, full, normed, packed, sems, out_sems = rest
    depth, columns = wq_ref.shape
    rows, share = own_ref.shape
    wide = 2 * HEAD_DIM
    part_rows = rows // 2
    core = lax.axis_index("tp")
    loads = {}
    for group in range(columns // wide):
        for part, ref in enumerate((wq_ref, wk_ref, wv_ref)):
            here = pl.ds(group * wide, wide)
            loads[group, part] = pltpu.make_async_copy(
                ref.at[:, here], weights.at[part, :, here], sems.at[3 * group + part]
            )
            loads[group, part].start()
    full[:, pl.ds(pl.multiple_of(core * share, 128), share)] = own_ref[...].astype(jnp.float32)
    full[:, pl.ds(pl.multiple_of((1 - core) * share, 128), share)] = other_ref[...].astype(jnp.float32)
    whole = full[...]
    centred = whole - jnp.mean(whole, axis=1, keepdims=True)
    variance = jnp.mean(centred * centred, axis=1, keepdims=True)
    normed[...] = (centred * lax.rsqrt(variance + 1e-06) * (1.0 + mod_ref[1]) + mod_ref[0]).astype(jnp.bfloat16)
    factor = math.log2(math.e) / math.sqrt(HEAD_DIM)
    near, far = (pl.ds(pl.multiple_of(side * part_rows, 32), part_rows) for side in (core, 1 - core))
    copies = []
    for group in range(columns // wide):
        for part in range(3):
            loads[group, part].wait()
            out = jnp.dot(
                normed[...], weights[part, :, group * wide:(group + 1) * wide], preferred_element_type=jnp.float32
            )
            if part == 0:
                out = out * factor
            for e in range(2):
                packed[2 * group + e, part] = out[:, e * HEAD_DIM:(e + 1) * HEAD_DIM].astype(jnp.bfloat16)
        for head in (2 * group, 2 * group + 1):
            for source, target in (
                (near, near_ref.at[owner_of(table, core, head)]), (far, far_ref.at[head]),
            ):
                copies.append(
                    pltpu.make_async_copy(packed.at[head, :, source], target, out_sems.at[len(copies)])
                )
                copies[-1].start()
    for copy in copies:
        copy.wait()


def project(own, other, mod, w_query, w_key, w_value, chips, table):
    rows, share = own.shape
    depth, columns = w_query.shape
    heads_here = columns // HEAD_DIM
    return pl.pallas_call(
        functools.partial(project_kernel, table),
        in_specs=[vmem_spec()] * 3 + [any_spec()] * 3,
        out_specs=[any_spec()] * 2,
        out_shape=[
            jax.ShapeDtypeStruct((chips, 3, rows // 2, HEAD_DIM), jnp.bfloat16),
            jax.ShapeDtypeStruct((heads_here, 3, rows // 2, HEAD_DIM), jnp.bfloat16),
        ],
        scratch_shapes=[
            pltpu.VMEM((3, depth, columns), jnp.bfloat16),
            pltpu.VMEM((rows, depth), jnp.float32),
            pltpu.VMEM((rows, depth), jnp.bfloat16),
            pltpu.VMEM((heads_here, 3, rows, HEAD_DIM), jnp.bfloat16),
            pltpu.SemaphoreType.DMA((3 * heads_here // 2,)),
            pltpu.SemaphoreType.DMA((2 * heads_here,)),
        ],
        compiler_params=pltpu.CompilerParams(vmem_limit_bytes=STREAM_LIMIT),
    )(own, other, mod, w_query, w_key, w_value)


def merge_kernel(table, near_ref, far_ref, out_ref, sems):
    core = lax.axis_index("tp")
    copies = [
        pltpu.make_async_copy(far_ref.at[head], out_ref.at[owner_of(table, 1 - core, head)], sems.at[head])
        for head in range(far_ref.shape[0])
    ]
    for copy in copies:
        copy.start()
    for copy in copies:
        copy.wait()


def merge(near, far, table):
    return pl.pallas_call(
        functools.partial(merge_kernel, table),
        in_specs=[any_spec()] * 2,
        out_specs=any_spec(),
        out_shape=jax.ShapeDtypeStruct(near.shape, near.dtype),
        scratch_shapes=[pltpu.SemaphoreType.DMA((far.shape[0],))],
        input_output_aliases={0: 0},
        compiler_params=pltpu.CompilerParams(vmem_limit_bytes=VMEM_LIMIT),
    )(near, far)


def attend_kernel(table, lengths_ref, near_ref, far_ref, out_ref, query, keys, values, result, top, total, sems):
    chips, part_rows = query.shape[:2]
    side = lax.axis_index("tp")
    chip = lax.axis_index("req")
    active = functools.reduce(jnp.logical_or, [chip == owner for owner in table[0] + table[1]])
    front = pl.ds(0, HEAD_DIM)
    videos = lengths_ref.shape[0]

    @pl.when(active)
    def _():
        copies = []
        for source, target in (
            (near_ref.at[:, 0], query.at[:, :, front]),
            (near_ref.at[:, 1], keys.at[:, side, :, front]),
            (near_ref.at[:, 2], values.at[:, side, :, front]),
            (far_ref.at[:, 1], keys.at[:, 1 - side, :, front]),
            (far_ref.at[:, 2], values.at[:, 1 - side, :, front]),
        ):
            copies.append(pltpu.make_async_copy(source, target, sems.at[len(copies)]))
            copies[-1].start()
        ends, end = [], jnp.int32(0)
        for video in range(videos):
            end = end + lengths_ref[video]
            ends.append(end)
        starts = [jnp.int32(0)] + ends[:-1]
        lane = lax.broadcasted_iota(jnp.int32, (1, HEAD_DIM), 1)
        lane_start = jnp.zeros((1, HEAD_DIM), jnp.int32)
        lane_stop = jnp.zeros((1, HEAD_DIM), jnp.int32)
        for video, (start, stop) in enumerate(zip(starts, ends)):
            lane_start = jnp.where(lane == video, start, lane_start)
            lane_stop = jnp.where(lane == video, stop, lane_stop)
        place = lax.broadcasted_iota(jnp.int32, (part_rows, HEAD_DIM), 0)

        def fill(number, carry):
            for part in range(2):
                index = (2 * number + part) * part_rows + place
                member = (index >= lane_start) & (index < lane_stop)
                keys[number, part, :, HEAD_DIM:] = jnp.where(member | (lane >= videos), 0.0, NEG).astype(jnp.bfloat16)
                values[number, part, :, HEAD_DIM:] = jnp.ones((part_rows, HEAD_DIM), jnp.bfloat16)
            index = (2 * number + side) * part_rows + place
            member = (index >= lane_start) & (index < lane_stop)
            query[number, :, HEAD_DIM:] = jnp.where(member, 1.0, 0.0).astype(jnp.bfloat16)
            return carry

        lax.fori_loop(0, chips, fill, 0)
        for copy in copies:
            copy.wait()
        block_rows = QUERY_CHIPS * part_rows
        key_rows = 2 * KEY_CHIPS * part_rows

        def query_block(block, carry):
            first = (2 * QUERY_CHIPS * block + side) * part_rows
            last = first + 2 * (QUERY_CHIPS - 1) * part_rows + part_rows - 1
            low, high = jnp.int32(0), jnp.int32(0)
            for start, stop in zip(starts, ends):
                low = jnp.where(first >= start, start, low)
                high = jnp.where(last >= start, stop, high)
            q = query[pl.ds(block * QUERY_CHIPS, QUERY_CHIPS)].reshape(block_rows, 2 * HEAD_DIM)
            top[...] = jnp.full(top.shape, 2 * NEG, jnp.float32)
            total[...] = jnp.zeros(total.shape, jnp.float32)

            def key_block(number, carry):
                here = pl.ds(number * KEY_CHIPS, KEY_CHIPS)
                k = keys[here].reshape(key_rows, 2 * HEAD_DIM)
                score = lax.dot_general(q, k, (((1,), (1,)), ((), ())), preferred_element_type=jnp.float32)
                tiles = [score[:, j:j + HEAD_DIM] for j in range(0, key_rows, HEAD_DIM)]
                most = jnp.max(functools.reduce(jnp.maximum, tiles), axis=1, keepdims=True)
                before = top[...]
                now = jnp.maximum(before, most)
                probs = jnp.concatenate([jnp.exp2(tile - now).astype(jnp.bfloat16) for tile in tiles], axis=1)
                v = values[here].reshape(key_rows, 2 * HEAD_DIM)
                update = jnp.dot(probs, v, preferred_element_type=jnp.float32)
                shrink = jnp.exp2(before - now)
                total[:, :HEAD_DIM] = total[:, :HEAD_DIM] * shrink + update[:, :HEAD_DIM]
                total[:, HEAD_DIM:] = total[:, HEAD_DIM:] * shrink + update[:, HEAD_DIM:]
                top[...] = now
                return carry

            lax.fori_loop(low // key_rows, (high + key_rows - 1) // key_rows, key_block, 0)
            out = (total[:, :HEAD_DIM] / total[:, HEAD_DIM:]).astype(jnp.bfloat16)
            result[pl.ds(block * QUERY_CHIPS, QUERY_CHIPS)] = out.reshape(QUERY_CHIPS, part_rows, HEAD_DIM)
            return carry

        lax.fori_loop(0, chips // QUERY_CHIPS, query_block, 0)
        copy = pltpu.make_async_copy(result, out_ref, sems.at[0])
        copy.start()
        copy.wait()


def attend(lengths, near, far, table):
    chips, _, part_rows, _ = near.shape
    block_rows = QUERY_CHIPS * part_rows
    return pl.pallas_call(
        functools.partial(attend_kernel, table),
        in_specs=[smem_spec()] + [any_spec()] * 2,
        out_specs=any_spec(),
        out_shape=jax.ShapeDtypeStruct((chips, part_rows, HEAD_DIM), jnp.bfloat16),
        scratch_shapes=[
            pltpu.VMEM((chips, part_rows, 2 * HEAD_DIM), jnp.bfloat16),
            pltpu.VMEM((chips, 2, part_rows, 2 * HEAD_DIM), jnp.bfloat16),
            pltpu.VMEM((chips, 2, part_rows, 2 * HEAD_DIM), jnp.bfloat16),
            pltpu.VMEM((chips, part_rows, HEAD_DIM), jnp.bfloat16),
            pltpu.VMEM((block_rows, HEAD_DIM), jnp.float32),
            pltpu.VMEM((block_rows, 2 * HEAD_DIM), jnp.float32),
            pltpu.SemaphoreType.DMA((5,)),
        ],
        compiler_params=pltpu.CompilerParams(vmem_limit_bytes=VMEM_LIMIT),
    )(lengths, near, far)


def combine_kernel(table, near_ref, far_ref, weight, mine, theirs, attended, sems):
    share = mine.shape[1]
    part_rows = near_ref.shape[1]
    core = lax.axis_index("tp")
    copies = []
    for head in range(len(table[0])):
        columns = pl.ds(head * HEAD_DIM, HEAD_DIM)
        owner = owner_of(table, core, head)
        for source, side in ((near_ref, core), (far_ref, 1 - core)):
            target = attended.at[pl.ds(pl.multiple_of(side * part_rows, 32), part_rows), columns]
            copies.append(pltpu.make_async_copy(source.at[owner], target, sems.at[len(copies)]))
            copies[-1].start()
    for copy in copies:
        copy.wait()
    left = attended[...]
    for out, where in ((theirs, 1 - core), (mine, core)):
        columns = pl.ds(pl.multiple_of(where * share, 128), share)
        out[...] = jnp.dot(left, weight[:, columns], preferred_element_type=jnp.float32).astype(out.dtype)


def combine(near, far, w_out, table):
    rows = 2 * near.shape[1]
    depth, width = w_out.shape
    return pl.pallas_call(
        functools.partial(combine_kernel, table),
        in_specs=[any_spec()] * 2 + [vmem_spec()],
        out_specs=[vmem_spec(), vmem_spec()],
        out_shape=[
            jax.ShapeDtypeStruct((rows, width // 2), jnp.float32),
            jax.ShapeDtypeStruct((rows, width // 2), jnp.bfloat16),
        ],
        scratch_shapes=[
            pltpu.VMEM((rows, depth), jnp.bfloat16),
            pltpu.SemaphoreType.DMA((2 * len(table[0]),)),
        ],
        compiler_params=pltpu.CompilerParams(vmem_limit_bytes=VMEM_LIMIT),
    )(near, far, w_out)


def finish_kernel(timestep_ref, mine, theirs, tokens, mod_ref, velocity, stepped):
    share = tokens.shape[1]
    core = lax.axis_index("tp")
    step_value = jnp.full((1, 128), timestep_ref[0], jnp.int32).astype(jnp.float32)
    delta = (noise_level(step_value - 1.0) - noise_level(step_value))[:, :1]
    gate = mod_ref[2, :, pl.ds(pl.multiple_of(core * share, 128), share)]
    branch = gate * (mine[...] + theirs[...].astype(jnp.float32))
    velocity[...] = branch.astype(jnp.bfloat16)
    stepped[...] = (tokens[...].astype(jnp.float32) + delta * branch).astype(jnp.bfloat16)


def finish(timestep, mine, theirs, tokens, mod):
    shape = jax.ShapeDtypeStruct(tokens.shape, jnp.bfloat16)
    return pl.pallas_call(
        finish_kernel,
        in_specs=[smem_spec()] + [vmem_spec()] * 4,
        out_specs=[vmem_spec(), vmem_spec()],
        out_shape=[shape, shape],
        compiler_params=pltpu.CompilerParams(vmem_limit_bytes=VMEM_LIMIT),
    )(timestep, mine, theirs, tokens, mod)


def make(mesh):
    chips, tp = mesh.shape["req"], mesh.shape["tp"]
    swap = [(0, 1), (1, 0)]

    def on_device(tokens, video_lengths, timestep, time_weight, block_mod, w_query, w_key, w_value, w_out):
        heads_here = w_query.shape[1] // HEAD_DIM
        table = owners(chips, tp, heads_here)
        other = lax.ppermute(tokens, "tp", swap)
        half_freq = time_weight.shape[0] // 2
        time_value = jnp.broadcast_to(timestep, (half_freq,)).astype(jnp.float32)
        sigma = noise_level(time_value)
        frequency = jnp.exp(-math.log(10000.0) * jnp.arange(half_freq, dtype=jnp.float32) / half_freq)
        angle = 1000.0 * sigma * frequency
        act = jax.nn.silu(jnp.concatenate([jnp.cos(angle), jnp.sin(angle)]))[None, :]
        mod = modulate(act, time_weight, block_mod)
        near, far = project(tokens, other, mod, w_query, w_key, w_value, chips, table)
        near = merge(near, lax.ppermute(far, "tp", swap), table)
        near = lax.all_to_all(near, "req", 0, 0, tiled=True)
        done = attend(video_lengths, near, lax.ppermute(near, "tp", swap), table)
        done = lax.all_to_all(done, "req", 0, 0, tiled=True)
        mine, theirs = combine(done, lax.ppermute(done, "tp", swap), w_out, table)
        theirs = lax.ppermute(theirs, "tp", swap)
        velocity, stepped = finish(timestep, mine, theirs, tokens, mod)
        return (velocity, stepped)

    return on_device


def solution(mesh):
    return jax.shard_map(
        make(mesh),
        mesh=mesh,
        in_specs=(
            P("req", "tp"), P(), P(), P(), P(), P(None, "tp"), P(None, "tp"), P(None, "tp"), P("tp", None),
        ),
        out_specs=(P("req", "tp"), P("req", "tp")),
        check_vma=False,
    )
```

time: 180 us -> 93 us (0.52)
  the two profiles are of different devices: /device:TPU:27 before, /device:TPU:0 now
where the time goes in v4:
time: 93 us; the launch traced here: 92.2 us
  blocking collectives  54.1 us (58%)
  Pallas kernels  25.2 us (27%)
  waiting for transfers between devices  8 us (9%)
  local copies, waits for them, and re-layouts  2 us (2%)
  between operations  1.41 us (2%)
    all_to_all x1, blocking collectives, on_device(): near = lax.all_to_all(near, 'req', 0, 0, tiled=True)  38.3 us
    all_to_all x1, blocking collectives, on_device(): done = lax.all_to_all(done, 'req', 0, 0, tiled=True)  15.9 us
    pallas_call x1, Pallas kernels, attend(): pl.pallas_call(functools.partial(attend_kernel, table), in_specs=[smem_sp...  11.9 us
    pallas_call x1, Pallas kernels, project(): pl.pallas_call(functools.partial(project_kernel, table), in_specs=[vmem_s...  7.1 us
    pallas_call x1, Pallas kernels, modulate(): pl.pallas_call(modulation_kernel, in_specs=[vmem_spec(), any_spec(), vmem...  3.88 us
    ppermute x1, waiting for transfers between devices, on_device(): done = attend(video_lengths, near, lax.ppermute(near, 'tp', swap), table)  2.84 us
    unnamed x12, local copies, waits for them, and re-layouts  2 us
    ppermute x1, waiting for transfers between devices, on_device(): near = merge(near, lax.ppermute(far, 'tp', swap), table)  1.99 us
  transfers between devices with their start and end apart: 5, of which 4 were waited for; matrix products, arithmetic and copies ran while one was open for 1% of the time, Pallas kernels for 4%

profile of v4, /device:TPU:0, one launch (start us, length us, event | category | flops | bytes accessed | tf_op | source)
XLA Modules:
  0.0 92.2 jit_solution(12433798009110768331)
XLA Ops:
  0.6 0.5 collective-permute-start
  1.9 0.6 divide_multiply_fusion.act_ref
  2.5 3.9 %shard_map.104.mod_ref = f32[3,1,1536]{2,1,0:T(1,128)} custom-call(f32[1,256]{1,0:T(1,128)} %divide_multiply_fusion.act_ref, f32[256,4608]{1,0:T(8,128)} %weight_ref.1, f32[3,1536]{1,0:T(4,128)} %block_ref.1), custom_call_target="tpu_custom_call" | custom-call | flops 2359296 | bytes 4718592 | tf_op jit(solution)/shard_map/pallas_call | solution.py:68
  6.4 0.0 collective-permute-done.other_ref
  6.4 0.0 copy-start.5
  6.4 0.7 copy-done.5
  7.1 7.1 %shard_map.105 = (bf16[16,3,96,128]{3,2,1,0:T(8,128)(2,1)}, bf16[6,3,96,128]{3,2,1,0:T(8,128)(2,1)}) custom-call(bf16[192,768]{1,0:T(8,128)(2,1)} %tokens.1, bf16[192,768]{1,0:T(8,128)(2,1)} %copy-done.5, f32[3,1,1536]{2,1,0:T(1,128)} %shard_map.104.mod_ref, bf16[1536,768]{1,0:T(8,128)(2,1)} %wq_ref.1, bf16[1536,768]{1,0:T(8,128)(2,1)} %wk_ref.1, ...), custom_call_target="tpu_custom_call" | custom-call | tf_op jit(solution)/shard_map/pallas_call | solution.py:129
  14.2 0.1 collective-permute-start.1
  14.3 2.0 %collective-permute-done.1.far_ref = bf16[6,3,96,128]{3,2,1,0:T(8,128)(2,1)S(1)} collective-permute-done((bf16[6,3,96,128]{3,2,1,0:T(8,128)(2,1)}, bf16[6,3,96,128]{3,2,1,0:T(8,128)(2,1)S(1)}, u32[]{:S(2)}, u32[]{:S(2)}) %collective-permute-start.1) | collective-permute-done | bytes 442400 | tf_op jit(solution)/shard_map/ppermute | solution.py:360
  16.3 0.0 copy-start
  16.3 1.3 %copy-done = bf16[16,3,96,128]{3,2,1,0:T(8,128)(2,1)S(1)} copy-done((bf16[16,3,96,128]{3,2,1,0:T(8,128)(2,1)S(1)}, bf16[16,3,96,128]{3,2,1,0:T(8,128)(2,1)}, u32[]{:S(2)}) %copy-start) | copy-done | bytes 1179672
  17.6 0.0 copy-start.4
  17.6 0.6 shard_map.106
  18.2 38.3 %all_to_all.10.near_ref = bf16[16,3,96,128]{3,2,1,0:T(8,128)(2,1)S(1)} all-to-all(bf16[16,3,96,128]{3,2,1,0:T(8,128)(2,1)S(1)} %shard_map.106), channel_id=1, replica_groups=mesh['req'=16,'tp'=2] {'req'}, dimensions={0} | all-to-all | bytes 2359296 | tf_op jit(solution)/shard_map/all_to_all | solution.py:361
  56.4 0.0 copy-start.1
  56.4 0.0 collective-permute-start.2
  56.4 2.8 %collective-permute-done.2.far_ref = bf16[16,3,96,128]{3,2,1,0:T(8,128)(2,1)S(1)} collective-permute-done((bf16[16,3,96,128]{3,2,1,0:T(8,128)(2,1)S(1)}, bf16[16,3,96,128]{3,2,1,0:T(8,128)(2,1)S(1)}, u32[]{:S(2)}, u32[]{:S(2)}) %collective-permute-start.2) | collective-permute-done | bytes 1179680 | tf_op jit(solution)/shard_map/ppermute | solution.py:362
  59.3 0.0 copy-done.4
  59.3 11.9 %shard_map.107 = bf16[16,96,128]{2,1,0:T(8,128)(2,1)S(1)} custom-call(s32[5]{0:T(128)S(1)} %copy-done.4, bf16[16,3,96,128]{3,2,1,0:T(8,128)(2,1)S(1)} %all_to_all.10.near_ref, bf16[16,3,96,128]{3,2,1,0:T(8,128)(2,1)S(1)} %collective-permute-done.2.far_ref), custom_call_target="tpu_custom_call" | custom-call | tf_op jit(solution)/shard_map/pallas_call | solution.py:265
  71.2 0.0 copy-start.2
  71.2 0.0 copy-start.3
  71.2 15.9 %all_to_all.11.near_ref = bf16[16,96,128]{2,1,0:T(8,128)(2,1)S(1)} all-to-all(bf16[16,96,128]{2,1,0:T(8,128)(2,1)S(1)} %shard_map.107), channel_id=1, replica_groups=mesh['req'=16,'tp'=2] {'req'}, dimensions={0} | all-to-all | bytes 786432 | tf_op jit(solution)/shard_map/all_to_all | solution.py:363
  87.1 0.0 collective-permute-start.3
  87.1 1.7 %collective-permute-done.3.far_ref = bf16[16,96,128]{2,1,0:T(8,128)(2,1)S(1)} collective-permute-done((bf16[16,96,128]{2,1,0:T(8,128)(2,1)S(1)}, bf16[16,96,128]{2,1,0:T(8,128)(2,1)S(1)}, u32[]{:S(2)}, u32[]{:S(2)}) %collective-permute-start.3) | collective-permute-done | bytes 393248 | tf_op jit(solution)/shard_map/ppermute | solution.py:364
  88.8 0.0 copy-done.1
  88.8 0.8 shard_map.108
  89.6 0.2 collective-permute-start.4
  89.8 1.4 %collective-permute-done.4.theirs = bf16[192,768]{1,0:T(8,128)(2,1)S(1)} collective-permute-done((bf16[192,768]{1,0:T(8,128)(2,1)S(1)}, bf16[192,768]{1,0:T(8,128)(2,1)S(1)}, u32[]{:S(2)}, u32[]{:S(2)}) %collective-permute-start.4) | collective-permute-done | bytes 294944 | tf_op jit(solution)/shard_map/ppermute | solution.py:365
  91.3 0.0 copy-done.2
  91.3 0.0 copy-done.3
  91.3 0.9 shard_map.109
  (1 shorter events, 0.0 us)
Async XLA Ops:
  0.6 5.8 %collective-permute-start = (bf16[192,768]{1,0:T(8,128)(2,1)}, bf16[192,768]{1,0:T(8,128)(2,1)S(1)}, u32[]{:S(2)}, u32[]{:S(2)}) collective-permute-start(bf16[192,768]{1,0:T(8,128)(2,1)} %tokens.1), channel_id=1, source_target_pairs={{0,1},{1,0},{2,3},{3,2},{4,5},{5,4},{6,7},{7,6},{8,9},{9,8},{10,11... | collective-permute-start | bytes 884744 | tf_op jit(solution)/shard_map/ppermute | solution.py:351
  6.4 0.7 copy-start.5
  14.2 2.1 %collective-permute-start.1 = (bf16[6,3,96,128]{3,2,1,0:T(8,128)(2,1)}, bf16[6,3,96,128]{3,2,1,0:T(8,128)(2,1)S(1)}, u32[]{:S(2)}, u32[]{:S(2)}) collective-permute-start(bf16[6,3,96,128]{3,2,1,0:T(8,128)(2,1)} %get-tuple-element.7), channel_id=1, source_target_pairs={{0,1},{1,0},{2,3},{3,2},{4,5},{5,4},{6,7},{7,6},{8,9},{9,8},{10,11... | collective-permute-start | bytes 1327112 | tf_op jit(solution)/shard_map/ppermute | solution.py:360
  16.3 1.3 %copy-start = (bf16[16,3,96,128]{3,2,1,0:T(8,128)(2,1)S(1)}, bf16[16,3,96,128]{3,2,1,0:T(8,128)(2,1)}, u32[]{:S(2)}) copy-start(bf16[16,3,96,128]{3,2,1,0:T(8,128)(2,1)} %get-tuple-element.6.near_ref) | copy-start | bytes 3538948
  17.6 41.7 %copy-start.4 = (s32[5]{0:T(128)S(1)}, s32[5]{0:T(128)}, u32[]{:S(2)}) copy-start(s32[5]{0:T(128)} %lengths_ref.1) | copy-start | bytes 64
  56.4 32.4 %copy-start.1 = (bf16[768,1536]{1,0:T(8,128)(2,1)S(1)}, bf16[768,1536]{1,0:T(8,128)(2,1)}, u32[]{:S(2)}) copy-start(bf16[768,1536]{1,0:T(8,128)(2,1)} %weight.1) | copy-start | bytes 7077892
  56.4 2.8 %collective-permute-start.2 = (bf16[16,3,96,128]{3,2,1,0:T(8,128)(2,1)S(1)}, bf16[16,3,96,128]{3,2,1,0:T(8,128)(2,1)S(1)}, u32[]{:S(2)}, u32[]{:S(2)}) collective-permute-start(bf16[16,3,96,128]{3,2,1,0:T(8,128)(2,1)S(1)} %all_to_all.10.near_ref), channel_id=1, source_target_pairs={{0,1},{1,0},{2,3},{3,2},{4,5},{5,4},{6,7},{7,6},{8,9},{9,8},{10,11... | collective-permute-start | bytes 3538952 | tf_op jit(solution)/shard_map/ppermute | solution.py:362
  71.2 20.1 %copy-start.2 = (bf16[192,768]{1,0:T(8,128)(2,1)S(1)}, bf16[192,768]{1,0:T(8,128)(2,1)}, u32[]{:S(2)}) copy-start(bf16[192,768]{1,0:T(8,128)(2,1)} %tokens.1) | copy-start | bytes 884740
  71.2 20.1 %copy-start.3 = (f32[3,1,1536]{2,1,0:T(1,128)S(1)}, f32[3,1,1536]{2,1,0:T(1,128)}, u32[]{:S(2)}) copy-start(f32[3,1,1536]{2,1,0:T(1,128)} %shard_map.104.mod_ref) | copy-start | bytes 55300
  87.1 1.7 %collective-permute-start.3 = (bf16[16,96,128]{2,1,0:T(8,128)(2,1)S(1)}, bf16[16,96,128]{2,1,0:T(8,128)(2,1)S(1)}, u32[]{:S(2)}, u32[]{:S(2)}) collective-permute-start(bf16[16,96,128]{2,1,0:T(8,128)(2,1)S(1)} %all_to_all.11.near_ref), channel_id=1, source_target_pairs={{0,1},{1,0},{2,3},{3,2},{4,5},{5,4},{6,7},{7,6},{8,9},{9,8},{10,11... | collective-permute-start | bytes 1179656 | tf_op jit(solution)/shard_map/ppermute | solution.py:364
  89.6 1.6 %collective-permute-start.4 = (bf16[192,768]{1,0:T(8,128)(2,1)S(1)}, bf16[192,768]{1,0:T(8,128)(2,1)S(1)}, u32[]{:S(2)}, u32[]{:S(2)}) collective-permute-start(bf16[192,768]{1,0:T(8,128)(2,1)S(1)} %get-tuple-element.9), channel_id=1, source_target_pairs={{0,1},{1,0},{2,3},{3,2},{4,5},{5,4},{6,7},{7,6},{8,9},{9,8},{10,11... | collective-permute-start | bytes 884744 | tf_op jit(solution)/shard_map/ppermute | solution.py:365

commit v5 on v4

--- a/solution.py
+++ b/solution.py
@@ -10,10 +10,10 @@
 
 HEAD_DIM = 128
 STEPS = 1000
-KEY_CHIPS = 4
+KEY_CHIPS = 16
 QUERY_CHIPS = 4
 NEG = -1e30
-STREAM_LIMIT = 56 * 1024 * 1024
+STREAM_LIMIT = 51 * 1024 * 1024
 VMEM_LIMIT = 32 * 1024 * 1024
 
 
@@ -43,107 +43,102 @@
     return pl.BlockSpec(memory_space=pltpu.SMEM)
 
 
-def modulation_kernel(act_ref, weight_ref, block_ref, out_ref, weight, sems):
-    freq, width = weight.shape[0], block_ref.shape[1]
-    parts = sems.shape[0]
-    rows = freq // parts
-    copies = []
-    for part in range(parts):
-        here = pl.ds(part * rows, rows)
-        copies.append(pltpu.make_async_copy(weight_ref.at[here], weight.at[here], sems.at[part]))
-        copies[-1].start()
-    act = jnp.transpose(jnp.broadcast_to(act_ref[...], (8, freq)))[:, :1]
-    for part in range(parts):
-        copies[part].wait()
-        here = slice(part * rows, (part + 1) * rows)
-        for k in range(3):
-            columns = slice(k * width, (k + 1) * width)
-            term = jnp.sum(act[here] * weight[here, columns], axis=0, keepdims=True)
-            out_ref[k] = term + (out_ref[k] if part else block_ref[k:k + 1, :])
-
-
-def modulate(act, time_weight, block_mod):
-    freq, wide = time_weight.shape
-    width = wide // 3
-    return pl.pallas_call(
-        modulation_kernel,
-        in_specs=[vmem_spec(), any_spec(), vmem_spec()],
-        out_specs=vmem_spec(),
-        out_shape=jax.ShapeDtypeStruct((3, 1, width), jnp.float32),
-        scratch_shapes=[pltpu.VMEM((freq, wide), jnp.float32), pltpu.SemaphoreType.DMA((8,))],
-        compiler_params=pltpu.CompilerParams(vmem_limit_bytes=STREAM_LIMIT),
-        cost_estimate=pl.CostEstimate(flops=2 * freq * wide, bytes_accessed=4 * freq * wide, transcendentals=0),
-    )(act, time_weight, block_mod)
-
-
-def project_kernel(table, own_ref, other_ref, mod_ref, wq_ref, wk_ref, wv_ref, *rest):
-    near_ref, far_ref, weights, full, normed, packed, sems, out_sems = rest
+def project_kernel(table, act_ref, block_ref, own_ref, other_ref, time_ref, wq_ref, wk_ref, wv_ref, *rest):
+    near_ref, far_ref, gate_ref, times, weights, full, normed, packed, sems, out_sems = rest
     depth, columns = wq_ref.shape
     rows, share = own_ref.shape
-    wide = 2 * HEAD_DIM
+    freq = times.shape[0]
     part_rows = rows // 2
     core = lax.axis_index("tp")
-    loads = {}
-    for group in range(columns // wide):
-        for part, ref in enumerate((wq_ref, wk_ref, wv_ref)):
-            here = pl.ds(group * wide, wide)
-            loads[group, part] = pltpu.make_async_copy(
-                ref.at[:, here], weights.at[part, :, here], sems.at[3 * group + part]
-            )
-            loads[group, part].start()
-    full[:, pl.ds(pl.multiple_of(core * share, 128), share)] = own_ref[...].astype(jnp.float32)
+    mine = pl.multiple_of(core * share, 128)
+    loads = []
+
+    def load(source, target):
+        loads.append(pltpu.make_async_copy(source, target, sems.at[len(loads)]))
+        loads[-1].start()
+
+    for part in range(2):
+        here = pl.ds(part * (freq // 2), freq // 2)
+        load(time_ref.at[here, pl.ds(0, 2 * depth)], times.at[here, pl.ds(0, 2 * depth)])
+    for part, ref in enumerate((wq_ref, wk_ref, wv_ref)):
+        for cut in range(2):
+            here = pl.ds(cut * (depth // 2), depth // 2)
+            load(ref.at[here], weights.at[part, here])
+    load(
+        time_ref.at[:, pl.ds(pl.multiple_of(2 * depth + core * share, 128), share)],
+        times.at[:, pl.ds(2 * depth, share)],
+    )
+    full[:, pl.ds(mine, share)] = own_ref[...].astype(jnp.float32)
     full[:, pl.ds(pl.multiple_of((1 - core) * share, 128), share)] = other_ref[...].astype(jnp.float32)
     whole = full[...]
     centred = whole - jnp.mean(whole, axis=1, keepdims=True)
     variance = jnp.mean(centred * centred, axis=1, keepdims=True)
-    normed[...] = (centred * lax.rsqrt(variance + 1e-06) * (1.0 + mod_ref[1]) + mod_ref[0]).astype(jnp.bfloat16)
+    full[...] = centred * lax.rsqrt(variance + 1e-06)
+    act = jnp.transpose(jnp.broadcast_to(act_ref[...], (8, freq)))[:, :1]
+    act = jnp.broadcast_to(act, (freq, HEAD_DIM))
+
+    def modulation(column):
+        return jnp.sum(act * times[:, column:column + HEAD_DIM], axis=0, keepdims=True)
+
+    loads[0].wait()
+    loads[1].wait()
+    for column in range(0, depth, HEAD_DIM):
+        here = slice(column, column + HEAD_DIM)
+        shift = modulation(column) + block_ref[0:1, here]
+        scale = modulation(depth + column) + block_ref[1:2, here]
+        normed[:, here] = (full[:, here] * (1.0 + scale) + shift).astype(jnp.bfloat16)
     factor = math.log2(math.e) / math.sqrt(HEAD_DIM)
-    near, far = (pl.ds(pl.multiple_of(side * part_rows, 32), part_rows) for side in (core, 1 - core))
-    copies = []
-    for group in range(columns // wide):
-        for part in range(3):
-            loads[group, part].wait()
+    for part in range(3):
+        loads[2 + 2 * part].wait()
+        loads[3 + 2 * part].wait()
+        for column in range(0, columns, 2 * HEAD_DIM):
             out = jnp.dot(
-                normed[...], weights[part, :, group * wide:(group + 1) * wide], preferred_element_type=jnp.float32
+                normed[...], weights[part, :, column:column + 2 * HEAD_DIM], preferred_element_type=jnp.float32
             )
             if part == 0:
                 out = out * factor
             for e in range(2):
-                packed[2 * group + e, part] = out[:, e * HEAD_DIM:(e + 1) * HEAD_DIM].astype(jnp.bfloat16)
-        for head in (2 * group, 2 * group + 1):
-            for source, target in (
-                (near, near_ref.at[owner_of(table, core, head)]), (far, far_ref.at[head]),
-            ):
-                copies.append(
-                    pltpu.make_async_copy(packed.at[head, :, source], target, out_sems.at[len(copies)])
-                )
-                copies[-1].start()
+                piece = out[:, e * HEAD_DIM:(e + 1) * HEAD_DIM].astype(jnp.bfloat16)
+                packed[column // HEAD_DIM + e, part] = piece
+    near, far = (pl.ds(pl.multiple_of(side * part_rows, 32), part_rows) for side in (core, 1 - core))
+    copies = []
+    for head in range(columns // HEAD_DIM):
+        for source, target in ((far, far_ref.at[head]), (near, near_ref.at[owner_of(table, core, head)])):
+            copies.append(pltpu.make_async_copy(packed.at[head, :, source], target, out_sems.at[len(copies)]))
+            copies[-1].start()
+    loads[8].wait()
+    for column in range(0, share, HEAD_DIM):
+        here = pl.ds(pl.multiple_of(mine + column, 128), HEAD_DIM)
+        gate_ref[:, column:column + HEAD_DIM] = modulation(2 * depth + column) + block_ref[2:3, here]
     for copy in copies:
         copy.wait()
 
 
-def project(own, other, mod, w_query, w_key, w_value, chips, table):
+def project(act, block_mod, own, other, time_weight, w_query, w_key, w_value, chips, table):
     rows, share = own.shape
     depth, columns = w_query.shape
+    freq = time_weight.shape[0]
     heads_here = columns // HEAD_DIM
     return pl.pallas_call(
         functools.partial(project_kernel, table),
-        in_specs=[vmem_spec()] * 3 + [any_spec()] * 3,
-        out_specs=[any_spec()] * 2,
+        in_specs=[vmem_spec()] * 4 + [any_spec()] * 4,
+        out_specs=[any_spec()] * 2 + [vmem_spec()],
         out_shape=[
             jax.ShapeDtypeStruct((chips, 3, rows // 2, HEAD_DIM), jnp.bfloat16),
             jax.ShapeDtypeStruct((heads_here, 3, rows // 2, HEAD_DIM), jnp.bfloat16),
+            jax.ShapeDtypeStruct((1, share), jnp.float32),
         ],
         scratch_shapes=[
+            pltpu.VMEM((freq, 2 * depth + share), jnp.float32),
             pltpu.VMEM((3, depth, columns), jnp.bfloat16),
             pltpu.VMEM((rows, depth), jnp.float32),
             pltpu.VMEM((rows, depth), jnp.bfloat16),
             pltpu.VMEM((heads_here, 3, rows, HEAD_DIM), jnp.bfloat16),
-            pltpu.SemaphoreType.DMA((3 * heads_here // 2,)),
+            pltpu.SemaphoreType.DMA((9,)),
             pltpu.SemaphoreType.DMA((2 * heads_here,)),
         ],
         compiler_params=pltpu.CompilerParams(vmem_limit_bytes=STREAM_LIMIT),
-    )(own, other, mod, w_query, w_key, w_value)
+    )(act, block_mod, own, other, time_weight, w_query, w_key, w_value)
 
 
 def merge_kernel(table, near_ref, far_ref, out_ref, sems):
@@ -219,6 +214,7 @@
             copy.wait()
         block_rows = QUERY_CHIPS * part_rows
         key_rows = 2 * KEY_CHIPS * part_rows
+        groups = chips // KEY_CHIPS
 
         def query_block(block, carry):
             first = (2 * QUERY_CHIPS * block + side) * part_rows
@@ -228,29 +224,43 @@
                 low = jnp.where(first >= start, start, low)
                 high = jnp.where(last >= start, stop, high)
             q = query[pl.ds(block * QUERY_CHIPS, QUERY_CHIPS)].reshape(block_rows, 2 * HEAD_DIM)
-            top[...] = jnp.full(top.shape, 2 * NEG, jnp.float32)
-            total[...] = jnp.zeros(total.shape, jnp.float32)
-
-            def key_block(number, carry):
-                here = pl.ds(number * KEY_CHIPS, KEY_CHIPS)
-                k = keys[here].reshape(key_rows, 2 * HEAD_DIM)
+
+            def scores(number):
+                k = keys[pl.ds(number * KEY_CHIPS, KEY_CHIPS)].reshape(key_rows, 2 * HEAD_DIM)
                 score = lax.dot_general(q, k, (((1,), (1,)), ((), ())), preferred_element_type=jnp.float32)
                 tiles = [score[:, j:j + HEAD_DIM] for j in range(0, key_rows, HEAD_DIM)]
                 most = jnp.max(functools.reduce(jnp.maximum, tiles), axis=1, keepdims=True)
-                before = top[...]
-                now = jnp.maximum(before, most)
+                return tiles, jnp.broadcast_to(most, (block_rows, HEAD_DIM))
+
+            def weigh(number, tiles, now):
                 probs = jnp.concatenate([jnp.exp2(tile - now).astype(jnp.bfloat16) for tile in tiles], axis=1)
-                v = values[here].reshape(key_rows, 2 * HEAD_DIM)
-                update = jnp.dot(probs, v, preferred_element_type=jnp.float32)
-                shrink = jnp.exp2(before - now)
-                total[:, :HEAD_DIM] = total[:, :HEAD_DIM] * shrink + update[:, :HEAD_DIM]
-                total[:, HEAD_DIM:] = total[:, HEAD_DIM:] * shrink + update[:, HEAD_DIM:]
-                top[...] = now
-                return carry
-
-            lax.fori_loop(low // key_rows, (high + key_rows - 1) // key_rows, key_block, 0)
-            out = (total[:, :HEAD_DIM] / total[:, HEAD_DIM:]).astype(jnp.bfloat16)
-            result[pl.ds(block * QUERY_CHIPS, QUERY_CHIPS)] = out.reshape(QUERY_CHIPS, part_rows, HEAD_DIM)
+                v = values[pl.ds(number * KEY_CHIPS, KEY_CHIPS)].reshape(key_rows, 2 * HEAD_DIM)
+                return jnp.dot(probs, v, preferred_element_type=jnp.float32)
+
+            if groups == 1:
+                tiles, now = scores(0)
+                update = weigh(0, tiles, now)
+                out = update[:, :HEAD_DIM] / update[:, HEAD_DIM:]
+            else:
+                top[...] = jnp.full(top.shape, 2 * NEG, jnp.float32)
+                total[...] = jnp.zeros(total.shape, jnp.float32)
+
+                def key_block(number, carry):
+                    tiles, most = scores(number)
+                    before = top[...]
+                    now = jnp.maximum(before, most)
+                    update = weigh(number, tiles, now)
+                    shrink = jnp.exp2(before - now)
+                    total[:, :HEAD_DIM] = total[:, :HEAD_DIM] * shrink + update[:, :HEAD_DIM]
+                    total[:, HEAD_DIM:] = total[:, HEAD_DIM:] * shrink + update[:, HEAD_DIM:]
+                    top[...] = now
+                    return carry
+
+                lax.fori_loop(low // key_rows, (high + key_rows - 1) // key_rows, key_block, 0)
+                out = total[:, :HEAD_DIM] / total[:, HEAD_DIM:]
+            result[pl.ds(block * QUERY_CHIPS, QUERY_CHIPS)] = out.astype(jnp.bfloat16).reshape(
+                QUERY_CHIPS, part_rows, HEAD_DIM
+            )
             return carry
 
         lax.fori_loop(0, chips // QUERY_CHIPS, query_block, 0)
@@ -319,18 +329,15 @@
     )(near, far, w_out)
 
 
-def finish_kernel(timestep_ref, mine, theirs, tokens, mod_ref, velocity, stepped):
-    share = tokens.shape[1]
-    core = lax.axis_index("tp")
+def finish_kernel(timestep_ref, mine, theirs, tokens, gate_ref, velocity, stepped):
     step_value = jnp.full((1, 128), timestep_ref[0], jnp.int32).astype(jnp.float32)
     delta = (noise_level(step_value - 1.0) - noise_level(step_value))[:, :1]
-    gate = mod_ref[2, :, pl.ds(pl.multiple_of(core * share, 128), share)]
-    branch = gate * (mine[...] + theirs[...].astype(jnp.float32))
+    branch = gate_ref[...] * (mine[...] + theirs[...].astype(jnp.float32))
     velocity[...] = branch.astype(jnp.bfloat16)
     stepped[...] = (tokens[...].astype(jnp.float32) + delta * branch).astype(jnp.bfloat16)
 
 
-def finish(timestep, mine, theirs, tokens, mod):
+def finish(timestep, mine, theirs, tokens, gate):
     shape = jax.ShapeDtypeStruct(tokens.shape, jnp.bfloat16)
     return pl.pallas_call(
         finish_kernel,
@@ -338,7 +345,7 @@
         out_specs=[vmem_spec(), vmem_spec()],
         out_shape=[shape, shape],
         compiler_params=pltpu.CompilerParams(vmem_limit_bytes=VMEM_LIMIT),
-    )(timestep, mine, theirs, tokens, mod)
+    )(timestep, mine, theirs, tokens, gate)
 
 
 def make(mesh):
@@ -355,15 +362,14 @@
         frequency = jnp.exp(-math.log(10000.0) * jnp.arange(half_freq, dtype=jnp.float32) / half_freq)
         angle = 1000.0 * sigma * frequency
         act = jax.nn.silu(jnp.concatenate([jnp.cos(angle), jnp.sin(angle)]))[None, :]
-        mod = modulate(act, time_weight, block_mod)
-        near, far = project(tokens, other, mod, w_query, w_key, w_value, chips, table)
+        near, far, gate = project(act, block_mod, tokens, other, time_weight, w_query, w_key, w_value, chips, table)
         near = merge(near, lax.ppermute(far, "tp", swap), table)
         near = lax.all_to_all(near, "req", 0, 0, tiled=True)
         done = attend(video_lengths, near, lax.ppermute(near, "tp", swap), table)
         done = lax.all_to_all(done, "req", 0, 0, tiled=True)
         mine, theirs = combine(done, lax.ppermute(done, "tp", swap), w_out, table)
         theirs = lax.ppermute(theirs, "tp", swap)
-        velocity, stepped = finish(timestep, mine, theirs, tokens, mod)
+        velocity, stepped = finish(timestep, mine, theirs, tokens, gate)
         return (velocity, stepped)
 
     return on_device

time: 93 us -> 87.5 us (0.941)
  Pallas kernels: 25.2 us -> 20.7 us
    pallas_call x1 -> x0, Pallas kernels: 3.88 us -> none  [modulate(): pl.pallas_call(modulation_kernel, in_specs=[vmem_spec(), any_spec(), vmem...]
    pallas_call x1, Pallas kernels: 7.1 us -> 5.68 us  [project(): pl.pallas_call(functools.partial(project_kernel, table), in_specs=[vmem_s...]
    unnamed x12 -> x8, local copies, waits for them, and re-layouts: 2 us -> 1.71 us
  transfers between devices with their start and end apart: 5 -> 5, of which waited for: 4 -> 5; matrix products, arithmetic and copies ran while one was open for 1% -> 0% of each run, Pallas kernels for 4% -> 0%
where the time goes in v5:
time: 87.5 us; the launch traced here: 87.2 us
  blocking collectives  54.1 us (62%)
  Pallas kernels  20.7 us (24%)
  waiting for transfers between devices  8.08 us (9%)
  local copies, waits for them, and re-layouts  1.71 us (2%)
  between operations  1.38 us (2%)
  starting transfers between devices  1.17 us (1%)
    all_to_all x1, blocking collectives, on_device(): near = lax.all_to_all(near, 'req', 0, 0, tiled=True)  38.3 us
    all_to_all x1, blocking collectives, on_device(): done = lax.all_to_all(done, 'req', 0, 0, tiled=True)  15.8 us
    pallas_call x1, Pallas kernels, attend(): pl.pallas_call(functools.partial(attend_kernel, table), in_specs=[smem_sp...  12.7 us
    pallas_call x1, Pallas kernels, project(): pl.pallas_call(functools.partial(project_kernel, table), in_specs=[vmem_s...  5.68 us
    ppermute x1, waiting for transfers between devices, on_device(): done = attend(video_lengths, near, lax.ppermute(near, 'tp', swap), table)  2.84 us
  transfers between devices with their start and end apart: 5, of which 5 were waited for; matrix products, arithmetic and copies ran while one was open for 0% of the time, Pallas kernels for 0%

profile of v5, /device:TPU:0, one launch (start us, length us, event | category | flops | bytes accessed | tf_op | source)
XLA Modules:
  0.0 87.2 jit_solution(6700197378310933235)
XLA Ops:
  0.6 0.5 collective-permute-start
  1.9 0.7 collective-permute-done.other_ref
  2.6 0.0 copy-start.1
  2.6 1.0 %copy-done.1 = bf16[192,768]{1,0:T(8,128)(2,1)S(1)} copy-done((bf16[192,768]{1,0:T(8,128)(2,1)S(1)}, bf16[192,768]{1,0:T(8,128)(2,1)}, u32[]{:S(2)}) %copy-start.1) | copy-done | bytes 294936
  3.5 0.0 copy-start.2
  3.5 0.7 copy-done.2
  4.3 5.7 %shard_map.104 = (bf16[16,3,96,128]{3,2,1,0:T(8,128)(2,1)S(1)}, bf16[6,3,96,128]{3,2,1,0:T(8,128)(2,1)S(1)}, f32[1,768]{1,0:T(1,128)S(1)}) custom-call(f32[1,256]{1,0:T(1,128)S(1)} %divide_multiply_fusion.act_ref, f32[3,1536]{1,0:T(4,128)S(1)} %copy-done.2, bf16[192,768]{1,0:T(8,128)(2,1)S(1)} %copy-done.1, ...), custom_call_target="tpu_custom_call" | custom-call | tf_op jit(solution)/shard_map/pallas_call | solution.py:122
  10.0 0.4 collective-permute-start.1
  10.4 1.4 %collective-permute-done.1.far_ref = bf16[6,3,96,128]{3,2,1,0:T(8,128)(2,1)S(1)} collective-permute-done((bf16[6,3,96,128]{3,2,1,0:T(8,128)(2,1)S(1)}, bf16[6,3,96,128]{3,2,1,0:T(8,128)(2,1)S(1)}, u32[]{:S(2)}, u32[]{:S(2)}) %collective-permute-start.1) | collective-permute-done | bytes 442400 | tf_op jit(solution)/shard_map/ppermute | solution.py:366
  11.8 0.0 copy-start.3
  11.8 0.6 shard_map.105
  12.4 38.3 %all_to_all.10.near_ref = bf16[16,3,96,128]{3,2,1,0:T(8,128)(2,1)S(1)} all-to-all(bf16[16,3,96,128]{3,2,1,0:T(8,128)(2,1)S(1)} %shard_map.105), channel_id=1, replica_groups=mesh['req'=16,'tp'=2] {'req'}, dimensions={0} | all-to-all | bytes 2359296 | tf_op jit(solution)/shard_map/all_to_all | solution.py:367
  50.7 0.0 copy-start
  50.7 0.0 collective-permute-start.2
  50.7 2.8 %collective-permute-done.2.far_ref = bf16[16,3,96,128]{3,2,1,0:T(8,128)(2,1)S(1)} collective-permute-done((bf16[16,3,96,128]{3,2,1,0:T(8,128)(2,1)S(1)}, bf16[16,3,96,128]{3,2,1,0:T(8,128)(2,1)S(1)}, u32[]{:S(2)}, u32[]{:S(2)}) %collective-permute-start.2) | collective-permute-done | bytes 1179680 | tf_op jit(solution)/shard_map/ppermute | solution.py:368
  53.6 0.0 copy-done.3
  53.6 12.7 %shard_map.106 = bf16[16,96,128]{2,1,0:T(8,128)(2,1)S(1)} custom-call(s32[5]{0:T(128)S(1)} %copy-done.3, bf16[16,3,96,128]{3,2,1,0:T(8,128)(2,1)S(1)} %all_to_all.10.near_ref, bf16[16,3,96,128]{3,2,1,0:T(8,128)(2,1)S(1)} %collective-permute-done.2.far_ref), custom_call_target="tpu_custom_call" | custom-call | tf_op jit(solution)/shard_map/pallas_call | solution.py:275
  66.3 15.8 %all_to_all.11.near_ref = bf16[16,96,128]{2,1,0:T(8,128)(2,1)S(1)} all-to-all(bf16[16,96,128]{2,1,0:T(8,128)(2,1)S(1)} %shard_map.106), channel_id=1, replica_groups=mesh['req'=16,'tp'=2] {'req'}, dimensions={0} | all-to-all | bytes 786432 | tf_op jit(solution)/shard_map/all_to_all | solution.py:369
  82.1 0.0 collective-permute-start.3
  82.1 1.7 %collective-permute-done.3.far_ref = bf16[16,96,128]{2,1,0:T(8,128)(2,1)S(1)} collective-permute-done((bf16[16,96,128]{2,1,0:T(8,128)(2,1)S(1)}, bf16[16,96,128]{2,1,0:T(8,128)(2,1)S(1)}, u32[]{:S(2)}, u32[]{:S(2)}) %collective-permute-start.3) | collective-permute-done | bytes 393248 | tf_op jit(solution)/shard_map/ppermute | solution.py:370
  83.8 0.0 copy-done
  83.8 0.8 shard_map.107
  84.6 0.2 collective-permute-start.4
  84.8 1.4 %collective-permute-done.4.theirs = bf16[192,768]{1,0:T(8,128)(2,1)S(1)} collective-permute-done((bf16[192,768]{1,0:T(8,128)(2,1)S(1)}, bf16[192,768]{1,0:T(8,128)(2,1)S(1)}, u32[]{:S(2)}, u32[]{:S(2)}) %collective-permute-start.4) | collective-permute-done | bytes 294944 | tf_op jit(solution)/shard_map/ppermute | solution.py:371
  86.3 0.9 %shard_map.108 = (bf16[192,768]{1,0:T(8,128)(2,1)}, bf16[192,768]{1,0:T(8,128)(2,1)}) custom-call(s32[1]{0:T(128)S(6)} %copy.13.timestep_ref, f32[192,768]{1,0:T(8,128)S(1)} %get-tuple-element.9.mine, bf16[192,768]{1,0:T(8,128)(2,1)S(1)} %collective-permute-done.4.theirs, bf16[192,768]{1,0:T(8,128)(2,1)S(1)} %copy-done.1, ...), custom_call_target="tpu_custom_call" | custom-call | tf_op jit(solution)/shard_map/pallas_call | solution.py:342
  (2 shorter events, 0.1 us)
Async XLA Ops:
  0.6 1.9 %collective-permute-start = (bf16[192,768]{1,0:T(8,128)(2,1)}, bf16[192,768]{1,0:T(8,128)(2,1)S(1)}, u32[]{:S(2)}, u32[]{:S(2)}) collective-permute-start(bf16[192,768]{1,0:T(8,128)(2,1)} %tokens.1), channel_id=1, source_target_pairs={{0,1},{1,0},{2,3},{3,2},{4,5},{5,4},{6,7},{7,6},{8,9},{9,8},{10,11... | collective-permute-start | bytes 884744 | tf_op jit(solution)/shard_map/ppermute | solution.py:358
  2.6 1.0 %copy-start.1 = (bf16[192,768]{1,0:T(8,128)(2,1)S(1)}, bf16[192,768]{1,0:T(8,128)(2,1)}, u32[]{:S(2)}) copy-start(bf16[192,768]{1,0:T(8,128)(2,1)} %tokens.1) | copy-start | bytes 884740
  3.5 0.7 copy-start.2
  10.0 1.9 %collective-permute-start.1 = (bf16[6,3,96,128]{3,2,1,0:T(8,128)(2,1)S(1)}, bf16[6,3,96,128]{3,2,1,0:T(8,128)(2,1)S(1)}, u32[]{:S(2)}, u32[]{:S(2)}) collective-permute-start(bf16[6,3,96,128]{3,2,1,0:T(8,128)(2,1)S(1)} %get-tuple-element.8), channel_id=1, source_target_pairs={{0,1},{1,0},{2,3},{3,2},{4,5},{5,4},{6,7},{7,6},{8,9},{9,8},{10,11... | collective-permute-start | bytes 1327112 | tf_op jit(solution)/shard_map/ppermute | solution.py:366
  11.8 41.8 %copy-start.3 = (s32[5]{0:T(128)S(1)}, s32[5]{0:T(128)}, u32[]{:S(2)}) copy-start(s32[5]{0:T(128)} %lengths_ref.1) | copy-start | bytes 64
  50.7 33.0 %copy-start = (bf16[768,1536]{1,0:T(8,128)(2,1)S(1)}, bf16[768,1536]{1,0:T(8,128)(2,1)}, u32[]{:S(2)}) copy-start(bf16[768,1536]{1,0:T(8,128)(2,1)} %weight.1) | copy-start | bytes 7077892
  50.7 2.8 %collective-permute-start.2 = (bf16[16,3,96,128]{3,2,1,0:T(8,128)(2,1)S(1)}, bf16[16,3,96,128]{3,2,1,0:T(8,128)(2,1)S(1)}, u32[]{:S(2)}, u32[]{:S(2)}) collective-permute-start(bf16[16,3,96,128]{3,2,1,0:T(8,128)(2,1)S(1)} %all_to_all.10.near_ref), channel_id=1, source_target_pairs={{0,1},{1,0},{2,3},{3,2},{4,5},{5,4},{6,7},{7,6},{8,9},{9,8},{10,11... | collective-permute-start | bytes 3538952 | tf_op jit(solution)/shard_map/ppermute | solution.py:368
  82.1 1.7 %collective-permute-start.3 = (bf16[16,96,128]{2,1,0:T(8,128)(2,1)S(1)}, bf16[16,96,128]{2,1,0:T(8,128)(2,1)S(1)}, u32[]{:S(2)}, u32[]{:S(2)}) collective-permute-start(bf16[16,96,128]{2,1,0:T(8,128)(2,1)S(1)} %all_to_all.11.near_ref), channel_id=1, source_target_pairs={{0,1},{1,0},{2,3},{3,2},{4,5},{5,4},{6,7},{7,6},{8,9},{9,8},{10,11... | collective-permute-start | bytes 1179656 | tf_op jit(solution)/shard_map/ppermute | solution.py:370
  84.6 1.6 %collective-permute-start.4 = (bf16[192,768]{1,0:T(8,128)(2,1)S(1)}, bf16[192,768]{1,0:T(8,128)(2,1)S(1)}, u32[]{:S(2)}, u32[]{:S(2)}) collective-permute-start(bf16[192,768]{1,0:T(8,128)(2,1)S(1)} %get-tuple-element.10), channel_id=1, source_target_pairs={{0,1},{1,0},{2,3},{3,2},{4,5},{5,4},{6,7},{7,6},{8,9},{9,8},{10,11... | collective-permute-start | bytes 884744 | tf_op jit(solution)/shard_map/ppermute | solution.py:371

commit v6 on v5

v6 whole, which is shorter than its diff:
```python
import functools
import math

import jax
import jax.numpy as jnp
from jax import lax
from jax.experimental import pallas as pl
from jax.experimental.pallas import tpu as pltpu
from jax.sharding import PartitionSpec as P

HEAD_DIM = 128
STEPS = 1000
QUERY_BLOCK = 384
KEY_GROUP = 3072
WINDOWS = (1024, 2048)
NEG = -1e30
STREAM_LIMIT = 51 * 1024 * 1024
VMEM_LIMIT = 32 * 1024 * 1024


def noise_level(step_value):
    frac = step_value / STEPS
    return 5.0 * frac / (1.0 + 4.0 * frac)


def pairs_out(chips, heads, colour):
    half = chips // 2
    pairs = []
    for chip in range(chips):
        side, slot, x = chip // half, chip % half // 2, chip % 2
        for core in range(2):
            source, target = chip * 2 + core, (core * half + (slot ^ colour) * 2 + x) * 2 + side
            if (slot ^ colour) < heads and source != target:
                pairs.append((source, target))
    return pairs


def place_of(colours):
    chip = lax.axis_index("req")
    slot = lax.rem(chip // 2, colours)
    return slot, lax.rem(chip, 2), chip // (2 * colours) == lax.axis_index("tp")


def any_spec():
    return pl.BlockSpec(memory_space=pl.ANY)


def vmem_spec():
    return pl.BlockSpec(memory_space=pltpu.VMEM)


def smem_spec():
    return pl.BlockSpec(memory_space=pltpu.SMEM)


def standardise(full, own_ref, other_ref):
    share = own_ref.shape[1]
    core = lax.axis_index("tp")
    full[:, pl.ds(pl.multiple_of(core * share, 128), share)] = own_ref[...].astype(jnp.float32)
    full[:, pl.ds(pl.multiple_of((1 - core) * share, 128), share)] = other_ref[...].astype(jnp.float32)
    whole = full[...]
    centred = whole - jnp.mean(whole, axis=1, keepdims=True)
    variance = jnp.mean(centred * centred, axis=1, keepdims=True)
    return centred * lax.rsqrt(variance + 1e-06)


def project_part(packed, normed, weight, part):
    out = jnp.dot(normed[...], weight, preferred_element_type=jnp.float32)
    if part == 0:
        out = out * (math.log2(math.e) / math.sqrt(HEAD_DIM))
    for head in range(out.shape[1] // HEAD_DIM):
        packed[head, part] = out[:, head * HEAD_DIM:(head + 1) * HEAD_DIM].astype(jnp.bfloat16)


def load_weights(load, refs, weights):
    depth, columns = weights.shape[1:]
    x = lax.rem(lax.axis_index("req"), 2)
    for part, ref in enumerate(refs):
        for cut in range(2):
            here = pl.ds(cut * (depth // 2), depth // 2)
            load(ref.at[here, pl.ds(pl.multiple_of(x * columns, 128), columns)], weights.at[part, here])


def project_kernel(act_ref, block_ref, own_ref, other_ref, time_ref, wq_ref, wk_ref, wv_ref, *rest):
    packed, mod_ref, gate_ref, weights, times, full, normed, sems = rest
    depth = full.shape[1]
    share = own_ref.shape[1]
    freq = times.shape[0]
    core = lax.axis_index("tp")
    loads = []

    def load(source, target):
        loads.append(pltpu.make_async_copy(source, target, sems.at[len(loads)]))
        loads[-1].start()

    for part in range(2):
        here = pl.ds(part * (freq // 2), freq // 2)
        load(time_ref.at[here, pl.ds(0, 2 * depth)], times.at[here, pl.ds(0, 2 * depth)])
    load_weights(load, (wq_ref, wk_ref, wv_ref), weights)
    load(
        time_ref.at[:, pl.ds(pl.multiple_of(2 * depth + core * share, 128), share)],
        times.at[:, pl.ds(2 * depth, share)],
    )
    full[...] = standardise(full, own_ref, other_ref)
    act = jnp.transpose(jnp.broadcast_to(act_ref[...], (8, freq)))[:, :1]
    act = jnp.broadcast_to(act, (freq, HEAD_DIM))

    def modulation(column):
        return jnp.sum(act * times[:, column:column + HEAD_DIM], axis=0, keepdims=True)

    loads[0].wait()
    loads[1].wait()
    for column in range(0, depth, HEAD_DIM):
        here = slice(column, column + HEAD_DIM)
        shift = modulation(column) + block_ref[0:1, here]
        scale = modulation(depth + column) + block_ref[1:2, here]
        mod_ref[0:1, here] = shift
        mod_ref[1:2, here] = scale
        normed[:, here] = (full[:, here] * (1.0 + scale) + shift).astype(jnp.bfloat16)
    for part in range(3):
        loads[2 + 2 * part].wait()
        loads[3 + 2 * part].wait()
        project_part(packed, normed, weights[part], part)
    loads[8].wait()
    for column in range(0, share, HEAD_DIM):
        here = pl.ds(pl.multiple_of(core * share + column, 128), HEAD_DIM)
        gate_ref[:, column:column + HEAD_DIM] = modulation(2 * depth + column) + block_ref[2:3, here]


def project(act, block_mod, own, other, time_weight, w_query, w_key, w_value):
    rows, share = own.shape
    depth, columns = w_query.shape
    columns = columns // 2
    freq = time_weight.shape[0]
    heads = columns // HEAD_DIM
    return pl.pallas_call(
        project_kernel,
        in_specs=[vmem_spec()] * 4 + [any_spec()] * 4,
        out_specs=[vmem_spec()] * 3,
        out_shape=[
            jax.ShapeDtypeStruct((heads, 3, rows, HEAD_DIM), jnp.bfloat16),
            jax.ShapeDtypeStruct((2, depth), jnp.float32),
            jax.ShapeDtypeStruct((1, share), jnp.float32),
        ],
        scratch_shapes=[
            pltpu.VMEM((3, depth, columns), jnp.bfloat16),
            pltpu.VMEM((freq, 2 * depth + share), jnp.float32),
            pltpu.VMEM((rows, depth), jnp.float32),
            pltpu.VMEM((rows, depth), jnp.bfloat16),
            pltpu.SemaphoreType.DMA((9,)),
        ],
        compiler_params=pltpu.CompilerParams(vmem_limit_bytes=STREAM_LIMIT),
        cost_estimate=pl.CostEstimate(flops=6 * rows * depth * columns, bytes_accessed=8 * 2**20, transcendentals=0),
    )(act, block_mod, own, other, time_weight, w_query, w_key, w_value)


def share_kernel(colours, near_ref, far_ref, mod_ref, mine, wq_ref, wk_ref, wv_ref, *rest):
    outs, (weights, full, normed, packed, load_sems, sems) = rest[:colours], rest[colours:]
    heads, _, rows, _ = mine.shape
    loads = []

    def load(source, target):
        loads.append(pltpu.make_async_copy(source, target, load_sems.at[len(loads)]))
        loads[-1].start()

    load_weights(load, (wq_ref, wk_ref, wv_ref), weights)
    slot, x, _ = place_of(colours)

    def each_copy(source, position, offset, act):
        for head in range(heads):
            for colour in range(colours):
                @pl.when((slot ^ colour) == head)
                def _():
                    here = pl.ds(pl.multiple_of(position * rows, 64), rows)
                    act(pltpu.make_async_copy(source.at[head], outs[colour].at[:, here], sems.at[offset + head]))

    each_copy(mine, x, 0, lambda copy: copy.start())
    scaled = standardise(full, near_ref, far_ref)
    normed[...] = (scaled * (1.0 + mod_ref[1:2, :]) + mod_ref[0:1, :]).astype(jnp.bfloat16)
    for part in range(3):
        loads[2 * part].wait()
        loads[2 * part + 1].wait()
        project_part(packed, normed, weights[part], part)
    each_copy(packed, 1 - x, heads, lambda copy: copy.start())
    each_copy(mine, x, 0, lambda copy: copy.wait())
    each_copy(packed, 1 - x, heads, lambda copy: copy.wait())


def project_shared(near, far, mod, mine, w_query, w_key, w_value, colours):
    heads, _, rows, _ = mine.shape
    depth = mod.shape[1]
    return pl.pallas_call(
        functools.partial(share_kernel, colours),
        in_specs=[vmem_spec()] * 3 + [any_spec()] * 4,
        out_specs=[any_spec()] * colours,
        out_shape=[jax.ShapeDtypeStruct((3, 2 * rows, HEAD_DIM), jnp.bfloat16)] * colours,
        scratch_shapes=[
            pltpu.VMEM((3, depth, heads * HEAD_DIM), jnp.bfloat16),
            pltpu.VMEM((rows, depth), jnp.float32),
            pltpu.VMEM((rows, depth), jnp.bfloat16),
            pltpu.VMEM(mine.shape, jnp.bfloat16),
            pltpu.SemaphoreType.DMA((6,)),
            pltpu.SemaphoreType.DMA((2 * heads,)),
        ],
        compiler_params=pltpu.CompilerParams(vmem_limit_bytes=STREAM_LIMIT),
    )(near, far, mod, mine, w_query, w_key, w_value)


def collect_kernel(colours, sent_ref, *refs):
    pieces, out, sems = refs[:colours], refs[colours], refs[colours + 1]
    own = place_of(colours)[2]

    def each_copy(act):
        for colour, piece in enumerate(pieces):
            copy = pltpu.make_async_copy(piece.at[pl.ds(1, 2)], out.at[colour], sems.at[colour])
            if colour:
                act(copy)
            else:
                pl.when(jnp.logical_not(own))(functools.partial(act, copy))
                local = pltpu.make_async_copy(sent_ref.at[pl.ds(1, 2)], out.at[colour], sems.at[colour])
                pl.when(own)(functools.partial(act, local))

    each_copy(lambda copy: copy.start())
    each_copy(lambda copy: copy.wait())


def collect(sent, pieces):
    _, rows, wide = sent.shape
    colours = len(pieces)
    return pl.pallas_call(
        functools.partial(collect_kernel, colours),
        in_specs=[any_spec()] * (colours + 1),
        out_specs=any_spec(),
        out_shape=jax.ShapeDtypeStruct((colours, 2, rows, wide), jnp.bfloat16),
        scratch_shapes=[pltpu.SemaphoreType.DMA((colours,))],
        compiler_params=pltpu.CompilerParams(vmem_limit_bytes=VMEM_LIMIT),
    )(sent, *pieces)


def attend_kernel(colours, heads, lengths_ref, sent_ref, *refs):
    pieces, swapped = refs[:colours], refs[colours]
    outs = refs[colours + 1:2 * colours + 1]
    query, keys, values, result, top, total, sems, out_sems = refs[2 * colours + 1:]
    rows = sent_ref.shape[1]
    own_rows, all_rows = query.shape[0], keys.shape[0]
    side = lax.axis_index("tp")
    slot, _, own = place_of(colours)
    front = pl.ds(0, HEAD_DIM)
    videos = lengths_ref.shape[0]

    def at(colour, which):
        return pl.ds(pl.multiple_of((slot ^ colour) * rows + which * own_rows, 128), rows)

    def each_copy(act):
        for colour in range(colours):
            def load(piece, colour=colour):
                for part, target in enumerate((
                    query.at[at(colour, 0), front],
                    keys.at[at(colour, side), front],
                    values.at[at(colour, side), front],
                )):
                    act(pltpu.make_async_copy(piece.at[part], target, sems.at[5 * colour + part]))

            if colour:
                load(pieces[colour])
            else:
                pl.when(jnp.logical_not(own))(functools.partial(load, pieces[0]))
                pl.when(own)(functools.partial(load, sent_ref))
            for part, target in enumerate((keys, values)):
                target = target.at[at(colour, 1 - side), front]
                act(pltpu.make_async_copy(swapped.at[colour, part], target, sems.at[5 * colour + 3 + part]))

    @pl.when(slot < heads)
    def _():
        each_copy(lambda copy: copy.start())
        ends, end = [], jnp.int32(0)
        for video in range(videos):
            end = end + lengths_ref[video]
            ends.append(end)
        starts = [jnp.int32(0)] + ends[:-1]
        lane = lax.broadcasted_iota(jnp.int32, (1, HEAD_DIM), 1)
        lane_start = jnp.zeros((1, HEAD_DIM), jnp.int32)
        lane_stop = jnp.zeros((1, HEAD_DIM), jnp.int32)
        for video, (start, stop) in enumerate(zip(starts, ends)):
            lane_start = jnp.where(lane == video, start, lane_start)
            lane_stop = jnp.where(lane == video, stop, lane_stop)
        place = lax.broadcasted_iota(jnp.int32, (HEAD_DIM, HEAD_DIM), 0)

        def inside(first):
            index = first + place
            return (index >= lane_start) & (index < lane_stop)

        def fill_query(block, carry):
            local = pl.multiple_of(block * HEAD_DIM, HEAD_DIM)
            member = inside(side * own_rows + local)
            query[pl.ds(local, HEAD_DIM), HEAD_DIM:] = jnp.where(member, 1.0, 0.0).astype(jnp.bfloat16)
            return carry

        def fill_keys(block, carry):
            begin = pl.multiple_of(block * HEAD_DIM, HEAD_DIM)
            keys[pl.ds(begin, HEAD_DIM), HEAD_DIM:] = jnp.where(
                inside(begin) | (lane >= videos), 0.0, NEG
            ).astype(jnp.bfloat16)
            values[pl.ds(begin, HEAD_DIM), HEAD_DIM:] = jnp.ones((HEAD_DIM, HEAD_DIM), jnp.bfloat16)
            return carry

        lax.fori_loop(0, own_rows // HEAD_DIM, fill_query, 0)
        lax.fori_loop(0, all_rows // HEAD_DIM, fill_keys, 0)
        each_copy(lambda copy: copy.wait())

        def query_block(block, carry):
            local = pl.multiple_of(block * QUERY_BLOCK, QUERY_BLOCK)
            first = side * own_rows + local
            last = first + QUERY_BLOCK - 1
            low, high = jnp.int32(0), jnp.int32(0)
            for start, stop in zip(starts, ends):
                low = jnp.where(first >= start, start, low)
                high = jnp.where(last >= start, stop, high)
            low = low // HEAD_DIM * HEAD_DIM

            def scores(begin, count):
                score = lax.dot_general(
                    query[pl.ds(local, QUERY_BLOCK), :], keys[pl.ds(begin, count), :], (((1,), (1,)), ((), ())),
                    preferred_element_type=jnp.float32,
                )
                tiles = [score[:, j:j + HEAD_DIM] for j in range(0, count, HEAD_DIM)]
                most = jnp.max(functools.reduce(jnp.maximum, tiles), axis=1, keepdims=True)
                return tiles, jnp.broadcast_to(most, (QUERY_BLOCK, HEAD_DIM))

            def weigh(begin, count, tiles, now):
                probs = jnp.concatenate([jnp.exp2(tile - now).astype(jnp.bfloat16) for tile in tiles], axis=1)
                return jnp.dot(probs, values[pl.ds(begin, count), :], preferred_element_type=jnp.float32)

            def store(update):
                out = update[:, :HEAD_DIM] / update[:, HEAD_DIM:]
                result[pl.ds(local, QUERY_BLOCK), :] = out.astype(jnp.bfloat16)

            def window(count):
                begin = pl.multiple_of(jnp.minimum(low, all_rows - count), HEAD_DIM)
                tiles, now = scores(begin, count)
                store(weigh(begin, count, tiles, now))

            def long():
                top[...] = jnp.full(top.shape, 2 * NEG, jnp.float32)
                total[...] = jnp.zeros(total.shape, jnp.float32)

                def key_block(number, carry):
                    begin = pl.multiple_of(number * KEY_GROUP, KEY_GROUP)
                    tiles, most = scores(begin, KEY_GROUP)
                    before = top[...]
                    now = jnp.maximum(before, most)
                    update = weigh(begin, KEY_GROUP, tiles, now)
                    shrink = jnp.exp2(before - now)
                    total[:, :HEAD_DIM] = total[:, :HEAD_DIM] * shrink + update[:, :HEAD_DIM]
                    total[:, HEAD_DIM:] = total[:, HEAD_DIM:] * shrink + update[:, HEAD_DIM:]
                    top[...] = now
                    return carry

                lax.fori_loop(low // KEY_GROUP, (high + KEY_GROUP - 1) // KEY_GROUP, key_block, 0)
                store(total)

            need = high - low
            small, middle = WINDOWS
            pl.when(need <= small)(lambda: window(small))
            pl.when((need > small) & (need <= middle))(lambda: window(middle))
            if all_rows == KEY_GROUP:
                pl.when(need > middle)(lambda: window(KEY_GROUP))
            else:
                pl.when(need > middle)(long)
            return carry

        lax.fori_loop(0, own_rows // QUERY_BLOCK, query_block, 0)
        copies = [
            pltpu.make_async_copy(result.at[at(colour, 0)], outs[colour], out_sems.at[colour])
            for colour in range(colours)
        ]
        for copy in copies:
            copy.start()
        for copy in copies:
            copy.wait()


def attend(lengths, sent, pieces, swapped, heads):
    rows = sent.shape[1]
    colours = len(pieces)
    own = colours * rows
    return pl.pallas_call(
        functools.partial(attend_kernel, colours, heads),
        in_specs=[smem_spec()] + [any_spec()] * (colours + 2),
        out_specs=[any_spec()] * colours,
        out_shape=[jax.ShapeDtypeStruct((rows, HEAD_DIM), jnp.bfloat16)] * colours,
        scratch_shapes=[
            pltpu.VMEM((own, 2 * HEAD_DIM), jnp.bfloat16),
            pltpu.VMEM((2 * own, 2 * HEAD_DIM), jnp.bfloat16),
            pltpu.VMEM((2 * own, 2 * HEAD_DIM), jnp.bfloat16),
            pltpu.VMEM((own, HEAD_DIM), jnp.bfloat16),
            pltpu.VMEM((QUERY_BLOCK, HEAD_DIM), jnp.float32),
            pltpu.VMEM((QUERY_BLOCK, 2 * HEAD_DIM), jnp.float32),
            pltpu.SemaphoreType.DMA((5 * colours,)),
            pltpu.SemaphoreType.DMA((colours,)),
        ],
        compiler_params=pltpu.CompilerParams(vmem_limit_bytes=VMEM_LIMIT),
    )(lengths, sent, *pieces, swapped)


def part_kernel(colours, done_ref, *refs):
    pieces, (keep, give, sems) = refs[:colours], refs[colours:]
    heads, rows, _ = keep.shape
    slot, x, own = place_of(colours)

    def each_copy(act):
        for head in range(heads):
            for number, (target, position) in enumerate(((give, 1 - x), (keep, x))):
                here = pl.ds(pl.multiple_of(position * rows, 64), rows)

                def move(piece, head=head, number=number, target=target, here=here):
                    act(pltpu.make_async_copy(piece.at[here], target.at[head], sems.at[2 * head + number]))

                for colour in range(colours):
                    right = (slot ^ colour) == head
                    if colour:
                        pl.when(right)(functools.partial(move, pieces[colour]))
                    else:
                        pl.when(right & jnp.logical_not(own))(functools.partial(move, pieces[0]))
                        pl.when(right & own)(functools.partial(move, done_ref))

    each_copy(lambda copy: copy.start())
    each_copy(lambda copy: copy.wait())


def part(done, pieces, heads):
    rows = done.shape[0] // 2
    shape = jax.ShapeDtypeStruct((heads, rows, HEAD_DIM), jnp.bfloat16)
    return pl.pallas_call(
        functools.partial(part_kernel, len(pieces)),
        in_specs=[any_spec()] * (len(pieces) + 1),
        out_specs=[any_spec()] * 2,
        out_shape=[shape, shape],
        scratch_shapes=[pltpu.SemaphoreType.DMA((2 * heads,))],
        compiler_params=pltpu.CompilerParams(vmem_limit_bytes=VMEM_LIMIT),
    )(done, *pieces)


def combine_kernel(keep_ref, got_ref, weight, mine, theirs, attended, sems):
    share = mine.shape[1]
    heads = keep_ref.shape[0]
    core = lax.axis_index("tp")
    x = lax.rem(lax.axis_index("req"), 2)
    copies = []
    for head in range(heads):
        for source, which in ((keep_ref, x), (got_ref, 1 - x)):
            columns = pl.ds(pl.multiple_of((which * heads + head) * HEAD_DIM, HEAD_DIM), HEAD_DIM)
            copies.append(pltpu.make_async_copy(source.at[head], attended.at[:, columns], sems.at[len(copies)]))
            copies[-1].start()
    for copy in copies:
        copy.wait()
    left = attended[...]
    for out, where in ((theirs, 1 - core), (mine, core)):
        columns = pl.ds(pl.multiple_of(where * share, 128), share)
        out[...] = jnp.dot(left, weight[:, columns], preferred_element_type=jnp.float32).astype(out.dtype)


def combine(keep, got, w_out):
    heads, rows, _ = keep.shape
    depth, width = w_out.shape
    return pl.pallas_call(
        combine_kernel,
        in_specs=[any_spec()] * 2 + [vmem_spec()],
        out_specs=[vmem_spec(), vmem_spec()],
        out_shape=[
            jax.ShapeDtypeStruct((rows, width // 2), jnp.float32),
            jax.ShapeDtypeStruct((rows, width // 2), jnp.bfloat16),
        ],
        scratch_shapes=[
            pltpu.VMEM((rows, depth), jnp.bfloat16),
            pltpu.SemaphoreType.DMA((2 * heads,)),
        ],
        compiler_params=pltpu.CompilerParams(vmem_limit_bytes=VMEM_LIMIT),
    )(keep, got, w_out)


def finish_kernel(timestep_ref, mine, theirs, tokens, gate_ref, velocity, stepped):
    step_value = jnp.full((1, 128), timestep_ref[0], jnp.int32).astype(jnp.float32)
    delta = (noise_level(step_value - 1.0) - noise_level(step_value))[:, :1]
    branch = gate_ref[...] * (mine[...] + theirs[...].astype(jnp.float32))
    velocity[...] = branch.astype(jnp.bfloat16)
    stepped[...] = (tokens[...].astype(jnp.float32) + delta * branch).astype(jnp.bfloat16)


def finish(timestep, mine, theirs, tokens, gate):
    shape = jax.ShapeDtypeStruct(tokens.shape, jnp.bfloat16)
    return pl.pallas_call(
        finish_kernel,
        in_specs=[smem_spec()] + [vmem_spec()] * 4,
        out_specs=[vmem_spec(), vmem_spec()],
        out_shape=[shape, shape],
        compiler_params=pltpu.CompilerParams(vmem_limit_bytes=VMEM_LIMIT),
    )(timestep, mine, theirs, tokens, gate)


def make(mesh):
    chips = mesh.shape["req"]
    colours = chips // 4
    swap = [(0, 1), (1, 0)]
    cross = [(chip, chip ^ 1) for chip in range(chips)]

    def on_device(tokens, video_lengths, timestep, time_weight, block_mod, w_query, w_key, w_value, w_out):
        heads = w_query.shape[1] // HEAD_DIM // 2
        routes = [pairs_out(chips, heads, colour) for colour in range(colours)]
        near = lax.ppermute(tokens, "req", cross)
        other = lax.ppermute(tokens, "tp", swap)
        half_freq = time_weight.shape[0] // 2
        time_value = jnp.broadcast_to(timestep, (half_freq,)).astype(jnp.float32)
        sigma = noise_level(time_value)
        frequency = jnp.exp(-math.log(10000.0) * jnp.arange(half_freq, dtype=jnp.float32) / half_freq)
        angle = 1000.0 * sigma * frequency
        act = jax.nn.silu(jnp.concatenate([jnp.cos(angle), jnp.sin(angle)]))[None, :]
        mine, mod, gate = project(act, block_mod, tokens, other, time_weight, w_query, w_key, w_value)
        near, mine, mod, gate = lax.optimization_barrier((near, mine, mod, gate))
        far = lax.ppermute(near, "tp", swap)
        sent = project_shared(near, far, mod, mine, w_query, w_key, w_value, colours)
        got = [lax.ppermute(piece, ("req", "tp"), route) for piece, route in zip(sent, routes)]
        swapped = lax.ppermute(collect(sent[0], got), "tp", swap)
        done = attend(video_lengths, sent[0], got, swapped, heads)
        back = [
            lax.ppermute(piece, ("req", "tp"), [(b, a) for a, b in route]) for piece, route in zip(done, routes)
        ]
        keep, give = part(done[0], back, heads)
        mine, theirs = combine(keep, lax.ppermute(give, "req", cross), w_out)
        theirs = lax.ppermute(theirs, "tp", swap)
        velocity, stepped = finish(timestep, mine, theirs, tokens, gate)
        return (velocity, stepped)

    return on_device


def solution(mesh):
    return jax.shard_map(
        make(mesh),
        mesh=mesh,
        in_specs=(
            P("req", "tp"), P(), P(), P(), P(), P(None, "tp"), P(None, "tp"), P(None, "tp"), P("tp", None),
        ),
        out_specs=(P("req", "tp"), P("req", "tp")),
        check_vma=False,
    )
```

time: 87.5 us -> 80.3 us (0.918)
  blocking collectives: 54.1 us -> 0 us
  waiting for transfers between devices: 8.08 us -> 33.8 us
  starting transfers between devices: 1.17 us -> 22.3 us
    all_to_all x2 -> x0, blocking collectives: 54.1 us -> none  [the longest x1 38.3 us: on_device(): near = lax.all_to_all(near, 'req', 0, 0, tiled=True)]
    ppermute x3 -> x12, waiting for transfers between devices: 5.98 us -> 32.6 us  [the longest x4 18.9 us: on_device(): lax.ppermute(piece, ('req', 'tp'), route)]
    ppermute x3 -> x12, starting transfers between devices: 0.45 us -> 17.1 us  [the longest x4 7.72 us: on_device(): lax.ppermute(piece, ('req', 'tp'), route)]
    ppermute x1, starting transfers between devices: 0.2 us -> 4.7 us  [on_device(): theirs = lax.ppermute(theirs, 'tp', swap)]
    pallas_call x4 -> x6, Pallas kernels: 19.8 us -> 19.7 us  [the longest x1 10.3 us: attend(): pl.pallas_call(functools.partial(attend_kernel, colours, heads), in_specs...]
  transfers between devices with their start and end apart: 5 -> 14, of which waited for: 5 -> 10; matrix products, arithmetic and copies ran while one was open for 0% -> 0% of each run, Pallas kernels for 0% -> 5%
where the time goes in v6:
time: 80.3 us; the launch traced here: 80 us
  waiting for transfers between devices  33.8 us (42%)
  starting transfers between devices  22.3 us (28%)
  Pallas kernels  20.6 us (26%)
  local copies, waits for them, and re-layouts  1.71 us (2%)
  between operations  1.49 us (2%)
    ppermute x4, waiting for transfers between devices, on_device(): lax.ppermute(piece, ('req', 'tp'), route)  18.9 us
    pallas_call x1, Pallas kernels, attend(): pl.pallas_call(functools.partial(attend_kernel, colours, heads), in_specs...  10.3 us
    ppermute x4, starting transfers between devices, on_device(): lax.ppermute(piece, ('req', 'tp'), route)  7.72 us
    ppermute x4, starting transfers between devices, on_device(): lax.ppermute(piece, ('req', 'tp'), [(b, a) for a, b in route])  6.27 us
    ppermute x1, waiting for transfers between devices, on_device(): mine, theirs = combine(keep, lax.ppermute(give, 'req', cross), w_out)  4.75 us
    ppermute x1, starting transfers between devices, on_device(): theirs = lax.ppermute(theirs, 'tp', swap)  4.7 us
    pallas_call x1, Pallas kernels, project(): pl.pallas_call(project_kernel, in_specs=[vmem_spec()] * 4 + [any_spec()]...  4.07 us
    ppermute x4, waiting for transfers between devices, on_device(): lax.ppermute(piece, ('req', 'tp'), [(b, a) for a, b in route])  3.83 us
  transfers between devices with their start and end apart: 14, of which 10 were waited for; matrix products, arithmetic and copies ran while one was open for 0% of the time, Pallas kernels for 5%

profile of v6, /device:TPU:0, one launch (start us, length us, event | category | flops | bytes accessed | tf_op | source)
XLA Modules:
  0.0 80.0 jit_solution(5994435608296764014)
XLA Ops:
  0.6 0.5 collective-permute-start.1
  1.1 2.6 %collective-permute-start = (bf16[192,768]{1,0:T(8,128)(2,1)}, bf16[192,768]{1,0:T(8,128)(2,1)S(1)}, u32[]{:S(2)}, u32[]{:S(2)}) collective-permute-start(bf16[192,768]{1,0:T(8,128)(2,1)} %tokens.1), channel_id=1, source_target_pairs={{0,2},{2,0},{4,6},{6,4},{8,10},{10,8},{12,14},{14,12},{16,18},{18,... | collective-permute-start | bytes 884744 | tf_op jit(solution)/shard_map/ppermute | solution.py:510
  4.5 1.0 %copy-done.1 = bf16[192,768]{1,0:T(8,128)(2,1)S(1)} copy-done((bf16[192,768]{1,0:T(8,128)(2,1)S(1)}, bf16[192,768]{1,0:T(8,128)(2,1)}, u32[]{:S(2)}) %copy-start.1) | copy-done | bytes 294936
  5.5 0.7 copy-done.3
  6.2 4.1 %shard_map.104 = (bf16[3,3,192,128]{3,2,1,0:T(8,128)(2,1)S(1)}, f32[2,1536]{1,0:T(2,128)S(1)}, f32[1,768]{1,0:T(1,128)S(1)}) custom-call(f32[1,256]{1,0:T(1,128)S(1)} %divide_multiply_fusion.act_ref, f32[3,1536]{1,0:T(4,128)S(1)} %copy-done.3, bf16[192,768]{1,0:T(8,128)(2,1)S(1)} %copy-done.1, bf16[192,768]{1,0:T(8,128)(2,1)S(1)} %collective-permute-done.1.other_ref, ...), custom_call_target="tpu_custom_call" | custom-call | flops 679477248 | bytes 8388608 | tf_op jit(solution)/shard_map/pallas_call | solution.py:136
  10.3 1.3 %collective-permute-done.near_ref = bf16[192,768]{1,0:T(8,128)(2,1)S(1)} collective-permute-done((bf16[192,768]{1,0:T(8,128)(2,1)}, bf16[192,768]{1,0:T(8,128)(2,1)S(1)}, u32[]{:S(2)}, u32[]{:S(2)}) %collective-permute-start) | collective-permute-done | bytes 294944 | tf_op jit(solution)/shard_map/ppermute | solution.py:510
  11.5 1.6 %collective-permute-done.2.far_ref = bf16[192,768]{1,0:T(8,128)(2,1)S(1)} collective-permute-done((bf16[192,768]{1,0:T(8,128)(2,1)S(1)}, bf16[192,768]{1,0:T(8,128)(2,1)S(1)}, u32[]{:S(2)}, u32[]{:S(2)}) %collective-permute-start.2) | collective-permute-done | bytes 294944 | tf_op jit(solution)/shard_map/ppermute | solution.py:520
  13.1 3.0 %shard_map.105 = (bf16[3,384,128]{2,1,0:T(8,128)(2,1)S(1)}, bf16[3,384,128]{2,1,0:T(8,128)(2,1)S(1)}, bf16[3,384,128]{2,1,0:T(8,128)(2,1)S(1)}, bf16[3,384,128]{2,1,0:T(8,128)(2,1)S(1)}) custom-call(bf16[192,768]{1,0:T(8,128)(2,1)S(1)} %collective-permute-done.near_ref, bf16[192,768]{1,0:T(8,128)(2,1)S(1)} %collective-permute-done.2.far_ref, ...), custom_call_target="tpu_custom_call" | custom-call | tf_op jit(solution)/shard_map/pallas_call | solution.py:192
  16.1 3.7 %collective-permute-start.4 = (bf16[3,384,128]{2,1,0:T(8,128)(2,1)S(1)}, bf16[3,384,128]{2,1,0:T(8,128)(2,1)S(1)}, u32[]{:S(2)}, u32[]{:S(2)}) collective-permute-start(bf16[3,384,128]{2,1,0:T(8,128)(2,1)S(1)} %get-tuple-element.28), channel_id=1, source_target_pairs={{0,4},{1,20},{2,6},{3,22},{4,0},{5,16},{6,2},{7,18},{12,8},{13,24}... | collective-permute-start | bytes 884744 | tf_op jit(solution)/shard_map/ppermute | solution.py:522
  19.8 1.9 %collective-permute-start.5 = (bf16[3,384,128]{2,1,0:T(8,128)(2,1)S(1)}, bf16[3,384,128]{2,1,0:T(8,128)(2,1)S(1)}, u32[]{:S(2)}, u32[]{:S(2)}) collective-permute-start(bf16[3,384,128]{2,1,0:T(8,128)(2,1)S(1)} %get-tuple-element.29), channel_id=1, source_target_pairs={{0,8},{1,24},{2,10},{3,26},{8,0},{9,16},{10,2},{11,18},{12,4},{13,... | collective-permute-start | bytes 884744 | tf_op jit(solution)/shard_map/ppermute | solution.py:522
  21.8 1.3 %collective-permute-start.6 = (bf16[3,384,128]{2,1,0:T(8,128)(2,1)S(1)}, bf16[3,384,128]{2,1,0:T(8,128)(2,1)S(1)}, u32[]{:S(2)}, u32[]{:S(2)}) collective-permute-start(bf16[3,384,128]{2,1,0:T(8,128)(2,1)S(1)} %get-tuple-element.30), channel_id=1, source_target_pairs={{4,8},{5,24},{6,10},{7,26},{8,4},{9,20},{10,6},{11,22},{12,0},{13,... | collective-permute-start | bytes 884744 | tf_op jit(solution)/shard_map/ppermute | solution.py:522
  23.1 0.8 %collective-permute-start.3 = (bf16[3,384,128]{2,1,0:T(8,128)(2,1)S(1)}, bf16[3,384,128]{2,1,0:T(8,128)(2,1)S(1)}, u32[]{:S(2)}, u32[]{:S(2)}) collective-permute-start(bf16[3,384,128]{2,1,0:T(8,128)(2,1)S(1)} %get-tuple-element.27.sent_ref), channel_id=1, source_target_pairs={{1,16},{3,18},{5,20},{7,22},{9,24},{11,26},{16,1},{18,3},{20,5},{2... | collective-permute-start | bytes 884744 | tf_op jit(solution)/shard_map/ppermute | solution.py:522
  23.9 3.3 %collective-permute-done.4.refs_1_ = bf16[3,384,128]{2,1,0:T(8,128)(2,1)S(1)} collective-permute-done((bf16[3,384,128]{2,1,0:T(8,128)(2,1)S(1)}, bf16[3,384,128]{2,1,0:T(8,128)(2,1)S(1)}, u32[]{:S(2)}, u32[]{:S(2)}) %collective-permute-start.4) | collective-permute-done | bytes 294944 | tf_op jit(solution)/shard_map/ppermute | solution.py:522
  27.2 3.5 %collective-permute-done.5.refs_2_ = bf16[3,384,128]{2,1,0:T(8,128)(2,1)S(1)} collective-permute-done((bf16[3,384,128]{2,1,0:T(8,128)(2,1)S(1)}, bf16[3,384,128]{2,1,0:T(8,128)(2,1)S(1)}, u32[]{:S(2)}, u32[]{:S(2)}) %collective-permute-start.5) | collective-permute-done | bytes 294944 | tf_op jit(solution)/shard_map/ppermute | solution.py:522
  30.7 12.1 %collective-permute-done.6.refs_3_ = bf16[3,384,128]{2,1,0:T(8,128)(2,1)S(1)} collective-permute-done((bf16[3,384,128]{2,1,0:T(8,128)(2,1)S(1)}, bf16[3,384,128]{2,1,0:T(8,128)(2,1)S(1)}, u32[]{:S(2)}, u32[]{:S(2)}) %collective-permute-start.6) | collective-permute-done | bytes 294944 | tf_op jit(solution)/shard_map/ppermute | solution.py:522
  42.8 1.0 %shard_map.106 = bf16[4,2,384,128]{3,2,1,0:T(8,128)(2,1)S(1)} custom-call(bf16[3,384,128]{2,1,0:T(8,128)(2,1)S(1)} %get-tuple-element.27.sent_ref, bf16[3,384,128]{2,1,0:T(8,128)(2,1)S(1)} %collective-permute-done.3.refs_0_, bf16[3,384,128]{2,1,0:T(8,128)(2,1)S(1)} %collective-permute-done.4.refs_1_, ...), custom_call_target="tpu_custom_call" | custom-call | tf_op jit(solution)/shard_map/pallas_call | solution.py:230
  43.9 0.1 collective-permute-start.7
  44.0 2.2 %collective-permute-done.7.refs_4_ = bf16[4,2,384,128]{3,2,1,0:T(8,128)(2,1)S(1)} collective-permute-done((bf16[4,2,384,128]{3,2,1,0:T(8,128)(2,1)S(1)}, bf16[4,2,384,128]{3,2,1,0:T(8,128)(2,1)S(1)}, u32[]{:S(2)}, u32[]{:S(2)}) %collective-permute-start.7) | collective-permute-done | bytes 786464 | tf_op jit(solution)/shard_map/ppermute | solution.py:523
  46.2 10.3 %shard_map.107 = (bf16[384,128]{1,0:T(8,128)(2,1)S(1)}, bf16[384,128]{1,0:T(8,128)(2,1)S(1)}, bf16[384,128]{1,0:T(8,128)(2,1)S(1)}, bf16[384,128]{1,0:T(8,128)(2,1)S(1)}) custom-call(s32[5]{0:T(128)S(1)} %copy-done.4, bf16[3,384,128]{2,1,0:T(8,128)(2,1)S(1)} %get-tuple-element.27.sent_ref, bf16[3,384,128]{2,1,0:T(8,128)(2,1)S(1)} %collective-permute-done.3.refs_0_, ...), custom_call_target="tpu_custom_call" | custom-call | tf_op jit(solution)/shard_map/pallas_call | solution.py:387
  56.5 2.4 %collective-permute-start.9 = (bf16[384,128]{1,0:T(8,128)(2,1)S(1)}, bf16[384,128]{1,0:T(8,128)(2,1)S(1)}, u32[]{:S(2)}, u32[]{:S(2)}) collective-permute-start(bf16[384,128]{1,0:T(8,128)(2,1)S(1)} %get-tuple-element.32), channel_id=1, source_target_pairs={{4,0},{20,1},{6,2},{22,3},{0,4},{16,5},{2,6},{18,7},{8,12},{24,13}... | collective-permute-start | bytes 294920 | tf_op jit(solution)/shard_map/ppermute | solution.py:526
  58.9 1.9 %collective-permute-start.10 = (bf16[384,128]{1,0:T(8,128)(2,1)S(1)}, bf16[384,128]{1,0:T(8,128)(2,1)S(1)}, u32[]{:S(2)}, u32[]{:S(2)}) collective-permute-start(bf16[384,128]{1,0:T(8,128)(2,1)S(1)} %get-tuple-element.33), channel_id=1, source_target_pairs={{8,0},{24,1},{10,2},{26,3},{0,8},{16,9},{2,10},{18,11},{4,12},{20,... | collective-permute-start | bytes 294920 | tf_op jit(solution)/shard_map/ppermute | solution.py:526
  60.8 1.3 %collective-permute-start.11 = (bf16[384,128]{1,0:T(8,128)(2,1)S(1)}, bf16[384,128]{1,0:T(8,128)(2,1)S(1)}, u32[]{:S(2)}, u32[]{:S(2)}) collective-permute-start(bf16[384,128]{1,0:T(8,128)(2,1)S(1)} %get-tuple-element.34), channel_id=1, source_target_pairs={{8,4},{24,5},{10,6},{26,7},{4,8},{20,9},{6,10},{22,11},{0,12},{16,... | collective-permute-start | bytes 294920 | tf_op jit(solution)/shard_map/ppermute | solution.py:526
  62.1 0.7 collective-permute-start.8
  62.8 0.2 collective-permute-done.9.refs_1_
  63.0 3.6 %collective-permute-done.10.refs_2_ = bf16[384,128]{1,0:T(8,128)(2,1)S(1)} collective-permute-done((bf16[384,128]{1,0:T(8,128)(2,1)S(1)}, bf16[384,128]{1,0:T(8,128)(2,1)S(1)}, u32[]{:S(2)}, u32[]{:S(2)}) %collective-permute-start.10) | collective-permute-done | bytes 98336 | tf_op jit(solution)/shard_map/ppermute | solution.py:526
  66.7 0.6 shard_map.108
  67.2 0.5 collective-permute-start.12
  67.7 4.8 %collective-permute-done.12.got_ref = bf16[3,192,128]{2,1,0:T(8,128)(2,1)S(1)} collective-permute-done((bf16[3,192,128]{2,1,0:T(8,128)(2,1)S(1)}, bf16[3,192,128]{2,1,0:T(8,128)(2,1)S(1)}, u32[]{:S(2)}, u32[]{:S(2)}) %collective-permute-start.12) | collective-permute-done | bytes 147488 | tf_op jit(solution)/shard_map/ppermute | solution.py:529
  72.5 0.8 shard_map.109
  73.2 4.7 %collective-permute-start.13 = (bf16[192,768]{1,0:T(8,128)(2,1)S(1)}, bf16[192,768]{1,0:T(8,128)(2,1)S(1)}, u32[]{:S(2)}, u32[]{:S(2)}) collective-permute-start(bf16[192,768]{1,0:T(8,128)(2,1)S(1)} %get-tuple-element.38), channel_id=1, source_target_pairs={{0,1},{1,0},{2,3},{3,2},{4,5},{5,4},{6,7},{7,6},{8,9},{9,8},{10,11... | collective-permute-start | bytes 884744 | tf_op jit(solution)/shard_map/ppermute | solution.py:530
  77.9 1.2 %collective-permute-done.13.theirs = bf16[192,768]{1,0:T(8,128)(2,1)S(1)} collective-permute-done((bf16[192,768]{1,0:T(8,128)(2,1)S(1)}, bf16[192,768]{1,0:T(8,128)(2,1)S(1)}, u32[]{:S(2)}, u32[]{:S(2)}) %collective-permute-start.13) | collective-permute-done | bytes 294944 | tf_op jit(solution)/shard_map/ppermute | solution.py:530
  79.1 0.9 %shard_map.110 = (bf16[192,768]{1,0:T(8,128)(2,1)}, bf16[192,768]{1,0:T(8,128)(2,1)}) custom-call(s32[1]{0:T(128)S(6)} %copy.11.timestep_ref, f32[192,768]{1,0:T(8,128)S(1)} %get-tuple-element.37.mine, bf16[192,768]{1,0:T(8,128)(2,1)S(1)} %collective-permute-done.13.theirs, bf16[192,768]{1,0:T(8,128)(2,1)S(1)} %copy-done.2, ...), custom_call_target="tpu_custom_call" | custom-call | tf_op jit(solution)/shard_map/pallas_call | solution.py:492
  (15 shorter events, 0.1 us)
Async XLA Ops:
  0.6 3.9 %collective-permute-start.1 = (bf16[192,768]{1,0:T(8,128)(2,1)}, bf16[192,768]{1,0:T(8,128)(2,1)S(1)}, u32[]{:S(2)}, u32[]{:S(2)}) collective-permute-start(bf16[192,768]{1,0:T(8,128)(2,1)} %tokens.1), channel_id=1, source_target_pairs={{0,1},{1,0},{2,3},{3,2},{4,5},{5,4},{6,7},{7,6},{8,9},{9,8},{10,11... | collective-permute-start | bytes 884744 | tf_op jit(solution)/shard_map/ppermute | solution.py:511
  1.1 10.4 %collective-permute-start = (bf16[192,768]{1,0:T(8,128)(2,1)}, bf16[192,768]{1,0:T(8,128)(2,1)S(1)}, u32[]{:S(2)}, u32[]{:S(2)}) collective-permute-start(bf16[192,768]{1,0:T(8,128)(2,1)} %tokens.1), channel_id=1, source_target_pairs={{0,2},{2,0},{4,6},{6,4},{8,10},{10,8},{12,14},{14,12},{16,18},{18,... | collective-permute-start | bytes 884744 | tf_op jit(solution)/shard_map/ppermute | solution.py:510
  4.5 1.0 %copy-start.1 = (bf16[192,768]{1,0:T(8,128)(2,1)S(1)}, bf16[192,768]{1,0:T(8,128)(2,1)}, u32[]{:S(2)}) copy-start(bf16[192,768]{1,0:T(8,128)(2,1)} %tokens.1) | copy-start | bytes 884740
  5.5 0.7 copy-start.3
  11.5 34.7 %copy-start.4 = (s32[5]{0:T(128)S(1)}, s32[5]{0:T(128)}, u32[]{:S(2)}) copy-start(s32[5]{0:T(128)} %lengths_ref.1) | copy-start | bytes 64
  11.5 1.6 %collective-permute-start.2 = (bf16[192,768]{1,0:T(8,128)(2,1)S(1)}, bf16[192,768]{1,0:T(8,128)(2,1)S(1)}, u32[]{:S(2)}, u32[]{:S(2)}) collective-permute-start(bf16[192,768]{1,0:T(8,128)(2,1)S(1)} %collective-permute-done.near_ref), channel_id=1, source_target_pairs={{0,1},{1,0},{2,3},{3,2},{4,5},{5,4},{6,7},{7,6},{8,9},{9,8},{10,11... | collective-permute-start | bytes 884744 | tf_op jit(solution)/shard_map/ppermute | solution.py:520
  16.1 11.1 %collective-permute-start.4 = (bf16[3,384,128]{2,1,0:T(8,128)(2,1)S(1)}, bf16[3,384,128]{2,1,0:T(8,128)(2,1)S(1)}, u32[]{:S(2)}, u32[]{:S(2)}) collective-permute-start(bf16[3,384,128]{2,1,0:T(8,128)(2,1)S(1)} %get-tuple-element.28), channel_id=1, source_target_pairs={{0,4},{1,20},{2,6},{3,22},{4,0},{5,16},{6,2},{7,18},{12,8},{13,24}... | collective-permute-start | bytes 884744 | tf_op jit(solution)/shard_map/ppermute | solution.py:522
  19.8 10.9 %collective-permute-start.5 = (bf16[3,384,128]{2,1,0:T(8,128)(2,1)S(1)}, bf16[3,384,128]{2,1,0:T(8,128)(2,1)S(1)}, u32[]{:S(2)}, u32[]{:S(2)}) collective-permute-start(bf16[3,384,128]{2,1,0:T(8,128)(2,1)S(1)} %get-tuple-element.29), channel_id=1, source_target_pairs={{0,8},{1,24},{2,10},{3,26},{8,0},{9,16},{10,2},{11,18},{12,4},{13,... | collective-permute-start | bytes 884744 | tf_op jit(solution)/shard_map/ppermute | solution.py:522
  21.8 21.0 %collective-permute-start.6 = (bf16[3,384,128]{2,1,0:T(8,128)(2,1)S(1)}, bf16[3,384,128]{2,1,0:T(8,128)(2,1)S(1)}, u32[]{:S(2)}, u32[]{:S(2)}) collective-permute-start(bf16[3,384,128]{2,1,0:T(8,128)(2,1)S(1)} %get-tuple-element.30), channel_id=1, source_target_pairs={{4,8},{5,24},{6,10},{7,26},{8,4},{9,20},{10,6},{11,22},{12,0},{13,... | collective-permute-start | bytes 884744 | tf_op jit(solution)/shard_map/ppermute | solution.py:522
  23.1 49.4 %copy-start = (bf16[768,1536]{1,0:T(8,128)(2,1)S(1)}, bf16[768,1536]{1,0:T(8,128)(2,1)}, u32[]{:S(2)}) copy-start(bf16[768,1536]{1,0:T(8,128)(2,1)} %weight.1) | copy-start | bytes 7077892
  23.1 19.7 %collective-permute-start.3 = (bf16[3,384,128]{2,1,0:T(8,128)(2,1)S(1)}, bf16[3,384,128]{2,1,0:T(8,128)(2,1)S(1)}, u32[]{:S(2)}, u32[]{:S(2)}) collective-permute-start(bf16[3,384,128]{2,1,0:T(8,128)(2,1)S(1)} %get-tuple-element.27.sent_ref), channel_id=1, source_target_pairs={{1,16},{3,18},{5,20},{7,22},{9,24},{11,26},{16,1},{18,3},{20,5},{2... | collective-permute-start | bytes 884744 | tf_op jit(solution)/shard_map/ppermute | solution.py:522
  43.9 35.3 %copy-start.2 = (bf16[192,768]{1,0:T(8,128)(2,1)S(1)}, bf16[192,768]{1,0:T(8,128)(2,1)}, u32[]{:S(2)}) copy-start(bf16[192,768]{1,0:T(8,128)(2,1)} %tokens.1) | copy-start | bytes 884740
  43.9 2.4 %collective-permute-start.7 = (bf16[4,2,384,128]{3,2,1,0:T(8,128)(2,1)S(1)}, bf16[4,2,384,128]{3,2,1,0:T(8,128)(2,1)S(1)}, u32[]{:S(2)}, u32[]{:S(2)}) collective-permute-start(bf16[4,2,384,128]{3,2,1,0:T(8,128)(2,1)S(1)} %shard_map.106), channel_id=1, source_target_pairs={{0,1},{1,0},{2,3},{3,2},{4,5},{5,4},{6,7},{7,6},{8,9},{9,8},{10,11... | collective-permute-start | bytes 2359304 | tf_op jit(solution)/shard_map/ppermute | solution.py:523
  56.5 6.5 %collective-permute-start.9 = (bf16[384,128]{1,0:T(8,128)(2,1)S(1)}, bf16[384,128]{1,0:T(8,128)(2,1)S(1)}, u32[]{:S(2)}, u32[]{:S(2)}) collective-permute-start(bf16[384,128]{1,0:T(8,128)(2,1)S(1)} %get-tuple-element.32), channel_id=1, source_target_pairs={{4,0},{20,1},{6,2},{22,3},{0,4},{16,5},{2,6},{18,7},{8,12},{24,13}... | collective-permute-start | bytes 294920 | tf_op jit(solution)/shard_map/ppermute | solution.py:526
  58.9 7.7 %collective-permute-start.10 = (bf16[384,128]{1,0:T(8,128)(2,1)S(1)}, bf16[384,128]{1,0:T(8,128)(2,1)S(1)}, u32[]{:S(2)}, u32[]{:S(2)}) collective-permute-start(bf16[384,128]{1,0:T(8,128)(2,1)S(1)} %get-tuple-element.33), channel_id=1, source_target_pairs={{8,0},{24,1},{10,2},{26,3},{0,8},{16,9},{2,10},{18,11},{4,12},{20,... | collective-permute-start | bytes 294920 | tf_op jit(solution)/shard_map/ppermute | solution.py:526
  60.8 5.8 %collective-permute-start.11 = (bf16[384,128]{1,0:T(8,128)(2,1)S(1)}, bf16[384,128]{1,0:T(8,128)(2,1)S(1)}, u32[]{:S(2)}, u32[]{:S(2)}) collective-permute-start(bf16[384,128]{1,0:T(8,128)(2,1)S(1)} %get-tuple-element.34), channel_id=1, source_target_pairs={{8,4},{24,5},{10,6},{26,7},{4,8},{20,9},{6,10},{22,11},{0,12},{16,... | collective-permute-start | bytes 294920 | tf_op jit(solution)/shard_map/ppermute | solution.py:526
  62.1 4.5 %collective-permute-start.8 = (bf16[384,128]{1,0:T(8,128)(2,1)S(1)}, bf16[384,128]{1,0:T(8,128)(2,1)S(1)}, u32[]{:S(2)}, u32[]{:S(2)}) collective-permute-start(bf16[384,128]{1,0:T(8,128)(2,1)S(1)} %get-tuple-element.31.done_ref), channel_id=1, source_target_pairs={{16,1},{18,3},{20,5},{22,7},{24,9},{26,11},{1,16},{3,18},{5,20},{7... | collective-permute-start | bytes 294920 | tf_op jit(solution)/shard_map/ppermute | solution.py:526
  67.2 5.2 %collective-permute-start.12 = (bf16[3,192,128]{2,1,0:T(8,128)(2,1)S(1)}, bf16[3,192,128]{2,1,0:T(8,128)(2,1)S(1)}, u32[]{:S(2)}, u32[]{:S(2)}) collective-permute-start(bf16[3,192,128]{2,1,0:T(8,128)(2,1)S(1)} %get-tuple-element.36), channel_id=1, source_target_pairs={{0,2},{2,0},{4,6},{6,4},{8,10},{10,8},{12,14},{14,12},{16,18},{18,... | collective-permute-start | bytes 442376 | tf_op jit(solution)/shard_map/ppermute | solution.py:529
  73.2 5.9 %collective-permute-start.13 = (bf16[192,768]{1,0:T(8,128)(2,1)S(1)}, bf16[192,768]{1,0:T(8,128)(2,1)S(1)}, u32[]{:S(2)}, u32[]{:S(2)}) collective-permute-start(bf16[192,768]{1,0:T(8,128)(2,1)S(1)} %get-tuple-element.38), channel_id=1, source_target_pairs={{0,1},{1,0},{2,3},{3,2},{4,5},{5,4},{6,7},{7,6},{8,9},{9,8},{10,11... | collective-permute-start | bytes 884744 | tf_op jit(solution)/shard_map/ppermute | solution.py:530

commit v7 on v6

--- a/solution.py
+++ b/solution.py
@@ -24,12 +24,13 @@
 
 
 def pairs_out(chips, heads, colour):
-    half = chips // 2
+    colours = chips // 4
     pairs = []
     for chip in range(chips):
-        side, slot, x = chip // half, chip % half // 2, chip % 2
+        side, bit, slot = chip // (2 * colours), chip // colours % 2, chip % colours
         for core in range(2):
-            source, target = chip * 2 + core, (core * half + (slot ^ colour) * 2 + x) * 2 + side
+            owner = (2 * side + core) * colours + (slot ^ colour)
+            source, target = chip * 2 + core, owner * 2 + bit
             if (slot ^ colour) < heads and source != target:
                 pairs.append((source, target))
     return pairs
@@ -37,8 +38,11 @@
 
 def place_of(colours):
     chip = lax.axis_index("req")
-    slot = lax.rem(chip // 2, colours)
-    return slot, lax.rem(chip, 2), chip // (2 * colours) == lax.axis_index("tp")
+    return (
+        lax.rem(chip, colours),
+        chip // (2 * colours),
+        lax.rem(chip // colours, 2) == lax.axis_index("tp"),
+    )
 
 
 def any_spec():
@@ -72,16 +76,15 @@
         packed[head, part] = out[:, head * HEAD_DIM:(head + 1) * HEAD_DIM].astype(jnp.bfloat16)
 
 
-def load_weights(load, refs, weights):
+def load_weights(load, refs, weights, side):
     depth, columns = weights.shape[1:]
-    x = lax.rem(lax.axis_index("req"), 2)
     for part, ref in enumerate(refs):
         for cut in range(2):
             here = pl.ds(cut * (depth // 2), depth // 2)
-            load(ref.at[here, pl.ds(pl.multiple_of(x * columns, 128), columns)], weights.at[part, here])
-
-
-def project_kernel(act_ref, block_ref, own_ref, other_ref, time_ref, wq_ref, wk_ref, wv_ref, *rest):
+            load(ref.at[here, pl.ds(pl.multiple_of(side * columns, 128), columns)], weights.at[part, here])
+
+
+def project_kernel(colours, act_ref, block_ref, own_ref, other_ref, time_ref, wq_ref, wk_ref, wv_ref, *rest):
     packed, mod_ref, gate_ref, weights, times, full, normed, sems = rest
     depth = full.shape[1]
     share = own_ref.shape[1]
@@ -96,7 +99,7 @@
     for part in range(2):
         here = pl.ds(part * (freq // 2), freq // 2)
         load(time_ref.at[here, pl.ds(0, 2 * depth)], times.at[here, pl.ds(0, 2 * depth)])
-    load_weights(load, (wq_ref, wk_ref, wv_ref), weights)
+    load_weights(load, (wq_ref, wk_ref, wv_ref), weights, place_of(colours)[1])
     load(
         time_ref.at[:, pl.ds(pl.multiple_of(2 * depth + core * share, 128), share)],
         times.at[:, pl.ds(2 * depth, share)],
@@ -127,14 +130,14 @@
         gate_ref[:, column:column + HEAD_DIM] = modulation(2 * depth + column) + block_ref[2:3, here]
 
 
-def project(act, block_mod, own, other, time_weight, w_query, w_key, w_value):
+def project(act, block_mod, own, other, time_weight, w_query, w_key, w_value, colours):
     rows, share = own.shape
     depth, columns = w_query.shape
     columns = columns // 2
     freq = time_weight.shape[0]
     heads = columns // HEAD_DIM
     return pl.pallas_call(
-        project_kernel,
+        functools.partial(project_kernel, colours),
         in_specs=[vmem_spec()] * 4 + [any_spec()] * 4,
         out_specs=[vmem_spec()] * 3,
         out_shape=[
@@ -157,14 +160,14 @@
 def share_kernel(colours, near_ref, far_ref, mod_ref, mine, wq_ref, wk_ref, wv_ref, *rest):
     outs, (weights, full, normed, packed, load_sems, sems) = rest[:colours], rest[colours:]
     heads, _, rows, _ = mine.shape
+    slot, side, _ = place_of(colours)
     loads = []
 
     def load(source, target):
         loads.append(pltpu.make_async_copy(source, target, load_sems.at[len(loads)]))
         loads[-1].start()
 
-    load_weights(load, (wq_ref, wk_ref, wv_ref), weights)
-    slot, x, _ = place_of(colours)
+    load_weights(load, (wq_ref, wk_ref, wv_ref), weights, side)
 
     def each_copy(source, position, offset, act):
         for head in range(heads):
@@ -174,16 +177,16 @@
                     here = pl.ds(pl.multiple_of(position * rows, 64), rows)
                     act(pltpu.make_async_copy(source.at[head], outs[colour].at[:, here], sems.at[offset + head]))
 
-    each_copy(mine, x, 0, lambda copy: copy.start())
+    each_copy(mine, side, 0, lambda copy: copy.start())
     scaled = standardise(full, near_ref, far_ref)
     normed[...] = (scaled * (1.0 + mod_ref[1:2, :]) + mod_ref[0:1, :]).astype(jnp.bfloat16)
     for part in range(3):
         loads[2 * part].wait()
         loads[2 * part + 1].wait()
         project_part(packed, normed, weights[part], part)
-    each_copy(packed, 1 - x, heads, lambda copy: copy.start())
-    each_copy(mine, x, 0, lambda copy: copy.wait())
-    each_copy(packed, 1 - x, heads, lambda copy: copy.wait())
+    each_copy(packed, 1 - side, heads, lambda copy: copy.start())
+    each_copy(mine, side, 0, lambda copy: copy.wait())
+    each_copy(packed, 1 - side, heads, lambda copy: copy.wait())
 
 
 def project_shared(near, far, mod, mine, w_query, w_key, w_value, colours):
@@ -243,32 +246,43 @@
     query, keys, values, result, top, total, sems, out_sems = refs[2 * colours + 1:]
     rows = sent_ref.shape[1]
     own_rows, all_rows = query.shape[0], keys.shape[0]
-    side = lax.axis_index("tp")
+    bit = lax.axis_index("tp")
     slot, _, own = place_of(colours)
+    quarter = own_rows // 2
+    rows = rows // 2
     front = pl.ds(0, HEAD_DIM)
     videos = lengths_ref.shape[0]
 
-    def at(colour, which):
-        return pl.ds(pl.multiple_of((slot ^ colour) * rows + which * own_rows, 128), rows)
+    def at(colour, side):
+        return pl.ds(pl.multiple_of((slot ^ colour) * rows + side * quarter, 64), rows)
+
+    def at_all(colour, which, side):
+        return pl.ds(pl.multiple_of((slot ^ colour) * rows + (2 * side + which) * quarter, 64), rows)
 
     def each_copy(act):
         for colour in range(colours):
             def load(piece, colour=colour):
-                for part, target in enumerate((
-                    query.at[at(colour, 0), front],
-                    keys.at[at(colour, side), front],
-                    values.at[at(colour, side), front],
-                )):
-                    act(pltpu.make_async_copy(piece.at[part], target, sems.at[5 * colour + part]))
+                for side in range(2):
+                    here = pl.ds(side * rows, rows)
+                    for part, target in enumerate((
+                        query.at[at(colour, side), front],
+                        keys.at[at_all(colour, bit, side), front],
+                        values.at[at_all(colour, bit, side), front],
+                    )):
+                        sem = sems.at[10 * colour + 5 * side + part]
+                        act(pltpu.make_async_copy(piece.at[part, here], target, sem))
 
             if colour:
                 load(pieces[colour])
             else:
                 pl.when(jnp.logical_not(own))(functools.partial(load, pieces[0]))
                 pl.when(own)(functools.partial(load, sent_ref))
-            for part, target in enumerate((keys, values)):
-                target = target.at[at(colour, 1 - side), front]
-                act(pltpu.make_async_copy(swapped.at[colour, part], target, sems.at[5 * colour + 3 + part]))
+            for side in range(2):
+                here = pl.ds(side * rows, rows)
+                for part, target in enumerate((keys, values)):
+                    target = target.at[at_all(colour, 1 - bit, side), front]
+                    sem = sems.at[10 * colour + 5 * side + 3 + part]
+                    act(pltpu.make_async_copy(swapped.at[colour, part, here], target, sem))
 
     @pl.when(slot < heads)
     def _():
@@ -286,13 +300,16 @@
             lane_stop = jnp.where(lane == video, stop, lane_stop)
         place = lax.broadcasted_iota(jnp.int32, (HEAD_DIM, HEAD_DIM), 0)
 
+        def token_of(local):
+            return local + jnp.where(local < quarter, bit, bit + 1) * quarter
+
         def inside(first):
             index = first + place
             return (index >= lane_start) & (index < lane_stop)
 
         def fill_query(block, carry):
             local = pl.multiple_of(block * HEAD_DIM, HEAD_DIM)
-            member = inside(side * own_rows + local)
+            member = inside(token_of(local))
             query[pl.ds(local, HEAD_DIM), HEAD_DIM:] = jnp.where(member, 1.0, 0.0).astype(jnp.bfloat16)
             return carry
 
@@ -310,7 +327,7 @@
 
         def query_block(block, carry):
             local = pl.multiple_of(block * QUERY_BLOCK, QUERY_BLOCK)
-            first = side * own_rows + local
+            first = token_of(local)
             last = first + QUERY_BLOCK - 1
             low, high = jnp.int32(0), jnp.int32(0)
             for start, stop in zip(starts, ends):
@@ -371,8 +388,10 @@
 
         lax.fori_loop(0, own_rows // QUERY_BLOCK, query_block, 0)
         copies = [
-            pltpu.make_async_copy(result.at[at(colour, 0)], outs[colour], out_sems.at[colour])
-            for colour in range(colours)
+            pltpu.make_async_copy(
+                result.at[at(colour, side)], outs[colour].at[pl.ds(side * rows, rows)], out_sems.at[2 * colour + side]
+            )
+            for colour in range(colours) for side in range(2)
         ]
         for copy in copies:
             copy.start()
@@ -396,8 +415,8 @@
             pltpu.VMEM((own, HEAD_DIM), jnp.bfloat16),
             pltpu.VMEM((QUERY_BLOCK, HEAD_DIM), jnp.float32),
             pltpu.VMEM((QUERY_BLOCK, 2 * HEAD_DIM), jnp.float32),
-            pltpu.SemaphoreType.DMA((5 * colours,)),
-            pltpu.SemaphoreType.DMA((colours,)),
+            pltpu.SemaphoreType.DMA((10 * colours,)),
+            pltpu.SemaphoreType.DMA((2 * colours,)),
         ],
         compiler_params=pltpu.CompilerParams(vmem_limit_bytes=VMEM_LIMIT),
     )(lengths, sent, *pieces, swapped)
@@ -406,11 +425,11 @@
 def part_kernel(colours, done_ref, *refs):
     pieces, (keep, give, sems) = refs[:colours], refs[colours:]
     heads, rows, _ = keep.shape
-    slot, x, own = place_of(colours)
+    slot, own_side, own = place_of(colours)
 
     def each_copy(act):
         for head in range(heads):
-            for number, (target, position) in enumerate(((give, 1 - x), (keep, x))):
+            for number, (target, position) in enumerate(((give, 1 - own_side), (keep, own_side))):
                 here = pl.ds(pl.multiple_of(position * rows, 64), rows)
 
                 def move(piece, head=head, number=number, target=target, here=here):
@@ -441,14 +460,14 @@
     )(done, *pieces)
 
 
-def combine_kernel(keep_ref, got_ref, weight, mine, theirs, attended, sems):
+def combine_kernel(colours, keep_ref, got_ref, weight, mine, theirs, attended, sems):
     share = mine.shape[1]
     heads = keep_ref.shape[0]
     core = lax.axis_index("tp")
-    x = lax.rem(lax.axis_index("req"), 2)
+    side = place_of(colours)[1]
     copies = []
     for head in range(heads):
-        for source, which in ((keep_ref, x), (got_ref, 1 - x)):
+        for source, which in ((keep_ref, side), (got_ref, 1 - side)):
             columns = pl.ds(pl.multiple_of((which * heads + head) * HEAD_DIM, HEAD_DIM), HEAD_DIM)
             copies.append(pltpu.make_async_copy(source.at[head], attended.at[:, columns], sems.at[len(copies)]))
             copies[-1].start()
@@ -460,11 +479,11 @@
         out[...] = jnp.dot(left, weight[:, columns], preferred_element_type=jnp.float32).astype(out.dtype)
 
 
-def combine(keep, got, w_out):
+def combine(keep, got, w_out, colours):
     heads, rows, _ = keep.shape
     depth, width = w_out.shape
     return pl.pallas_call(
-        combine_kernel,
+        functools.partial(combine_kernel, colours),
         in_specs=[any_spec()] * 2 + [vmem_spec()],
         out_specs=[vmem_spec(), vmem_spec()],
         out_shape=[
@@ -502,7 +521,7 @@
     chips = mesh.shape["req"]
     colours = chips // 4
     swap = [(0, 1), (1, 0)]
-    cross = [(chip, chip ^ 1) for chip in range(chips)]
+    cross = [(chip, (chip + chips // 2) % chips) for chip in range(chips)]
 
     def on_device(tokens, video_lengths, timestep, time_weight, block_mod, w_query, w_key, w_value, w_out):
         heads = w_query.shape[1] // HEAD_DIM // 2
@@ -515,7 +534,7 @@
         frequency = jnp.exp(-math.log(10000.0) * jnp.arange(half_freq, dtype=jnp.float32) / half_freq)
         angle = 1000.0 * sigma * frequency
         act = jax.nn.silu(jnp.concatenate([jnp.cos(angle), jnp.sin(angle)]))[None, :]
-        mine, mod, gate = project(act, block_mod, tokens, other, time_weight, w_query, w_key, w_value)
+        mine, mod, gate = project(act, block_mod, tokens, other, time_weight, w_query, w_key, w_value, colours)
         near, mine, mod, gate = lax.optimization_barrier((near, mine, mod, gate))
         far = lax.ppermute(near, "tp", swap)
         sent = project_shared(near, far, mod, mine, w_query, w_key, w_value, colours)
@@ -526,7 +545,7 @@
             lax.ppermute(piece, ("req", "tp"), [(b, a) for a, b in route]) for piece, route in zip(done, routes)
         ]
         keep, give = part(done[0], back, heads)
-        mine, theirs = combine(keep, lax.ppermute(give, "req", cross), w_out)
+        mine, theirs = combine(keep, lax.ppermute(give, "req", cross), w_out, colours)
         theirs = lax.ppermute(theirs, "tp", swap)
         velocity, stepped = finish(timestep, mine, theirs, tokens, gate)
         return (velocity, stepped)

time: 80.3 us -> 84.1 us (1.047)
  starting transfers between devices: 22.3 us -> 27.1 us
  Pallas kernels: 20.6 us -> 19.3 us
    ppermute x1, waiting for transfers between devices: 1.25 us -> 7.69 us  [on_device(): near = lax.ppermute(tokens, 'req', cross)]
    ppermute x4, waiting for transfers between devices: 18.9 us -> 14 us  [on_device(): lax.ppermute(piece, ('req', 'tp'), route)]
    ppermute x1, starting transfers between devices: 4.7 us -> 7.52 us  [on_device(): theirs = lax.ppermute(theirs, 'tp', swap)]
    pallas_call x1, Pallas kernels: 10.3 us -> 9 us  [attend(): pl.pallas_call(functools.partial(attend_kernel, colours, heads), in_specs...]
    ppermute x4, waiting for transfers between devices: 3.83 us -> 2.61 us  [on_device(): lax.ppermute(piece, ('req', 'tp'), [(b, a) for a, b in route])]
    ppermute x1, starting transfers between devices: 0.45 us -> 1.57 us  [on_device(): lax.ppermute(give, 'req', cross)]
    ppermute x1, starting transfers between devices: 2.57 us -> 3.66 us  [on_device(): near = lax.ppermute(tokens, 'req', cross)]
  transfers between devices with their start and end apart: 14 -> 14, of which waited for: 10 -> 9; matrix products, arithmetic and copies ran while one was open for 0% -> 0% of each run, Pallas kernels for 5% -> 5%
where the time goes in v7:
time: 84.1 us; the launch traced here: 83.7 us
  waiting for transfers between devices  34 us (40%)
  starting transfers between devices  27.1 us (32%)
  Pallas kernels  19.3 us (23%)
  local copies, waits for them, and re-layouts  1.71 us (2%)
  between operations  1.5 us (2%)
    ppermute x4, waiting for transfers between devices, on_device(): lax.ppermute(piece, ('req', 'tp'), route)  14 us
    pallas_call x1, Pallas kernels, attend(): pl.pallas_call(functools.partial(attend_kernel, colours, heads), in_specs...  9 us
    ppermute x1, waiting for transfers between devices, on_device(): near = lax.ppermute(tokens, 'req', cross)  7.69 us
    ppermute x1, starting transfers between devices, on_device(): theirs = lax.ppermute(theirs, 'tp', swap)  7.52 us
    ppermute x4, starting transfers between devices, on_device(): lax.ppermute(piece, ('req', 'tp'), route)  7.48 us
    ppermute x4, starting transfers between devices, on_device(): lax.ppermute(piece, ('req', 'tp'), [(b, a) for a, b in route])  6.27 us
    ppermute x1, waiting for transfers between devices, on_device(): lax.ppermute(give, 'req', cross)  4.64 us
    pallas_call x1, Pallas kernels, project(): pl.pallas_call(functools.partial(project_kernel, colours), in_specs=[vmem...  3.95 us
  transfers between devices with their start and end apart: 14, of which 9 were waited for; matrix products, arithmetic and copies ran while one was open for 0% of the time, Pallas kernels for 5%

profile of v7, /device:TPU:0, one launch (start us, length us, event | category | flops | bytes accessed | tf_op | source)
XLA Modules:
  0.0 83.7 jit_solution(1823347617535135375)
XLA Ops:
  0.6 0.5 collective-permute-start.1
  1.1 3.7 %collective-permute-start = (bf16[192,768]{1,0:T(8,128)(2,1)}, bf16[192,768]{1,0:T(8,128)(2,1)S(1)}, u32[]{:S(2)}, u32[]{:S(2)}) collective-permute-start(bf16[192,768]{1,0:T(8,128)(2,1)} %tokens.1), channel_id=1, source_target_pairs={{0,16},{2,18},{4,20},{6,22},{8,24},{10,26},{12,28},{14,30},{16,0},... | collective-permute-start | bytes 884744 | tf_op jit(solution)/shard_map/ppermute | solution.py:529
  5.6 1.0 %copy-done.1 = bf16[192,768]{1,0:T(8,128)(2,1)S(1)} copy-done((bf16[192,768]{1,0:T(8,128)(2,1)S(1)}, bf16[192,768]{1,0:T(8,128)(2,1)}, u32[]{:S(2)}) %copy-start.1) | copy-done | bytes 294936
  6.6 0.7 copy-done.3
  7.3 4.0 %shard_map.104 = (bf16[3,3,192,128]{3,2,1,0:T(8,128)(2,1)S(1)}, f32[2,1536]{1,0:T(2,128)S(1)}, f32[1,768]{1,0:T(1,128)S(1)}) custom-call(f32[1,256]{1,0:T(1,128)S(1)} %divide_multiply_fusion.act_ref, f32[3,1536]{1,0:T(4,128)S(1)} %copy-done.3, bf16[192,768]{1,0:T(8,128)(2,1)S(1)} %copy-done.1, bf16[192,768]{1,0:T(8,128)(2,1)S(1)} %collective-permute-done.1.other_ref, ...), custom_call_target="tpu_custom_call" | custom-call | flops 679477248 | bytes 8388608 | tf_op jit(solution)/shard_map/pallas_call | solution.py:139
  11.3 7.7 %collective-permute-done.near_ref = bf16[192,768]{1,0:T(8,128)(2,1)S(1)} collective-permute-done((bf16[192,768]{1,0:T(8,128)(2,1)}, bf16[192,768]{1,0:T(8,128)(2,1)S(1)}, u32[]{:S(2)}, u32[]{:S(2)}) %collective-permute-start) | collective-permute-done | bytes 294944 | tf_op jit(solution)/shard_map/ppermute | solution.py:529
  18.9 1.6 %collective-permute-done.2.far_ref = bf16[192,768]{1,0:T(8,128)(2,1)S(1)} collective-permute-done((bf16[192,768]{1,0:T(8,128)(2,1)S(1)}, bf16[192,768]{1,0:T(8,128)(2,1)S(1)}, u32[]{:S(2)}, u32[]{:S(2)}) %collective-permute-start.2) | collective-permute-done | bytes 294944 | tf_op jit(solution)/shard_map/ppermute | solution.py:539
  20.5 3.0 %shard_map.105 = (bf16[3,384,128]{2,1,0:T(8,128)(2,1)S(1)}, bf16[3,384,128]{2,1,0:T(8,128)(2,1)S(1)}, bf16[3,384,128]{2,1,0:T(8,128)(2,1)S(1)}, bf16[3,384,128]{2,1,0:T(8,128)(2,1)S(1)}) custom-call(bf16[192,768]{1,0:T(8,128)(2,1)S(1)} %collective-permute-done.near_ref, bf16[192,768]{1,0:T(8,128)(2,1)S(1)} %collective-permute-done.2.far_ref, ...), custom_call_target="tpu_custom_call" | custom-call | tf_op jit(solution)/shard_map/pallas_call | solution.py:195
  23.6 3.5 %collective-permute-start.4 = (bf16[3,384,128]{2,1,0:T(8,128)(2,1)S(1)}, bf16[3,384,128]{2,1,0:T(8,128)(2,1)S(1)}, u32[]{:S(2)}, u32[]{:S(2)}) collective-permute-start(bf16[3,384,128]{2,1,0:T(8,128)(2,1)S(1)} %get-tuple-element.28), channel_id=1, source_target_pairs={{0,2},{1,10},{2,0},{3,8},{6,4},{7,12},{8,3},{9,11},{10,1},{11,9},{... | collective-permute-start | bytes 884744 | tf_op jit(solution)/shard_map/ppermute | solution.py:541
  27.0 1.9 %collective-permute-start.5 = (bf16[3,384,128]{2,1,0:T(8,128)(2,1)S(1)}, bf16[3,384,128]{2,1,0:T(8,128)(2,1)S(1)}, u32[]{:S(2)}, u32[]{:S(2)}) collective-permute-start(bf16[3,384,128]{2,1,0:T(8,128)(2,1)S(1)} %get-tuple-element.29), channel_id=1, source_target_pairs={{0,4},{1,12},{4,0},{5,8},{6,2},{7,10},{8,5},{9,13},{12,1},{13,9},{... | collective-permute-start | bytes 884744 | tf_op jit(solution)/shard_map/ppermute | solution.py:541
  29.0 1.3 %collective-permute-start.6 = (bf16[3,384,128]{2,1,0:T(8,128)(2,1)S(1)}, bf16[3,384,128]{2,1,0:T(8,128)(2,1)S(1)}, u32[]{:S(2)}, u32[]{:S(2)}) collective-permute-start(bf16[3,384,128]{2,1,0:T(8,128)(2,1)S(1)} %get-tuple-element.30), channel_id=1, source_target_pairs={{2,4},{3,12},{4,2},{5,10},{6,0},{7,8},{10,5},{11,13},{12,3},{13,11... | collective-permute-start | bytes 884744 | tf_op jit(solution)/shard_map/ppermute | solution.py:541
  30.3 0.8 collective-permute-start.3
  31.1 4.2 %collective-permute-done.4.refs_1_ = bf16[3,384,128]{2,1,0:T(8,128)(2,1)S(1)} collective-permute-done((bf16[3,384,128]{2,1,0:T(8,128)(2,1)S(1)}, bf16[3,384,128]{2,1,0:T(8,128)(2,1)S(1)}, u32[]{:S(2)}, u32[]{:S(2)}) %collective-permute-start.4) | collective-permute-done | bytes 294944 | tf_op jit(solution)/shard_map/ppermute | solution.py:541
  35.4 9.8 %collective-permute-done.5.refs_2_ = bf16[3,384,128]{2,1,0:T(8,128)(2,1)S(1)} collective-permute-done((bf16[3,384,128]{2,1,0:T(8,128)(2,1)S(1)}, bf16[3,384,128]{2,1,0:T(8,128)(2,1)S(1)}, u32[]{:S(2)}, u32[]{:S(2)}) %collective-permute-start.5) | collective-permute-done | bytes 294944 | tf_op jit(solution)/shard_map/ppermute | solution.py:541
  45.1 1.1 %shard_map.106 = bf16[4,2,384,128]{3,2,1,0:T(8,128)(2,1)S(1)} custom-call(bf16[3,384,128]{2,1,0:T(8,128)(2,1)S(1)} %get-tuple-element.27.sent_ref, bf16[3,384,128]{2,1,0:T(8,128)(2,1)S(1)} %collective-permute-done.3.refs_0_, bf16[3,384,128]{2,1,0:T(8,128)(2,1)S(1)} %collective-permute-done.4.refs_1_, ...), custom_call_target="tpu_custom_call" | custom-call | tf_op jit(solution)/shard_map/pallas_call | solution.py:233
  46.2 0.0 copy-start.2
  46.2 0.1 collective-permute-start.7
  46.3 2.3 %collective-permute-done.7.refs_4_ = bf16[4,2,384,128]{3,2,1,0:T(8,128)(2,1)S(1)} collective-permute-done((bf16[4,2,384,128]{3,2,1,0:T(8,128)(2,1)S(1)}, bf16[4,2,384,128]{3,2,1,0:T(8,128)(2,1)S(1)}, u32[]{:S(2)}, u32[]{:S(2)}) %collective-permute-start.7) | collective-permute-done | bytes 786464 | tf_op jit(solution)/shard_map/ppermute | solution.py:542
  48.6 9.0 %shard_map.107 = (bf16[384,128]{1,0:T(8,128)(2,1)S(1)}, bf16[384,128]{1,0:T(8,128)(2,1)S(1)}, bf16[384,128]{1,0:T(8,128)(2,1)S(1)}, bf16[384,128]{1,0:T(8,128)(2,1)S(1)}) custom-call(s32[5]{0:T(128)S(1)} %copy-done.4, bf16[3,384,128]{2,1,0:T(8,128)(2,1)S(1)} %get-tuple-element.27.sent_ref, bf16[3,384,128]{2,1,0:T(8,128)(2,1)S(1)} %collective-permute-done.3.refs_0_, ...), custom_call_target="tpu_custom_call" | custom-call | tf_op jit(solution)/shard_map/pallas_call | solution.py:406
  57.6 2.4 %collective-permute-start.9 = (bf16[384,128]{1,0:T(8,128)(2,1)S(1)}, bf16[384,128]{1,0:T(8,128)(2,1)S(1)}, u32[]{:S(2)}, u32[]{:S(2)}) collective-permute-start(bf16[384,128]{1,0:T(8,128)(2,1)S(1)} %get-tuple-element.32), channel_id=1, source_target_pairs={{2,0},{10,1},{0,2},{8,3},{4,6},{12,7},{3,8},{11,9},{1,10},{9,11},{... | collective-permute-start | bytes 294920 | tf_op jit(solution)/shard_map/ppermute | solution.py:545
  60.0 1.9 %collective-permute-start.10 = (bf16[384,128]{1,0:T(8,128)(2,1)S(1)}, bf16[384,128]{1,0:T(8,128)(2,1)S(1)}, u32[]{:S(2)}, u32[]{:S(2)}) collective-permute-start(bf16[384,128]{1,0:T(8,128)(2,1)S(1)} %get-tuple-element.33), channel_id=1, source_target_pairs={{4,0},{12,1},{0,4},{8,5},{2,6},{10,7},{5,8},{13,9},{1,12},{9,13},{... | collective-permute-start | bytes 294920 | tf_op jit(solution)/shard_map/ppermute | solution.py:545
  61.9 1.3 %collective-permute-start.11 = (bf16[384,128]{1,0:T(8,128)(2,1)S(1)}, bf16[384,128]{1,0:T(8,128)(2,1)S(1)}, u32[]{:S(2)}, u32[]{:S(2)}) collective-permute-start(bf16[384,128]{1,0:T(8,128)(2,1)S(1)} %get-tuple-element.34), channel_id=1, source_target_pairs={{4,2},{12,3},{2,4},{10,5},{0,6},{8,7},{5,10},{13,11},{3,12},{11,13... | collective-permute-start | bytes 294920 | tf_op jit(solution)/shard_map/ppermute | solution.py:545
  63.2 0.7 collective-permute-start.8
  63.9 0.2 collective-permute-done.9.refs_1_
  64.1 2.4 %collective-permute-done.10.refs_2_ = bf16[384,128]{1,0:T(8,128)(2,1)S(1)} collective-permute-done((bf16[384,128]{1,0:T(8,128)(2,1)S(1)}, bf16[384,128]{1,0:T(8,128)(2,1)S(1)}, u32[]{:S(2)}, u32[]{:S(2)}) %collective-permute-start.10) | collective-permute-done | bytes 98336 | tf_op jit(solution)/shard_map/ppermute | solution.py:545
  66.5 0.6 shard_map.108
  67.1 1.6 %collective-permute-start.12 = (bf16[3,192,128]{2,1,0:T(8,128)(2,1)S(1)}, bf16[3,192,128]{2,1,0:T(8,128)(2,1)S(1)}, u32[]{:S(2)}, u32[]{:S(2)}) collective-permute-start(bf16[3,192,128]{2,1,0:T(8,128)(2,1)S(1)} %get-tuple-element.36), channel_id=1, source_target_pairs={{0,16},{2,18},{4,20},{6,22},{8,24},{10,26},{12,28},{14,30},{16,0},... | collective-permute-start | bytes 442376 | tf_op jit(solution)/shard_map/ppermute | solution.py:548
  68.7 4.6 %collective-permute-done.12.got_ref = bf16[3,192,128]{2,1,0:T(8,128)(2,1)S(1)} collective-permute-done((bf16[3,192,128]{2,1,0:T(8,128)(2,1)S(1)}, bf16[3,192,128]{2,1,0:T(8,128)(2,1)S(1)}, u32[]{:S(2)}, u32[]{:S(2)}) %collective-permute-start.12) | collective-permute-done | bytes 147488 | tf_op jit(solution)/shard_map/ppermute | solution.py:548
  73.3 0.8 shard_map.109
  74.1 7.5 %collective-permute-start.13 = (bf16[192,768]{1,0:T(8,128)(2,1)S(1)}, bf16[192,768]{1,0:T(8,128)(2,1)S(1)}, u32[]{:S(2)}, u32[]{:S(2)}) collective-permute-start(bf16[192,768]{1,0:T(8,128)(2,1)S(1)} %get-tuple-element.38), channel_id=1, source_target_pairs={{0,1},{1,0},{2,3},{3,2},{4,5},{5,4},{6,7},{7,6},{8,9},{9,8},{10,11... | collective-permute-start | bytes 884744 | tf_op jit(solution)/shard_map/ppermute | solution.py:549
  81.6 1.2 %collective-permute-done.13.theirs = bf16[192,768]{1,0:T(8,128)(2,1)S(1)} collective-permute-done((bf16[192,768]{1,0:T(8,128)(2,1)S(1)}, bf16[192,768]{1,0:T(8,128)(2,1)S(1)}, u32[]{:S(2)}, u32[]{:S(2)}) %collective-permute-start.13) | collective-permute-done | bytes 294944 | tf_op jit(solution)/shard_map/ppermute | solution.py:549
  82.8 0.9 %shard_map.110 = (bf16[192,768]{1,0:T(8,128)(2,1)}, bf16[192,768]{1,0:T(8,128)(2,1)}) custom-call(s32[1]{0:T(128)S(6)} %copy.11.timestep_ref, f32[192,768]{1,0:T(8,128)S(1)} %get-tuple-element.37.mine, bf16[192,768]{1,0:T(8,128)(2,1)S(1)} %collective-permute-done.13.theirs, bf16[192,768]{1,0:T(8,128)(2,1)S(1)} %copy-done.2, ...), custom_call_target="tpu_custom_call" | custom-call | tf_op jit(solution)/shard_map/pallas_call | solution.py:511
  (15 shorter events, 0.1 us)
Async XLA Ops:
  0.6 5.0 %collective-permute-start.1 = (bf16[192,768]{1,0:T(8,128)(2,1)}, bf16[192,768]{1,0:T(8,128)(2,1)S(1)}, u32[]{:S(2)}, u32[]{:S(2)}) collective-permute-start(bf16[192,768]{1,0:T(8,128)(2,1)} %tokens.1), channel_id=1, source_target_pairs={{0,1},{1,0},{2,3},{3,2},{4,5},{5,4},{6,7},{7,6},{8,9},{9,8},{10,11... | collective-permute-start | bytes 884744 | tf_op jit(solution)/shard_map/ppermute | solution.py:530
  1.1 17.8 %collective-permute-start = (bf16[192,768]{1,0:T(8,128)(2,1)}, bf16[192,768]{1,0:T(8,128)(2,1)S(1)}, u32[]{:S(2)}, u32[]{:S(2)}) collective-permute-start(bf16[192,768]{1,0:T(8,128)(2,1)} %tokens.1), channel_id=1, source_target_pairs={{0,16},{2,18},{4,20},{6,22},{8,24},{10,26},{12,28},{14,30},{16,0},... | collective-permute-start | bytes 884744 | tf_op jit(solution)/shard_map/ppermute | solution.py:529
  5.6 1.0 %copy-start.1 = (bf16[192,768]{1,0:T(8,128)(2,1)S(1)}, bf16[192,768]{1,0:T(8,128)(2,1)}, u32[]{:S(2)}) copy-start(bf16[192,768]{1,0:T(8,128)(2,1)} %tokens.1) | copy-start | bytes 884740
  6.6 0.7 copy-start.3
  18.9 29.6 %copy-start.4 = (s32[5]{0:T(128)S(1)}, s32[5]{0:T(128)}, u32[]{:S(2)}) copy-start(s32[5]{0:T(128)} %lengths_ref.1) | copy-start | bytes 64
  18.9 1.6 %collective-permute-start.2 = (bf16[192,768]{1,0:T(8,128)(2,1)S(1)}, bf16[192,768]{1,0:T(8,128)(2,1)S(1)}, u32[]{:S(2)}, u32[]{:S(2)}) collective-permute-start(bf16[192,768]{1,0:T(8,128)(2,1)S(1)} %collective-permute-done.near_ref), channel_id=1, source_target_pairs={{0,1},{1,0},{2,3},{3,2},{4,5},{5,4},{6,7},{7,6},{8,9},{9,8},{10,11... | collective-permute-start | bytes 884744 | tf_op jit(solution)/shard_map/ppermute | solution.py:539
  23.6 11.8 %collective-permute-start.4 = (bf16[3,384,128]{2,1,0:T(8,128)(2,1)S(1)}, bf16[3,384,128]{2,1,0:T(8,128)(2,1)S(1)}, u32[]{:S(2)}, u32[]{:S(2)}) collective-permute-start(bf16[3,384,128]{2,1,0:T(8,128)(2,1)S(1)} %get-tuple-element.28), channel_id=1, source_target_pairs={{0,2},{1,10},{2,0},{3,8},{6,4},{7,12},{8,3},{9,11},{10,1},{11,9},{... | collective-permute-start | bytes 884744 | tf_op jit(solution)/shard_map/ppermute | solution.py:541
  27.0 18.1 %collective-permute-start.5 = (bf16[3,384,128]{2,1,0:T(8,128)(2,1)S(1)}, bf16[3,384,128]{2,1,0:T(8,128)(2,1)S(1)}, u32[]{:S(2)}, u32[]{:S(2)}) collective-permute-start(bf16[3,384,128]{2,1,0:T(8,128)(2,1)S(1)} %get-tuple-element.29), channel_id=1, source_target_pairs={{0,4},{1,12},{4,0},{5,8},{6,2},{7,10},{8,5},{9,13},{12,1},{13,9},{... | collective-permute-start | bytes 884744 | tf_op jit(solution)/shard_map/ppermute | solution.py:541
  29.0 16.2 %collective-permute-start.6 = (bf16[3,384,128]{2,1,0:T(8,128)(2,1)S(1)}, bf16[3,384,128]{2,1,0:T(8,128)(2,1)S(1)}, u32[]{:S(2)}, u32[]{:S(2)}) collective-permute-start(bf16[3,384,128]{2,1,0:T(8,128)(2,1)S(1)} %get-tuple-element.30), channel_id=1, source_target_pairs={{2,4},{3,12},{4,2},{5,10},{6,0},{7,8},{10,5},{11,13},{12,3},{13,11... | collective-permute-start | bytes 884744 | tf_op jit(solution)/shard_map/ppermute | solution.py:541
  30.3 43.0 %copy-start = (bf16[768,1536]{1,0:T(8,128)(2,1)S(1)}, bf16[768,1536]{1,0:T(8,128)(2,1)}, u32[]{:S(2)}) copy-start(bf16[768,1536]{1,0:T(8,128)(2,1)} %weight.1) | copy-start | bytes 7077892
  30.3 14.9 %collective-permute-start.3 = (bf16[3,384,128]{2,1,0:T(8,128)(2,1)S(1)}, bf16[3,384,128]{2,1,0:T(8,128)(2,1)S(1)}, u32[]{:S(2)}, u32[]{:S(2)}) collective-permute-start(bf16[3,384,128]{2,1,0:T(8,128)(2,1)S(1)} %get-tuple-element.27.sent_ref), channel_id=1, source_target_pairs={{1,8},{3,10},{5,12},{8,1},{10,3},{12,5},{17,24},{19,26},{21,28},{2... | collective-permute-start | bytes 884744 | tf_op jit(solution)/shard_map/ppermute | solution.py:541
  46.2 36.6 %copy-start.2 = (bf16[192,768]{1,0:T(8,128)(2,1)S(1)}, bf16[192,768]{1,0:T(8,128)(2,1)}, u32[]{:S(2)}) copy-start(bf16[192,768]{1,0:T(8,128)(2,1)} %tokens.1) | copy-start | bytes 884740
  46.2 2.4 %collective-permute-start.7 = (bf16[4,2,384,128]{3,2,1,0:T(8,128)(2,1)S(1)}, bf16[4,2,384,128]{3,2,1,0:T(8,128)(2,1)S(1)}, u32[]{:S(2)}, u32[]{:S(2)}) collective-permute-start(bf16[4,2,384,128]{3,2,1,0:T(8,128)(2,1)S(1)} %shard_map.106), channel_id=1, source_target_pairs={{0,1},{1,0},{2,3},{3,2},{4,5},{5,4},{6,7},{7,6},{8,9},{9,8},{10,11... | collective-permute-start | bytes 2359304 | tf_op jit(solution)/shard_map/ppermute | solution.py:542
  57.6 6.5 %collective-permute-start.9 = (bf16[384,128]{1,0:T(8,128)(2,1)S(1)}, bf16[384,128]{1,0:T(8,128)(2,1)S(1)}, u32[]{:S(2)}, u32[]{:S(2)}) collective-permute-start(bf16[384,128]{1,0:T(8,128)(2,1)S(1)} %get-tuple-element.32), channel_id=1, source_target_pairs={{2,0},{10,1},{0,2},{8,3},{4,6},{12,7},{3,8},{11,9},{1,10},{9,11},{... | collective-permute-start | bytes 294920 | tf_op jit(solution)/shard_map/ppermute | solution.py:545
  60.0 6.5 %collective-permute-start.10 = (bf16[384,128]{1,0:T(8,128)(2,1)S(1)}, bf16[384,128]{1,0:T(8,128)(2,1)S(1)}, u32[]{:S(2)}, u32[]{:S(2)}) collective-permute-start(bf16[384,128]{1,0:T(8,128)(2,1)S(1)} %get-tuple-element.33), channel_id=1, source_target_pairs={{4,0},{12,1},{0,4},{8,5},{2,6},{10,7},{5,8},{13,9},{1,12},{9,13},{... | collective-permute-start | bytes 294920 | tf_op jit(solution)/shard_map/ppermute | solution.py:545
  61.9 4.6 %collective-permute-start.11 = (bf16[384,128]{1,0:T(8,128)(2,1)S(1)}, bf16[384,128]{1,0:T(8,128)(2,1)S(1)}, u32[]{:S(2)}, u32[]{:S(2)}) collective-permute-start(bf16[384,128]{1,0:T(8,128)(2,1)S(1)} %get-tuple-element.34), channel_id=1, source_target_pairs={{4,2},{12,3},{2,4},{10,5},{0,6},{8,7},{5,10},{13,11},{3,12},{11,13... | collective-permute-start | bytes 294920 | tf_op jit(solution)/shard_map/ppermute | solution.py:545
  63.2 3.3 %collective-permute-start.8 = (bf16[384,128]{1,0:T(8,128)(2,1)S(1)}, bf16[384,128]{1,0:T(8,128)(2,1)S(1)}, u32[]{:S(2)}, u32[]{:S(2)}) collective-permute-start(bf16[384,128]{1,0:T(8,128)(2,1)S(1)} %get-tuple-element.31.done_ref), channel_id=1, source_target_pairs={{8,1},{10,3},{12,5},{1,8},{3,10},{5,12},{24,17},{26,19},{28,21},{1... | collective-permute-start | bytes 294920 | tf_op jit(solution)/shard_map/ppermute | solution.py:545
  67.1 6.2 %collective-permute-start.12 = (bf16[3,192,128]{2,1,0:T(8,128)(2,1)S(1)}, bf16[3,192,128]{2,1,0:T(8,128)(2,1)S(1)}, u32[]{:S(2)}, u32[]{:S(2)}) collective-permute-start(bf16[3,192,128]{2,1,0:T(8,128)(2,1)S(1)} %get-tuple-element.36), channel_id=1, source_target_pairs={{0,16},{2,18},{4,20},{6,22},{8,24},{10,26},{12,28},{14,30},{16,0},... | collective-permute-start | bytes 442376 | tf_op jit(solution)/shard_map/ppermute | solution.py:548
  74.1 8.7 %collective-permute-start.13 = (bf16[192,768]{1,0:T(8,128)(2,1)S(1)}, bf16[192,768]{1,0:T(8,128)(2,1)S(1)}, u32[]{:S(2)}, u32[]{:S(2)}) collective-permute-start(bf16[192,768]{1,0:T(8,128)(2,1)S(1)} %get-tuple-element.38), channel_id=1, source_target_pairs={{0,1},{1,0},{2,3},{3,2},{4,5},{5,4},{6,7},{7,6},{8,9},{9,8},{10,11... | collective-permute-start | bytes 884744 | tf_op jit(solution)/shard_map/ppermute | solution.py:549

commit v8 on v6

--- a/solution.py
+++ b/solution.py
@@ -12,7 +12,7 @@
 STEPS = 1000
 QUERY_BLOCK = 384
 KEY_GROUP = 3072
-WINDOWS = (1024, 2048)
+WINDOWS = (512, 1024, 1536, 2048, 2560)
 NEG = -1e30
 STREAM_LIMIT = 51 * 1024 * 1024
 VMEM_LIMIT = 32 * 1024 * 1024
@@ -30,15 +30,14 @@
         side, slot, x = chip // half, chip % half // 2, chip % 2
         for core in range(2):
             source, target = chip * 2 + core, (core * half + (slot ^ colour) * 2 + x) * 2 + side
-            if (slot ^ colour) < heads and source != target:
+            if (slot ^ colour) < heads:
                 pairs.append((source, target))
     return pairs
 
 
 def place_of(colours):
     chip = lax.axis_index("req")
-    slot = lax.rem(chip // 2, colours)
-    return slot, lax.rem(chip, 2), chip // (2 * colours) == lax.axis_index("tp")
+    return lax.rem(chip // 2, colours), lax.rem(chip, 2)
 
 
 def any_spec():
@@ -164,7 +163,7 @@
         loads[-1].start()
 
     load_weights(load, (wq_ref, wk_ref, wv_ref), weights)
-    slot, x, _ = place_of(colours)
+    slot, x = place_of(colours)
 
     def each_copy(source, position, offset, act):
         for head in range(heads):
@@ -206,45 +205,13 @@
     )(near, far, mod, mine, w_query, w_key, w_value)
 
 
-def collect_kernel(colours, sent_ref, *refs):
-    pieces, out, sems = refs[:colours], refs[colours], refs[colours + 1]
-    own = place_of(colours)[2]
-
-    def each_copy(act):
-        for colour, piece in enumerate(pieces):
-            copy = pltpu.make_async_copy(piece.at[pl.ds(1, 2)], out.at[colour], sems.at[colour])
-            if colour:
-                act(copy)
-            else:
-                pl.when(jnp.logical_not(own))(functools.partial(act, copy))
-                local = pltpu.make_async_copy(sent_ref.at[pl.ds(1, 2)], out.at[colour], sems.at[colour])
-                pl.when(own)(functools.partial(act, local))
-
-    each_copy(lambda copy: copy.start())
-    each_copy(lambda copy: copy.wait())
-
-
-def collect(sent, pieces):
-    _, rows, wide = sent.shape
-    colours = len(pieces)
-    return pl.pallas_call(
-        functools.partial(collect_kernel, colours),
-        in_specs=[any_spec()] * (colours + 1),
-        out_specs=any_spec(),
-        out_shape=jax.ShapeDtypeStruct((colours, 2, rows, wide), jnp.bfloat16),
-        scratch_shapes=[pltpu.SemaphoreType.DMA((colours,))],
-        compiler_params=pltpu.CompilerParams(vmem_limit_bytes=VMEM_LIMIT),
-    )(sent, *pieces)
-
-
-def attend_kernel(colours, heads, lengths_ref, sent_ref, *refs):
-    pieces, swapped = refs[:colours], refs[colours]
-    outs = refs[colours + 1:2 * colours + 1]
-    query, keys, values, result, top, total, sems, out_sems = refs[2 * colours + 1:]
-    rows = sent_ref.shape[1]
+def attend_kernel(colours, heads, lengths_ref, *refs):
+    pieces, swapped, outs = refs[:colours], refs[colours:2 * colours], refs[2 * colours:3 * colours]
+    query, keys, values, result, top, total, sems, out_sems = refs[3 * colours:]
+    rows = pieces[0].shape[1]
     own_rows, all_rows = query.shape[0], keys.shape[0]
     side = lax.axis_index("tp")
-    slot, _, own = place_of(colours)
+    slot, _ = place_of(colours)
     front = pl.ds(0, HEAD_DIM)
     videos = lengths_ref.shape[0]
 
@@ -253,22 +220,15 @@
 
     def each_copy(act):
         for colour in range(colours):
-            def load(piece, colour=colour):
-                for part, target in enumerate((
-                    query.at[at(colour, 0), front],
-                    keys.at[at(colour, side), front],
-                    values.at[at(colour, side), front],
-                )):
-                    act(pltpu.make_async_copy(piece.at[part], target, sems.at[5 * colour + part]))
-
-            if colour:
-                load(pieces[colour])
-            else:
-                pl.when(jnp.logical_not(own))(functools.partial(load, pieces[0]))
-                pl.when(own)(functools.partial(load, sent_ref))
-            for part, target in enumerate((keys, values)):
-                target = target.at[at(colour, 1 - side), front]
-                act(pltpu.make_async_copy(swapped.at[colour, part], target, sems.at[5 * colour + 3 + part]))
+            near, far = pieces[colour], swapped[colour]
+            for number, (source, target) in enumerate((
+                (near.at[0], query.at[at(colour, 0), front]),
+                (near.at[1], keys.at[at(colour, side), front]),
+                (near.at[2], values.at[at(colour, side), front]),
+                (far.at[1], keys.at[at(colour, 1 - side), front]),
+                (far.at[2], values.at[at(colour, 1 - side), front]),
+            )):
+                act(pltpu.make_async_copy(source, target, sems.at[5 * colour + number]))
 
     @pl.when(slot < heads)
     def _():
@@ -308,6 +268,8 @@
         lax.fori_loop(0, all_rows // HEAD_DIM, fill_keys, 0)
         each_copy(lambda copy: copy.wait())
 
+        sub = QUERY_BLOCK // 2
+
         def query_block(block, carry):
             local = pl.multiple_of(block * QUERY_BLOCK, QUERY_BLOCK)
             first = side * own_rows + local
@@ -318,35 +280,39 @@
                 high = jnp.where(last >= start, stop, high)
             low = low // HEAD_DIM * HEAD_DIM
 
-            def scores(begin, count):
+            def scores(offset, begin, count):
+                q = query[pl.ds(pl.multiple_of(local + offset, 64), sub), :]
                 score = lax.dot_general(
-                    query[pl.ds(local, QUERY_BLOCK), :], keys[pl.ds(begin, count), :], (((1,), (1,)), ((), ())),
-                    preferred_element_type=jnp.float32,
+                    q, keys[pl.ds(begin, count), :], (((1,), (1,)), ((), ())), preferred_element_type=jnp.float32
                 )
                 tiles = [score[:, j:j + HEAD_DIM] for j in range(0, count, HEAD_DIM)]
                 most = jnp.max(functools.reduce(jnp.maximum, tiles), axis=1, keepdims=True)
-                return tiles, jnp.broadcast_to(most, (QUERY_BLOCK, HEAD_DIM))
+                return tiles, jnp.broadcast_to(most, (sub, HEAD_DIM))
 
             def weigh(begin, count, tiles, now):
                 probs = jnp.concatenate([jnp.exp2(tile - now).astype(jnp.bfloat16) for tile in tiles], axis=1)
                 return jnp.dot(probs, values[pl.ds(begin, count), :], preferred_element_type=jnp.float32)
 
-            def store(update):
+            def store(offset, update):
                 out = update[:, :HEAD_DIM] / update[:, HEAD_DIM:]
-                result[pl.ds(local, QUERY_BLOCK), :] = out.astype(jnp.bfloat16)
+                result[pl.ds(pl.multiple_of(local + offset, 64), sub), :] = out.astype(jnp.bfloat16)
 
             def window(count):
                 begin = pl.multiple_of(jnp.minimum(low, all_rows - count), HEAD_DIM)
-                tiles, now = scores(begin, count)
-                store(weigh(begin, count, tiles, now))
-
-            def long():
+                tiles, now = scores(0, begin, count)
+                for offset in range(0, QUERY_BLOCK, sub):
+                    later = scores(offset + sub, begin, count) if offset + sub < QUERY_BLOCK else None
+                    store(offset, weigh(begin, count, tiles, now))
+                    if later is not None:
+                        tiles, now = later
+
+            def long(offset):
                 top[...] = jnp.full(top.shape, 2 * NEG, jnp.float32)
                 total[...] = jnp.zeros(total.shape, jnp.float32)
 
                 def key_block(number, carry):
                     begin = pl.multiple_of(number * KEY_GROUP, KEY_GROUP)
-                    tiles, most = scores(begin, KEY_GROUP)
+                    tiles, most = scores(offset, begin, KEY_GROUP)
                     before = top[...]
                     now = jnp.maximum(before, most)
                     update = weigh(begin, KEY_GROUP, tiles, now)
@@ -357,16 +323,22 @@
                     return carry
 
                 lax.fori_loop(low // KEY_GROUP, (high + KEY_GROUP - 1) // KEY_GROUP, key_block, 0)
-                store(total)
+                store(offset, total)
 
             need = high - low
-            small, middle = WINDOWS
-            pl.when(need <= small)(lambda: window(small))
-            pl.when((need > small) & (need <= middle))(lambda: window(middle))
-            if all_rows == KEY_GROUP:
-                pl.when(need > middle)(lambda: window(KEY_GROUP))
-            else:
-                pl.when(need > middle)(long)
+            floor = 0
+            for count in WINDOWS:
+                pl.when((need > floor) & (need <= count))(functools.partial(window, count))
+                floor = count
+
+            @pl.when(need > floor)
+            def _():
+                if all_rows == KEY_GROUP:
+                    window(KEY_GROUP)
+                else:
+                    for offset in range(0, QUERY_BLOCK, sub):
+                        long(offset)
+
             return carry
 
         lax.fori_loop(0, own_rows // QUERY_BLOCK, query_block, 0)
@@ -380,13 +352,13 @@
             copy.wait()
 
 
-def attend(lengths, sent, pieces, swapped, heads):
-    rows = sent.shape[1]
+def attend(lengths, pieces, swapped, heads):
+    rows = pieces[0].shape[1]
     colours = len(pieces)
     own = colours * rows
     return pl.pallas_call(
         functools.partial(attend_kernel, colours, heads),
-        in_specs=[smem_spec()] + [any_spec()] * (colours + 2),
+        in_specs=[smem_spec()] + [any_spec()] * (2 * colours),
         out_specs=[any_spec()] * colours,
         out_shape=[jax.ShapeDtypeStruct((rows, HEAD_DIM), jnp.bfloat16)] * colours,
         scratch_shapes=[
@@ -394,51 +366,45 @@
             pltpu.VMEM((2 * own, 2 * HEAD_DIM), jnp.bfloat16),
             pltpu.VMEM((2 * own, 2 * HEAD_DIM), jnp.bfloat16),
             pltpu.VMEM((own, HEAD_DIM), jnp.bfloat16),
-            pltpu.VMEM((QUERY_BLOCK, HEAD_DIM), jnp.float32),
-            pltpu.VMEM((QUERY_BLOCK, 2 * HEAD_DIM), jnp.float32),
+            pltpu.VMEM((QUERY_BLOCK // 2, HEAD_DIM), jnp.float32),
+            pltpu.VMEM((QUERY_BLOCK // 2, 2 * HEAD_DIM), jnp.float32),
             pltpu.SemaphoreType.DMA((5 * colours,)),
             pltpu.SemaphoreType.DMA((colours,)),
         ],
         compiler_params=pltpu.CompilerParams(vmem_limit_bytes=VMEM_LIMIT),
-    )(lengths, sent, *pieces, swapped)
-
-
-def part_kernel(colours, done_ref, *refs):
+    )(lengths, *pieces, *swapped)
+
+
+def part_kernel(colours, *refs):
     pieces, (keep, give, sems) = refs[:colours], refs[colours:]
     heads, rows, _ = keep.shape
-    slot, x, own = place_of(colours)
+    slot, x = place_of(colours)
 
     def each_copy(act):
         for head in range(heads):
             for number, (target, position) in enumerate(((give, 1 - x), (keep, x))):
                 here = pl.ds(pl.multiple_of(position * rows, 64), rows)
-
-                def move(piece, head=head, number=number, target=target, here=here):
-                    act(pltpu.make_async_copy(piece.at[here], target.at[head], sems.at[2 * head + number]))
-
                 for colour in range(colours):
-                    right = (slot ^ colour) == head
-                    if colour:
-                        pl.when(right)(functools.partial(move, pieces[colour]))
-                    else:
-                        pl.when(right & jnp.logical_not(own))(functools.partial(move, pieces[0]))
-                        pl.when(right & own)(functools.partial(move, done_ref))
+                    @pl.when((slot ^ colour) == head)
+                    def _():
+                        source = pieces[colour].at[here]
+                        act(pltpu.make_async_copy(source, target.at[head], sems.at[2 * head + number]))
 
     each_copy(lambda copy: copy.start())
     each_copy(lambda copy: copy.wait())
 
 
-def part(done, pieces, heads):
-    rows = done.shape[0] // 2
+def part(pieces, heads):
+    rows = pieces[0].shape[0] // 2
     shape = jax.ShapeDtypeStruct((heads, rows, HEAD_DIM), jnp.bfloat16)
     return pl.pallas_call(
         functools.partial(part_kernel, len(pieces)),
-        in_specs=[any_spec()] * (len(pieces) + 1),
+        in_specs=[any_spec()] * len(pieces),
         out_specs=[any_spec()] * 2,
         out_shape=[shape, shape],
         scratch_shapes=[pltpu.SemaphoreType.DMA((2 * heads,))],
         compiler_params=pltpu.CompilerParams(vmem_limit_bytes=VMEM_LIMIT),
-    )(done, *pieces)
+    )(*pieces)
 
 
 def combine_kernel(keep_ref, got_ref, weight, mine, theirs, attended, sems):
@@ -520,12 +486,12 @@
         far = lax.ppermute(near, "tp", swap)
         sent = project_shared(near, far, mod, mine, w_query, w_key, w_value, colours)
         got = [lax.ppermute(piece, ("req", "tp"), route) for piece, route in zip(sent, routes)]
-        swapped = lax.ppermute(collect(sent[0], got), "tp", swap)
-        done = attend(video_lengths, sent[0], got, swapped, heads)
+        swapped = [lax.ppermute(piece, "tp", swap) for piece in got]
+        done = attend(video_lengths, got, swapped, heads)
         back = [
             lax.ppermute(piece, ("req", "tp"), [(b, a) for a, b in route]) for piece, route in zip(done, routes)
         ]
-        keep, give = part(done[0], back, heads)
+        keep, give = part(back, heads)
         mine, theirs = combine(keep, lax.ppermute(give, "req", cross), w_out)
         theirs = lax.ppermute(theirs, "tp", swap)
         velocity, stepped = finish(timestep, mine, theirs, tokens, gate)

time: 80.3 us -> 80.3 us (level)
  the two profiles are of different devices: /device:TPU:0 before, /device:TPU:27 now
where the time goes in v8:
time: 80.3 us; the launch traced here: 79.9 us
  starting transfers between devices  43.5 us (54%)
  Pallas kernels  17.8 us (22%)
  waiting for transfers between devices  15.3 us (19%)
  local copies, waits for them, and re-layouts  1.71 us (2%)
  between operations  1.5 us (2%)
    ppermute x4, starting transfers between devices, on_device(): lax.ppermute(piece, ('req', 'tp'), [(b, a) for a, b in route])  12.2 us
    ppermute x4, starting transfers between devices, on_device(): swapped = [lax.ppermute(piece, 'tp', swap) for piece in got]  11.4 us
    ppermute x1, starting transfers between devices, on_device(): theirs = lax.ppermute(theirs, 'tp', swap)  9.33 us
    pallas_call x1, Pallas kernels, attend(): pl.pallas_call(functools.partial(attend_kernel, colours, heads), in_specs...  8.54 us
    ppermute x4, starting transfers between devices, on_device(): lax.ppermute(piece, ('req', 'tp'), route)  8.09 us
    ppermute x4, waiting for transfers between devices, on_device(): lax.ppermute(piece, ('req', 'tp'), [(b, a) for a, b in route])  4.66 us
    pallas_call x1, Pallas kernels, project(): pl.pallas_call(project_kernel, in_specs=[vmem_spec()] * 4 + [any_spec()]...  4.06 us
    ppermute x1, waiting for transfers between devices, on_device(): mine, theirs = combine(keep, lax.ppermute(give, 'req', cross), w_out)  3.44 us
  transfers between devices with their start and end apart: 17, of which 9 were waited for; matrix products, arithmetic and copies ran while one was open for 0% of the time, Pallas kernels for 5%

profile of v8, /device:TPU:27, one launch (start us, length us, event | category | flops | bytes accessed | tf_op | source)
XLA Modules:
  0.0 79.9 jit_solution(8538482721668154040)
XLA Ops:
  0.6 0.7 collective-permute-start.1
  2.4 0.4 collective-permute-done.1.other_ref
  2.8 1.0 %copy-done.1 = bf16[192,768]{1,0:T(8,128)(2,1)S(1)} copy-done((bf16[192,768]{1,0:T(8,128)(2,1)S(1)}, bf16[192,768]{1,0:T(8,128)(2,1)}, u32[]{:S(2)}) %copy-start.1) | copy-done | bytes 294936
  3.8 0.7 copy-done.3
  4.5 4.1 %shard_map.104 = (bf16[3,3,192,128]{3,2,1,0:T(8,128)(2,1)S(1)}, f32[2,1536]{1,0:T(2,128)S(1)}, f32[1,768]{1,0:T(1,128)S(1)}) custom-call(f32[1,256]{1,0:T(1,128)S(1)} %divide_multiply_fusion.act_ref, f32[3,1536]{1,0:T(4,128)S(1)} %copy-done.3, bf16[192,768]{1,0:T(8,128)(2,1)S(1)} %copy-done.1, bf16[192,768]{1,0:T(8,128)(2,1)S(1)} %collective-permute-done.1.other_ref, ...), custom_call_target="tpu_custom_call" | custom-call | flops 679477248 | bytes 8388608 | tf_op jit(solution)/shard_map/pallas_call | solution.py:135
  8.6 1.6 %collective-permute-done.near_ref = bf16[192,768]{1,0:T(8,128)(2,1)S(1)} collective-permute-done((bf16[192,768]{1,0:T(8,128)(2,1)}, bf16[192,768]{1,0:T(8,128)(2,1)S(1)}, u32[]{:S(2)}, u32[]{:S(2)}) %collective-permute-start) | collective-permute-done | bytes 294944 | tf_op jit(solution)/shard_map/ppermute | solution.py:476
  10.2 0.8 %collective-permute-start.2 = (bf16[192,768]{1,0:T(8,128)(2,1)S(1)}, bf16[192,768]{1,0:T(8,128)(2,1)S(1)}, u32[]{:S(2)}, u32[]{:S(2)}) collective-permute-start(bf16[192,768]{1,0:T(8,128)(2,1)S(1)} %collective-permute-done.near_ref), channel_id=1, source_target_pairs={{0,1},{1,0},{2,3},{3,2},{4,5},{5,4},{6,7},{7,6},{8,9},{9,8},{10,11... | collective-permute-start | bytes 884744 | tf_op jit(solution)/shard_map/ppermute | solution.py:486
  11.0 1.2 %collective-permute-done.2.far_ref = bf16[192,768]{1,0:T(8,128)(2,1)S(1)} collective-permute-done((bf16[192,768]{1,0:T(8,128)(2,1)S(1)}, bf16[192,768]{1,0:T(8,128)(2,1)S(1)}, u32[]{:S(2)}, u32[]{:S(2)}) %collective-permute-start.2) | collective-permute-done | bytes 294944 | tf_op jit(solution)/shard_map/ppermute | solution.py:486
  12.2 3.0 %shard_map.105 = (bf16[3,384,128]{2,1,0:T(8,128)(2,1)S(1)}, bf16[3,384,128]{2,1,0:T(8,128)(2,1)S(1)}, bf16[3,384,128]{2,1,0:T(8,128)(2,1)S(1)}, bf16[3,384,128]{2,1,0:T(8,128)(2,1)S(1)}) custom-call(bf16[192,768]{1,0:T(8,128)(2,1)S(1)} %collective-permute-done.near_ref, bf16[192,768]{1,0:T(8,128)(2,1)S(1)} %collective-permute-done.2.far_ref, ...), custom_call_target="tpu_custom_call" | custom-call | tf_op jit(solution)/shard_map/pallas_call | solution.py:191
  15.3 0.8 %collective-permute-start.3 = (bf16[3,384,128]{2,1,0:T(8,128)(2,1)S(1)}, bf16[3,384,128]{2,1,0:T(8,128)(2,1)S(1)}, u32[]{:S(2)}, u32[]{:S(2)}) collective-permute-start(bf16[3,384,128]{2,1,0:T(8,128)(2,1)S(1)} %get-tuple-element.27), channel_id=1, source_target_pairs={{0,0},{1,16},{2,2},{3,18},{4,4},{5,20},{6,6},{7,22},{8,8},{9,24},{... | collective-permute-start | bytes 884744 | tf_op jit(solution)/shard_map/ppermute | solution.py:488
  16.1 1.3 %collective-permute-start.4 = (bf16[3,384,128]{2,1,0:T(8,128)(2,1)S(1)}, bf16[3,384,128]{2,1,0:T(8,128)(2,1)S(1)}, u32[]{:S(2)}, u32[]{:S(2)}) collective-permute-start(bf16[3,384,128]{2,1,0:T(8,128)(2,1)S(1)} %get-tuple-element.28), channel_id=1, source_target_pairs={{0,4},{1,20},{2,6},{3,22},{4,0},{5,16},{6,2},{7,18},{12,8},{13,24}... | collective-permute-start | bytes 884744 | tf_op jit(solution)/shard_map/ppermute | solution.py:488
  17.4 3.9 %collective-permute-start.5 = (bf16[3,384,128]{2,1,0:T(8,128)(2,1)S(1)}, bf16[3,384,128]{2,1,0:T(8,128)(2,1)S(1)}, u32[]{:S(2)}, u32[]{:S(2)}) collective-permute-start(bf16[3,384,128]{2,1,0:T(8,128)(2,1)S(1)} %get-tuple-element.29), channel_id=1, source_target_pairs={{0,8},{1,24},{2,10},{3,26},{8,0},{9,16},{10,2},{11,18},{12,4},{13,... | collective-permute-start | bytes 884744 | tf_op jit(solution)/shard_map/ppermute | solution.py:488
  21.4 2.1 %collective-permute-start.6 = (bf16[3,384,128]{2,1,0:T(8,128)(2,1)S(1)}, bf16[3,384,128]{2,1,0:T(8,128)(2,1)S(1)}, u32[]{:S(2)}, u32[]{:S(2)}) collective-permute-start(bf16[3,384,128]{2,1,0:T(8,128)(2,1)S(1)} %get-tuple-element.30), channel_id=1, source_target_pairs={{4,8},{5,24},{6,10},{7,26},{8,4},{9,20},{10,6},{11,22},{12,0},{13,... | collective-permute-start | bytes 884744 | tf_op jit(solution)/shard_map/ppermute | solution.py:488
  23.4 6.5 %collective-permute-start.7 = (bf16[3,384,128]{2,1,0:T(8,128)(2,1)S(1)}, bf16[3,384,128]{2,1,0:T(8,128)(2,1)S(1)}, u32[]{:S(2)}, u32[]{:S(2)}) collective-permute-start(bf16[3,384,128]{2,1,0:T(8,128)(2,1)S(1)} %collective-permute-done.3.refs_0_), channel_id=1, source_target_pairs={{0,1},{1,0},{2,3},{3,2},{4,5},{5,4},{6,7},{7,6},{8,9},{9,8},{10,11... | collective-permute-start | bytes 884744 | tf_op jit(solution)/shard_map/ppermute | solution.py:489
  29.9 2.1 %collective-permute-start.8 = (bf16[3,384,128]{2,1,0:T(8,128)(2,1)S(1)}, bf16[3,384,128]{2,1,0:T(8,128)(2,1)S(1)}, u32[]{:S(2)}, u32[]{:S(2)}) collective-permute-start(bf16[3,384,128]{2,1,0:T(8,128)(2,1)S(1)} %collective-permute-done.4.refs_1_), channel_id=1, source_target_pairs={{0,1},{1,0},{2,3},{3,2},{4,5},{5,4},{6,7},{7,6},{8,9},{9,8},{10,11... | collective-permute-start | bytes 884744 | tf_op jit(solution)/shard_map/ppermute | solution.py:489
  32.0 2.6 %collective-permute-start.9 = (bf16[3,384,128]{2,1,0:T(8,128)(2,1)S(1)}, bf16[3,384,128]{2,1,0:T(8,128)(2,1)S(1)}, u32[]{:S(2)}, u32[]{:S(2)}) collective-permute-start(bf16[3,384,128]{2,1,0:T(8,128)(2,1)S(1)} %collective-permute-done.5.refs_2_), channel_id=1, source_target_pairs={{0,1},{1,0},{2,3},{3,2},{4,5},{5,4},{6,7},{7,6},{8,9},{9,8},{10,11... | collective-permute-start | bytes 884744 | tf_op jit(solution)/shard_map/ppermute | solution.py:489
  34.6 1.5 %collective-permute-done.6.refs_3_ = bf16[3,384,128]{2,1,0:T(8,128)(2,1)S(1)} collective-permute-done((bf16[3,384,128]{2,1,0:T(8,128)(2,1)S(1)}, bf16[3,384,128]{2,1,0:T(8,128)(2,1)S(1)}, u32[]{:S(2)}, u32[]{:S(2)}) %collective-permute-start.6) | collective-permute-done | bytes 294944 | tf_op jit(solution)/shard_map/ppermute | solution.py:488
  36.3 1.3 %collective-permute-done.10.refs_7_ = bf16[3,384,128]{2,1,0:T(8,128)(2,1)S(1)} collective-permute-done((bf16[3,384,128]{2,1,0:T(8,128)(2,1)S(1)}, bf16[3,384,128]{2,1,0:T(8,128)(2,1)S(1)}, u32[]{:S(2)}, u32[]{:S(2)}) %collective-permute-start.10) | collective-permute-done | bytes 294944 | tf_op jit(solution)/shard_map/ppermute | solution.py:489
  37.7 8.5 %shard_map.106 = (bf16[384,128]{1,0:T(8,128)(2,1)S(1)}, bf16[384,128]{1,0:T(8,128)(2,1)S(1)}, bf16[384,128]{1,0:T(8,128)(2,1)S(1)}, bf16[384,128]{1,0:T(8,128)(2,1)S(1)}) custom-call(s32[5]{0:T(128)S(1)} %copy-done.4, bf16[3,384,128]{2,1,0:T(8,128)(2,1)S(1)} %collective-permute-done.3.refs_0_, bf16[3,384,128]{2,1,0:T(8,128)(2,1)S(1)} %collective-permute-done.4.refs_1_, ...), custom_call_target="tpu_custom_call" | custom-call | tf_op jit(solution)/shard_map/pallas_call | solution.py:359
  46.2 0.7 collective-permute-start.11
  46.9 1.3 %collective-permute-start.12 = (bf16[384,128]{1,0:T(8,128)(2,1)S(1)}, bf16[384,128]{1,0:T(8,128)(2,1)S(1)}, u32[]{:S(2)}, u32[]{:S(2)}) collective-permute-start(bf16[384,128]{1,0:T(8,128)(2,1)S(1)} %get-tuple-element.32), channel_id=1, source_target_pairs={{4,0},{20,1},{6,2},{22,3},{0,4},{16,5},{2,6},{18,7},{8,12},{24,13}... | collective-permute-start | bytes 294920 | tf_op jit(solution)/shard_map/ppermute | solution.py:492
  48.2 8.0 %collective-permute-start.13 = (bf16[384,128]{1,0:T(8,128)(2,1)S(1)}, bf16[384,128]{1,0:T(8,128)(2,1)S(1)}, u32[]{:S(2)}, u32[]{:S(2)}) collective-permute-start(bf16[384,128]{1,0:T(8,128)(2,1)S(1)} %get-tuple-element.33), channel_id=1, source_target_pairs={{8,0},{24,1},{10,2},{26,3},{0,8},{16,9},{2,10},{18,11},{4,12},{20,... | collective-permute-start | bytes 294920 | tf_op jit(solution)/shard_map/ppermute | solution.py:492
  56.2 2.3 %collective-permute-start.14 = (bf16[384,128]{1,0:T(8,128)(2,1)S(1)}, bf16[384,128]{1,0:T(8,128)(2,1)S(1)}, u32[]{:S(2)}, u32[]{:S(2)}) collective-permute-start(bf16[384,128]{1,0:T(8,128)(2,1)S(1)} %get-tuple-element.34), channel_id=1, source_target_pairs={{8,4},{24,5},{10,6},{26,7},{4,8},{20,9},{6,10},{22,11},{0,12},{16,... | collective-permute-start | bytes 294920 | tf_op jit(solution)/shard_map/ppermute | solution.py:492
  58.5 0.5 collective-permute-done.13.refs_2_
  59.0 4.1 %collective-permute-done.14.refs_3_ = bf16[384,128]{1,0:T(8,128)(2,1)S(1)} collective-permute-done((bf16[384,128]{1,0:T(8,128)(2,1)S(1)}, bf16[384,128]{1,0:T(8,128)(2,1)S(1)}, u32[]{:S(2)}, u32[]{:S(2)}) %collective-permute-start.14) | collective-permute-done | bytes 98336 | tf_op jit(solution)/shard_map/ppermute | solution.py:492
  63.1 0.5 shard_map.107
  63.6 0.6 collective-permute-start.15
  64.3 3.4 %collective-permute-done.15.got_ref = bf16[3,192,128]{2,1,0:T(8,128)(2,1)S(1)} collective-permute-done((bf16[3,192,128]{2,1,0:T(8,128)(2,1)S(1)}, bf16[3,192,128]{2,1,0:T(8,128)(2,1)S(1)}, u32[]{:S(2)}, u32[]{:S(2)}) %collective-permute-start.15) | collective-permute-done | bytes 147488 | tf_op jit(solution)/shard_map/ppermute | solution.py:495
  67.7 0.8 shard_map.108
  68.5 9.3 %collective-permute-start.16 = (bf16[192,768]{1,0:T(8,128)(2,1)S(1)}, bf16[192,768]{1,0:T(8,128)(2,1)S(1)}, u32[]{:S(2)}, u32[]{:S(2)}) collective-permute-start(bf16[192,768]{1,0:T(8,128)(2,1)S(1)} %get-tuple-element.38), channel_id=1, source_target_pairs={{0,1},{1,0},{2,3},{3,2},{4,5},{5,4},{6,7},{7,6},{8,9},{9,8},{10,11... | collective-permute-start | bytes 884744 | tf_op jit(solution)/shard_map/ppermute | solution.py:496
  77.8 1.2 %collective-permute-done.16.theirs = bf16[192,768]{1,0:T(8,128)(2,1)S(1)} collective-permute-done((bf16[192,768]{1,0:T(8,128)(2,1)S(1)}, bf16[192,768]{1,0:T(8,128)(2,1)S(1)}, u32[]{:S(2)}, u32[]{:S(2)}) %collective-permute-start.16) | collective-permute-done | bytes 294944 | tf_op jit(solution)/shard_map/ppermute | solution.py:496
  79.0 0.9 %shard_map.109 = (bf16[192,768]{1,0:T(8,128)(2,1)}, bf16[192,768]{1,0:T(8,128)(2,1)}) custom-call(s32[1]{0:T(128)S(6)} %copy.11.timestep_ref, f32[192,768]{1,0:T(8,128)S(1)} %get-tuple-element.37.mine, bf16[192,768]{1,0:T(8,128)(2,1)S(1)} %collective-permute-done.16.theirs, bf16[192,768]{1,0:T(8,128)(2,1)S(1)} %copy-done.2, ...), custom_call_target="tpu_custom_call" | custom-call | tf_op jit(solution)/shard_map/pallas_call | solution.py:458
  (20 shorter events, 0.6 us)
Async XLA Ops:
  0.6 2.2 %collective-permute-start.1 = (bf16[192,768]{1,0:T(8,128)(2,1)}, bf16[192,768]{1,0:T(8,128)(2,1)S(1)}, u32[]{:S(2)}, u32[]{:S(2)}) collective-permute-start(bf16[192,768]{1,0:T(8,128)(2,1)} %tokens.1), channel_id=1, source_target_pairs={{0,1},{1,0},{2,3},{3,2},{4,5},{5,4},{6,7},{7,6},{8,9},{9,8},{10,11... | collective-permute-start | bytes 884744 | tf_op jit(solution)/shard_map/ppermute | solution.py:477
  1.4 8.8 %collective-permute-start = (bf16[192,768]{1,0:T(8,128)(2,1)}, bf16[192,768]{1,0:T(8,128)(2,1)S(1)}, u32[]{:S(2)}, u32[]{:S(2)}) collective-permute-start(bf16[192,768]{1,0:T(8,128)(2,1)} %tokens.1), channel_id=1, source_target_pairs={{0,2},{2,0},{4,6},{6,4},{8,10},{10,8},{12,14},{14,12},{16,18},{18,... | collective-permute-start | bytes 884744 | tf_op jit(solution)/shard_map/ppermute | solution.py:476
  2.8 1.0 %copy-start.1 = (bf16[192,768]{1,0:T(8,128)(2,1)S(1)}, bf16[192,768]{1,0:T(8,128)(2,1)}, u32[]{:S(2)}) copy-start(bf16[192,768]{1,0:T(8,128)(2,1)} %tokens.1) | copy-start | bytes 884740
  3.8 0.7 copy-start.3
  10.2 27.5 %copy-start.4 = (s32[5]{0:T(128)S(1)}, s32[5]{0:T(128)}, u32[]{:S(2)}) copy-start(s32[5]{0:T(128)} %lengths_ref.1) | copy-start | bytes 64
  10.2 2.1 %collective-permute-start.2 = (bf16[192,768]{1,0:T(8,128)(2,1)S(1)}, bf16[192,768]{1,0:T(8,128)(2,1)S(1)}, u32[]{:S(2)}, u32[]{:S(2)}) collective-permute-start(bf16[192,768]{1,0:T(8,128)(2,1)S(1)} %collective-permute-done.near_ref), channel_id=1, source_target_pairs={{0,1},{1,0},{2,3},{3,2},{4,5},{5,4},{6,7},{7,6},{8,9},{9,8},{10,11... | collective-permute-start | bytes 884744 | tf_op jit(solution)/shard_map/ppermute | solution.py:486
  15.3 52.4 %copy-start = (bf16[768,1536]{1,0:T(8,128)(2,1)S(1)}, bf16[768,1536]{1,0:T(8,128)(2,1)}, u32[]{:S(2)}) copy-start(bf16[768,1536]{1,0:T(8,128)(2,1)} %weight.1) | copy-start | bytes 7077892
  15.3 8.1 %collective-permute-start.3 = (bf16[3,384,128]{2,1,0:T(8,128)(2,1)S(1)}, bf16[3,384,128]{2,1,0:T(8,128)(2,1)S(1)}, u32[]{:S(2)}, u32[]{:S(2)}) collective-permute-start(bf16[3,384,128]{2,1,0:T(8,128)(2,1)S(1)} %get-tuple-element.27), channel_id=1, source_target_pairs={{0,0},{1,16},{2,2},{3,18},{4,4},{5,20},{6,6},{7,22},{8,8},{9,24},{... | collective-permute-start | bytes 884744 | tf_op jit(solution)/shard_map/ppermute | solution.py:488
  16.1 13.8 %collective-permute-start.4 = (bf16[3,384,128]{2,1,0:T(8,128)(2,1)S(1)}, bf16[3,384,128]{2,1,0:T(8,128)(2,1)S(1)}, u32[]{:S(2)}, u32[]{:S(2)}) collective-permute-start(bf16[3,384,128]{2,1,0:T(8,128)(2,1)S(1)} %get-tuple-element.28), channel_id=1, source_target_pairs={{0,4},{1,20},{2,6},{3,22},{4,0},{5,16},{6,2},{7,18},{12,8},{13,24}... | collective-permute-start | bytes 884744 | tf_op jit(solution)/shard_map/ppermute | solution.py:488
  17.4 14.6 %collective-permute-start.5 = (bf16[3,384,128]{2,1,0:T(8,128)(2,1)S(1)}, bf16[3,384,128]{2,1,0:T(8,128)(2,1)S(1)}, u32[]{:S(2)}, u32[]{:S(2)}) collective-permute-start(bf16[3,384,128]{2,1,0:T(8,128)(2,1)S(1)} %get-tuple-element.29), channel_id=1, source_target_pairs={{0,8},{1,24},{2,10},{3,26},{8,0},{9,16},{10,2},{11,18},{12,4},{13,... | collective-permute-start | bytes 884744 | tf_op jit(solution)/shard_map/ppermute | solution.py:488
  21.3 57.7 %copy-start.2 = (bf16[192,768]{1,0:T(8,128)(2,1)S(1)}, bf16[192,768]{1,0:T(8,128)(2,1)}, u32[]{:S(2)}) copy-start(bf16[192,768]{1,0:T(8,128)(2,1)} %tokens.1) | copy-start | bytes 884740
  21.4 14.7 %collective-permute-start.6 = (bf16[3,384,128]{2,1,0:T(8,128)(2,1)S(1)}, bf16[3,384,128]{2,1,0:T(8,128)(2,1)S(1)}, u32[]{:S(2)}, u32[]{:S(2)}) collective-permute-start(bf16[3,384,128]{2,1,0:T(8,128)(2,1)S(1)} %get-tuple-element.30), channel_id=1, source_target_pairs={{4,8},{5,24},{6,10},{7,26},{8,4},{9,20},{10,6},{11,22},{12,0},{13,... | collective-permute-start | bytes 884744 | tf_op jit(solution)/shard_map/ppermute | solution.py:488
  23.4 12.9 %collective-permute-start.7 = (bf16[3,384,128]{2,1,0:T(8,128)(2,1)S(1)}, bf16[3,384,128]{2,1,0:T(8,128)(2,1)S(1)}, u32[]{:S(2)}, u32[]{:S(2)}) collective-permute-start(bf16[3,384,128]{2,1,0:T(8,128)(2,1)S(1)} %collective-permute-done.3.refs_0_), channel_id=1, source_target_pairs={{0,1},{1,0},{2,3},{3,2},{4,5},{5,4},{6,7},{7,6},{8,9},{9,8},{10,11... | collective-permute-start | bytes 884744 | tf_op jit(solution)/shard_map/ppermute | solution.py:489
  29.9 6.5 %collective-permute-start.8 = (bf16[3,384,128]{2,1,0:T(8,128)(2,1)S(1)}, bf16[3,384,128]{2,1,0:T(8,128)(2,1)S(1)}, u32[]{:S(2)}, u32[]{:S(2)}) collective-permute-start(bf16[3,384,128]{2,1,0:T(8,128)(2,1)S(1)} %collective-permute-done.4.refs_1_), channel_id=1, source_target_pairs={{0,1},{1,0},{2,3},{3,2},{4,5},{5,4},{6,7},{7,6},{8,9},{9,8},{10,11... | collective-permute-start | bytes 884744 | tf_op jit(solution)/shard_map/ppermute | solution.py:489
  32.0 4.3 %collective-permute-start.9 = (bf16[3,384,128]{2,1,0:T(8,128)(2,1)S(1)}, bf16[3,384,128]{2,1,0:T(8,128)(2,1)S(1)}, u32[]{:S(2)}, u32[]{:S(2)}) collective-permute-start(bf16[3,384,128]{2,1,0:T(8,128)(2,1)S(1)} %collective-permute-done.5.refs_2_), channel_id=1, source_target_pairs={{0,1},{1,0},{2,3},{3,2},{4,5},{5,4},{6,7},{7,6},{8,9},{9,8},{10,11... | collective-permute-start | bytes 884744 | tf_op jit(solution)/shard_map/ppermute | solution.py:489
  36.1 1.6 %collective-permute-start.10 = (bf16[3,384,128]{2,1,0:T(8,128)(2,1)S(1)}, bf16[3,384,128]{2,1,0:T(8,128)(2,1)S(1)}, u32[]{:S(2)}, u32[]{:S(2)}) collective-permute-start(bf16[3,384,128]{2,1,0:T(8,128)(2,1)S(1)} %collective-permute-done.6.refs_3_), channel_id=1, source_target_pairs={{0,1},{1,0},{2,3},{3,2},{4,5},{5,4},{6,7},{7,6},{8,9},{9,8},{10,11... | collective-permute-start | bytes 884744 | tf_op jit(solution)/shard_map/ppermute | solution.py:489
  46.2 12.2 %collective-permute-start.11 = (bf16[384,128]{1,0:T(8,128)(2,1)S(1)}, bf16[384,128]{1,0:T(8,128)(2,1)S(1)}, u32[]{:S(2)}, u32[]{:S(2)}) collective-permute-start(bf16[384,128]{1,0:T(8,128)(2,1)S(1)} %get-tuple-element.31), channel_id=1, source_target_pairs={{0,0},{16,1},{2,2},{18,3},{4,4},{20,5},{6,6},{22,7},{8,8},{24,9},{... | collective-permute-start | bytes 294920 | tf_op jit(solution)/shard_map/ppermute | solution.py:492
  46.9 11.6 %collective-permute-start.12 = (bf16[384,128]{1,0:T(8,128)(2,1)S(1)}, bf16[384,128]{1,0:T(8,128)(2,1)S(1)}, u32[]{:S(2)}, u32[]{:S(2)}) collective-permute-start(bf16[384,128]{1,0:T(8,128)(2,1)S(1)} %get-tuple-element.32), channel_id=1, source_target_pairs={{4,0},{20,1},{6,2},{22,3},{0,4},{16,5},{2,6},{18,7},{8,12},{24,13}... | collective-permute-start | bytes 294920 | tf_op jit(solution)/shard_map/ppermute | solution.py:492
  48.2 10.8 %collective-permute-start.13 = (bf16[384,128]{1,0:T(8,128)(2,1)S(1)}, bf16[384,128]{1,0:T(8,128)(2,1)S(1)}, u32[]{:S(2)}, u32[]{:S(2)}) collective-permute-start(bf16[384,128]{1,0:T(8,128)(2,1)S(1)} %get-tuple-element.33), channel_id=1, source_target_pairs={{8,0},{24,1},{10,2},{26,3},{0,8},{16,9},{2,10},{18,11},{4,12},{20,... | collective-permute-start | bytes 294920 | tf_op jit(solution)/shard_map/ppermute | solution.py:492
  56.2 7.0 %collective-permute-start.14 = (bf16[384,128]{1,0:T(8,128)(2,1)S(1)}, bf16[384,128]{1,0:T(8,128)(2,1)S(1)}, u32[]{:S(2)}, u32[]{:S(2)}) collective-permute-start(bf16[384,128]{1,0:T(8,128)(2,1)S(1)} %get-tuple-element.34), channel_id=1, source_target_pairs={{8,4},{24,5},{10,6},{26,7},{4,8},{20,9},{6,10},{22,11},{0,12},{16,... | collective-permute-start | bytes 294920 | tf_op jit(solution)/shard_map/ppermute | solution.py:492
  63.6 4.1 %collective-permute-start.15 = (bf16[3,192,128]{2,1,0:T(8,128)(2,1)S(1)}, bf16[3,192,128]{2,1,0:T(8,128)(2,1)S(1)}, u32[]{:S(2)}, u32[]{:S(2)}) collective-permute-start(bf16[3,192,128]{2,1,0:T(8,128)(2,1)S(1)} %get-tuple-element.36), channel_id=1, source_target_pairs={{0,2},{2,0},{4,6},{6,4},{8,10},{10,8},{12,14},{14,12},{16,18},{18,... | collective-permute-start | bytes 442376 | tf_op jit(solution)/shard_map/ppermute | solution.py:495
  68.5 10.5 %collective-permute-start.16 = (bf16[192,768]{1,0:T(8,128)(2,1)S(1)}, bf16[192,768]{1,0:T(8,128)(2,1)S(1)}, u32[]{:S(2)}, u32[]{:S(2)}) collective-permute-start(bf16[192,768]{1,0:T(8,128)(2,1)S(1)} %get-tuple-element.38), channel_id=1, source_target_pairs={{0,1},{1,0},{2,3},{3,2},{4,5},{5,4},{6,7},{7,6},{8,9},{9,8},{10,11... | collective-permute-start | bytes 884744 | tf_op jit(solution)/shard_map/ppermute | solution.py:496

commit v9 on v8

--- a/solution.py
+++ b/solution.py
@@ -23,21 +23,27 @@
     return 5.0 * frac / (1.0 + 4.0 * frac)
 
 
+def turned(colours, side):
+    return colours // 2 * (1 - side)
+
+
 def pairs_out(chips, heads, colour):
     half = chips // 2
+    colours = half // 2
     pairs = []
     for chip in range(chips):
-        side, slot, x = chip // half, chip % half // 2, chip % 2
+        side, x = chip // half, chip % 2
+        slot = chip % half // 2 ^ turned(colours, side)
         for core in range(2):
-            source, target = chip * 2 + core, (core * half + (slot ^ colour) * 2 + x) * 2 + side
+            place = slot ^ colour ^ turned(colours, core)
             if (slot ^ colour) < heads:
-                pairs.append((source, target))
+                pairs.append((chip * 2 + core, (core * half + place * 2 + x) * 2 + side))
     return pairs
 
 
 def place_of(colours):
     chip = lax.axis_index("req")
-    return lax.rem(chip // 2, colours), lax.rem(chip, 2)
+    return lax.rem(chip // 2, colours) ^ turned(colours, chip // (2 * colours)), lax.rem(chip, 2)
 
 
 def any_spec():
@@ -215,18 +221,19 @@
     front = pl.ds(0, HEAD_DIM)
     videos = lengths_ref.shape[0]
 
-    def at(colour, which):
-        return pl.ds(pl.multiple_of((slot ^ colour) * rows + which * own_rows, 128), rows)
+    def at(colour, which, whole):
+        place = slot ^ colour ^ turned(colours, which)
+        return pl.ds(pl.multiple_of(place * rows + (which * own_rows if whole else 0), 128), rows)
 
     def each_copy(act):
         for colour in range(colours):
             near, far = pieces[colour], swapped[colour]
             for number, (source, target) in enumerate((
-                (near.at[0], query.at[at(colour, 0), front]),
-                (near.at[1], keys.at[at(colour, side), front]),
-                (near.at[2], values.at[at(colour, side), front]),
-                (far.at[1], keys.at[at(colour, 1 - side), front]),
-                (far.at[2], values.at[at(colour, 1 - side), front]),
+                (near.at[0], query.at[at(colour, side, False), front]),
+                (near.at[1], keys.at[at(colour, side, True), front]),
+                (near.at[2], values.at[at(colour, side, True), front]),
+                (far.at[1], keys.at[at(colour, 1 - side, True), front]),
+                (far.at[2], values.at[at(colour, 1 - side, True), front]),
             )):
                 act(pltpu.make_async_copy(source, target, sems.at[5 * colour + number]))
 
@@ -343,7 +350,7 @@
 
         lax.fori_loop(0, own_rows // QUERY_BLOCK, query_block, 0)
         copies = [
-            pltpu.make_async_copy(result.at[at(colour, 0)], outs[colour], out_sems.at[colour])
+            pltpu.make_async_copy(result.at[at(colour, side, False)], outs[colour], out_sems.at[colour])
             for colour in range(colours)
         ]
         for copy in copies:

time: 80.3 us -> 77.8 us (0.969)
  the two profiles are of different devices: /device:TPU:27 before, /device:TPU:0 now
where the time goes in v9:
time: 77.8 us; the launch traced here: 77.1 us
  starting transfers between devices  42.1 us (54%)
  Pallas kernels  17.3 us (22%)
  waiting for transfers between devices  14.4 us (19%)
  local copies, waits for them, and re-layouts  1.71 us (2%)
  between operations  1.51 us (2%)
    ppermute x4, starting transfers between devices, on_device(): swapped = [lax.ppermute(piece, 'tp', swap) for piece in got]  18.6 us
    ppermute x4, starting transfers between devices, on_device(): lax.ppermute(piece, ('req', 'tp'), route)  10 us
    pallas_call x1, Pallas kernels, attend(): pl.pallas_call(functools.partial(attend_kernel, colours, heads), in_specs...  8.07 us
    ppermute x4, starting transfers between devices, on_device(): lax.ppermute(piece, ('req', 'tp'), [(b, a) for a, b in route])  5.8 us
    ppermute x4, waiting for transfers between devices, on_device(): lax.ppermute(piece, ('req', 'tp'), [(b, a) for a, b in route])  5.46 us
    pallas_call x1, Pallas kernels, project(): pl.pallas_call(project_kernel, in_specs=[vmem_spec()] * 4 + [any_spec()]...  4.07 us
    ppermute x1, waiting for transfers between devices, on_device(): mine, theirs = combine(keep, lax.ppermute(give, 'req', cross), w_out)  3.65 us
    ppermute x1, starting transfers between devices, on_device(): theirs = lax.ppermute(theirs, 'tp', swap)  3.04 us
  transfers between devices with their start and end apart: 17, of which 7 were waited for; matrix products, arithmetic and copies ran while one was open for 0% of the time, Pallas kernels for 5%

profile of v9, /device:TPU:0, one launch (start us, length us, event | category | flops | bytes accessed | tf_op | source)
XLA Modules:
  0.0 77.1 jit_solution(3413136669476569845)
XLA Ops:
  0.6 0.5 collective-permute-start.1
  1.1 2.6 %collective-permute-start = (bf16[192,768]{1,0:T(8,128)(2,1)}, bf16[192,768]{1,0:T(8,128)(2,1)S(1)}, u32[]{:S(2)}, u32[]{:S(2)}) collective-permute-start(bf16[192,768]{1,0:T(8,128)(2,1)} %tokens.1), channel_id=1, source_target_pairs={{0,2},{2,0},{4,6},{6,4},{8,10},{10,8},{12,14},{14,12},{16,18},{18,... | collective-permute-start | bytes 884744 | tf_op jit(solution)/shard_map/ppermute | solution.py:483
  4.5 1.0 %copy-done.1 = bf16[192,768]{1,0:T(8,128)(2,1)S(1)} copy-done((bf16[192,768]{1,0:T(8,128)(2,1)S(1)}, bf16[192,768]{1,0:T(8,128)(2,1)}, u32[]{:S(2)}) %copy-start.1) | copy-done | bytes 294936
  5.5 0.7 copy-done.3
  6.2 4.1 %shard_map.104 = (bf16[3,3,192,128]{3,2,1,0:T(8,128)(2,1)S(1)}, f32[2,1536]{1,0:T(2,128)S(1)}, f32[1,768]{1,0:T(1,128)S(1)}) custom-call(f32[1,256]{1,0:T(1,128)S(1)} %divide_multiply_fusion.act_ref, f32[3,1536]{1,0:T(4,128)S(1)} %copy-done.3, bf16[192,768]{1,0:T(8,128)(2,1)S(1)} %copy-done.1, bf16[192,768]{1,0:T(8,128)(2,1)S(1)} %collective-permute-done.1.other_ref, ...), custom_call_target="tpu_custom_call" | custom-call | flops 679477248 | bytes 8388608 | tf_op jit(solution)/shard_map/pallas_call | solution.py:141
  10.3 1.3 %collective-permute-done.near_ref = bf16[192,768]{1,0:T(8,128)(2,1)S(1)} collective-permute-done((bf16[192,768]{1,0:T(8,128)(2,1)}, bf16[192,768]{1,0:T(8,128)(2,1)S(1)}, u32[]{:S(2)}, u32[]{:S(2)}) %collective-permute-start) | collective-permute-done | bytes 294944 | tf_op jit(solution)/shard_map/ppermute | solution.py:483
  11.5 1.6 %collective-permute-done.2.far_ref = bf16[192,768]{1,0:T(8,128)(2,1)S(1)} collective-permute-done((bf16[192,768]{1,0:T(8,128)(2,1)S(1)}, bf16[192,768]{1,0:T(8,128)(2,1)S(1)}, u32[]{:S(2)}, u32[]{:S(2)}) %collective-permute-start.2) | collective-permute-done | bytes 294944 | tf_op jit(solution)/shard_map/ppermute | solution.py:493
  13.1 3.0 %shard_map.105 = (bf16[3,384,128]{2,1,0:T(8,128)(2,1)S(1)}, bf16[3,384,128]{2,1,0:T(8,128)(2,1)S(1)}, bf16[3,384,128]{2,1,0:T(8,128)(2,1)S(1)}, bf16[3,384,128]{2,1,0:T(8,128)(2,1)S(1)}) custom-call(bf16[192,768]{1,0:T(8,128)(2,1)S(1)} %collective-permute-done.near_ref, bf16[192,768]{1,0:T(8,128)(2,1)S(1)} %collective-permute-done.2.far_ref, ...), custom_call_target="tpu_custom_call" | custom-call | tf_op jit(solution)/shard_map/pallas_call | solution.py:197
  16.2 0.0 copy-start
  16.2 0.8 %collective-permute-start.3 = (bf16[3,384,128]{2,1,0:T(8,128)(2,1)S(1)}, bf16[3,384,128]{2,1,0:T(8,128)(2,1)S(1)}, u32[]{:S(2)}, u32[]{:S(2)}) collective-permute-start(bf16[3,384,128]{2,1,0:T(8,128)(2,1)S(1)} %get-tuple-element.27), channel_id=1, source_target_pairs={{0,0},{1,24},{2,2},{3,26},{8,8},{9,16},{10,10},{11,18},{12,12},{13... | collective-permute-start | bytes 884744 | tf_op jit(solution)/shard_map/ppermute | solution.py:495
  17.0 1.3 %collective-permute-start.4 = (bf16[3,384,128]{2,1,0:T(8,128)(2,1)S(1)}, bf16[3,384,128]{2,1,0:T(8,128)(2,1)S(1)}, u32[]{:S(2)}, u32[]{:S(2)}) collective-permute-start(bf16[3,384,128]{2,1,0:T(8,128)(2,1)S(1)} %get-tuple-element.28), channel_id=1, source_target_pairs={{4,0},{5,24},{6,2},{7,26},{8,12},{9,20},{10,14},{11,22},{12,8},{13... | collective-permute-start | bytes 884744 | tf_op jit(solution)/shard_map/ppermute | solution.py:495
  18.3 5.9 %collective-permute-start.5 = (bf16[3,384,128]{2,1,0:T(8,128)(2,1)S(1)}, bf16[3,384,128]{2,1,0:T(8,128)(2,1)S(1)}, u32[]{:S(2)}, u32[]{:S(2)}) collective-permute-start(bf16[3,384,128]{2,1,0:T(8,128)(2,1)S(1)} %get-tuple-element.29), channel_id=1, source_target_pairs={{0,8},{1,16},{2,10},{3,18},{4,12},{5,20},{6,14},{7,22},{8,0},{9,24... | collective-permute-start | bytes 884744 | tf_op jit(solution)/shard_map/ppermute | solution.py:495
  24.2 2.1 %collective-permute-start.6 = (bf16[3,384,128]{2,1,0:T(8,128)(2,1)S(1)}, bf16[3,384,128]{2,1,0:T(8,128)(2,1)S(1)}, u32[]{:S(2)}, u32[]{:S(2)}) collective-permute-start(bf16[3,384,128]{2,1,0:T(8,128)(2,1)S(1)} %get-tuple-element.30), channel_id=1, source_target_pairs={{0,12},{1,20},{2,14},{3,22},{4,8},{5,16},{6,10},{7,18},{12,0},{13,... | collective-permute-start | bytes 884744 | tf_op jit(solution)/shard_map/ppermute | solution.py:495
  26.3 3.6 %collective-permute-start.7 = (bf16[3,384,128]{2,1,0:T(8,128)(2,1)S(1)}, bf16[3,384,128]{2,1,0:T(8,128)(2,1)S(1)}, u32[]{:S(2)}, u32[]{:S(2)}) collective-permute-start(bf16[3,384,128]{2,1,0:T(8,128)(2,1)S(1)} %collective-permute-done.3.refs_0_), channel_id=1, source_target_pairs={{0,1},{1,0},{2,3},{3,2},{4,5},{5,4},{6,7},{7,6},{8,9},{9,8},{10,11... | collective-permute-start | bytes 884744 | tf_op jit(solution)/shard_map/ppermute | solution.py:496
  29.9 6.4 %collective-permute-start.8 = (bf16[3,384,128]{2,1,0:T(8,128)(2,1)S(1)}, bf16[3,384,128]{2,1,0:T(8,128)(2,1)S(1)}, u32[]{:S(2)}, u32[]{:S(2)}) collective-permute-start(bf16[3,384,128]{2,1,0:T(8,128)(2,1)S(1)} %collective-permute-done.4.refs_1_), channel_id=1, source_target_pairs={{0,1},{1,0},{2,3},{3,2},{4,5},{5,4},{6,7},{7,6},{8,9},{9,8},{10,11... | collective-permute-start | bytes 884744 | tf_op jit(solution)/shard_map/ppermute | solution.py:496
  36.2 5.3 %collective-permute-start.9 = (bf16[3,384,128]{2,1,0:T(8,128)(2,1)S(1)}, bf16[3,384,128]{2,1,0:T(8,128)(2,1)S(1)}, u32[]{:S(2)}, u32[]{:S(2)}) collective-permute-start(bf16[3,384,128]{2,1,0:T(8,128)(2,1)S(1)} %collective-permute-done.5.refs_2_), channel_id=1, source_target_pairs={{0,1},{1,0},{2,3},{3,2},{4,5},{5,4},{6,7},{7,6},{8,9},{9,8},{10,11... | collective-permute-start | bytes 884744 | tf_op jit(solution)/shard_map/ppermute | solution.py:496
  41.6 3.3 %collective-permute-start.10 = (bf16[3,384,128]{2,1,0:T(8,128)(2,1)S(1)}, bf16[3,384,128]{2,1,0:T(8,128)(2,1)S(1)}, u32[]{:S(2)}, u32[]{:S(2)}) collective-permute-start(bf16[3,384,128]{2,1,0:T(8,128)(2,1)S(1)} %collective-permute-done.6.refs_3_), channel_id=1, source_target_pairs={{0,1},{1,0},{2,3},{3,2},{4,5},{5,4},{6,7},{7,6},{8,9},{9,8},{10,11... | collective-permute-start | bytes 884744 | tf_op jit(solution)/shard_map/ppermute | solution.py:496
  44.9 1.2 %collective-permute-done.10.refs_7_ = bf16[3,384,128]{2,1,0:T(8,128)(2,1)S(1)} collective-permute-done((bf16[3,384,128]{2,1,0:T(8,128)(2,1)S(1)}, bf16[3,384,128]{2,1,0:T(8,128)(2,1)S(1)}, u32[]{:S(2)}, u32[]{:S(2)}) %collective-permute-start.10) | collective-permute-done | bytes 294944 | tf_op jit(solution)/shard_map/ppermute | solution.py:496
  46.1 8.1 %shard_map.106 = (bf16[384,128]{1,0:T(8,128)(2,1)S(1)}, bf16[384,128]{1,0:T(8,128)(2,1)S(1)}, bf16[384,128]{1,0:T(8,128)(2,1)S(1)}, bf16[384,128]{1,0:T(8,128)(2,1)S(1)}) custom-call(s32[5]{0:T(128)S(1)} %copy-done.4, bf16[3,384,128]{2,1,0:T(8,128)(2,1)S(1)} %collective-permute-done.3.refs_0_, bf16[3,384,128]{2,1,0:T(8,128)(2,1)S(1)} %collective-permute-done.4.refs_1_, ...), custom_call_target="tpu_custom_call" | custom-call | tf_op jit(solution)/shard_map/pallas_call | solution.py:366
  54.2 0.7 collective-permute-start.11
  54.8 1.3 %collective-permute-start.12 = (bf16[384,128]{1,0:T(8,128)(2,1)S(1)}, bf16[384,128]{1,0:T(8,128)(2,1)S(1)}, u32[]{:S(2)}, u32[]{:S(2)}) collective-permute-start(bf16[384,128]{1,0:T(8,128)(2,1)S(1)} %get-tuple-element.32), channel_id=1, source_target_pairs={{0,4},{24,5},{2,6},{26,7},{12,8},{20,9},{14,10},{22,11},{8,12},{16... | collective-permute-start | bytes 294920 | tf_op jit(solution)/shard_map/ppermute | solution.py:499
  56.1 1.9 %collective-permute-start.13 = (bf16[384,128]{1,0:T(8,128)(2,1)S(1)}, bf16[384,128]{1,0:T(8,128)(2,1)S(1)}, u32[]{:S(2)}, u32[]{:S(2)}) collective-permute-start(bf16[384,128]{1,0:T(8,128)(2,1)S(1)} %get-tuple-element.33), channel_id=1, source_target_pairs={{8,0},{16,1},{10,2},{18,3},{12,4},{20,5},{14,6},{22,7},{0,8},{24,9... | collective-permute-start | bytes 294920 | tf_op jit(solution)/shard_map/ppermute | solution.py:499
  58.1 1.9 %collective-permute-start.14 = (bf16[384,128]{1,0:T(8,128)(2,1)S(1)}, bf16[384,128]{1,0:T(8,128)(2,1)S(1)}, u32[]{:S(2)}, u32[]{:S(2)}) collective-permute-start(bf16[384,128]{1,0:T(8,128)(2,1)S(1)} %get-tuple-element.34), channel_id=1, source_target_pairs={{12,0},{20,1},{14,2},{22,3},{8,4},{16,5},{10,6},{18,7},{0,12},{24,... | collective-permute-start | bytes 294920 | tf_op jit(solution)/shard_map/ppermute | solution.py:499
  60.0 4.2 %collective-permute-done.13.refs_2_ = bf16[384,128]{1,0:T(8,128)(2,1)S(1)} collective-permute-done((bf16[384,128]{1,0:T(8,128)(2,1)S(1)}, bf16[384,128]{1,0:T(8,128)(2,1)S(1)}, u32[]{:S(2)}, u32[]{:S(2)}) %collective-permute-start.13) | collective-permute-done | bytes 98336 | tf_op jit(solution)/shard_map/ppermute | solution.py:499
  64.2 1.3 %collective-permute-done.14.refs_3_ = bf16[384,128]{1,0:T(8,128)(2,1)S(1)} collective-permute-done((bf16[384,128]{1,0:T(8,128)(2,1)S(1)}, bf16[384,128]{1,0:T(8,128)(2,1)S(1)}, u32[]{:S(2)}, u32[]{:S(2)}) %collective-permute-start.14) | collective-permute-done | bytes 98336 | tf_op jit(solution)/shard_map/ppermute | solution.py:499
  65.5 0.5 shard_map.107
  66.0 1.6 %collective-permute-start.15 = (bf16[3,192,128]{2,1,0:T(8,128)(2,1)S(1)}, bf16[3,192,128]{2,1,0:T(8,128)(2,1)S(1)}, u32[]{:S(2)}, u32[]{:S(2)}) collective-permute-start(bf16[3,192,128]{2,1,0:T(8,128)(2,1)S(1)} %get-tuple-element.36), channel_id=1, source_target_pairs={{0,2},{2,0},{4,6},{6,4},{8,10},{10,8},{12,14},{14,12},{16,18},{18,... | collective-permute-start | bytes 442376 | tf_op jit(solution)/shard_map/ppermute | solution.py:502
  67.6 3.6 %collective-permute-done.15.got_ref = bf16[3,192,128]{2,1,0:T(8,128)(2,1)S(1)} collective-permute-done((bf16[3,192,128]{2,1,0:T(8,128)(2,1)S(1)}, bf16[3,192,128]{2,1,0:T(8,128)(2,1)S(1)}, u32[]{:S(2)}, u32[]{:S(2)}) %collective-permute-start.15) | collective-permute-done | bytes 147488 | tf_op jit(solution)/shard_map/ppermute | solution.py:502
  71.2 0.8 shard_map.108
  72.0 3.0 %collective-permute-start.16 = (bf16[192,768]{1,0:T(8,128)(2,1)S(1)}, bf16[192,768]{1,0:T(8,128)(2,1)S(1)}, u32[]{:S(2)}, u32[]{:S(2)}) collective-permute-start(bf16[192,768]{1,0:T(8,128)(2,1)S(1)} %get-tuple-element.38), channel_id=1, source_target_pairs={{0,1},{1,0},{2,3},{3,2},{4,5},{5,4},{6,7},{7,6},{8,9},{9,8},{10,11... | collective-permute-start | bytes 884744 | tf_op jit(solution)/shard_map/ppermute | solution.py:503
  75.0 1.2 %collective-permute-done.16.theirs = bf16[192,768]{1,0:T(8,128)(2,1)S(1)} collective-permute-done((bf16[192,768]{1,0:T(8,128)(2,1)S(1)}, bf16[192,768]{1,0:T(8,128)(2,1)S(1)}, u32[]{:S(2)}, u32[]{:S(2)}) %collective-permute-start.16) | collective-permute-done | bytes 294944 | tf_op jit(solution)/shard_map/ppermute | solution.py:503
  76.2 0.9 %shard_map.109 = (bf16[192,768]{1,0:T(8,128)(2,1)}, bf16[192,768]{1,0:T(8,128)(2,1)}) custom-call(s32[1]{0:T(128)S(6)} %copy.11.timestep_ref, f32[192,768]{1,0:T(8,128)S(1)} %get-tuple-element.37.mine, bf16[192,768]{1,0:T(8,128)(2,1)S(1)} %collective-permute-done.16.theirs, bf16[192,768]{1,0:T(8,128)(2,1)S(1)} %copy-done.2, ...), custom_call_target="tpu_custom_call" | custom-call | tf_op jit(solution)/shard_map/pallas_call | solution.py:465
  (20 shorter events, 0.1 us)
Async XLA Ops:
  0.6 3.9 %collective-permute-start.1 = (bf16[192,768]{1,0:T(8,128)(2,1)}, bf16[192,768]{1,0:T(8,128)(2,1)S(1)}, u32[]{:S(2)}, u32[]{:S(2)}) collective-permute-start(bf16[192,768]{1,0:T(8,128)(2,1)} %tokens.1), channel_id=1, source_target_pairs={{0,1},{1,0},{2,3},{3,2},{4,5},{5,4},{6,7},{7,6},{8,9},{9,8},{10,11... | collective-permute-start | bytes 884744 | tf_op jit(solution)/shard_map/ppermute | solution.py:484
  1.1 10.4 %collective-permute-start = (bf16[192,768]{1,0:T(8,128)(2,1)}, bf16[192,768]{1,0:T(8,128)(2,1)S(1)}, u32[]{:S(2)}, u32[]{:S(2)}) collective-permute-start(bf16[192,768]{1,0:T(8,128)(2,1)} %tokens.1), channel_id=1, source_target_pairs={{0,2},{2,0},{4,6},{6,4},{8,10},{10,8},{12,14},{14,12},{16,18},{18,... | collective-permute-start | bytes 884744 | tf_op jit(solution)/shard_map/ppermute | solution.py:483
  4.5 1.0 %copy-start.1 = (bf16[192,768]{1,0:T(8,128)(2,1)S(1)}, bf16[192,768]{1,0:T(8,128)(2,1)}, u32[]{:S(2)}) copy-start(bf16[192,768]{1,0:T(8,128)(2,1)} %tokens.1) | copy-start | bytes 884740
  5.5 0.7 copy-start.3
  11.5 34.6 %copy-start.4 = (s32[5]{0:T(128)S(1)}, s32[5]{0:T(128)}, u32[]{:S(2)}) copy-start(s32[5]{0:T(128)} %lengths_ref.1) | copy-start | bytes 64
  11.5 1.6 %collective-permute-start.2 = (bf16[192,768]{1,0:T(8,128)(2,1)S(1)}, bf16[192,768]{1,0:T(8,128)(2,1)S(1)}, u32[]{:S(2)}, u32[]{:S(2)}) collective-permute-start(bf16[192,768]{1,0:T(8,128)(2,1)S(1)} %collective-permute-done.near_ref), channel_id=1, source_target_pairs={{0,1},{1,0},{2,3},{3,2},{4,5},{5,4},{6,7},{7,6},{8,9},{9,8},{10,11... | collective-permute-start | bytes 884744 | tf_op jit(solution)/shard_map/ppermute | solution.py:493
  16.2 55.1 %copy-start = (bf16[768,1536]{1,0:T(8,128)(2,1)S(1)}, bf16[768,1536]{1,0:T(8,128)(2,1)}, u32[]{:S(2)}) copy-start(bf16[768,1536]{1,0:T(8,128)(2,1)} %weight.1) | copy-start | bytes 7077892
  16.2 10.1 %collective-permute-start.3 = (bf16[3,384,128]{2,1,0:T(8,128)(2,1)S(1)}, bf16[3,384,128]{2,1,0:T(8,128)(2,1)S(1)}, u32[]{:S(2)}, u32[]{:S(2)}) collective-permute-start(bf16[3,384,128]{2,1,0:T(8,128)(2,1)S(1)} %get-tuple-element.27), channel_id=1, source_target_pairs={{0,0},{1,24},{2,2},{3,26},{8,8},{9,16},{10,10},{11,18},{12,12},{13... | collective-permute-start | bytes 884744 | tf_op jit(solution)/shard_map/ppermute | solution.py:495
  17.0 12.9 %collective-permute-start.4 = (bf16[3,384,128]{2,1,0:T(8,128)(2,1)S(1)}, bf16[3,384,128]{2,1,0:T(8,128)(2,1)S(1)}, u32[]{:S(2)}, u32[]{:S(2)}) collective-permute-start(bf16[3,384,128]{2,1,0:T(8,128)(2,1)S(1)} %get-tuple-element.28), channel_id=1, source_target_pairs={{4,0},{5,24},{6,2},{7,26},{8,12},{9,20},{10,14},{11,22},{12,8},{13... | collective-permute-start | bytes 884744 | tf_op jit(solution)/shard_map/ppermute | solution.py:495
  18.3 17.9 %collective-permute-start.5 = (bf16[3,384,128]{2,1,0:T(8,128)(2,1)S(1)}, bf16[3,384,128]{2,1,0:T(8,128)(2,1)S(1)}, u32[]{:S(2)}, u32[]{:S(2)}) collective-permute-start(bf16[3,384,128]{2,1,0:T(8,128)(2,1)S(1)} %get-tuple-element.29), channel_id=1, source_target_pairs={{0,8},{1,16},{2,10},{3,18},{4,12},{5,20},{6,14},{7,22},{8,0},{9,24... | collective-permute-start | bytes 884744 | tf_op jit(solution)/shard_map/ppermute | solution.py:495
  24.2 52.1 %copy-start.2 = (bf16[192,768]{1,0:T(8,128)(2,1)S(1)}, bf16[192,768]{1,0:T(8,128)(2,1)}, u32[]{:S(2)}) copy-start(bf16[192,768]{1,0:T(8,128)(2,1)} %tokens.1) | copy-start | bytes 884740
  24.2 17.4 %collective-permute-start.6 = (bf16[3,384,128]{2,1,0:T(8,128)(2,1)S(1)}, bf16[3,384,128]{2,1,0:T(8,128)(2,1)S(1)}, u32[]{:S(2)}, u32[]{:S(2)}) collective-permute-start(bf16[3,384,128]{2,1,0:T(8,128)(2,1)S(1)} %get-tuple-element.30), channel_id=1, source_target_pairs={{0,12},{1,20},{2,14},{3,22},{4,8},{5,16},{6,10},{7,18},{12,0},{13,... | collective-permute-start | bytes 884744 | tf_op jit(solution)/shard_map/ppermute | solution.py:495
  26.3 18.6 %collective-permute-start.7 = (bf16[3,384,128]{2,1,0:T(8,128)(2,1)S(1)}, bf16[3,384,128]{2,1,0:T(8,128)(2,1)S(1)}, u32[]{:S(2)}, u32[]{:S(2)}) collective-permute-start(bf16[3,384,128]{2,1,0:T(8,128)(2,1)S(1)} %collective-permute-done.3.refs_0_), channel_id=1, source_target_pairs={{0,1},{1,0},{2,3},{3,2},{4,5},{5,4},{6,7},{7,6},{8,9},{9,8},{10,11... | collective-permute-start | bytes 884744 | tf_op jit(solution)/shard_map/ppermute | solution.py:496
  29.9 15.0 %collective-permute-start.8 = (bf16[3,384,128]{2,1,0:T(8,128)(2,1)S(1)}, bf16[3,384,128]{2,1,0:T(8,128)(2,1)S(1)}, u32[]{:S(2)}, u32[]{:S(2)}) collective-permute-start(bf16[3,384,128]{2,1,0:T(8,128)(2,1)S(1)} %collective-permute-done.4.refs_1_), channel_id=1, source_target_pairs={{0,1},{1,0},{2,3},{3,2},{4,5},{5,4},{6,7},{7,6},{8,9},{9,8},{10,11... | collective-permute-start | bytes 884744 | tf_op jit(solution)/shard_map/ppermute | solution.py:496
  36.2 8.7 %collective-permute-start.9 = (bf16[3,384,128]{2,1,0:T(8,128)(2,1)S(1)}, bf16[3,384,128]{2,1,0:T(8,128)(2,1)S(1)}, u32[]{:S(2)}, u32[]{:S(2)}) collective-permute-start(bf16[3,384,128]{2,1,0:T(8,128)(2,1)S(1)} %collective-permute-done.5.refs_2_), channel_id=1, source_target_pairs={{0,1},{1,0},{2,3},{3,2},{4,5},{5,4},{6,7},{7,6},{8,9},{9,8},{10,11... | collective-permute-start | bytes 884744 | tf_op jit(solution)/shard_map/ppermute | solution.py:496
  41.6 4.5 %collective-permute-start.10 = (bf16[3,384,128]{2,1,0:T(8,128)(2,1)S(1)}, bf16[3,384,128]{2,1,0:T(8,128)(2,1)S(1)}, u32[]{:S(2)}, u32[]{:S(2)}) collective-permute-start(bf16[3,384,128]{2,1,0:T(8,128)(2,1)S(1)} %collective-permute-done.6.refs_3_), channel_id=1, source_target_pairs={{0,1},{1,0},{2,3},{3,2},{4,5},{5,4},{6,7},{7,6},{8,9},{9,8},{10,11... | collective-permute-start | bytes 884744 | tf_op jit(solution)/shard_map/ppermute | solution.py:496
  54.2 5.8 %collective-permute-start.11 = (bf16[384,128]{1,0:T(8,128)(2,1)S(1)}, bf16[384,128]{1,0:T(8,128)(2,1)S(1)}, u32[]{:S(2)}, u32[]{:S(2)}) collective-permute-start(bf16[384,128]{1,0:T(8,128)(2,1)S(1)} %get-tuple-element.31), channel_id=1, source_target_pairs={{0,0},{24,1},{2,2},{26,3},{8,8},{16,9},{10,10},{18,11},{12,12},{20... | collective-permute-start | bytes 294920 | tf_op jit(solution)/shard_map/ppermute | solution.py:499
  54.8 5.2 %collective-permute-start.12 = (bf16[384,128]{1,0:T(8,128)(2,1)S(1)}, bf16[384,128]{1,0:T(8,128)(2,1)S(1)}, u32[]{:S(2)}, u32[]{:S(2)}) collective-permute-start(bf16[384,128]{1,0:T(8,128)(2,1)S(1)} %get-tuple-element.32), channel_id=1, source_target_pairs={{0,4},{24,5},{2,6},{26,7},{12,8},{20,9},{14,10},{22,11},{8,12},{16... | collective-permute-start | bytes 294920 | tf_op jit(solution)/shard_map/ppermute | solution.py:499
  56.1 8.1 %collective-permute-start.13 = (bf16[384,128]{1,0:T(8,128)(2,1)S(1)}, bf16[384,128]{1,0:T(8,128)(2,1)S(1)}, u32[]{:S(2)}, u32[]{:S(2)}) collective-permute-start(bf16[384,128]{1,0:T(8,128)(2,1)S(1)} %get-tuple-element.33), channel_id=1, source_target_pairs={{8,0},{16,1},{10,2},{18,3},{12,4},{20,5},{14,6},{22,7},{0,8},{24,9... | collective-permute-start | bytes 294920 | tf_op jit(solution)/shard_map/ppermute | solution.py:499
  58.1 7.4 %collective-permute-start.14 = (bf16[384,128]{1,0:T(8,128)(2,1)S(1)}, bf16[384,128]{1,0:T(8,128)(2,1)S(1)}, u32[]{:S(2)}, u32[]{:S(2)}) collective-permute-start(bf16[384,128]{1,0:T(8,128)(2,1)S(1)} %get-tuple-element.34), channel_id=1, source_target_pairs={{12,0},{20,1},{14,2},{22,3},{8,4},{16,5},{10,6},{18,7},{0,12},{24,... | collective-permute-start | bytes 294920 | tf_op jit(solution)/shard_map/ppermute | solution.py:499
  66.0 5.2 %collective-permute-start.15 = (bf16[3,192,128]{2,1,0:T(8,128)(2,1)S(1)}, bf16[3,192,128]{2,1,0:T(8,128)(2,1)S(1)}, u32[]{:S(2)}, u32[]{:S(2)}) collective-permute-start(bf16[3,192,128]{2,1,0:T(8,128)(2,1)S(1)} %get-tuple-element.36), channel_id=1, source_target_pairs={{0,2},{2,0},{4,6},{6,4},{8,10},{10,8},{12,14},{14,12},{16,18},{18,... | collective-permute-start | bytes 442376 | tf_op jit(solution)/shard_map/ppermute | solution.py:502
  72.0 4.3 %collective-permute-start.16 = (bf16[192,768]{1,0:T(8,128)(2,1)S(1)}, bf16[192,768]{1,0:T(8,128)(2,1)S(1)}, u32[]{:S(2)}, u32[]{:S(2)}) collective-permute-start(bf16[192,768]{1,0:T(8,128)(2,1)S(1)} %get-tuple-element.38), channel_id=1, source_target_pairs={{0,1},{1,0},{2,3},{3,2},{4,5},{5,4},{6,7},{7,6},{8,9},{9,8},{10,11... | collective-permute-start | bytes 884744 | tf_op jit(solution)/shard_map/ppermute | solution.py:503

commit v10 on v9

--- a/solution.py
+++ b/solution.py
@@ -160,15 +160,8 @@
 
 
 def share_kernel(colours, near_ref, far_ref, mod_ref, mine, wq_ref, wk_ref, wv_ref, *rest):
-    outs, (weights, full, normed, packed, load_sems, sems) = rest[:colours], rest[colours:]
+    outs, (full, normed, packed, sems) = rest[:colours], rest[colours:]
     heads, _, rows, _ = mine.shape
-    loads = []
-
-    def load(source, target):
-        loads.append(pltpu.make_async_copy(source, target, load_sems.at[len(loads)]))
-        loads[-1].start()
-
-    load_weights(load, (wq_ref, wk_ref, wv_ref), weights)
     slot, x = place_of(colours)
 
     def each_copy(source, position, offset, act):
@@ -182,10 +175,9 @@
     each_copy(mine, x, 0, lambda copy: copy.start())
     scaled = standardise(full, near_ref, far_ref)
     normed[...] = (scaled * (1.0 + mod_ref[1:2, :]) + mod_ref[0:1, :]).astype(jnp.bfloat16)
-    for part in range(3):
-        loads[2 * part].wait()
-        loads[2 * part + 1].wait()
-        project_part(packed, normed, weights[part], part)
+    columns = pl.ds(pl.multiple_of(x * heads * HEAD_DIM, HEAD_DIM), heads * HEAD_DIM)
+    for part, ref in enumerate((wq_ref, wk_ref, wv_ref)):
+        project_part(packed, normed, ref[:, columns], part)
     each_copy(packed, 1 - x, heads, lambda copy: copy.start())
     each_copy(mine, x, 0, lambda copy: copy.wait())
     each_copy(packed, 1 - x, heads, lambda copy: copy.wait())
@@ -196,18 +188,16 @@
     depth = mod.shape[1]
     return pl.pallas_call(
         functools.partial(share_kernel, colours),
-        in_specs=[vmem_spec()] * 3 + [any_spec()] * 4,
+        in_specs=[vmem_spec()] * 3 + [any_spec()] + [vmem_spec()] * 3,
         out_specs=[any_spec()] * colours,
         out_shape=[jax.ShapeDtypeStruct((3, 2 * rows, HEAD_DIM), jnp.bfloat16)] * colours,
         scratch_shapes=[
-            pltpu.VMEM((3, depth, heads * HEAD_DIM), jnp.bfloat16),
             pltpu.VMEM((rows, depth), jnp.float32),
             pltpu.VMEM((rows, depth), jnp.bfloat16),
             pltpu.VMEM(mine.shape, jnp.bfloat16),
-            pltpu.SemaphoreType.DMA((6,)),
             pltpu.SemaphoreType.DMA((2 * heads,)),
         ],
-        compiler_params=pltpu.CompilerParams(vmem_limit_bytes=STREAM_LIMIT),
+        compiler_params=pltpu.CompilerParams(vmem_limit_bytes=VMEM_LIMIT),
     )(near, far, mod, mine, w_query, w_key, w_value)
 
 

time: 77.8 us -> 76.6 us (0.985)
  Pallas kernels: 17.3 us -> 16.5 us
    pallas_call x1, Pallas kernels: 3.03 us -> 2.1 us  [project_shared(): pl.pallas_call(functools.partial(share_kernel, colours), in_specs=[vmem_s...]
    unnamed x10 -> x14, local copies, waits for them, and re-layouts: 1.71 us -> 2.42 us
where the time goes in v10:
time: 76.6 us; the launch traced here: 76.2 us
  starting transfers between devices  42 us (55%)
  Pallas kernels  16.5 us (22%)
  waiting for transfers between devices  13.7 us (18%)
  local copies, waits for them, and re-layouts  2.42 us (3%)
  between operations  1.53 us (2%)
    ppermute x4, starting transfers between devices, on_device(): swapped = [lax.ppermute(piece, 'tp', swap) for piece in got]  18.7 us
    ppermute x4, starting transfers between devices, on_device(): lax.ppermute(piece, ('req', 'tp'), route)  9.9 us
    pallas_call x1, Pallas kernels, attend(): pl.pallas_call(functools.partial(attend_kernel, colours, heads), in_specs...  8.14 us
    ppermute x4, starting transfers between devices, on_device(): lax.ppermute(piece, ('req', 'tp'), [(b, a) for a, b in route])  5.8 us
    ppermute x4, waiting for transfers between devices, on_device(): lax.ppermute(piece, ('req', 'tp'), [(b, a) for a, b in route])  5.48 us
    pallas_call x1, Pallas kernels, project(): pl.pallas_call(project_kernel, in_specs=[vmem_spec()] * 4 + [any_spec()]...  4.07 us
    ppermute x1, waiting for transfers between devices, on_device(): mine, theirs = combine(keep, lax.ppermute(give, 'req', cross), w_out)  3.7 us
    ppermute x1, starting transfers between devices, on_device(): theirs = lax.ppermute(theirs, 'tp', swap)  3.02 us
  transfers between devices with their start and end apart: 17, of which 7 were waited for; matrix products, arithmetic and copies ran while one was open for 0% of the time, Pallas kernels for 5%

profile of v10, /device:TPU:0, one launch (start us, length us, event | category | flops | bytes accessed | tf_op | source)
XLA Modules:
  0.0 76.2 jit_solution(16775363577417838481)
XLA Ops:
  0.6 0.5 collective-permute-start.1
  1.1 2.6 %collective-permute-start = (bf16[192,768]{1,0:T(8,128)(2,1)}, bf16[192,768]{1,0:T(8,128)(2,1)S(1)}, u32[]{:S(2)}, u32[]{:S(2)}) collective-permute-start(bf16[192,768]{1,0:T(8,128)(2,1)} %tokens.1), channel_id=1, source_target_pairs={{0,2},{2,0},{4,6},{6,4},{8,10},{10,8},{12,14},{14,12},{16,18},{18,... | collective-permute-start | bytes 884744 | tf_op jit(solution)/shard_map/ppermute | solution.py:473
  4.5 0.0 copy-start.2
  4.5 1.1 %copy-done.4 = bf16[192,768]{1,0:T(8,128)(2,1)S(1)} copy-done((bf16[192,768]{1,0:T(8,128)(2,1)S(1)}, bf16[192,768]{1,0:T(8,128)(2,1)}, u32[]{:S(2)}) %copy-start.4) | copy-done | bytes 294936
  5.6 1.3 %copy-done.5 = f32[3,1536]{1,0:T(4,128)S(1)} copy-done((f32[3,1536]{1,0:T(4,128)S(1)}, f32[3,1536]{1,0:T(4,128)}, u32[]{:S(2)}) %copy-start.5) | copy-done | bytes 18456
  6.9 4.1 %shard_map.104 = (bf16[3,3,192,128]{3,2,1,0:T(8,128)(2,1)S(1)}, f32[2,1536]{1,0:T(2,128)S(1)}, f32[1,768]{1,0:T(1,128)S(1)}) custom-call(f32[1,256]{1,0:T(1,128)S(1)} %divide_multiply_fusion.act_ref, f32[3,1536]{1,0:T(4,128)S(1)} %copy-done.5, bf16[192,768]{1,0:T(8,128)(2,1)S(1)} %copy-done.4, bf16[192,768]{1,0:T(8,128)(2,1)S(1)} %collective-permute-done.1.other_ref, ...), custom_call_target="tpu_custom_call" | custom-call | flops 679477248 | bytes 8388608 | tf_op jit(solution)/shard_map/pallas_call | solution.py:141
  11.0 0.5 collective-permute-done.near_ref
  11.5 1.6 %collective-permute-done.2.far_ref = bf16[192,768]{1,0:T(8,128)(2,1)S(1)} collective-permute-done((bf16[192,768]{1,0:T(8,128)(2,1)S(1)}, bf16[192,768]{1,0:T(8,128)(2,1)S(1)}, u32[]{:S(2)}, u32[]{:S(2)}) %collective-permute-start.2) | collective-permute-done | bytes 294944 | tf_op jit(solution)/shard_map/ppermute | solution.py:483
  13.1 2.1 %shard_map.105 = (bf16[3,384,128]{2,1,0:T(8,128)(2,1)S(1)}, bf16[3,384,128]{2,1,0:T(8,128)(2,1)S(1)}, bf16[3,384,128]{2,1,0:T(8,128)(2,1)S(1)}, bf16[3,384,128]{2,1,0:T(8,128)(2,1)S(1)}) custom-call(bf16[192,768]{1,0:T(8,128)(2,1)S(1)} %collective-permute-done.near_ref, bf16[192,768]{1,0:T(8,128)(2,1)S(1)} %collective-permute-done.2.far_ref, ...), custom_call_target="tpu_custom_call" | custom-call | tf_op jit(solution)/shard_map/pallas_call | solution.py:189
  15.2 0.8 %collective-permute-start.3 = (bf16[3,384,128]{2,1,0:T(8,128)(2,1)S(1)}, bf16[3,384,128]{2,1,0:T(8,128)(2,1)S(1)}, u32[]{:S(2)}, u32[]{:S(2)}) collective-permute-start(bf16[3,384,128]{2,1,0:T(8,128)(2,1)S(1)} %get-tuple-element.27), channel_id=1, source_target_pairs={{0,0},{1,24},{2,2},{3,26},{8,8},{9,16},{10,10},{11,18},{12,12},{13... | collective-permute-start | bytes 884744 | tf_op jit(solution)/shard_map/ppermute | solution.py:485
  16.1 1.3 %collective-permute-start.4 = (bf16[3,384,128]{2,1,0:T(8,128)(2,1)S(1)}, bf16[3,384,128]{2,1,0:T(8,128)(2,1)S(1)}, u32[]{:S(2)}, u32[]{:S(2)}) collective-permute-start(bf16[3,384,128]{2,1,0:T(8,128)(2,1)S(1)} %get-tuple-element.28), channel_id=1, source_target_pairs={{4,0},{5,24},{6,2},{7,26},{8,12},{9,20},{10,14},{11,22},{12,8},{13... | collective-permute-start | bytes 884744 | tf_op jit(solution)/shard_map/ppermute | solution.py:485
  17.4 5.9 %collective-permute-start.5 = (bf16[3,384,128]{2,1,0:T(8,128)(2,1)S(1)}, bf16[3,384,128]{2,1,0:T(8,128)(2,1)S(1)}, u32[]{:S(2)}, u32[]{:S(2)}) collective-permute-start(bf16[3,384,128]{2,1,0:T(8,128)(2,1)S(1)} %get-tuple-element.29), channel_id=1, source_target_pairs={{0,8},{1,16},{2,10},{3,18},{4,12},{5,20},{6,14},{7,22},{8,0},{9,24... | collective-permute-start | bytes 884744 | tf_op jit(solution)/shard_map/ppermute | solution.py:485
  23.2 1.9 %collective-permute-start.6 = (bf16[3,384,128]{2,1,0:T(8,128)(2,1)S(1)}, bf16[3,384,128]{2,1,0:T(8,128)(2,1)S(1)}, u32[]{:S(2)}, u32[]{:S(2)}) collective-permute-start(bf16[3,384,128]{2,1,0:T(8,128)(2,1)S(1)} %get-tuple-element.30), channel_id=1, source_target_pairs={{0,12},{1,20},{2,14},{3,22},{4,8},{5,16},{6,10},{7,18},{12,0},{13,... | collective-permute-start | bytes 884744 | tf_op jit(solution)/shard_map/ppermute | solution.py:485
  25.2 3.6 %collective-permute-start.7 = (bf16[3,384,128]{2,1,0:T(8,128)(2,1)S(1)}, bf16[3,384,128]{2,1,0:T(8,128)(2,1)S(1)}, u32[]{:S(2)}, u32[]{:S(2)}) collective-permute-start(bf16[3,384,128]{2,1,0:T(8,128)(2,1)S(1)} %collective-permute-done.3.refs_0_), channel_id=1, source_target_pairs={{0,1},{1,0},{2,3},{3,2},{4,5},{5,4},{6,7},{7,6},{8,9},{9,8},{10,11... | collective-permute-start | bytes 884744 | tf_op jit(solution)/shard_map/ppermute | solution.py:486
  28.8 6.5 %collective-permute-start.8 = (bf16[3,384,128]{2,1,0:T(8,128)(2,1)S(1)}, bf16[3,384,128]{2,1,0:T(8,128)(2,1)S(1)}, u32[]{:S(2)}, u32[]{:S(2)}) collective-permute-start(bf16[3,384,128]{2,1,0:T(8,128)(2,1)S(1)} %collective-permute-done.4.refs_1_), channel_id=1, source_target_pairs={{0,1},{1,0},{2,3},{3,2},{4,5},{5,4},{6,7},{7,6},{8,9},{9,8},{10,11... | collective-permute-start | bytes 884744 | tf_op jit(solution)/shard_map/ppermute | solution.py:486
  35.3 5.3 %collective-permute-start.9 = (bf16[3,384,128]{2,1,0:T(8,128)(2,1)S(1)}, bf16[3,384,128]{2,1,0:T(8,128)(2,1)S(1)}, u32[]{:S(2)}, u32[]{:S(2)}) collective-permute-start(bf16[3,384,128]{2,1,0:T(8,128)(2,1)S(1)} %collective-permute-done.5.refs_2_), channel_id=1, source_target_pairs={{0,1},{1,0},{2,3},{3,2},{4,5},{5,4},{6,7},{7,6},{8,9},{9,8},{10,11... | collective-permute-start | bytes 884744 | tf_op jit(solution)/shard_map/ppermute | solution.py:486
  40.6 3.3 %collective-permute-start.10 = (bf16[3,384,128]{2,1,0:T(8,128)(2,1)S(1)}, bf16[3,384,128]{2,1,0:T(8,128)(2,1)S(1)}, u32[]{:S(2)}, u32[]{:S(2)}) collective-permute-start(bf16[3,384,128]{2,1,0:T(8,128)(2,1)S(1)} %collective-permute-done.6.refs_3_), channel_id=1, source_target_pairs={{0,1},{1,0},{2,3},{3,2},{4,5},{5,4},{6,7},{7,6},{8,9},{9,8},{10,11... | collective-permute-start | bytes 884744 | tf_op jit(solution)/shard_map/ppermute | solution.py:486
  43.9 1.2 %collective-permute-done.10.refs_7_ = bf16[3,384,128]{2,1,0:T(8,128)(2,1)S(1)} collective-permute-done((bf16[3,384,128]{2,1,0:T(8,128)(2,1)S(1)}, bf16[3,384,128]{2,1,0:T(8,128)(2,1)S(1)}, u32[]{:S(2)}, u32[]{:S(2)}) %collective-permute-start.10) | collective-permute-done | bytes 294944 | tf_op jit(solution)/shard_map/ppermute | solution.py:486
  45.1 8.1 %shard_map.106 = (bf16[384,128]{1,0:T(8,128)(2,1)S(1)}, bf16[384,128]{1,0:T(8,128)(2,1)S(1)}, bf16[384,128]{1,0:T(8,128)(2,1)S(1)}, bf16[384,128]{1,0:T(8,128)(2,1)S(1)}) custom-call(s32[5]{0:T(128)S(1)} %copy-done.6, bf16[3,384,128]{2,1,0:T(8,128)(2,1)S(1)} %collective-permute-done.3.refs_0_, bf16[3,384,128]{2,1,0:T(8,128)(2,1)S(1)} %collective-permute-done.4.refs_1_, ...), custom_call_target="tpu_custom_call" | custom-call | tf_op jit(solution)/shard_map/pallas_call | solution.py:356
  53.2 0.7 collective-permute-start.11
  53.9 1.3 %collective-permute-start.12 = (bf16[384,128]{1,0:T(8,128)(2,1)S(1)}, bf16[384,128]{1,0:T(8,128)(2,1)S(1)}, u32[]{:S(2)}, u32[]{:S(2)}) collective-permute-start(bf16[384,128]{1,0:T(8,128)(2,1)S(1)} %get-tuple-element.32), channel_id=1, source_target_pairs={{0,4},{24,5},{2,6},{26,7},{12,8},{20,9},{14,10},{22,11},{8,12},{16... | collective-permute-start | bytes 294920 | tf_op jit(solution)/shard_map/ppermute | solution.py:489
  55.2 1.9 %collective-permute-start.13 = (bf16[384,128]{1,0:T(8,128)(2,1)S(1)}, bf16[384,128]{1,0:T(8,128)(2,1)S(1)}, u32[]{:S(2)}, u32[]{:S(2)}) collective-permute-start(bf16[384,128]{1,0:T(8,128)(2,1)S(1)} %get-tuple-element.33), channel_id=1, source_target_pairs={{8,0},{16,1},{10,2},{18,3},{12,4},{20,5},{14,6},{22,7},{0,8},{24,9... | collective-permute-start | bytes 294920 | tf_op jit(solution)/shard_map/ppermute | solution.py:489
  57.1 1.9 %collective-permute-start.14 = (bf16[384,128]{1,0:T(8,128)(2,1)S(1)}, bf16[384,128]{1,0:T(8,128)(2,1)S(1)}, u32[]{:S(2)}, u32[]{:S(2)}) collective-permute-start(bf16[384,128]{1,0:T(8,128)(2,1)S(1)} %get-tuple-element.34), channel_id=1, source_target_pairs={{12,0},{20,1},{14,2},{22,3},{8,4},{16,5},{10,6},{18,7},{0,12},{24,... | collective-permute-start | bytes 294920 | tf_op jit(solution)/shard_map/ppermute | solution.py:489
  59.1 5.3 %collective-permute-done.13.refs_2_ = bf16[384,128]{1,0:T(8,128)(2,1)S(1)} collective-permute-done((bf16[384,128]{1,0:T(8,128)(2,1)S(1)}, bf16[384,128]{1,0:T(8,128)(2,1)S(1)}, u32[]{:S(2)}, u32[]{:S(2)}) %collective-permute-start.13) | collective-permute-done | bytes 98336 | tf_op jit(solution)/shard_map/ppermute | solution.py:489
  64.4 0.2 collective-permute-done.14.refs_3_
  64.6 0.5 shard_map.107
  65.1 1.5 %collective-permute-start.15 = (bf16[3,192,128]{2,1,0:T(8,128)(2,1)S(1)}, bf16[3,192,128]{2,1,0:T(8,128)(2,1)S(1)}, u32[]{:S(2)}, u32[]{:S(2)}) collective-permute-start(bf16[3,192,128]{2,1,0:T(8,128)(2,1)S(1)} %get-tuple-element.36), channel_id=1, source_target_pairs={{0,2},{2,0},{4,6},{6,4},{8,10},{10,8},{12,14},{14,12},{16,18},{18,... | collective-permute-start | bytes 442376 | tf_op jit(solution)/shard_map/ppermute | solution.py:492
  66.6 3.7 %collective-permute-done.15.got_ref = bf16[3,192,128]{2,1,0:T(8,128)(2,1)S(1)} collective-permute-done((bf16[3,192,128]{2,1,0:T(8,128)(2,1)S(1)}, bf16[3,192,128]{2,1,0:T(8,128)(2,1)S(1)}, u32[]{:S(2)}, u32[]{:S(2)}) %collective-permute-start.15) | collective-permute-done | bytes 147488 | tf_op jit(solution)/shard_map/ppermute | solution.py:492
  70.3 0.8 shard_map.108
  71.1 3.0 %collective-permute-start.16 = (bf16[192,768]{1,0:T(8,128)(2,1)S(1)}, bf16[192,768]{1,0:T(8,128)(2,1)S(1)}, u32[]{:S(2)}, u32[]{:S(2)}) collective-permute-start(bf16[192,768]{1,0:T(8,128)(2,1)S(1)} %get-tuple-element.38), channel_id=1, source_target_pairs={{0,1},{1,0},{2,3},{3,2},{4,5},{5,4},{6,7},{7,6},{8,9},{9,8},{10,11... | collective-permute-start | bytes 884744 | tf_op jit(solution)/shard_map/ppermute | solution.py:493
  74.1 1.2 %collective-permute-done.16.theirs = bf16[192,768]{1,0:T(8,128)(2,1)S(1)} collective-permute-done((bf16[192,768]{1,0:T(8,128)(2,1)S(1)}, bf16[192,768]{1,0:T(8,128)(2,1)S(1)}, u32[]{:S(2)}, u32[]{:S(2)}) %collective-permute-start.16) | collective-permute-done | bytes 294944 | tf_op jit(solution)/shard_map/ppermute | solution.py:493
  75.3 0.9 %shard_map.109 = (bf16[192,768]{1,0:T(8,128)(2,1)}, bf16[192,768]{1,0:T(8,128)(2,1)}) custom-call(s32[1]{0:T(128)S(6)} %copy.11.timestep_ref, f32[192,768]{1,0:T(8,128)S(1)} %get-tuple-element.37.mine, bf16[192,768]{1,0:T(8,128)(2,1)S(1)} %collective-permute-done.16.theirs, bf16[192,768]{1,0:T(8,128)(2,1)S(1)} %copy-done.4, ...), custom_call_target="tpu_custom_call" | custom-call | tf_op jit(solution)/shard_map/pallas_call | solution.py:455
  (24 shorter events, 0.1 us)
Async XLA Ops:
  0.6 3.9 %collective-permute-start.1 = (bf16[192,768]{1,0:T(8,128)(2,1)}, bf16[192,768]{1,0:T(8,128)(2,1)S(1)}, u32[]{:S(2)}, u32[]{:S(2)}) collective-permute-start(bf16[192,768]{1,0:T(8,128)(2,1)} %tokens.1), channel_id=1, source_target_pairs={{0,1},{1,0},{2,3},{3,2},{4,5},{5,4},{6,7},{7,6},{8,9},{9,8},{10,11... | collective-permute-start | bytes 884744 | tf_op jit(solution)/shard_map/ppermute | solution.py:474
  1.1 10.4 %collective-permute-start = (bf16[192,768]{1,0:T(8,128)(2,1)}, bf16[192,768]{1,0:T(8,128)(2,1)S(1)}, u32[]{:S(2)}, u32[]{:S(2)}) collective-permute-start(bf16[192,768]{1,0:T(8,128)(2,1)} %tokens.1), channel_id=1, source_target_pairs={{0,2},{2,0},{4,6},{6,4},{8,10},{10,8},{12,14},{14,12},{16,18},{18,... | collective-permute-start | bytes 884744 | tf_op jit(solution)/shard_map/ppermute | solution.py:473
  4.5 8.6 %copy-start = (bf16[1536,768]{1,0:T(8,128)(2,1)S(1)}, bf16[1536,768]{1,0:T(8,128)(2,1)}, u32[]{:S(2)}) copy-start(bf16[1536,768]{1,0:T(8,128)(2,1)} %wq_ref.3) | copy-start | bytes 7077892
  4.5 8.6 %copy-start.1 = (bf16[1536,768]{1,0:T(8,128)(2,1)S(1)}, bf16[1536,768]{1,0:T(8,128)(2,1)}, u32[]{:S(2)}) copy-start(bf16[1536,768]{1,0:T(8,128)(2,1)} %wk_ref.3) | copy-start | bytes 7077892
  4.5 8.6 %copy-start.2 = (bf16[1536,768]{1,0:T(8,128)(2,1)S(1)}, bf16[1536,768]{1,0:T(8,128)(2,1)}, u32[]{:S(2)}) copy-start(bf16[1536,768]{1,0:T(8,128)(2,1)} %wv_ref.3) | copy-start | bytes 7077892
  4.5 1.1 %copy-start.4 = (bf16[192,768]{1,0:T(8,128)(2,1)S(1)}, bf16[192,768]{1,0:T(8,128)(2,1)}, u32[]{:S(2)}) copy-start(bf16[192,768]{1,0:T(8,128)(2,1)} %tokens.1) | copy-start | bytes 884740
  5.6 1.3 %copy-start.5 = (f32[3,1536]{1,0:T(4,128)S(1)}, f32[3,1536]{1,0:T(4,128)}, u32[]{:S(2)}) copy-start(f32[3,1536]{1,0:T(4,128)} %block_ref.1) | copy-start | bytes 55300
  11.5 33.6 %copy-start.6 = (s32[5]{0:T(128)S(1)}, s32[5]{0:T(128)}, u32[]{:S(2)}) copy-start(s32[5]{0:T(128)} %lengths_ref.1) | copy-start | bytes 64
  11.5 1.6 %collective-permute-start.2 = (bf16[192,768]{1,0:T(8,128)(2,1)S(1)}, bf16[192,768]{1,0:T(8,128)(2,1)S(1)}, u32[]{:S(2)}, u32[]{:S(2)}) collective-permute-start(bf16[192,768]{1,0:T(8,128)(2,1)S(1)} %collective-permute-done.near_ref), channel_id=1, source_target_pairs={{0,1},{1,0},{2,3},{3,2},{4,5},{5,4},{6,7},{7,6},{8,9},{9,8},{10,11... | collective-permute-start | bytes 884744 | tf_op jit(solution)/shard_map/ppermute | solution.py:483
  15.2 55.1 %copy-start.3 = (bf16[768,1536]{1,0:T(8,128)(2,1)S(1)}, bf16[768,1536]{1,0:T(8,128)(2,1)}, u32[]{:S(2)}) copy-start(bf16[768,1536]{1,0:T(8,128)(2,1)} %weight.1) | copy-start | bytes 7077892
  15.2 9.9 %collective-permute-start.3 = (bf16[3,384,128]{2,1,0:T(8,128)(2,1)S(1)}, bf16[3,384,128]{2,1,0:T(8,128)(2,1)S(1)}, u32[]{:S(2)}, u32[]{:S(2)}) collective-permute-start(bf16[3,384,128]{2,1,0:T(8,128)(2,1)S(1)} %get-tuple-element.27), channel_id=1, source_target_pairs={{0,0},{1,24},{2,2},{3,26},{8,8},{9,16},{10,10},{11,18},{12,12},{13... | collective-permute-start | bytes 884744 | tf_op jit(solution)/shard_map/ppermute | solution.py:485
  16.1 12.7 %collective-permute-start.4 = (bf16[3,384,128]{2,1,0:T(8,128)(2,1)S(1)}, bf16[3,384,128]{2,1,0:T(8,128)(2,1)S(1)}, u32[]{:S(2)}, u32[]{:S(2)}) collective-permute-start(bf16[3,384,128]{2,1,0:T(8,128)(2,1)S(1)} %get-tuple-element.28), channel_id=1, source_target_pairs={{4,0},{5,24},{6,2},{7,26},{8,12},{9,20},{10,14},{11,22},{12,8},{13... | collective-permute-start | bytes 884744 | tf_op jit(solution)/shard_map/ppermute | solution.py:485
  17.4 17.9 %collective-permute-start.5 = (bf16[3,384,128]{2,1,0:T(8,128)(2,1)S(1)}, bf16[3,384,128]{2,1,0:T(8,128)(2,1)S(1)}, u32[]{:S(2)}, u32[]{:S(2)}) collective-permute-start(bf16[3,384,128]{2,1,0:T(8,128)(2,1)S(1)} %get-tuple-element.29), channel_id=1, source_target_pairs={{0,8},{1,16},{2,10},{3,18},{4,12},{5,20},{6,14},{7,22},{8,0},{9,24... | collective-permute-start | bytes 884744 | tf_op jit(solution)/shard_map/ppermute | solution.py:485
  23.2 17.4 %collective-permute-start.6 = (bf16[3,384,128]{2,1,0:T(8,128)(2,1)S(1)}, bf16[3,384,128]{2,1,0:T(8,128)(2,1)S(1)}, u32[]{:S(2)}, u32[]{:S(2)}) collective-permute-start(bf16[3,384,128]{2,1,0:T(8,128)(2,1)S(1)} %get-tuple-element.30), channel_id=1, source_target_pairs={{0,12},{1,20},{2,14},{3,22},{4,8},{5,16},{6,10},{7,18},{12,0},{13,... | collective-permute-start | bytes 884744 | tf_op jit(solution)/shard_map/ppermute | solution.py:485
  25.2 18.7 %collective-permute-start.7 = (bf16[3,384,128]{2,1,0:T(8,128)(2,1)S(1)}, bf16[3,384,128]{2,1,0:T(8,128)(2,1)S(1)}, u32[]{:S(2)}, u32[]{:S(2)}) collective-permute-start(bf16[3,384,128]{2,1,0:T(8,128)(2,1)S(1)} %collective-permute-done.3.refs_0_), channel_id=1, source_target_pairs={{0,1},{1,0},{2,3},{3,2},{4,5},{5,4},{6,7},{7,6},{8,9},{9,8},{10,11... | collective-permute-start | bytes 884744 | tf_op jit(solution)/shard_map/ppermute | solution.py:486
  28.8 15.1 %collective-permute-start.8 = (bf16[3,384,128]{2,1,0:T(8,128)(2,1)S(1)}, bf16[3,384,128]{2,1,0:T(8,128)(2,1)S(1)}, u32[]{:S(2)}, u32[]{:S(2)}) collective-permute-start(bf16[3,384,128]{2,1,0:T(8,128)(2,1)S(1)} %collective-permute-done.4.refs_1_), channel_id=1, source_target_pairs={{0,1},{1,0},{2,3},{3,2},{4,5},{5,4},{6,7},{7,6},{8,9},{9,8},{10,11... | collective-permute-start | bytes 884744 | tf_op jit(solution)/shard_map/ppermute | solution.py:486
  35.3 8.6 %collective-permute-start.9 = (bf16[3,384,128]{2,1,0:T(8,128)(2,1)S(1)}, bf16[3,384,128]{2,1,0:T(8,128)(2,1)S(1)}, u32[]{:S(2)}, u32[]{:S(2)}) collective-permute-start(bf16[3,384,128]{2,1,0:T(8,128)(2,1)S(1)} %collective-permute-done.5.refs_2_), channel_id=1, source_target_pairs={{0,1},{1,0},{2,3},{3,2},{4,5},{5,4},{6,7},{7,6},{8,9},{9,8},{10,11... | collective-permute-start | bytes 884744 | tf_op jit(solution)/shard_map/ppermute | solution.py:486
  40.6 4.5 %collective-permute-start.10 = (bf16[3,384,128]{2,1,0:T(8,128)(2,1)S(1)}, bf16[3,384,128]{2,1,0:T(8,128)(2,1)S(1)}, u32[]{:S(2)}, u32[]{:S(2)}) collective-permute-start(bf16[3,384,128]{2,1,0:T(8,128)(2,1)S(1)} %collective-permute-done.6.refs_3_), channel_id=1, source_target_pairs={{0,1},{1,0},{2,3},{3,2},{4,5},{5,4},{6,7},{7,6},{8,9},{9,8},{10,11... | collective-permute-start | bytes 884744 | tf_op jit(solution)/shard_map/ppermute | solution.py:486
  53.2 5.8 %collective-permute-start.11 = (bf16[384,128]{1,0:T(8,128)(2,1)S(1)}, bf16[384,128]{1,0:T(8,128)(2,1)S(1)}, u32[]{:S(2)}, u32[]{:S(2)}) collective-permute-start(bf16[384,128]{1,0:T(8,128)(2,1)S(1)} %get-tuple-element.31), channel_id=1, source_target_pairs={{0,0},{24,1},{2,2},{26,3},{8,8},{16,9},{10,10},{18,11},{12,12},{20... | collective-permute-start | bytes 294920 | tf_op jit(solution)/shard_map/ppermute | solution.py:489
  53.9 5.2 %collective-permute-start.12 = (bf16[384,128]{1,0:T(8,128)(2,1)S(1)}, bf16[384,128]{1,0:T(8,128)(2,1)S(1)}, u32[]{:S(2)}, u32[]{:S(2)}) collective-permute-start(bf16[384,128]{1,0:T(8,128)(2,1)S(1)} %get-tuple-element.32), channel_id=1, source_target_pairs={{0,4},{24,5},{2,6},{26,7},{12,8},{20,9},{14,10},{22,11},{8,12},{16... | collective-permute-start | bytes 294920 | tf_op jit(solution)/shard_map/ppermute | solution.py:489
  55.2 9.1 %collective-permute-start.13 = (bf16[384,128]{1,0:T(8,128)(2,1)S(1)}, bf16[384,128]{1,0:T(8,128)(2,1)S(1)}, u32[]{:S(2)}, u32[]{:S(2)}) collective-permute-start(bf16[384,128]{1,0:T(8,128)(2,1)S(1)} %get-tuple-element.33), channel_id=1, source_target_pairs={{8,0},{16,1},{10,2},{18,3},{12,4},{20,5},{14,6},{22,7},{0,8},{24,9... | collective-permute-start | bytes 294920 | tf_op jit(solution)/shard_map/ppermute | solution.py:489
  57.1 7.4 %collective-permute-start.14 = (bf16[384,128]{1,0:T(8,128)(2,1)S(1)}, bf16[384,128]{1,0:T(8,128)(2,1)S(1)}, u32[]{:S(2)}, u32[]{:S(2)}) collective-permute-start(bf16[384,128]{1,0:T(8,128)(2,1)S(1)} %get-tuple-element.34), channel_id=1, source_target_pairs={{12,0},{20,1},{14,2},{22,3},{8,4},{16,5},{10,6},{18,7},{0,12},{24,... | collective-permute-start | bytes 294920 | tf_op jit(solution)/shard_map/ppermute | solution.py:489
  65.1 5.2 %collective-permute-start.15 = (bf16[3,192,128]{2,1,0:T(8,128)(2,1)S(1)}, bf16[3,192,128]{2,1,0:T(8,128)(2,1)S(1)}, u32[]{:S(2)}, u32[]{:S(2)}) collective-permute-start(bf16[3,192,128]{2,1,0:T(8,128)(2,1)S(1)} %get-tuple-element.36), channel_id=1, source_target_pairs={{0,2},{2,0},{4,6},{6,4},{8,10},{10,8},{12,14},{14,12},{16,18},{18,... | collective-permute-start | bytes 442376 | tf_op jit(solution)/shard_map/ppermute | solution.py:492
  71.1 4.2 %collective-permute-start.16 = (bf16[192,768]{1,0:T(8,128)(2,1)S(1)}, bf16[192,768]{1,0:T(8,128)(2,1)S(1)}, u32[]{:S(2)}, u32[]{:S(2)}) collective-permute-start(bf16[192,768]{1,0:T(8,128)(2,1)S(1)} %get-tuple-element.38), channel_id=1, source_target_pairs={{0,1},{1,0},{2,3},{3,2},{4,5},{5,4},{6,7},{7,6},{8,9},{9,8},{10,11... | collective-permute-start | bytes 884744 | tf_op jit(solution)/shard_map/ppermute | solution.py:493

commit v11 on v10

--- a/solution.py
+++ b/solution.py
@@ -12,7 +12,8 @@
 STEPS = 1000
 QUERY_BLOCK = 384
 KEY_GROUP = 3072
-WINDOWS = (512, 1024, 1536, 2048, 2560)
+WINDOWS = (1280, 2048, 2560)
+PARTS = 3
 NEG = -1e30
 STREAM_LIMIT = 51 * 1024 * 1024
 VMEM_LIMIT = 32 * 1024 * 1024
@@ -265,7 +266,7 @@
         lax.fori_loop(0, all_rows // HEAD_DIM, fill_keys, 0)
         each_copy(lambda copy: copy.wait())
 
-        sub = QUERY_BLOCK // 2
+        sub = QUERY_BLOCK // PARTS
 
         def query_block(block, carry):
             local = pl.multiple_of(block * QUERY_BLOCK, QUERY_BLOCK)
@@ -363,8 +364,8 @@
             pltpu.VMEM((2 * own, 2 * HEAD_DIM), jnp.bfloat16),
             pltpu.VMEM((2 * own, 2 * HEAD_DIM), jnp.bfloat16),
             pltpu.VMEM((own, HEAD_DIM), jnp.bfloat16),
-            pltpu.VMEM((QUERY_BLOCK // 2, HEAD_DIM), jnp.float32),
-            pltpu.VMEM((QUERY_BLOCK // 2, 2 * HEAD_DIM), jnp.float32),
+            pltpu.VMEM((QUERY_BLOCK // PARTS, HEAD_DIM), jnp.float32),
+            pltpu.VMEM((QUERY_BLOCK // PARTS, 2 * HEAD_DIM), jnp.float32),
             pltpu.SemaphoreType.DMA((5 * colours,)),
             pltpu.SemaphoreType.DMA((colours,)),
         ],

time: 76.6 us -> 78 us (1.018)
  Pallas kernels: 16.5 us -> 17.9 us
    pallas_call x1, Pallas kernels: 8.14 us -> 9.56 us  [attend(): pl.pallas_call(functools.partial(attend_kernel, colours, heads), in_specs...]
  transfers between devices with their start and end apart: 17 -> 17, of which waited for: 7 -> 6; matrix products, arithmetic and copies ran while one was open for 0% -> 0% of each run, Pallas kernels for 5% -> 5%
where the time goes in v11:
time: 78 us; the launch traced here: 77.6 us
  starting transfers between devices  42 us (54%)
  Pallas kernels  17.9 us (23%)
  waiting for transfers between devices  13.7 us (18%)
  local copies, waits for them, and re-layouts  2.42 us (3%)
  between operations  1.53 us (2%)
    ppermute x4, starting transfers between devices, on_device(): swapped = [lax.ppermute(piece, 'tp', swap) for piece in got]  18.7 us
    ppermute x4, starting transfers between devices, on_device(): lax.ppermute(piece, ('req', 'tp'), route)  9.9 us
    pallas_call x1, Pallas kernels, attend(): pl.pallas_call(functools.partial(attend_kernel, colours, heads), in_specs...  9.56 us
    ppermute x4, starting transfers between devices, on_device(): lax.ppermute(piece, ('req', 'tp'), [(b, a) for a, b in route])  5.8 us
    ppermute x4, waiting for transfers between devices, on_device(): lax.ppermute(piece, ('req', 'tp'), [(b, a) for a, b in route])  5.48 us
    pallas_call x1, Pallas kernels, project(): pl.pallas_call(project_kernel, in_specs=[vmem_spec()] * 4 + [any_spec()]...  4.07 us
    ppermute x1, waiting for transfers between devices, on_device(): mine, theirs = combine(keep, lax.ppermute(give, 'req', cross), w_out)  3.69 us
    ppermute x1, starting transfers between devices, on_device(): theirs = lax.ppermute(theirs, 'tp', swap)  3.01 us
  transfers between devices with their start and end apart: 17, of which 6 were waited for; matrix products, arithmetic and copies ran while one was open for 0% of the time, Pallas kernels for 5%

profile of v11, /device:TPU:0, one launch (start us, length us, event | category | flops | bytes accessed | tf_op | source)
XLA Modules:
  0.0 77.6 jit_solution(10530836029022077707)
XLA Ops:
  0.6 0.5 collective-permute-start.1
  1.1 2.6 %collective-permute-start = (bf16[192,768]{1,0:T(8,128)(2,1)}, bf16[192,768]{1,0:T(8,128)(2,1)S(1)}, u32[]{:S(2)}, u32[]{:S(2)}) collective-permute-start(bf16[192,768]{1,0:T(8,128)(2,1)} %tokens.1), channel_id=1, source_target_pairs={{0,2},{2,0},{4,6},{6,4},{8,10},{10,8},{12,14},{14,12},{16,18},{18,... | collective-permute-start | bytes 884744 | tf_op jit(solution)/shard_map/ppermute | solution.py:474
  4.5 0.0 copy-start.1
  4.5 1.1 %copy-done.4 = bf16[192,768]{1,0:T(8,128)(2,1)S(1)} copy-done((bf16[192,768]{1,0:T(8,128)(2,1)S(1)}, bf16[192,768]{1,0:T(8,128)(2,1)}, u32[]{:S(2)}) %copy-start.4) | copy-done | bytes 294936
  5.6 1.3 %copy-done.5 = f32[3,1536]{1,0:T(4,128)S(1)} copy-done((f32[3,1536]{1,0:T(4,128)S(1)}, f32[3,1536]{1,0:T(4,128)}, u32[]{:S(2)}) %copy-start.5) | copy-done | bytes 18456
  6.9 4.1 %shard_map.104 = (bf16[3,3,192,128]{3,2,1,0:T(8,128)(2,1)S(1)}, f32[2,1536]{1,0:T(2,128)S(1)}, f32[1,768]{1,0:T(1,128)S(1)}) custom-call(f32[1,256]{1,0:T(1,128)S(1)} %divide_multiply_fusion.act_ref, f32[3,1536]{1,0:T(4,128)S(1)} %copy-done.5, bf16[192,768]{1,0:T(8,128)(2,1)S(1)} %copy-done.4, bf16[192,768]{1,0:T(8,128)(2,1)S(1)} %collective-permute-done.1.other_ref, ...), custom_call_target="tpu_custom_call" | custom-call | flops 679477248 | bytes 8388608 | tf_op jit(solution)/shard_map/pallas_call | solution.py:142
  11.0 0.5 collective-permute-done.near_ref
  11.5 1.6 %collective-permute-done.2.far_ref = bf16[192,768]{1,0:T(8,128)(2,1)S(1)} collective-permute-done((bf16[192,768]{1,0:T(8,128)(2,1)S(1)}, bf16[192,768]{1,0:T(8,128)(2,1)S(1)}, u32[]{:S(2)}, u32[]{:S(2)}) %collective-permute-start.2) | collective-permute-done | bytes 294944 | tf_op jit(solution)/shard_map/ppermute | solution.py:484
  13.1 2.1 %shard_map.105 = (bf16[3,384,128]{2,1,0:T(8,128)(2,1)S(1)}, bf16[3,384,128]{2,1,0:T(8,128)(2,1)S(1)}, bf16[3,384,128]{2,1,0:T(8,128)(2,1)S(1)}, bf16[3,384,128]{2,1,0:T(8,128)(2,1)S(1)}) custom-call(bf16[192,768]{1,0:T(8,128)(2,1)S(1)} %collective-permute-done.near_ref, bf16[192,768]{1,0:T(8,128)(2,1)S(1)} %collective-permute-done.2.far_ref, ...), custom_call_target="tpu_custom_call" | custom-call | tf_op jit(solution)/shard_map/pallas_call | solution.py:190
  15.2 0.8 %collective-permute-start.3 = (bf16[3,384,128]{2,1,0:T(8,128)(2,1)S(1)}, bf16[3,384,128]{2,1,0:T(8,128)(2,1)S(1)}, u32[]{:S(2)}, u32[]{:S(2)}) collective-permute-start(bf16[3,384,128]{2,1,0:T(8,128)(2,1)S(1)} %get-tuple-element.27), channel_id=1, source_target_pairs={{0,0},{1,24},{2,2},{3,26},{8,8},{9,16},{10,10},{11,18},{12,12},{13... | collective-permute-start | bytes 884744 | tf_op jit(solution)/shard_map/ppermute | solution.py:486
  16.1 1.3 %collective-permute-start.4 = (bf16[3,384,128]{2,1,0:T(8,128)(2,1)S(1)}, bf16[3,384,128]{2,1,0:T(8,128)(2,1)S(1)}, u32[]{:S(2)}, u32[]{:S(2)}) collective-permute-start(bf16[3,384,128]{2,1,0:T(8,128)(2,1)S(1)} %get-tuple-element.28), channel_id=1, source_target_pairs={{4,0},{5,24},{6,2},{7,26},{8,12},{9,20},{10,14},{11,22},{12,8},{13... | collective-permute-start | bytes 884744 | tf_op jit(solution)/shard_map/ppermute | solution.py:486
  17.4 5.9 %collective-permute-start.5 = (bf16[3,384,128]{2,1,0:T(8,128)(2,1)S(1)}, bf16[3,384,128]{2,1,0:T(8,128)(2,1)S(1)}, u32[]{:S(2)}, u32[]{:S(2)}) collective-permute-start(bf16[3,384,128]{2,1,0:T(8,128)(2,1)S(1)} %get-tuple-element.29), channel_id=1, source_target_pairs={{0,8},{1,16},{2,10},{3,18},{4,12},{5,20},{6,14},{7,22},{8,0},{9,24... | collective-permute-start | bytes 884744 | tf_op jit(solution)/shard_map/ppermute | solution.py:486
  23.2 1.9 %collective-permute-start.6 = (bf16[3,384,128]{2,1,0:T(8,128)(2,1)S(1)}, bf16[3,384,128]{2,1,0:T(8,128)(2,1)S(1)}, u32[]{:S(2)}, u32[]{:S(2)}) collective-permute-start(bf16[3,384,128]{2,1,0:T(8,128)(2,1)S(1)} %get-tuple-element.30), channel_id=1, source_target_pairs={{0,12},{1,20},{2,14},{3,22},{4,8},{5,16},{6,10},{7,18},{12,0},{13,... | collective-permute-start | bytes 884744 | tf_op jit(solution)/shard_map/ppermute | solution.py:486
  25.2 3.6 %collective-permute-start.7 = (bf16[3,384,128]{2,1,0:T(8,128)(2,1)S(1)}, bf16[3,384,128]{2,1,0:T(8,128)(2,1)S(1)}, u32[]{:S(2)}, u32[]{:S(2)}) collective-permute-start(bf16[3,384,128]{2,1,0:T(8,128)(2,1)S(1)} %collective-permute-done.3.refs_0_), channel_id=1, source_target_pairs={{0,1},{1,0},{2,3},{3,2},{4,5},{5,4},{6,7},{7,6},{8,9},{9,8},{10,11... | collective-permute-start | bytes 884744 | tf_op jit(solution)/shard_map/ppermute | solution.py:487
  28.8 6.5 %collective-permute-start.8 = (bf16[3,384,128]{2,1,0:T(8,128)(2,1)S(1)}, bf16[3,384,128]{2,1,0:T(8,128)(2,1)S(1)}, u32[]{:S(2)}, u32[]{:S(2)}) collective-permute-start(bf16[3,384,128]{2,1,0:T(8,128)(2,1)S(1)} %collective-permute-done.4.refs_1_), channel_id=1, source_target_pairs={{0,1},{1,0},{2,3},{3,2},{4,5},{5,4},{6,7},{7,6},{8,9},{9,8},{10,11... | collective-permute-start | bytes 884744 | tf_op jit(solution)/shard_map/ppermute | solution.py:487
  35.3 5.3 %collective-permute-start.9 = (bf16[3,384,128]{2,1,0:T(8,128)(2,1)S(1)}, bf16[3,384,128]{2,1,0:T(8,128)(2,1)S(1)}, u32[]{:S(2)}, u32[]{:S(2)}) collective-permute-start(bf16[3,384,128]{2,1,0:T(8,128)(2,1)S(1)} %collective-permute-done.5.refs_2_), channel_id=1, source_target_pairs={{0,1},{1,0},{2,3},{3,2},{4,5},{5,4},{6,7},{7,6},{8,9},{9,8},{10,11... | collective-permute-start | bytes 884744 | tf_op jit(solution)/shard_map/ppermute | solution.py:487
  40.6 3.3 %collective-permute-start.10 = (bf16[3,384,128]{2,1,0:T(8,128)(2,1)S(1)}, bf16[3,384,128]{2,1,0:T(8,128)(2,1)S(1)}, u32[]{:S(2)}, u32[]{:S(2)}) collective-permute-start(bf16[3,384,128]{2,1,0:T(8,128)(2,1)S(1)} %collective-permute-done.6.refs_3_), channel_id=1, source_target_pairs={{0,1},{1,0},{2,3},{3,2},{4,5},{5,4},{6,7},{7,6},{8,9},{9,8},{10,11... | collective-permute-start | bytes 884744 | tf_op jit(solution)/shard_map/ppermute | solution.py:487
  43.9 1.2 %collective-permute-done.10.refs_7_ = bf16[3,384,128]{2,1,0:T(8,128)(2,1)S(1)} collective-permute-done((bf16[3,384,128]{2,1,0:T(8,128)(2,1)S(1)}, bf16[3,384,128]{2,1,0:T(8,128)(2,1)S(1)}, u32[]{:S(2)}, u32[]{:S(2)}) %collective-permute-start.10) | collective-permute-done | bytes 294944 | tf_op jit(solution)/shard_map/ppermute | solution.py:487
  45.1 9.6 %shard_map.106 = (bf16[384,128]{1,0:T(8,128)(2,1)S(1)}, bf16[384,128]{1,0:T(8,128)(2,1)S(1)}, bf16[384,128]{1,0:T(8,128)(2,1)S(1)}, bf16[384,128]{1,0:T(8,128)(2,1)S(1)}) custom-call(s32[5]{0:T(128)S(1)} %copy-done.6, bf16[3,384,128]{2,1,0:T(8,128)(2,1)S(1)} %collective-permute-done.3.refs_0_, bf16[3,384,128]{2,1,0:T(8,128)(2,1)S(1)} %collective-permute-done.4.refs_1_, ...), custom_call_target="tpu_custom_call" | custom-call | tf_op jit(solution)/shard_map/pallas_call | solution.py:357
  54.7 0.7 collective-permute-start.11
  55.3 1.3 %collective-permute-start.12 = (bf16[384,128]{1,0:T(8,128)(2,1)S(1)}, bf16[384,128]{1,0:T(8,128)(2,1)S(1)}, u32[]{:S(2)}, u32[]{:S(2)}) collective-permute-start(bf16[384,128]{1,0:T(8,128)(2,1)S(1)} %get-tuple-element.32), channel_id=1, source_target_pairs={{0,4},{24,5},{2,6},{26,7},{12,8},{20,9},{14,10},{22,11},{8,12},{16... | collective-permute-start | bytes 294920 | tf_op jit(solution)/shard_map/ppermute | solution.py:490
  56.6 1.9 %collective-permute-start.13 = (bf16[384,128]{1,0:T(8,128)(2,1)S(1)}, bf16[384,128]{1,0:T(8,128)(2,1)S(1)}, u32[]{:S(2)}, u32[]{:S(2)}) collective-permute-start(bf16[384,128]{1,0:T(8,128)(2,1)S(1)} %get-tuple-element.33), channel_id=1, source_target_pairs={{8,0},{16,1},{10,2},{18,3},{12,4},{20,5},{14,6},{22,7},{0,8},{24,9... | collective-permute-start | bytes 294920 | tf_op jit(solution)/shard_map/ppermute | solution.py:490
  58.6 1.9 %collective-permute-start.14 = (bf16[384,128]{1,0:T(8,128)(2,1)S(1)}, bf16[384,128]{1,0:T(8,128)(2,1)S(1)}, u32[]{:S(2)}, u32[]{:S(2)}) collective-permute-start(bf16[384,128]{1,0:T(8,128)(2,1)S(1)} %get-tuple-element.34), channel_id=1, source_target_pairs={{12,0},{20,1},{14,2},{22,3},{8,4},{16,5},{10,6},{18,7},{0,12},{24,... | collective-permute-start | bytes 294920 | tf_op jit(solution)/shard_map/ppermute | solution.py:490
  60.5 5.5 %collective-permute-done.13.refs_2_ = bf16[384,128]{1,0:T(8,128)(2,1)S(1)} collective-permute-done((bf16[384,128]{1,0:T(8,128)(2,1)S(1)}, bf16[384,128]{1,0:T(8,128)(2,1)S(1)}, u32[]{:S(2)}, u32[]{:S(2)}) %collective-permute-start.13) | collective-permute-done | bytes 98336 | tf_op jit(solution)/shard_map/ppermute | solution.py:490
  66.0 0.0 collective-permute-done.14.refs_3_
  66.0 0.5 shard_map.107
  66.5 1.5 %collective-permute-start.15 = (bf16[3,192,128]{2,1,0:T(8,128)(2,1)S(1)}, bf16[3,192,128]{2,1,0:T(8,128)(2,1)S(1)}, u32[]{:S(2)}, u32[]{:S(2)}) collective-permute-start(bf16[3,192,128]{2,1,0:T(8,128)(2,1)S(1)} %get-tuple-element.36), channel_id=1, source_target_pairs={{0,2},{2,0},{4,6},{6,4},{8,10},{10,8},{12,14},{14,12},{16,18},{18,... | collective-permute-start | bytes 442376 | tf_op jit(solution)/shard_map/ppermute | solution.py:493
  68.0 3.7 %collective-permute-done.15.got_ref = bf16[3,192,128]{2,1,0:T(8,128)(2,1)S(1)} collective-permute-done((bf16[3,192,128]{2,1,0:T(8,128)(2,1)S(1)}, bf16[3,192,128]{2,1,0:T(8,128)(2,1)S(1)}, u32[]{:S(2)}, u32[]{:S(2)}) %collective-permute-start.15) | collective-permute-done | bytes 147488 | tf_op jit(solution)/shard_map/ppermute | solution.py:493
  71.7 0.8 shard_map.108
  72.5 3.0 %collective-permute-start.16 = (bf16[192,768]{1,0:T(8,128)(2,1)S(1)}, bf16[192,768]{1,0:T(8,128)(2,1)S(1)}, u32[]{:S(2)}, u32[]{:S(2)}) collective-permute-start(bf16[192,768]{1,0:T(8,128)(2,1)S(1)} %get-tuple-element.38), channel_id=1, source_target_pairs={{0,1},{1,0},{2,3},{3,2},{4,5},{5,4},{6,7},{7,6},{8,9},{9,8},{10,11... | collective-permute-start | bytes 884744 | tf_op jit(solution)/shard_map/ppermute | solution.py:494
  75.5 1.2 %collective-permute-done.16.theirs = bf16[192,768]{1,0:T(8,128)(2,1)S(1)} collective-permute-done((bf16[192,768]{1,0:T(8,128)(2,1)S(1)}, bf16[192,768]{1,0:T(8,128)(2,1)S(1)}, u32[]{:S(2)}, u32[]{:S(2)}) %collective-permute-start.16) | collective-permute-done | bytes 294944 | tf_op jit(solution)/shard_map/ppermute | solution.py:494
  76.7 0.9 %shard_map.109 = (bf16[192,768]{1,0:T(8,128)(2,1)}, bf16[192,768]{1,0:T(8,128)(2,1)}) custom-call(s32[1]{0:T(128)S(6)} %copy.11.timestep_ref, f32[192,768]{1,0:T(8,128)S(1)} %get-tuple-element.37.mine, bf16[192,768]{1,0:T(8,128)(2,1)S(1)} %collective-permute-done.16.theirs, bf16[192,768]{1,0:T(8,128)(2,1)S(1)} %copy-done.4, ...), custom_call_target="tpu_custom_call" | custom-call | tf_op jit(solution)/shard_map/pallas_call | solution.py:456
  (24 shorter events, 0.1 us)
Async XLA Ops:
  0.6 3.9 %collective-permute-start.1 = (bf16[192,768]{1,0:T(8,128)(2,1)}, bf16[192,768]{1,0:T(8,128)(2,1)S(1)}, u32[]{:S(2)}, u32[]{:S(2)}) collective-permute-start(bf16[192,768]{1,0:T(8,128)(2,1)} %tokens.1), channel_id=1, source_target_pairs={{0,1},{1,0},{2,3},{3,2},{4,5},{5,4},{6,7},{7,6},{8,9},{9,8},{10,11... | collective-permute-start | bytes 884744 | tf_op jit(solution)/shard_map/ppermute | solution.py:475
  1.1 10.4 %collective-permute-start = (bf16[192,768]{1,0:T(8,128)(2,1)}, bf16[192,768]{1,0:T(8,128)(2,1)S(1)}, u32[]{:S(2)}, u32[]{:S(2)}) collective-permute-start(bf16[192,768]{1,0:T(8,128)(2,1)} %tokens.1), channel_id=1, source_target_pairs={{0,2},{2,0},{4,6},{6,4},{8,10},{10,8},{12,14},{14,12},{16,18},{18,... | collective-permute-start | bytes 884744 | tf_op jit(solution)/shard_map/ppermute | solution.py:474
  4.5 8.6 %copy-start = (bf16[1536,768]{1,0:T(8,128)(2,1)S(1)}, bf16[1536,768]{1,0:T(8,128)(2,1)}, u32[]{:S(2)}) copy-start(bf16[1536,768]{1,0:T(8,128)(2,1)} %wq_ref.3) | copy-start | bytes 7077892
  4.5 8.6 %copy-start.1 = (bf16[1536,768]{1,0:T(8,128)(2,1)S(1)}, bf16[1536,768]{1,0:T(8,128)(2,1)}, u32[]{:S(2)}) copy-start(bf16[1536,768]{1,0:T(8,128)(2,1)} %wk_ref.3) | copy-start | bytes 7077892
  4.5 8.6 %copy-start.2 = (bf16[1536,768]{1,0:T(8,128)(2,1)S(1)}, bf16[1536,768]{1,0:T(8,128)(2,1)}, u32[]{:S(2)}) copy-start(bf16[1536,768]{1,0:T(8,128)(2,1)} %wv_ref.3) | copy-start | bytes 7077892
  4.5 1.1 %copy-start.4 = (bf16[192,768]{1,0:T(8,128)(2,1)S(1)}, bf16[192,768]{1,0:T(8,128)(2,1)}, u32[]{:S(2)}) copy-start(bf16[192,768]{1,0:T(8,128)(2,1)} %tokens.1) | copy-start | bytes 884740
  5.6 1.3 %copy-start.5 = (f32[3,1536]{1,0:T(4,128)S(1)}, f32[3,1536]{1,0:T(4,128)}, u32[]{:S(2)}) copy-start(f32[3,1536]{1,0:T(4,128)} %block_ref.1) | copy-start | bytes 55300
  11.5 33.6 %copy-start.6 = (s32[5]{0:T(128)S(1)}, s32[5]{0:T(128)}, u32[]{:S(2)}) copy-start(s32[5]{0:T(128)} %lengths_ref.1) | copy-start | bytes 64
  11.5 1.6 %collective-permute-start.2 = (bf16[192,768]{1,0:T(8,128)(2,1)S(1)}, bf16[192,768]{1,0:T(8,128)(2,1)S(1)}, u32[]{:S(2)}, u32[]{:S(2)}) collective-permute-start(bf16[192,768]{1,0:T(8,128)(2,1)S(1)} %collective-permute-done.near_ref), channel_id=1, source_target_pairs={{0,1},{1,0},{2,3},{3,2},{4,5},{5,4},{6,7},{7,6},{8,9},{9,8},{10,11... | collective-permute-start | bytes 884744 | tf_op jit(solution)/shard_map/ppermute | solution.py:484
  15.2 56.5 %copy-start.3 = (bf16[768,1536]{1,0:T(8,128)(2,1)S(1)}, bf16[768,1536]{1,0:T(8,128)(2,1)}, u32[]{:S(2)}) copy-start(bf16[768,1536]{1,0:T(8,128)(2,1)} %weight.1) | copy-start | bytes 7077892
  15.2 9.9 %collective-permute-start.3 = (bf16[3,384,128]{2,1,0:T(8,128)(2,1)S(1)}, bf16[3,384,128]{2,1,0:T(8,128)(2,1)S(1)}, u32[]{:S(2)}, u32[]{:S(2)}) collective-permute-start(bf16[3,384,128]{2,1,0:T(8,128)(2,1)S(1)} %get-tuple-element.27), channel_id=1, source_target_pairs={{0,0},{1,24},{2,2},{3,26},{8,8},{9,16},{10,10},{11,18},{12,12},{13... | collective-permute-start | bytes 884744 | tf_op jit(solution)/shard_map/ppermute | solution.py:486
  16.1 12.7 %collective-permute-start.4 = (bf16[3,384,128]{2,1,0:T(8,128)(2,1)S(1)}, bf16[3,384,128]{2,1,0:T(8,128)(2,1)S(1)}, u32[]{:S(2)}, u32[]{:S(2)}) collective-permute-start(bf16[3,384,128]{2,1,0:T(8,128)(2,1)S(1)} %get-tuple-element.28), channel_id=1, source_target_pairs={{4,0},{5,24},{6,2},{7,26},{8,12},{9,20},{10,14},{11,22},{12,8},{13... | collective-permute-start | bytes 884744 | tf_op jit(solution)/shard_map/ppermute | solution.py:486
  17.4 17.9 %collective-permute-start.5 = (bf16[3,384,128]{2,1,0:T(8,128)(2,1)S(1)}, bf16[3,384,128]{2,1,0:T(8,128)(2,1)S(1)}, u32[]{:S(2)}, u32[]{:S(2)}) collective-permute-start(bf16[3,384,128]{2,1,0:T(8,128)(2,1)S(1)} %get-tuple-element.29), channel_id=1, source_target_pairs={{0,8},{1,16},{2,10},{3,18},{4,12},{5,20},{6,14},{7,22},{8,0},{9,24... | collective-permute-start | bytes 884744 | tf_op jit(solution)/shard_map/ppermute | solution.py:486
  23.2 17.4 %collective-permute-start.6 = (bf16[3,384,128]{2,1,0:T(8,128)(2,1)S(1)}, bf16[3,384,128]{2,1,0:T(8,128)(2,1)S(1)}, u32[]{:S(2)}, u32[]{:S(2)}) collective-permute-start(bf16[3,384,128]{2,1,0:T(8,128)(2,1)S(1)} %get-tuple-element.30), channel_id=1, source_target_pairs={{0,12},{1,20},{2,14},{3,22},{4,8},{5,16},{6,10},{7,18},{12,0},{13,... | collective-permute-start | bytes 884744 | tf_op jit(solution)/shard_map/ppermute | solution.py:486
  25.2 18.7 %collective-permute-start.7 = (bf16[3,384,128]{2,1,0:T(8,128)(2,1)S(1)}, bf16[3,384,128]{2,1,0:T(8,128)(2,1)S(1)}, u32[]{:S(2)}, u32[]{:S(2)}) collective-permute-start(bf16[3,384,128]{2,1,0:T(8,128)(2,1)S(1)} %collective-permute-done.3.refs_0_), channel_id=1, source_target_pairs={{0,1},{1,0},{2,3},{3,2},{4,5},{5,4},{6,7},{7,6},{8,9},{9,8},{10,11... | collective-permute-start | bytes 884744 | tf_op jit(solution)/shard_map/ppermute | solution.py:487
  28.8 15.1 %collective-permute-start.8 = (bf16[3,384,128]{2,1,0:T(8,128)(2,1)S(1)}, bf16[3,384,128]{2,1,0:T(8,128)(2,1)S(1)}, u32[]{:S(2)}, u32[]{:S(2)}) collective-permute-start(bf16[3,384,128]{2,1,0:T(8,128)(2,1)S(1)} %collective-permute-done.4.refs_1_), channel_id=1, source_target_pairs={{0,1},{1,0},{2,3},{3,2},{4,5},{5,4},{6,7},{7,6},{8,9},{9,8},{10,11... | collective-permute-start | bytes 884744 | tf_op jit(solution)/shard_map/ppermute | solution.py:487
  35.3 8.6 %collective-permute-start.9 = (bf16[3,384,128]{2,1,0:T(8,128)(2,1)S(1)}, bf16[3,384,128]{2,1,0:T(8,128)(2,1)S(1)}, u32[]{:S(2)}, u32[]{:S(2)}) collective-permute-start(bf16[3,384,128]{2,1,0:T(8,128)(2,1)S(1)} %collective-permute-done.5.refs_2_), channel_id=1, source_target_pairs={{0,1},{1,0},{2,3},{3,2},{4,5},{5,4},{6,7},{7,6},{8,9},{9,8},{10,11... | collective-permute-start | bytes 884744 | tf_op jit(solution)/shard_map/ppermute | solution.py:487
  40.6 4.5 %collective-permute-start.10 = (bf16[3,384,128]{2,1,0:T(8,128)(2,1)S(1)}, bf16[3,384,128]{2,1,0:T(8,128)(2,1)S(1)}, u32[]{:S(2)}, u32[]{:S(2)}) collective-permute-start(bf16[3,384,128]{2,1,0:T(8,128)(2,1)S(1)} %collective-permute-done.6.refs_3_), channel_id=1, source_target_pairs={{0,1},{1,0},{2,3},{3,2},{4,5},{5,4},{6,7},{7,6},{8,9},{9,8},{10,11... | collective-permute-start | bytes 884744 | tf_op jit(solution)/shard_map/ppermute | solution.py:487
  54.7 5.8 %collective-permute-start.11 = (bf16[384,128]{1,0:T(8,128)(2,1)S(1)}, bf16[384,128]{1,0:T(8,128)(2,1)S(1)}, u32[]{:S(2)}, u32[]{:S(2)}) collective-permute-start(bf16[384,128]{1,0:T(8,128)(2,1)S(1)} %get-tuple-element.31), channel_id=1, source_target_pairs={{0,0},{24,1},{2,2},{26,3},{8,8},{16,9},{10,10},{18,11},{12,12},{20... | collective-permute-start | bytes 294920 | tf_op jit(solution)/shard_map/ppermute | solution.py:490
  55.3 5.2 %collective-permute-start.12 = (bf16[384,128]{1,0:T(8,128)(2,1)S(1)}, bf16[384,128]{1,0:T(8,128)(2,1)S(1)}, u32[]{:S(2)}, u32[]{:S(2)}) collective-permute-start(bf16[384,128]{1,0:T(8,128)(2,1)S(1)} %get-tuple-element.32), channel_id=1, source_target_pairs={{0,4},{24,5},{2,6},{26,7},{12,8},{20,9},{14,10},{22,11},{8,12},{16... | collective-permute-start | bytes 294920 | tf_op jit(solution)/shard_map/ppermute | solution.py:490
  56.6 9.3 %collective-permute-start.13 = (bf16[384,128]{1,0:T(8,128)(2,1)S(1)}, bf16[384,128]{1,0:T(8,128)(2,1)S(1)}, u32[]{:S(2)}, u32[]{:S(2)}) collective-permute-start(bf16[384,128]{1,0:T(8,128)(2,1)S(1)} %get-tuple-element.33), channel_id=1, source_target_pairs={{8,0},{16,1},{10,2},{18,3},{12,4},{20,5},{14,6},{22,7},{0,8},{24,9... | collective-permute-start | bytes 294920 | tf_op jit(solution)/shard_map/ppermute | solution.py:490
  58.6 7.4 %collective-permute-start.14 = (bf16[384,128]{1,0:T(8,128)(2,1)S(1)}, bf16[384,128]{1,0:T(8,128)(2,1)S(1)}, u32[]{:S(2)}, u32[]{:S(2)}) collective-permute-start(bf16[384,128]{1,0:T(8,128)(2,1)S(1)} %get-tuple-element.34), channel_id=1, source_target_pairs={{12,0},{20,1},{14,2},{22,3},{8,4},{16,5},{10,6},{18,7},{0,12},{24,... | collective-permute-start | bytes 294920 | tf_op jit(solution)/shard_map/ppermute | solution.py:490
  66.5 5.2 %collective-permute-start.15 = (bf16[3,192,128]{2,1,0:T(8,128)(2,1)S(1)}, bf16[3,192,128]{2,1,0:T(8,128)(2,1)S(1)}, u32[]{:S(2)}, u32[]{:S(2)}) collective-permute-start(bf16[3,192,128]{2,1,0:T(8,128)(2,1)S(1)} %get-tuple-element.36), channel_id=1, source_target_pairs={{0,2},{2,0},{4,6},{6,4},{8,10},{10,8},{12,14},{14,12},{16,18},{18,... | collective-permute-start | bytes 442376 | tf_op jit(solution)/shard_map/ppermute | solution.py:493
  72.5 4.2 %collective-permute-start.16 = (bf16[192,768]{1,0:T(8,128)(2,1)S(1)}, bf16[192,768]{1,0:T(8,128)(2,1)S(1)}, u32[]{:S(2)}, u32[]{:S(2)}) collective-permute-start(bf16[192,768]{1,0:T(8,128)(2,1)S(1)} %get-tuple-element.38), channel_id=1, source_target_pairs={{0,1},{1,0},{2,3},{3,2},{4,5},{5,4},{6,7},{7,6},{8,9},{9,8},{10,11... | collective-permute-start | bytes 884744 | tf_op jit(solution)/shard_map/ppermute | solution.py:494

commit v12 on v11

--- a/solution.py
+++ b/solution.py
@@ -405,8 +405,29 @@
     )(*pieces)
 
 
-def combine_kernel(keep_ref, got_ref, weight, mine, theirs, attended, sems):
-    share = mine.shape[1]
+def multiply(attended, weight, out, where):
+    share = out.shape[1]
+    columns = pl.ds(pl.multiple_of(where * share, 128), share)
+    out[...] = jnp.dot(attended[...], weight[:, columns], preferred_element_type=jnp.float32).astype(out.dtype)
+
+
+def own_kernel(attended, weight, mine):
+    multiply(attended, weight, mine, lax.axis_index("tp"))
+
+
+def own_part(attended, w_out):
+    rows, width = attended.shape[0], w_out.shape[1]
+    return pl.pallas_call(
+        own_kernel,
+        in_specs=[vmem_spec()] * 2,
+        out_specs=vmem_spec(),
+        out_shape=jax.ShapeDtypeStruct((rows, width // 2), jnp.float32),
+        compiler_params=pltpu.CompilerParams(vmem_limit_bytes=VMEM_LIMIT),
+        cost_estimate=pl.CostEstimate(flops=rows * width * w_out.shape[0], bytes_accessed=2**20, transcendentals=0),
+    )(attended, w_out)
+
+
+def combine_kernel(keep_ref, got_ref, weight, theirs, attended, sems):
     heads = keep_ref.shape[0]
     core = lax.axis_index("tp")
     x = lax.rem(lax.axis_index("req"), 2)
@@ -418,10 +439,7 @@
             copies[-1].start()
     for copy in copies:
         copy.wait()
-    left = attended[...]
-    for out, where in ((theirs, 1 - core), (mine, core)):
-        columns = pl.ds(pl.multiple_of(where * share, 128), share)
-        out[...] = jnp.dot(left, weight[:, columns], preferred_element_type=jnp.float32).astype(out.dtype)
+    multiply(attended, weight, theirs, 1 - core)
 
 
 def combine(keep, got, w_out):
@@ -432,11 +450,10 @@
         in_specs=[any_spec()] * 2 + [vmem_spec()],
         out_specs=[vmem_spec(), vmem_spec()],
         out_shape=[
-            jax.ShapeDtypeStruct((rows, width // 2), jnp.float32),
             jax.ShapeDtypeStruct((rows, width // 2), jnp.bfloat16),
+            jax.ShapeDtypeStruct((rows, depth), jnp.bfloat16),
         ],
         scratch_shapes=[
-            pltpu.VMEM((rows, depth), jnp.bfloat16),
             pltpu.SemaphoreType.DMA((2 * heads,)),
         ],
         compiler_params=pltpu.CompilerParams(vmem_limit_bytes=VMEM_LIMIT),
@@ -490,8 +507,9 @@
             lax.ppermute(piece, ("req", "tp"), [(b, a) for a, b in route]) for piece, route in zip(done, routes)
         ]
         keep, give = part(back, heads)
-        mine, theirs = combine(keep, lax.ppermute(give, "req", cross), w_out)
+        theirs, attended = combine(keep, lax.ppermute(give, "req", cross), w_out)
         theirs = lax.ppermute(theirs, "tp", swap)
+        mine = own_part(attended, w_out)
         velocity, stepped = finish(timestep, mine, theirs, tokens, gate)
         return (velocity, stepped)
 

time: 78 us -> 77.1 us (0.988); the launches traced: 77.6 us -> 77.5 us
  transfers between devices with their start and end apart: 17 -> 17, of which waited for: 6 -> 7; matrix products, arithmetic and copies ran while one was open for 0% -> 0% of each run, Pallas kernels for 5% -> 6%
where the time goes in v12:
time: 77.1 us; the launch traced here: 77.5 us
  starting transfers between devices  42.1 us (55%)
  Pallas kernels  18.2 us (24%)
  waiting for transfers between devices  13.3 us (17%)
  local copies, waits for them, and re-layouts  2.42 us (3%)
  between operations  1.54 us (2%)
    ppermute x4, starting transfers between devices, on_device(): swapped = [lax.ppermute(piece, 'tp', swap) for piece in got]  18.7 us
    ppermute x4, starting transfers between devices, on_device(): lax.ppermute(piece, ('req', 'tp'), route)  9.9 us
    pallas_call x1, Pallas kernels, attend(): pl.pallas_call(functools.partial(attend_kernel, colours, heads), in_specs...  9.69 us
    ppermute x4, starting transfers between devices, on_device(): lax.ppermute(piece, ('req', 'tp'), [(b, a) for a, b in route])  5.8 us
    ppermute x4, waiting for transfers between devices, on_device(): lax.ppermute(piece, ('req', 'tp'), [(b, a) for a, b in route])  5.46 us
    pallas_call x1, Pallas kernels, project(): pl.pallas_call(project_kernel, in_specs=[vmem_spec()] * 4 + [any_spec()]...  4.07 us
    ppermute x1, waiting for transfers between devices, on_device(): theirs, attended = combine(keep, lax.ppermute(give, 'req', cross), w_out)  3.67 us
    ppermute x1, starting transfers between devices, on_device(): theirs = lax.ppermute(theirs, 'tp', swap)  3.05 us
  transfers between devices with their start and end apart: 17, of which 7 were waited for; matrix products, arithmetic and copies ran while one was open for 0% of the time, Pallas kernels for 6%

profile of v12, /device:TPU:0, one launch (start us, length us, event | category | flops | bytes accessed | tf_op | source)
XLA Modules:
  0.0 77.5 jit_solution(12494352655246999857)
XLA Ops:
  0.6 0.5 collective-permute-start.1
  1.1 2.6 %collective-permute-start = (bf16[192,768]{1,0:T(8,128)(2,1)}, bf16[192,768]{1,0:T(8,128)(2,1)S(1)}, u32[]{:S(2)}, u32[]{:S(2)}) collective-permute-start(bf16[192,768]{1,0:T(8,128)(2,1)} %tokens.1), channel_id=1, source_target_pairs={{0,2},{2,0},{4,6},{6,4},{8,10},{10,8},{12,14},{14,12},{16,18},{18,... | collective-permute-start | bytes 884744 | tf_op jit(solution)/shard_map/ppermute | solution.py:491
  4.5 1.1 %copy-done.4 = bf16[192,768]{1,0:T(8,128)(2,1)S(1)} copy-done((bf16[192,768]{1,0:T(8,128)(2,1)S(1)}, bf16[192,768]{1,0:T(8,128)(2,1)}, u32[]{:S(2)}) %copy-start.4) | copy-done | bytes 294936
  5.6 1.3 %copy-done.5 = f32[3,1536]{1,0:T(4,128)S(1)} copy-done((f32[3,1536]{1,0:T(4,128)S(1)}, f32[3,1536]{1,0:T(4,128)}, u32[]{:S(2)}) %copy-start.5) | copy-done | bytes 18456
  6.9 4.1 %shard_map.104 = (bf16[3,3,192,128]{3,2,1,0:T(8,128)(2,1)S(1)}, f32[2,1536]{1,0:T(2,128)S(1)}, f32[1,768]{1,0:T(1,128)S(1)}) custom-call(f32[1,256]{1,0:T(1,128)S(1)} %divide_multiply_fusion.act_ref, f32[3,1536]{1,0:T(4,128)S(1)} %copy-done.5, bf16[192,768]{1,0:T(8,128)(2,1)S(1)} %copy-done.4, bf16[192,768]{1,0:T(8,128)(2,1)S(1)} %collective-permute-done.1.other_ref, ...), custom_call_target="tpu_custom_call" | custom-call | flops 679477248 | bytes 8388608 | tf_op jit(solution)/shard_map/pallas_call | solution.py:142
  11.0 0.5 collective-permute-done.near_ref
  11.5 1.6 %collective-permute-done.2.far_ref = bf16[192,768]{1,0:T(8,128)(2,1)S(1)} collective-permute-done((bf16[192,768]{1,0:T(8,128)(2,1)S(1)}, bf16[192,768]{1,0:T(8,128)(2,1)S(1)}, u32[]{:S(2)}, u32[]{:S(2)}) %collective-permute-start.2) | collective-permute-done | bytes 294944 | tf_op jit(solution)/shard_map/ppermute | solution.py:501
  13.1 2.1 %shard_map.105 = (bf16[3,384,128]{2,1,0:T(8,128)(2,1)S(1)}, bf16[3,384,128]{2,1,0:T(8,128)(2,1)S(1)}, bf16[3,384,128]{2,1,0:T(8,128)(2,1)S(1)}, bf16[3,384,128]{2,1,0:T(8,128)(2,1)S(1)}) custom-call(bf16[192,768]{1,0:T(8,128)(2,1)S(1)} %collective-permute-done.near_ref, bf16[192,768]{1,0:T(8,128)(2,1)S(1)} %collective-permute-done.2.far_ref, ...), custom_call_target="tpu_custom_call" | custom-call | tf_op jit(solution)/shard_map/pallas_call | solution.py:190
  15.2 0.8 %collective-permute-start.3 = (bf16[3,384,128]{2,1,0:T(8,128)(2,1)S(1)}, bf16[3,384,128]{2,1,0:T(8,128)(2,1)S(1)}, u32[]{:S(2)}, u32[]{:S(2)}) collective-permute-start(bf16[3,384,128]{2,1,0:T(8,128)(2,1)S(1)} %get-tuple-element.27), channel_id=1, source_target_pairs={{0,0},{1,24},{2,2},{3,26},{8,8},{9,16},{10,10},{11,18},{12,12},{13... | collective-permute-start | bytes 884744 | tf_op jit(solution)/shard_map/ppermute | solution.py:503
  16.1 1.3 %collective-permute-start.4 = (bf16[3,384,128]{2,1,0:T(8,128)(2,1)S(1)}, bf16[3,384,128]{2,1,0:T(8,128)(2,1)S(1)}, u32[]{:S(2)}, u32[]{:S(2)}) collective-permute-start(bf16[3,384,128]{2,1,0:T(8,128)(2,1)S(1)} %get-tuple-element.28), channel_id=1, source_target_pairs={{4,0},{5,24},{6,2},{7,26},{8,12},{9,20},{10,14},{11,22},{12,8},{13... | collective-permute-start | bytes 884744 | tf_op jit(solution)/shard_map/ppermute | solution.py:503
  17.4 5.9 %collective-permute-start.5 = (bf16[3,384,128]{2,1,0:T(8,128)(2,1)S(1)}, bf16[3,384,128]{2,1,0:T(8,128)(2,1)S(1)}, u32[]{:S(2)}, u32[]{:S(2)}) collective-permute-start(bf16[3,384,128]{2,1,0:T(8,128)(2,1)S(1)} %get-tuple-element.29), channel_id=1, source_target_pairs={{0,8},{1,16},{2,10},{3,18},{4,12},{5,20},{6,14},{7,22},{8,0},{9,24... | collective-permute-start | bytes 884744 | tf_op jit(solution)/shard_map/ppermute | solution.py:503
  23.2 1.9 %collective-permute-start.6 = (bf16[3,384,128]{2,1,0:T(8,128)(2,1)S(1)}, bf16[3,384,128]{2,1,0:T(8,128)(2,1)S(1)}, u32[]{:S(2)}, u32[]{:S(2)}) collective-permute-start(bf16[3,384,128]{2,1,0:T(8,128)(2,1)S(1)} %get-tuple-element.30), channel_id=1, source_target_pairs={{0,12},{1,20},{2,14},{3,22},{4,8},{5,16},{6,10},{7,18},{12,0},{13,... | collective-permute-start | bytes 884744 | tf_op jit(solution)/shard_map/ppermute | solution.py:503
  25.2 3.6 %collective-permute-start.7 = (bf16[3,384,128]{2,1,0:T(8,128)(2,1)S(1)}, bf16[3,384,128]{2,1,0:T(8,128)(2,1)S(1)}, u32[]{:S(2)}, u32[]{:S(2)}) collective-permute-start(bf16[3,384,128]{2,1,0:T(8,128)(2,1)S(1)} %collective-permute-done.3.refs_0_), channel_id=1, source_target_pairs={{0,1},{1,0},{2,3},{3,2},{4,5},{5,4},{6,7},{7,6},{8,9},{9,8},{10,11... | collective-permute-start | bytes 884744 | tf_op jit(solution)/shard_map/ppermute | solution.py:504
  28.8 6.5 %collective-permute-start.8 = (bf16[3,384,128]{2,1,0:T(8,128)(2,1)S(1)}, bf16[3,384,128]{2,1,0:T(8,128)(2,1)S(1)}, u32[]{:S(2)}, u32[]{:S(2)}) collective-permute-start(bf16[3,384,128]{2,1,0:T(8,128)(2,1)S(1)} %collective-permute-done.4.refs_1_), channel_id=1, source_target_pairs={{0,1},{1,0},{2,3},{3,2},{4,5},{5,4},{6,7},{7,6},{8,9},{9,8},{10,11... | collective-permute-start | bytes 884744 | tf_op jit(solution)/shard_map/ppermute | solution.py:504
  35.3 5.3 %collective-permute-start.9 = (bf16[3,384,128]{2,1,0:T(8,128)(2,1)S(1)}, bf16[3,384,128]{2,1,0:T(8,128)(2,1)S(1)}, u32[]{:S(2)}, u32[]{:S(2)}) collective-permute-start(bf16[3,384,128]{2,1,0:T(8,128)(2,1)S(1)} %collective-permute-done.5.refs_2_), channel_id=1, source_target_pairs={{0,1},{1,0},{2,3},{3,2},{4,5},{5,4},{6,7},{7,6},{8,9},{9,8},{10,11... | collective-permute-start | bytes 884744 | tf_op jit(solution)/shard_map/ppermute | solution.py:504
  40.6 3.3 %collective-permute-start.10 = (bf16[3,384,128]{2,1,0:T(8,128)(2,1)S(1)}, bf16[3,384,128]{2,1,0:T(8,128)(2,1)S(1)}, u32[]{:S(2)}, u32[]{:S(2)}) collective-permute-start(bf16[3,384,128]{2,1,0:T(8,128)(2,1)S(1)} %collective-permute-done.6.refs_3_), channel_id=1, source_target_pairs={{0,1},{1,0},{2,3},{3,2},{4,5},{5,4},{6,7},{7,6},{8,9},{9,8},{10,11... | collective-permute-start | bytes 884744 | tf_op jit(solution)/shard_map/ppermute | solution.py:504
  43.9 1.2 %collective-permute-done.10.refs_7_ = bf16[3,384,128]{2,1,0:T(8,128)(2,1)S(1)} collective-permute-done((bf16[3,384,128]{2,1,0:T(8,128)(2,1)S(1)}, bf16[3,384,128]{2,1,0:T(8,128)(2,1)S(1)}, u32[]{:S(2)}, u32[]{:S(2)}) %collective-permute-start.10) | collective-permute-done | bytes 294944 | tf_op jit(solution)/shard_map/ppermute | solution.py:504
  45.1 9.7 %shard_map.106 = (bf16[384,128]{1,0:T(8,128)(2,1)S(1)}, bf16[384,128]{1,0:T(8,128)(2,1)S(1)}, bf16[384,128]{1,0:T(8,128)(2,1)S(1)}, bf16[384,128]{1,0:T(8,128)(2,1)S(1)}) custom-call(s32[5]{0:T(128)S(1)} %copy-done.6, bf16[3,384,128]{2,1,0:T(8,128)(2,1)S(1)} %collective-permute-done.3.refs_0_, bf16[3,384,128]{2,1,0:T(8,128)(2,1)S(1)} %collective-permute-done.4.refs_1_, ...), custom_call_target="tpu_custom_call" | custom-call | tf_op jit(solution)/shard_map/pallas_call | solution.py:357
  54.8 0.7 collective-permute-start.11
  55.5 1.3 %collective-permute-start.12 = (bf16[384,128]{1,0:T(8,128)(2,1)S(1)}, bf16[384,128]{1,0:T(8,128)(2,1)S(1)}, u32[]{:S(2)}, u32[]{:S(2)}) collective-permute-start(bf16[384,128]{1,0:T(8,128)(2,1)S(1)} %get-tuple-element.32), channel_id=1, source_target_pairs={{0,4},{24,5},{2,6},{26,7},{12,8},{20,9},{14,10},{22,11},{8,12},{16... | collective-permute-start | bytes 294920 | tf_op jit(solution)/shard_map/ppermute | solution.py:507
  56.8 1.9 %collective-permute-start.13 = (bf16[384,128]{1,0:T(8,128)(2,1)S(1)}, bf16[384,128]{1,0:T(8,128)(2,1)S(1)}, u32[]{:S(2)}, u32[]{:S(2)}) collective-permute-start(bf16[384,128]{1,0:T(8,128)(2,1)S(1)} %get-tuple-element.33), channel_id=1, source_target_pairs={{8,0},{16,1},{10,2},{18,3},{12,4},{20,5},{14,6},{22,7},{0,8},{24,9... | collective-permute-start | bytes 294920 | tf_op jit(solution)/shard_map/ppermute | solution.py:507
  58.7 1.9 %collective-permute-start.14 = (bf16[384,128]{1,0:T(8,128)(2,1)S(1)}, bf16[384,128]{1,0:T(8,128)(2,1)S(1)}, u32[]{:S(2)}, u32[]{:S(2)}) collective-permute-start(bf16[384,128]{1,0:T(8,128)(2,1)S(1)} %get-tuple-element.34), channel_id=1, source_target_pairs={{12,0},{20,1},{14,2},{22,3},{8,4},{16,5},{10,6},{18,7},{0,12},{24,... | collective-permute-start | bytes 294920 | tf_op jit(solution)/shard_map/ppermute | solution.py:507
  60.6 4.3 %collective-permute-done.13.refs_2_ = bf16[384,128]{1,0:T(8,128)(2,1)S(1)} collective-permute-done((bf16[384,128]{1,0:T(8,128)(2,1)S(1)}, bf16[384,128]{1,0:T(8,128)(2,1)S(1)}, u32[]{:S(2)}, u32[]{:S(2)}) %collective-permute-start.13) | collective-permute-done | bytes 98336 | tf_op jit(solution)/shard_map/ppermute | solution.py:507
  65.0 1.2 %collective-permute-done.14.refs_3_ = bf16[384,128]{1,0:T(8,128)(2,1)S(1)} collective-permute-done((bf16[384,128]{1,0:T(8,128)(2,1)S(1)}, bf16[384,128]{1,0:T(8,128)(2,1)S(1)}, u32[]{:S(2)}, u32[]{:S(2)}) %collective-permute-start.14) | collective-permute-done | bytes 98336 | tf_op jit(solution)/shard_map/ppermute | solution.py:507
  66.1 0.5 shard_map.107
  66.6 1.5 %collective-permute-start.15 = (bf16[3,192,128]{2,1,0:T(8,128)(2,1)S(1)}, bf16[3,192,128]{2,1,0:T(8,128)(2,1)S(1)}, u32[]{:S(2)}, u32[]{:S(2)}) collective-permute-start(bf16[3,192,128]{2,1,0:T(8,128)(2,1)S(1)} %get-tuple-element.36), channel_id=1, source_target_pairs={{0,2},{2,0},{4,6},{6,4},{8,10},{10,8},{12,14},{14,12},{16,18},{18,... | collective-permute-start | bytes 442376 | tf_op jit(solution)/shard_map/ppermute | solution.py:510
  68.2 3.7 %collective-permute-done.15.got_ref = bf16[3,192,128]{2,1,0:T(8,128)(2,1)S(1)} collective-permute-done((bf16[3,192,128]{2,1,0:T(8,128)(2,1)S(1)}, bf16[3,192,128]{2,1,0:T(8,128)(2,1)S(1)}, u32[]{:S(2)}, u32[]{:S(2)}) %collective-permute-start.15) | collective-permute-done | bytes 147488 | tf_op jit(solution)/shard_map/ppermute | solution.py:510
  71.8 0.5 shard_map.108
  72.4 3.0 %collective-permute-start.16 = (bf16[192,768]{1,0:T(8,128)(2,1)S(1)}, bf16[192,768]{1,0:T(8,128)(2,1)S(1)}, u32[]{:S(2)}, u32[]{:S(2)}) collective-permute-start(bf16[192,768]{1,0:T(8,128)(2,1)S(1)} %get-tuple-element.38), channel_id=1, source_target_pairs={{0,1},{1,0},{2,3},{3,2},{4,5},{5,4},{6,7},{7,6},{8,9},{9,8},{10,11... | collective-permute-start | bytes 884744 | tf_op jit(solution)/shard_map/ppermute | solution.py:511
  75.4 0.4 shard_map.109.mine
  75.8 0.8 %collective-permute-done.16.theirs = bf16[192,768]{1,0:T(8,128)(2,1)S(1)} collective-permute-done((bf16[192,768]{1,0:T(8,128)(2,1)S(1)}, bf16[192,768]{1,0:T(8,128)(2,1)S(1)}, u32[]{:S(2)}, u32[]{:S(2)}) %collective-permute-start.16) | collective-permute-done | bytes 294944 | tf_op jit(solution)/shard_map/ppermute | solution.py:511
  76.6 0.9 %shard_map.110 = (bf16[192,768]{1,0:T(8,128)(2,1)}, bf16[192,768]{1,0:T(8,128)(2,1)}) custom-call(s32[1]{0:T(128)S(6)} %copy.11.timestep_ref, f32[192,768]{1,0:T(8,128)S(1)} %shard_map.109.mine, bf16[192,768]{1,0:T(8,128)(2,1)S(1)} %collective-permute-done.16.theirs, bf16[192,768]{1,0:T(8,128)(2,1)S(1)} %copy-done.4, f32[1,768]{1,0:T(1,128)S(1)} %get-tuple-element.39.gate_ref), custom_call_target="tpu_custom_call" | custom-call | tf_op jit(solution)/shard_map/pallas_call | solution.py:473
  (25 shorter events, 0.1 us)
Async XLA Ops:
  0.6 3.9 %collective-permute-start.1 = (bf16[192,768]{1,0:T(8,128)(2,1)}, bf16[192,768]{1,0:T(8,128)(2,1)S(1)}, u32[]{:S(2)}, u32[]{:S(2)}) collective-permute-start(bf16[192,768]{1,0:T(8,128)(2,1)} %tokens.1), channel_id=1, source_target_pairs={{0,1},{1,0},{2,3},{3,2},{4,5},{5,4},{6,7},{7,6},{8,9},{9,8},{10,11... | collective-permute-start | bytes 884744 | tf_op jit(solution)/shard_map/ppermute | solution.py:492
  1.1 10.4 %collective-permute-start = (bf16[192,768]{1,0:T(8,128)(2,1)}, bf16[192,768]{1,0:T(8,128)(2,1)S(1)}, u32[]{:S(2)}, u32[]{:S(2)}) collective-permute-start(bf16[192,768]{1,0:T(8,128)(2,1)} %tokens.1), channel_id=1, source_target_pairs={{0,2},{2,0},{4,6},{6,4},{8,10},{10,8},{12,14},{14,12},{16,18},{18,... | collective-permute-start | bytes 884744 | tf_op jit(solution)/shard_map/ppermute | solution.py:491
  4.5 8.6 %copy-start.1 = (bf16[1536,768]{1,0:T(8,128)(2,1)S(1)}, bf16[1536,768]{1,0:T(8,128)(2,1)}, u32[]{:S(2)}) copy-start(bf16[1536,768]{1,0:T(8,128)(2,1)} %wq_ref.3) | copy-start | bytes 7077892
  4.5 8.6 %copy-start.2 = (bf16[1536,768]{1,0:T(8,128)(2,1)S(1)}, bf16[1536,768]{1,0:T(8,128)(2,1)}, u32[]{:S(2)}) copy-start(bf16[1536,768]{1,0:T(8,128)(2,1)} %wk_ref.3) | copy-start | bytes 7077892
  4.5 8.6 %copy-start.3 = (bf16[1536,768]{1,0:T(8,128)(2,1)S(1)}, bf16[1536,768]{1,0:T(8,128)(2,1)}, u32[]{:S(2)}) copy-start(bf16[1536,768]{1,0:T(8,128)(2,1)} %wv_ref.3) | copy-start | bytes 7077892
  4.5 1.1 %copy-start.4 = (bf16[192,768]{1,0:T(8,128)(2,1)S(1)}, bf16[192,768]{1,0:T(8,128)(2,1)}, u32[]{:S(2)}) copy-start(bf16[192,768]{1,0:T(8,128)(2,1)} %tokens.1) | copy-start | bytes 884740
  5.6 1.3 %copy-start.5 = (f32[3,1536]{1,0:T(4,128)S(1)}, f32[3,1536]{1,0:T(4,128)}, u32[]{:S(2)}) copy-start(f32[3,1536]{1,0:T(4,128)} %block_ref.1) | copy-start | bytes 55300
  11.5 33.6 %copy-start.6 = (s32[5]{0:T(128)S(1)}, s32[5]{0:T(128)}, u32[]{:S(2)}) copy-start(s32[5]{0:T(128)} %lengths_ref.1) | copy-start | bytes 64
  11.5 1.6 %collective-permute-start.2 = (bf16[192,768]{1,0:T(8,128)(2,1)S(1)}, bf16[192,768]{1,0:T(8,128)(2,1)S(1)}, u32[]{:S(2)}, u32[]{:S(2)}) collective-permute-start(bf16[192,768]{1,0:T(8,128)(2,1)S(1)} %collective-permute-done.near_ref), channel_id=1, source_target_pairs={{0,1},{1,0},{2,3},{3,2},{4,5},{5,4},{6,7},{7,6},{8,9},{9,8},{10,11... | collective-permute-start | bytes 884744 | tf_op jit(solution)/shard_map/ppermute | solution.py:501
  15.2 56.6 %copy-start = (bf16[768,1536]{1,0:T(8,128)(2,1)S(1)}, bf16[768,1536]{1,0:T(8,128)(2,1)}, u32[]{:S(2)}) copy-start(bf16[768,1536]{1,0:T(8,128)(2,1)} %weight.3) | copy-start | bytes 7077892
  15.2 9.9 %collective-permute-start.3 = (bf16[3,384,128]{2,1,0:T(8,128)(2,1)S(1)}, bf16[3,384,128]{2,1,0:T(8,128)(2,1)S(1)}, u32[]{:S(2)}, u32[]{:S(2)}) collective-permute-start(bf16[3,384,128]{2,1,0:T(8,128)(2,1)S(1)} %get-tuple-element.27), channel_id=1, source_target_pairs={{0,0},{1,24},{2,2},{3,26},{8,8},{9,16},{10,10},{11,18},{12,12},{13... | collective-permute-start | bytes 884744 | tf_op jit(solution)/shard_map/ppermute | solution.py:503
  16.1 12.7 %collective-permute-start.4 = (bf16[3,384,128]{2,1,0:T(8,128)(2,1)S(1)}, bf16[3,384,128]{2,1,0:T(8,128)(2,1)S(1)}, u32[]{:S(2)}, u32[]{:S(2)}) collective-permute-start(bf16[3,384,128]{2,1,0:T(8,128)(2,1)S(1)} %get-tuple-element.28), channel_id=1, source_target_pairs={{4,0},{5,24},{6,2},{7,26},{8,12},{9,20},{10,14},{11,22},{12,8},{13... | collective-permute-start | bytes 884744 | tf_op jit(solution)/shard_map/ppermute | solution.py:503
  17.4 17.9 %collective-permute-start.5 = (bf16[3,384,128]{2,1,0:T(8,128)(2,1)S(1)}, bf16[3,384,128]{2,1,0:T(8,128)(2,1)S(1)}, u32[]{:S(2)}, u32[]{:S(2)}) collective-permute-start(bf16[3,384,128]{2,1,0:T(8,128)(2,1)S(1)} %get-tuple-element.29), channel_id=1, source_target_pairs={{0,8},{1,16},{2,10},{3,18},{4,12},{5,20},{6,14},{7,22},{8,0},{9,24... | collective-permute-start | bytes 884744 | tf_op jit(solution)/shard_map/ppermute | solution.py:503
  23.2 17.4 %collective-permute-start.6 = (bf16[3,384,128]{2,1,0:T(8,128)(2,1)S(1)}, bf16[3,384,128]{2,1,0:T(8,128)(2,1)S(1)}, u32[]{:S(2)}, u32[]{:S(2)}) collective-permute-start(bf16[3,384,128]{2,1,0:T(8,128)(2,1)S(1)} %get-tuple-element.30), channel_id=1, source_target_pairs={{0,12},{1,20},{2,14},{3,22},{4,8},{5,16},{6,10},{7,18},{12,0},{13,... | collective-permute-start | bytes 884744 | tf_op jit(solution)/shard_map/ppermute | solution.py:503
  25.2 18.7 %collective-permute-start.7 = (bf16[3,384,128]{2,1,0:T(8,128)(2,1)S(1)}, bf16[3,384,128]{2,1,0:T(8,128)(2,1)S(1)}, u32[]{:S(2)}, u32[]{:S(2)}) collective-permute-start(bf16[3,384,128]{2,1,0:T(8,128)(2,1)S(1)} %collective-permute-done.3.refs_0_), channel_id=1, source_target_pairs={{0,1},{1,0},{2,3},{3,2},{4,5},{5,4},{6,7},{7,6},{8,9},{9,8},{10,11... | collective-permute-start | bytes 884744 | tf_op jit(solution)/shard_map/ppermute | solution.py:504
  28.8 15.1 %collective-permute-start.8 = (bf16[3,384,128]{2,1,0:T(8,128)(2,1)S(1)}, bf16[3,384,128]{2,1,0:T(8,128)(2,1)S(1)}, u32[]{:S(2)}, u32[]{:S(2)}) collective-permute-start(bf16[3,384,128]{2,1,0:T(8,128)(2,1)S(1)} %collective-permute-done.4.refs_1_), channel_id=1, source_target_pairs={{0,1},{1,0},{2,3},{3,2},{4,5},{5,4},{6,7},{7,6},{8,9},{9,8},{10,11... | collective-permute-start | bytes 884744 | tf_op jit(solution)/shard_map/ppermute | solution.py:504
  35.3 8.6 %collective-permute-start.9 = (bf16[3,384,128]{2,1,0:T(8,128)(2,1)S(1)}, bf16[3,384,128]{2,1,0:T(8,128)(2,1)S(1)}, u32[]{:S(2)}, u32[]{:S(2)}) collective-permute-start(bf16[3,384,128]{2,1,0:T(8,128)(2,1)S(1)} %collective-permute-done.5.refs_2_), channel_id=1, source_target_pairs={{0,1},{1,0},{2,3},{3,2},{4,5},{5,4},{6,7},{7,6},{8,9},{9,8},{10,11... | collective-permute-start | bytes 884744 | tf_op jit(solution)/shard_map/ppermute | solution.py:504
  40.6 4.5 %collective-permute-start.10 = (bf16[3,384,128]{2,1,0:T(8,128)(2,1)S(1)}, bf16[3,384,128]{2,1,0:T(8,128)(2,1)S(1)}, u32[]{:S(2)}, u32[]{:S(2)}) collective-permute-start(bf16[3,384,128]{2,1,0:T(8,128)(2,1)S(1)} %collective-permute-done.6.refs_3_), channel_id=1, source_target_pairs={{0,1},{1,0},{2,3},{3,2},{4,5},{5,4},{6,7},{7,6},{8,9},{9,8},{10,11... | collective-permute-start | bytes 884744 | tf_op jit(solution)/shard_map/ppermute | solution.py:504
  54.8 5.8 %collective-permute-start.11 = (bf16[384,128]{1,0:T(8,128)(2,1)S(1)}, bf16[384,128]{1,0:T(8,128)(2,1)S(1)}, u32[]{:S(2)}, u32[]{:S(2)}) collective-permute-start(bf16[384,128]{1,0:T(8,128)(2,1)S(1)} %get-tuple-element.31), channel_id=1, source_target_pairs={{0,0},{24,1},{2,2},{26,3},{8,8},{16,9},{10,10},{18,11},{12,12},{20... | collective-permute-start | bytes 294920 | tf_op jit(solution)/shard_map/ppermute | solution.py:507
  55.5 5.2 %collective-permute-start.12 = (bf16[384,128]{1,0:T(8,128)(2,1)S(1)}, bf16[384,128]{1,0:T(8,128)(2,1)S(1)}, u32[]{:S(2)}, u32[]{:S(2)}) collective-permute-start(bf16[384,128]{1,0:T(8,128)(2,1)S(1)} %get-tuple-element.32), channel_id=1, source_target_pairs={{0,4},{24,5},{2,6},{26,7},{12,8},{20,9},{14,10},{22,11},{8,12},{16... | collective-permute-start | bytes 294920 | tf_op jit(solution)/shard_map/ppermute | solution.py:507
  56.8 8.2 %collective-permute-start.13 = (bf16[384,128]{1,0:T(8,128)(2,1)S(1)}, bf16[384,128]{1,0:T(8,128)(2,1)S(1)}, u32[]{:S(2)}, u32[]{:S(2)}) collective-permute-start(bf16[384,128]{1,0:T(8,128)(2,1)S(1)} %get-tuple-element.33), channel_id=1, source_target_pairs={{8,0},{16,1},{10,2},{18,3},{12,4},{20,5},{14,6},{22,7},{0,8},{24,9... | collective-permute-start | bytes 294920 | tf_op jit(solution)/shard_map/ppermute | solution.py:507
  58.7 7.4 %collective-permute-start.14 = (bf16[384,128]{1,0:T(8,128)(2,1)S(1)}, bf16[384,128]{1,0:T(8,128)(2,1)S(1)}, u32[]{:S(2)}, u32[]{:S(2)}) collective-permute-start(bf16[384,128]{1,0:T(8,128)(2,1)S(1)} %get-tuple-element.34), channel_id=1, source_target_pairs={{12,0},{20,1},{14,2},{22,3},{8,4},{16,5},{10,6},{18,7},{0,12},{24,... | collective-permute-start | bytes 294920 | tf_op jit(solution)/shard_map/ppermute | solution.py:507
  66.6 5.2 %collective-permute-start.15 = (bf16[3,192,128]{2,1,0:T(8,128)(2,1)S(1)}, bf16[3,192,128]{2,1,0:T(8,128)(2,1)S(1)}, u32[]{:S(2)}, u32[]{:S(2)}) collective-permute-start(bf16[3,192,128]{2,1,0:T(8,128)(2,1)S(1)} %get-tuple-element.36), channel_id=1, source_target_pairs={{0,2},{2,0},{4,6},{6,4},{8,10},{10,8},{12,14},{14,12},{16,18},{18,... | collective-permute-start | bytes 442376 | tf_op jit(solution)/shard_map/ppermute | solution.py:510
  72.4 4.3 %collective-permute-start.16 = (bf16[192,768]{1,0:T(8,128)(2,1)S(1)}, bf16[192,768]{1,0:T(8,128)(2,1)S(1)}, u32[]{:S(2)}, u32[]{:S(2)}) collective-permute-start(bf16[192,768]{1,0:T(8,128)(2,1)S(1)} %get-tuple-element.38), channel_id=1, source_target_pairs={{0,1},{1,0},{2,3},{3,2},{4,5},{5,4},{6,7},{7,6},{8,9},{9,8},{10,11... | collective-permute-start | bytes 884744 | tf_op jit(solution)/shard_map/ppermute | solution.py:511
